TPU v7x, 32 devices: a whole 2x2x4 slice. The times are simulated.
32 devices in a mesh: sweep: 4 (over z), plane: 8 (over y, x, core).
Axes of the slice: x: 2, y: 2, z: 4, core: 2. Of those that a mesh axis runs over, the one named last changes fastest.
Arguments:
- rhs_field: float32 [8, 2, 8, 8192], P('sweep', None, None, 'plane'), may hold values from -6 to 6
- front_inverse: bfloat16 [8, 2, 4096, 4096], P('sweep', None, 'plane'), may hold values from -1.5 to 1.5
- interior_scale: float32 [8, 8192], P('sweep', 'plane'), may hold values from 0.7 to 1.2
- forward_coupling: float32 [8, 8192], P('sweep', 'plane'), may hold values from 0.85 to 1
- backward_coupling: float32 [8, 8192], P('sweep', 'plane'), may hold values from 0.85 to 1
- front_cells: int32 [8, 4096], P('sweep', 'plane'), may hold values from 0 to 1023, as said below
- section_layers: int32 [4], replicated, may hold values from 1 to 2, 6 in all
Outputs:
- sweep_out: float32 [8, 2, 8, 8192], P('sweep', None, None, 'plane')
Inputs may be any that keep to these rules, and one draw needn't show every extreme that they name: `front_cells`: entry f of a layer indexes a cell within the brick of device f // 512 of plane; the 512 entries of one layer and device are distinct, and the two layers of one section name disjoint cells on every device. `section_layers`: A section with 1 has no second layer.
All inputs are finite; a program needn't handle non-finite values.
Results may differ from a plain program's by a relative error of at most 0.0044.
Values may be sent and summed in bfloat16 or wider, within the bound.
No kernel may reach another device: no remote copies, remote signals or barrier semaphores. Data moves between devices by JAX's collectives and lax.ppermute only.
A program may use at most 64 MiB of HBM per device.

v0:
```python
import jax
import jax.numpy as jnp
from jax import lax
from jax.sharding import PartitionSpec as P


def from_behind(block, axis, distance):
    devices = range(lax.axis_size(axis))
    route = [(i - distance, i) for i in devices if i - distance in devices]
    return lax.ppermute(block, axis, route)


def select_cells(layer_field, picked):
    return jnp.take(layer_field, picked, axis=2)


def place_cells(layer_field, picked, values):
    return layer_field.at[:, :, picked].set(values)


def front_solve(pieces, inverse):
    layer_slots, parts_count, columns_count, owned = pieces.shape
    doubled = parts_count * columns_count
    shard_piece = lax.all_gather(pieces, "plane", axis=3, tiled=True)
    number = shard_piece.shape[3]
    stacked = shard_piece.reshape(layer_slots, doubled, number)
    direct = jnp.einsum("sin,srn->sri", inverse[:, 0], stacked, preferred_element_type=jnp.float32)
    crossed = jnp.einsum("sin,srn->sri", inverse[:, 1], stacked, preferred_element_type=jnp.float32)
    real_part = direct[:, :columns_count] - crossed[:, columns_count:]
    imag_part = direct[:, columns_count:] + crossed[:, :columns_count]
    return jnp.stack([real_part, imag_part], axis=1)


def forward_section(sources, incoming, inverse, interior, coupling, picked, active):
    first_res = sources[0] - coupling[0] * incoming
    first_local = interior[0] * first_res
    second_trial = sources[1] - coupling[1] * first_local
    pieces = jnp.stack(
        [select_cells(first_res, picked[0]), select_cells(second_trial, picked[1])]
    ).astype(jnp.bfloat16)
    solved = front_solve(pieces, inverse)
    first_sol = place_cells(first_local, picked[0], solved[0])
    second_res = sources[1] - coupling[1] * first_sol
    second_sol = place_cells(interior[1] * second_res, picked[1], solved[1])
    outgoing = jnp.where(active, second_sol, first_sol)
    return (jnp.stack([first_sol, second_sol]), outgoing)


def backward_section(forward_part, incoming, inverse, interior, coupling, picked, active):
    first_fwd = forward_part[0]
    second_fwd = forward_part[1]
    second_z = coupling[1] * incoming
    second_local = second_fwd - interior[1] * second_z
    first_trial = coupling[0] * jnp.where(active, second_local, incoming)
    pieces = jnp.stack(
        [select_cells(first_trial, picked[0]), select_cells(second_z, picked[1])]
    ).astype(jnp.bfloat16)
    solved = front_solve(pieces, inverse)
    second_sol = place_cells(
        second_local, picked[1], select_cells(second_fwd, picked[1]) - solved[1]
    )
    first_z = coupling[0] * jnp.where(active, second_sol, incoming)
    first_sol = place_cells(
        first_fwd - interior[0] * first_z, picked[0], select_cells(first_fwd, picked[0]) - solved[0]
    )
    return (jnp.stack([first_sol, jnp.where(active, second_sol, 0.0)]), first_sol)


def forward_send(outgoing):
    return from_behind(outgoing, "sweep", 1)


def backward_send(outgoing):
    return from_behind(outgoing, "sweep", -1)


def run_chain(section_step, passer, chain_rank, inputs, batch_width, sections):
    total_cols = inputs.shape[2]
    batches = total_cols // batch_width
    result = jnp.zeros(inputs.shape, jnp.float32)
    incoming = jnp.zeros((inputs.shape[1], batch_width, inputs.shape[3]), jnp.float32)

    def segment_step(segment_index, loop_state):
        arriving, gathered = loop_state
        batch_index = segment_index - chain_rank
        in_range = (batch_index >= 0) & (batch_index < batches)
        values, outgoing = section_step(inputs, arriving)
        previous = gathered
        gathered = jnp.where(in_range, values, previous)
        return (passer(outgoing), gathered)

    finished, result = lax.fori_loop(0, sections + batches - 1, segment_step, (incoming, result))
    return result


def shards(
    rhs_field,
    front_inverse,
    interior_scale,
    forward_coupling,
    backward_coupling,
    front_cells,
    section_layers,
):
    sections = lax.axis_size("sweep")
    own_index = lax.axis_index("sweep")
    active = section_layers[own_index] == 2
    total_cols = rhs_field.shape[2]
    forward_result = run_chain(
        lambda window, incoming: forward_section(
            window, incoming, front_inverse, interior_scale, forward_coupling, front_cells, active
        ),
        forward_send,
        own_index,
        rhs_field,
        total_cols,
        sections,
    )
    return run_chain(
        lambda window, incoming: backward_section(
            window, incoming, front_inverse, interior_scale, backward_coupling, front_cells, active
        ),
        backward_send,
        sections - 1 - own_index,
        forward_result,
        total_cols,
        sections,
    )


def solution(mesh):
    in_specs = (
        P("sweep", None, None, "plane"),
        P("sweep", None, "plane", None),
        P("sweep", "plane"),
        P("sweep", "plane"),
        P("sweep", "plane"),
        P("sweep", "plane"),
        P(),
    )
    out_specs = P("sweep", None, None, "plane")
    return jax.shard_map(shards, mesh=mesh, in_specs=in_specs, out_specs=out_specs, check_vma=False)
```

profile of v0, /device:TPU:0, one launch (start us, length us, event | category | flops | bytes accessed | tf_op | source)
XLA Modules:
  0.0 556.1 jit_solution(1584699018965920461)
XLA Ops:
  1.9 14.0 %copy.138 = bf16[2,2,512,4096]{3,2,0,1:T(8,128)(2,1)} copy(bf16[2,2,512,4096]{3,2,1,0:T(8,128)(2,1)} %param.14) | data formatting | bytes 33554432
  16.0 264.9 %while.33 = (s32[]{:T(128)}, f32[2,8,1024]{2,1,0:T(8,128)S(1)}, f32[2,2,8,1024]{3,2,1,0:T(8,128)S(1)}, pred[]{:T(512)}, f32[2,1024]{1,0:T(2,128)S(1)}, /*index=5...) while((s32[]{:T(128)}, f32[2,8,1024]{2,1,0:T(8,128)S(1)}, ...), condition=%wide.region_3.0_spmd.clone, body=%wide.region_0.4_spmd.clone.sunk | while | flops 268793856 | bytes 21043400 | solution.py:92
  25.7 10.8 %all_gather.19 = bf16[2,2,8,4096]{3,2,1,0:T(8,128)(2,1)S(1)} all-gather(bf16[2,2,8,512]{3,2,1,0:T(8,128)(2,1)S(1)} %pad_maximum_fusion.6), channel_id=1, replica_groups=mesh['sweep'=4,'plane'=8] {'plane'}, dimensions={3}, use_global_device_ids=true | all-gather | bytes 294912 | tf_op jit(solution)/shard_map/while/body/eval_jaxpr/all_gather | solution.py:24
  48.6 13.6 %scatter_fusion = f32[2,8,1024]{1,0,2:T(2,128)S(1)} fusion(f32[2,8,1024]{1,0,2:T(2,128)S(1)} %copy.167, s32[512]{0:T(512)S(1)} %bitcast.256, f32[512,2,8]{2,1,0:T(2,128)S(1)} %copy.172), kind=kCustom, calls=%fused_computation.6.clone.clone.1 | custom fusion | bytes 100352 | tf_op jit(solution)/shard_map/while/body/eval_jaxpr/scatter | solution.py:18
  63.4 13.6 %scatter_fusion.1 = f32[2,8,1024]{1,0,2:T(2,128)S(1)} fusion(f32[2,8,1024]{1,0,2:T(2,128)S(1)} %copy.174, s32[512]{0:T(512)S(1)} %bitcast.255, f32[512,2,8]{2,1,0:T(2,128)S(1)} %copy.175), kind=kCustom, calls=%fused_computation.7.clone.clone.1 | custom fusion | bytes 100352 | tf_op jit(solution)/shard_map/while/body/eval_jaxpr/scatter | solution.py:18
  92.6 9.3 %all_gather.19 = bf16[2,2,8,4096]{3,2,1,0:T(8,128)(2,1)S(1)} all-gather(bf16[2,2,8,512]{3,2,1,0:T(8,128)(2,1)S(1)} %pad_maximum_fusion.6), channel_id=1, replica_groups=mesh['sweep'=4,'plane'=8] {'plane'}, dimensions={3}, use_global_device_ids=true | all-gather | bytes 294912 | tf_op jit(solution)/shard_map/while/body/eval_jaxpr/all_gather | solution.py:24
  114.1 13.6 %scatter_fusion = f32[2,8,1024]{1,0,2:T(2,128)S(1)} fusion(f32[2,8,1024]{1,0,2:T(2,128)S(1)} %copy.167, s32[512]{0:T(512)S(1)} %bitcast.256, f32[512,2,8]{2,1,0:T(2,128)S(1)} %copy.172), kind=kCustom, calls=%fused_computation.6.clone.clone.1 | custom fusion | bytes 100352 | tf_op jit(solution)/shard_map/while/body/eval_jaxpr/scatter | solution.py:18
  128.9 13.6 %scatter_fusion.1 = f32[2,8,1024]{1,0,2:T(2,128)S(1)} fusion(f32[2,8,1024]{1,0,2:T(2,128)S(1)} %copy.174, s32[512]{0:T(512)S(1)} %bitcast.255, f32[512,2,8]{2,1,0:T(2,128)S(1)} %copy.175), kind=kCustom, calls=%fused_computation.7.clone.clone.1 | custom fusion | bytes 100352 | tf_op jit(solution)/shard_map/while/body/eval_jaxpr/scatter | solution.py:18
  179.4 13.6 %scatter_fusion = f32[2,8,1024]{1,0,2:T(2,128)S(1)} fusion(f32[2,8,1024]{1,0,2:T(2,128)S(1)} %copy.167, s32[512]{0:T(512)S(1)} %bitcast.256, f32[512,2,8]{2,1,0:T(2,128)S(1)} %copy.172), kind=kCustom, calls=%fused_computation.6.clone.clone.1 | custom fusion | bytes 100352 | tf_op jit(solution)/shard_map/while/body/eval_jaxpr/scatter | solution.py:18
  194.2 13.6 %scatter_fusion.1 = f32[2,8,1024]{1,0,2:T(2,128)S(1)} fusion(f32[2,8,1024]{1,0,2:T(2,128)S(1)} %copy.174, s32[512]{0:T(512)S(1)} %bitcast.255, f32[512,2,8]{2,1,0:T(2,128)S(1)} %copy.175), kind=kCustom, calls=%fused_computation.7.clone.clone.1 | custom fusion | bytes 100352 | tf_op jit(solution)/shard_map/while/body/eval_jaxpr/scatter | solution.py:18
  224.3 9.3 %all_gather.19 = bf16[2,2,8,4096]{3,2,1,0:T(8,128)(2,1)S(1)} all-gather(bf16[2,2,8,512]{3,2,1,0:T(8,128)(2,1)S(1)} %pad_maximum_fusion.6), channel_id=1, replica_groups=mesh['sweep'=4,'plane'=8] {'plane'}, dimensions={3}, use_global_device_ids=true | all-gather | bytes 294912 | tf_op jit(solution)/shard_map/while/body/eval_jaxpr/all_gather | solution.py:24
  245.7 13.6 %scatter_fusion = f32[2,8,1024]{1,0,2:T(2,128)S(1)} fusion(f32[2,8,1024]{1,0,2:T(2,128)S(1)} %copy.167, s32[512]{0:T(512)S(1)} %bitcast.256, f32[512,2,8]{2,1,0:T(2,128)S(1)} %copy.172), kind=kCustom, calls=%fused_computation.6.clone.clone.1 | custom fusion | bytes 100352 | tf_op jit(solution)/shard_map/while/body/eval_jaxpr/scatter | solution.py:18
  260.5 13.6 %scatter_fusion.1 = f32[2,8,1024]{1,0,2:T(2,128)S(1)} fusion(f32[2,8,1024]{1,0,2:T(2,128)S(1)} %copy.174, s32[512]{0:T(512)S(1)} %bitcast.255, f32[512,2,8]{2,1,0:T(2,128)S(1)} %copy.175), kind=kCustom, calls=%fused_computation.7.clone.clone.1 | custom fusion | bytes 100352 | tf_op jit(solution)/shard_map/while/body/eval_jaxpr/scatter | solution.py:18
  291.9 263.6 %while.34 = (s32[]{:T(128)}, f32[2,8,1024]{2,1,0:T(8,128)S(1)}, f32[2,2,8,1024]{3,2,1,0:T(8,128)S(1)}, f32[2,2,8,1024]{3,2,1,0:T(8,128)S(1)}, f32[2,1024]{1,0:T(...) while((s32[]{:T(128)}, f32[2,8,1024]{2,1,0:T(8,128)S(1)}, ...), condition=%wide.region_7.9_spmd.clone, body=%wide.region_4.8_spmd.clone.sunk | while | flops 268826624 | bytes 20846808 | solution.py:92
  322.1 13.6 %scatter_fusion.2 = f32[2,8,1024]{1,0,2:T(2,128)S(1)} fusion(f32[2,8,1024]{1,0,2:T(2,128)S(1)} %copy.179, s32[512]{0:T(512)S(1)} %bitcast.257, f32[512,2,8]{2,1,0:T(2,128)S(1)} %copy.184), kind=kCustom, calls=%fused_computation.8.clone.clone.1 | custom fusion | bytes 100352 | tf_op jit(solution)/shard_map/while/body/eval_jaxpr/scatter | solution.py:18
  336.9 13.6 %scatter_fusion.3 = f32[2,8,1024]{1,0,2:T(2,128)S(1)} fusion(f32[2,8,1024]{1,0,2:T(2,128)S(1)} %copy.186, s32[512]{0:T(512)S(1)} %bitcast.254, f32[512,2,8]{2,1,0:T(2,128)S(1)} %copy.187), kind=kCustom, calls=%fused_computation.9.clone.clone.1 | custom fusion | bytes 100352 | tf_op jit(solution)/shard_map/while/body/eval_jaxpr/scatter | solution.py:18
  367.6 9.3 %all_gather.20 = bf16[2,2,8,4096]{3,2,1,0:T(8,128)(2,1)S(1)} all-gather(bf16[2,2,8,512]{3,2,1,0:T(8,128)(2,1)S(1)} %pad_maximum_fusion.7), channel_id=1, replica_groups=mesh['sweep'=4,'plane'=8] {'plane'}, dimensions={3}, use_global_device_ids=true | all-gather | bytes 294912 | tf_op jit(solution)/shard_map/while/body/eval_jaxpr/all_gather | solution.py:24
  389.0 13.6 %scatter_fusion.2 = f32[2,8,1024]{1,0,2:T(2,128)S(1)} fusion(f32[2,8,1024]{1,0,2:T(2,128)S(1)} %copy.179, s32[512]{0:T(512)S(1)} %bitcast.257, f32[512,2,8]{2,1,0:T(2,128)S(1)} %copy.184), kind=kCustom, calls=%fused_computation.8.clone.clone.1 | custom fusion | bytes 100352 | tf_op jit(solution)/shard_map/while/body/eval_jaxpr/scatter | solution.py:18
  403.8 13.6 %scatter_fusion.3 = f32[2,8,1024]{1,0,2:T(2,128)S(1)} fusion(f32[2,8,1024]{1,0,2:T(2,128)S(1)} %copy.186, s32[512]{0:T(512)S(1)} %bitcast.254, f32[512,2,8]{2,1,0:T(2,128)S(1)} %copy.187), kind=kCustom, calls=%fused_computation.9.clone.clone.1 | custom fusion | bytes 100352 | tf_op jit(solution)/shard_map/while/body/eval_jaxpr/scatter | solution.py:18
  454.3 13.6 %scatter_fusion.2 = f32[2,8,1024]{1,0,2:T(2,128)S(1)} fusion(f32[2,8,1024]{1,0,2:T(2,128)S(1)} %copy.179, s32[512]{0:T(512)S(1)} %bitcast.257, f32[512,2,8]{2,1,0:T(2,128)S(1)} %copy.184), kind=kCustom, calls=%fused_computation.8.clone.clone.1 | custom fusion | bytes 100352 | tf_op jit(solution)/shard_map/while/body/eval_jaxpr/scatter | solution.py:18
  469.1 13.6 %scatter_fusion.3 = f32[2,8,1024]{1,0,2:T(2,128)S(1)} fusion(f32[2,8,1024]{1,0,2:T(2,128)S(1)} %copy.186, s32[512]{0:T(512)S(1)} %bitcast.254, f32[512,2,8]{2,1,0:T(2,128)S(1)} %copy.187), kind=kCustom, calls=%fused_computation.9.clone.clone.1 | custom fusion | bytes 100352 | tf_op jit(solution)/shard_map/while/body/eval_jaxpr/scatter | solution.py:18
  499.0 9.3 %all_gather.20 = bf16[2,2,8,4096]{3,2,1,0:T(8,128)(2,1)S(1)} all-gather(bf16[2,2,8,512]{3,2,1,0:T(8,128)(2,1)S(1)} %pad_maximum_fusion.7), channel_id=1, replica_groups=mesh['sweep'=4,'plane'=8] {'plane'}, dimensions={3}, use_global_device_ids=true | all-gather | bytes 294912 | tf_op jit(solution)/shard_map/while/body/eval_jaxpr/all_gather | solution.py:24
  520.4 13.6 %scatter_fusion.2 = f32[2,8,1024]{1,0,2:T(2,128)S(1)} fusion(f32[2,8,1024]{1,0,2:T(2,128)S(1)} %copy.179, s32[512]{0:T(512)S(1)} %bitcast.257, f32[512,2,8]{2,1,0:T(2,128)S(1)} %copy.184), kind=kCustom, calls=%fused_computation.8.clone.clone.1 | custom fusion | bytes 100352 | tf_op jit(solution)/shard_map/while/body/eval_jaxpr/scatter | solution.py:18
  535.2 13.6 %scatter_fusion.3 = f32[2,8,1024]{1,0,2:T(2,128)S(1)} fusion(f32[2,8,1024]{1,0,2:T(2,128)S(1)} %copy.186, s32[512]{0:T(512)S(1)} %bitcast.254, f32[512,2,8]{2,1,0:T(2,128)S(1)} %copy.187), kind=kCustom, calls=%fused_computation.9.clone.clone.1 | custom fusion | bytes 100352 | tf_op jit(solution)/shard_map/while/body/eval_jaxpr/scatter | solution.py:18
  (311 shorter events, 274.7 us)
Async XLA Ops:
  1.9 14.1 %copy-start = (f32[2,2,8,1024]{3,2,1,0:T(8,128)S(1)}, f32[2,2,8,1024]{3,2,1,0:T(8,128)}, u32[]{:S(2)}) copy-start(f32[2,2,8,1024]{3,2,1,0:T(8,128)} %param.13) | copy-start | bytes 393220
  1.9 14.1 %copy-start.2 = (s32[2,512]{1,0:T(2,128)S(1)}, s32[2,512]{1,0:T(2,128)}, u32[]{:S(2)}) copy-start(s32[2,512]{1,0:T(2,128)} %param.18) | copy-start | bytes 12292
  1.9 14.1 %copy-start.3 = (f32[2,1024]{1,0:T(2,128)S(1)}, f32[2,1024]{1,0:T(2,128)}, u32[]{:S(2)}) copy-start(f32[2,1024]{1,0:T(2,128)} %param.15) | copy-start | bytes 24580
  77.6 5.4 collective-permute-start
  143.0 6.2 %collective-permute-start = (f32[2,8,1024]{2,1,0:T(8,128)S(1)}, f32[2,8,1024]{2,1,0:T(8,128)S(1)}, u32[]{:S(2)}, u32[]{:S(2)}) collective-permute-start(f32[2,8,1024]{2,1,0:T(8,128)S(1)} %copy.176), channel_id=1, source_target_pairs={{0,8},{8,16},{16,24},{1,9},{9,17},{17,25},{2,10},{10,18},{18,26},{... | collective-permute-start | bytes 196616 | tf_op jit(solution)/shard_map/while/body/eval_jaxpr/ppermute | solution.py:10
  208.3 6.2 %collective-permute-start = (f32[2,8,1024]{2,1,0:T(8,128)S(1)}, f32[2,8,1024]{2,1,0:T(8,128)S(1)}, u32[]{:S(2)}, u32[]{:S(2)}) collective-permute-start(f32[2,8,1024]{2,1,0:T(8,128)S(1)} %copy.176), channel_id=1, source_target_pairs={{0,8},{8,16},{16,24},{1,9},{9,17},{17,25},{2,10},{10,18},{18,26},{... | collective-permute-start | bytes 196616 | tf_op jit(solution)/shard_map/while/body/eval_jaxpr/ppermute | solution.py:10
  274.6 6.2 %collective-permute-start = (f32[2,8,1024]{2,1,0:T(8,128)S(1)}, f32[2,8,1024]{2,1,0:T(8,128)S(1)}, u32[]{:S(2)}, u32[]{:S(2)}) collective-permute-start(f32[2,8,1024]{2,1,0:T(8,128)S(1)} %copy.176), channel_id=1, source_target_pairs={{0,8},{8,16},{16,24},{1,9},{9,17},{17,25},{2,10},{10,18},{18,26},{... | collective-permute-start | bytes 196616 | tf_op jit(solution)/shard_map/while/body/eval_jaxpr/ppermute | solution.py:10
  350.9 6.9 %collective-permute-start.1 = (f32[2,8,1024]{2,1,0:T(8,128)S(1)}, f32[2,8,1024]{2,1,0:T(8,128)S(1)}, u32[]{:S(2)}, u32[]{:S(2)}) collective-permute-start(f32[2,8,1024]{2,1,0:T(8,128)S(1)} %copy.188), channel_id=1, source_target_pairs={{8,0},{16,8},{24,16},{9,1},{17,9},{25,17},{10,2},{18,10},{26,18},{... | collective-permute-start | bytes 196616 | tf_op jit(solution)/shard_map/while/body/eval_jaxpr/ppermute | solution.py:10
  417.8 6.2 %collective-permute-start.1 = (f32[2,8,1024]{2,1,0:T(8,128)S(1)}, f32[2,8,1024]{2,1,0:T(8,128)S(1)}, u32[]{:S(2)}, u32[]{:S(2)}) collective-permute-start(f32[2,8,1024]{2,1,0:T(8,128)S(1)} %copy.188), channel_id=1, source_target_pairs={{8,0},{16,8},{24,16},{9,1},{17,9},{25,17},{10,2},{18,10},{26,18},{... | collective-permute-start | bytes 196616 | tf_op jit(solution)/shard_map/while/body/eval_jaxpr/ppermute | solution.py:10
  483.0 6.2 %collective-permute-start.1 = (f32[2,8,1024]{2,1,0:T(8,128)S(1)}, f32[2,8,1024]{2,1,0:T(8,128)S(1)}, u32[]{:S(2)}, u32[]{:S(2)}) collective-permute-start(f32[2,8,1024]{2,1,0:T(8,128)S(1)} %copy.188), channel_id=1, source_target_pairs={{8,0},{16,8},{24,16},{9,1},{17,9},{25,17},{10,2},{18,10},{26,18},{... | collective-permute-start | bytes 196616 | tf_op jit(solution)/shard_map/while/body/eval_jaxpr/ppermute | solution.py:10
  549.2 6.2 %collective-permute-start.1 = (f32[2,8,1024]{2,1,0:T(8,128)S(1)}, f32[2,8,1024]{2,1,0:T(8,128)S(1)}, u32[]{:S(2)}, u32[]{:S(2)}) collective-permute-start(f32[2,8,1024]{2,1,0:T(8,128)S(1)} %copy.188), channel_id=1, source_target_pairs={{8,0},{16,8},{24,16},{9,1},{17,9},{25,17},{10,2},{18,10},{26,18},{... | collective-permute-start | bytes 196616 | tf_op jit(solution)/shard_map/while/body/eval_jaxpr/ppermute | solution.py:10
  555.5 0.7 copy-start.1
where the time goes:
time: 558 us; the launch traced here: 556 us
  local copies, waits for them, and re-layouts  313 us (56%)
  matrix products  90.4 us (16%)
  blocking collectives  72.9 us (13%)
  other arithmetic  33.7 us (6%)
  waiting for transfers between devices  22.5 us (4%)
  starting transfers between devices  21.7 us (4%)
    scatter x28, local copies, waits for them, and re-layouts, place_cells(): return layer_field.at[:, :, picked].set(values)  222 us
    all_gather x8, blocking collectives, front_solve(): shard_piece = lax.all_gather(pieces, 'plane', axis=3, tiled=True)  72.9 us
    dot_general x8, matrix products, front_solve(): jnp.einsum('sin,srn->sri', inverse[:, 0], stacked, preferred_element_type...  45.3 us
    dot_general x8, matrix products, front_solve(): jnp.einsum('sin,srn->sri', inverse[:, 1], stacked, preferred_element_type...  45.1 us
    gather x18, local copies, waits for them, and re-layouts, select_cells(): return jnp.take(layer_field, picked, axis=2)  38.6 us
    ppermute x8, waiting for transfers between devices, from_behind(): return lax.ppermute(block, axis, route)  22.5 us
    ppermute x8, starting transfers between devices, from_behind(): return lax.ppermute(block, axis, route)  21.7 us
    unnamed x11, local copies, waits for them, and re-layouts  15.1 us
  transfers between devices with their start and end apart: 8, of which 8 were waited for; matrix products, arithmetic and copies ran while one was open for 1% of the time, Pallas kernels for 0%

commit v1 on v0

v1 whole, which is shorter than its diff:
```python
import functools

import jax
import jax.numpy as jnp
from jax import lax
from jax.experimental import pallas as pl
from jax.experimental.pallas import tpu as pltpu
from jax.sharding import PartitionSpec as P

LANES = 128
ISC, FWD, BWD, PICK = 0, 2, 4, 6
F32, BF16 = jnp.float32, jnp.bfloat16


def split(field):
    return [field[:, at:at + LANES] for at in range(0, field.shape[1], LANES)]


def gather_lanes(chunks, index, beyond=None):
    result = []
    for place, part in enumerate(split(index)):
        part = jnp.broadcast_to(part, chunks[0].shape)
        lane, chunk = part & (LANES - 1), part >> (LANES.bit_length() - 1)
        total = jnp.zeros(chunks[0].shape, F32) if beyond is None else beyond[place]
        for number, source in enumerate(chunks):
            found = jnp.take_along_axis(source, lane, axis=1, mode="promise_in_bounds")
            total = jnp.where(chunk == number, found, total)
        result.append(total)
    return result


def scaled(row, chunks):
    return [part * chunk for part, chunk in zip(split(row), chunks)]


def minus(left, right):
    return [a - b for a, b in zip(left, right)]


def choose(flag, left, right):
    return [jnp.where(flag, a, b) for a, b in zip(left, right)]


def rounded(chunks):
    return [c.astype(BF16).astype(F32) for c in chunks]


def row_of(ref, at):
    return ref[at:at + 1, :]


def picks(ref, at, width):
    return ref[at:at + 1, :width].astype(jnp.int32)


def forward_front(rhs_a, rhs_b, small, incoming, width):
    first = rhs_a if incoming is None else minus(rhs_a, scaled(row_of(small, FWD), incoming))
    second = minus(rhs_b, scaled(row_of(small, FWD + 1), scaled(row_of(small, ISC), first)))
    return (
        gather_lanes(rounded(first), picks(small, PICK, width))
        + gather_lanes(rounded(second), picks(small, PICK + 1, width))
    )


def backward_front(small, incoming, second_fwd, both, width):
    z = scaled(row_of(small, BWD + 1), incoming)
    local = minus(second_fwd, scaled(row_of(small, ISC + 1), z))
    first = scaled(row_of(small, BWD), choose(both, local, incoming))
    return (
        gather_lanes(rounded(first), picks(small, PICK, width))
        + gather_lanes(rounded(z), picks(small, PICK + 1, width))
    )


def write_packet(ref, fronts, field):
    at = 0
    for chunk in fronts:
        ref[at] = chunk.astype(BF16)
        at += 1
    high = [c.astype(BF16) for c in field]
    low = [(c - h.astype(F32)).astype(BF16) for c, h in zip(field, high)]
    for chunk in high + low:
        ref[at] = chunk
        at += 1


def read_field(ref, start, count):
    return [
        ref[start + i].astype(F32) + ref[start + count + i].astype(F32) for i in range(count)
    ]


def solve(gathered, inverse, stacked, solved, layer):
    owners, slots = gathered.shape[:2]
    per_layer = slots // 2
    half = gathered.shape[2] // 2
    for owner in range(owners):
        for i in range(per_layer):
            at = (owner * per_layer + i) * LANES
            piece = gathered[owner, layer * per_layer + i]
            wide = piece.astype(F32)
            turned = jnp.concatenate([-wide[half:], wide[:half]], axis=0)
            stacked[0, :, at:at + LANES] = piece
            stacked[1, :, at:at + LANES] = turned.astype(BF16)
    dims = (((1,), (1,)), ((), ()))
    out = lax.dot_general(inverse[layer, 0], stacked[0], dims, preferred_element_type=F32)
    out = out + lax.dot_general(inverse[layer, 1], stacked[1], dims, preferred_element_type=F32)
    rows = out.shape[0]
    if rows % LANES:
        out = jnp.concatenate([out, jnp.zeros((-rows % LANES, out.shape[1]), F32)], axis=0)
    solved[layer] = out.T


def places(picked_column, cells):
    rows = picked_column.shape[0]
    cell = lax.broadcasted_iota(jnp.int32, (rows, cells), 1)
    row = lax.broadcasted_iota(jnp.int32, (rows, cells), 0)
    return jnp.max(jnp.where(picked_column == cell, row, -1), axis=0, keepdims=True)


def first_kernel(width, rhs, isc, fwd, bwd, picked, column, packet, small, place, front):
    cells = rhs.shape[-1]
    count = rhs.shape[1]
    small[ISC:ISC + 2, :] = isc[...]
    small[FWD:FWD + 2, :] = fwd[...]
    small[BWD:BWD + 2, :] = bwd[...]
    small[PICK:PICK + 2, :] = jnp.full((2, cells), -1, F32)
    small[PICK:PICK + 2, :width] = picked[...].astype(F32)
    packet[0:count, :] = rhs[0]
    packet[count:2 * count, :] = rhs[1]
    packet[2 * count:, :] = small[...]
    for layer in range(2):
        place[layer:layer + 1, :] = places(column[layer], cells)
    chunks = forward_front(split(rhs[0]), split(rhs[1]), small, None, width)
    for owner in range(front.shape[0]):
        for at, chunk in enumerate(chunks):
            front[owner, at] = chunk.astype(BF16)


def forward_kernel(
    step, sections, width, layers, gathered, inverse, rhs, small, place, after, incoming,
    before, kept, packet, stacked, solved,
):
    own = lax.axis_index("sweep")
    cells = rhs.shape[-1]
    count = cells // LANES
    fronts = 2 * width // LANES
    rows = rhs.shape[1]

    @pl.when(own != step)
    def _():
        kept[...] = before[...]

    @pl.when(own == step)
    def _():
        both = layers[own] == 2
        solve(gathered, inverse, stacked, solved, 0)

        @pl.when(both)
        def _():
            solve(gathered, inverse, stacked, solved, 1)

        arriving = None if step == 0 else read_field(incoming, fronts, count)
        rhs_a, rhs_b = split(rhs[0]), split(rhs[1])
        first_res = rhs_a
        if arriving is not None:
            first_res = minus(rhs_a, scaled(row_of(small, FWD), arriving))
        first = gather_lanes(
            split(solved[0]), place[0:1, :], scaled(row_of(small, ISC), first_res)
        )
        second_res = minus(rhs_b, scaled(row_of(small, FWD + 1), first))
        second = gather_lanes(
            split(solved[1]), place[1:2, :], scaled(row_of(small, ISC + 1), second_res)
        )
        for i in range(count):
            kept[0, :, i * LANES:(i + 1) * LANES] = first[i]
            kept[1, :, i * LANES:(i + 1) * LANES] = second[i]
        if step < sections - 1:
            outgoing = choose(both, second, first)
            ahead = after.at[2 * rows:]
            chunks = forward_front(
                split(after[0:rows, :]), split(after[rows:2 * rows, :]), ahead, outgoing, width
            )
            write_packet(packet, chunks, outgoing)
        else:
            z = scaled(row_of(small, BWD), choose(both, second, [jnp.zeros_like(c) for c in first]))
            chunks = gather_lanes(rounded(z), picks(small, PICK, width))
            for owner in range(packet.shape[0]):
                for at, chunk in enumerate(chunks):
                    packet[owner, at] = chunk.astype(BF16)
                for at in range(len(chunks), fronts):
                    packet[owner, at] = jnp.zeros_like(chunks[0]).astype(BF16)


def backward_kernel(
    step, sections, width, layers, gathered, inverse, small, place, behind, held, kept,
    incoming, before, result, packet, stacked, solved,
):
    own = lax.axis_index("sweep")
    cells = kept.shape[-1]
    count = cells // LANES
    fronts = 2 * width // LANES
    last = step == sections - 1

    @pl.when(own != step)
    def _():
        result[...] = before[...]

    @pl.when(own == step)
    def _():
        both = layers[own] == 2

        def first_solve():
            solve(gathered, inverse, stacked, solved, 0)

        if last:
            pl.when(both)(first_solve)
        else:
            first_solve()

            @pl.when(both)
            def _():
                solve(gathered, inverse, stacked, solved, 1)

        first_fwd, second_fwd = split(kept[0]), split(kept[1])
        zero = [jnp.zeros_like(c) for c in first_fwd]
        if last:
            second, arriving = second_fwd, zero
        else:
            arriving = read_field(incoming, fronts, count)
            z = scaled(row_of(small, BWD + 1), arriving)
            local = scaled(row_of(small, ISC + 1), z)
            second = minus(second_fwd, gather_lanes(split(solved[1]), place[1:2, :], local))
        following = choose(both, second, arriving)
        z = scaled(row_of(small, BWD), following)
        local = scaled(row_of(small, ISC), z)
        change = gather_lanes(split(solved[0]), place[0:1, :], local)
        if last:
            change = choose(both, change, zero)
        first = minus(first_fwd, change)
        second = choose(both, second, zero)
        for i in range(count):
            result[0, :, i * LANES:(i + 1) * LANES] = first[i]
            result[1, :, i * LANES:(i + 1) * LANES] = second[i]
        if step > 0:
            chunks = backward_front(
                behind, first, read_field(held, fronts, count), layers[own - 1] == 2, width
            )
            write_packet(packet, chunks, first)


def whole(space=pltpu.VMEM):
    return pl.BlockSpec(memory_space=space)


def call(kernel, operands, outs, scratch, name):
    specs = [whole(pltpu.SMEM) if o.ndim == 1 else whole() for o in operands]
    return pl.pallas_call(
        kernel,
        in_specs=specs,
        out_specs=[whole()] * len(outs),
        out_shape=[jax.ShapeDtypeStruct(s, t) for s, t in outs],
        scratch_shapes=scratch,
        compiler_params=pltpu.CompilerParams(vmem_limit_bytes=8 * 2**20),
        name=name,
    )(*operands)


def shards(
    rhs_field,
    front_inverse,
    interior_scale,
    forward_coupling,
    backward_coupling,
    front_cells,
    section_layers,
):
    sections, planes = lax.axis_size("sweep"), lax.axis_size("plane")
    layer_slots, parts, columns, cells = rhs_field.shape
    rows = parts * columns
    owned, order = front_inverse.shape[2:]
    width = -(-owned // LANES) * LANES
    count, per_layer = cells // LANES, width // LANES
    fronts = 2 * per_layer

    rhs = rhs_field.reshape(layer_slots, rows, cells)
    picked = jnp.pad(front_cells, ((0, 0), (0, width - owned)), constant_values=-1)
    inverse = pltpu.with_memory_space_constraint(front_inverse, pltpu.VMEM)

    front_shape = ((planes, fronts, rows, LANES), BF16)
    packet_shape = ((fronts + 2 * count, rows, LANES), BF16)
    field_shape = ((layer_slots, rows, cells), F32)
    scratch = [
        pltpu.VMEM((2, rows, order), BF16),
        pltpu.VMEM((2, rows, width), F32),
    ]

    def exchange(spread):
        gathered = lax.all_to_all(spread, "plane", 0, 0)
        if owned != width:
            gathered = gathered.reshape(planes, 2, per_layer, rows, LANES)
            gathered = gathered.transpose(1, 3, 0, 2, 4).reshape(2, rows, planes, width)
            gathered = gathered[..., :owned].reshape(2, rows, order // LANES, LANES)
            gathered = gathered.transpose(0, 2, 1, 3).reshape(1, 2 * order // LANES, rows, LANES)
        return gathered

    def everywhere(packet):
        return jnp.broadcast_to(packet[None, :fronts], front_shape[0])

    packet, small, place, front = call(
        functools.partial(first_kernel, width),
        [rhs, interior_scale, forward_coupling, backward_coupling, picked,
         front_cells[:, :, None]],
        [((2 * rows + 8, cells), F32), ((8, cells), F32), ((2, cells), jnp.int32), front_shape],
        [],
        "first_fronts",
    )
    upward = [(i, i + 1) for i in range(sections - 1)]
    downward = [(i + 1, i) for i in range(sections - 1)]
    after = lax.ppermute(packet, "sweep", downward)
    behind = lax.ppermute(small, "sweep", upward)

    kept = jnp.zeros(field_shape[0], F32)
    held = jnp.zeros(packet_shape[0], BF16)
    incoming = held
    for step in range(sections):
        final = step == sections - 1
        gathered = exchange(front)
        kept, packet = call(
            functools.partial(forward_kernel, step, sections, width),
            [section_layers, gathered, inverse, rhs, small, place, after, incoming, kept],
            [field_shape, front_shape if final else packet_shape],
            scratch,
            f"forward_section_{step}",
        )
        if final:
            front = packet
        else:
            incoming = lax.ppermute(packet, "sweep", [(step, step + 1)])
            held = jnp.where(lax.axis_index("sweep") == step + 1, incoming, held)
            front = everywhere(incoming)

    result = kept
    for step in reversed(range(sections)):
        gathered = exchange(front)
        result, packet = call(
            functools.partial(backward_kernel, step, sections, width),
            [section_layers, gathered, inverse, small, place, behind, held, kept, incoming, result],
            [field_shape, packet_shape],
            scratch,
            f"backward_section_{step}",
        )
        if step:
            incoming = lax.ppermute(packet, "sweep", [(step, step - 1)])
            front = everywhere(incoming)
    return result.reshape(rhs_field.shape)


def solution(mesh):
    in_specs = (
        P("sweep", None, None, "plane"),
        P("sweep", None, "plane", None),
        P("sweep", "plane"),
        P("sweep", "plane"),
        P("sweep", "plane"),
        P("sweep", "plane"),
        P(),
    )
    out_specs = P("sweep", None, None, "plane")
    return jax.shard_map(shards, mesh=mesh, in_specs=in_specs, out_specs=out_specs, check_vma=False)
```

time: 558 us -> 180 us (0.32)
  local copies, waits for them, and re-layouts: 313 us -> 30.2 us
  matrix products: 90.4 us -> 0 us
  other arithmetic: 33.7 us -> 0.02 us
  waiting for transfers between devices: 22.5 us -> 55 us
  blocking collectives: 72.9 us -> 48.5 us
  Pallas kernels: 0 us -> 13.4 us
  starting transfers between devices: 21.7 us -> 32 us
    scatter x28 -> x0, local copies, waits for them, and re-layouts: 222 us -> none  [place_cells(): return layer_field.at[:, :, picked].set(values)]
    dot_general x16 -> x0, matrix products: 90.4 us -> none  [the longest x8 45.3 us: front_solve(): jnp.einsum('sin,srn->sri', inverse[:, 0], stacked, preferred_element_type...]
    all_gather x8 -> x0, blocking collectives: 72.9 us -> none  [front_solve(): shard_piece = lax.all_gather(pieces, 'plane', axis=3, tiled=True)]
    all_to_all x0 -> x5, blocking collectives: none -> 48.5 us  [exchange(): gathered = lax.all_to_all(spread, 'plane', 0, 0)]
    gather x18 -> x0, local copies, waits for them, and re-layouts: 38.6 us -> none  [select_cells(): return jnp.take(layer_field, picked, axis=2)]
    another operation x36 -> x0, other arithmetic: 28.3 us -> none  [the longest x12 14.1 us: forward_section(): jnp.stack([select_cells(first_res, picked[0]), select_cells(second_trial,...]
    ppermute x8, waiting for transfers between devices: 22.5 us -> 48.1 us  [the longest x3 38.6 us: shards(): incoming = lax.ppermute(packet, 'sweep', [(step, step - 1)])]
    pallas_call x0 -> x9, Pallas kernels: none -> 13.4 us  [call(): pl.pallas_call(kernel, in_specs=specs, out_specs=[whole()] * len(outs), o...]
  transfers between devices with their start and end apart: 8 -> 11, of which waited for: 8 -> 4; matrix products, arithmetic and copies ran while one was open for 1% -> 0% of each run, Pallas kernels for 0% -> 1%
where the time goes in v1:
time: 180 us; the launch traced here: 179 us
  waiting for transfers between devices  55 us (31%)
  blocking collectives  48.5 us (27%)
  starting transfers between devices  32 us (18%)
  local copies, waits for them, and re-layouts  30.2 us (17%)
  Pallas kernels  13.4 us (7%)
    all_to_all x5, blocking collectives, exchange(): gathered = lax.all_to_all(spread, 'plane', 0, 0)  48.5 us
    ppermute x3, waiting for transfers between devices, shards(): incoming = lax.ppermute(packet, 'sweep', [(step, step - 1)])  38.6 us
    unnamed x36, local copies, waits for them, and re-layouts  28.3 us
    pallas_call x9, Pallas kernels, call(): pl.pallas_call(kernel, in_specs=specs, out_specs=[whole()] * len(outs), o...  13.4 us
    all_to_all x3, starting transfers between devices, exchange(): gathered = lax.all_to_all(spread, 'plane', 0, 0)  12.7 us
    ppermute x1, starting transfers between devices, shards(): behind = lax.ppermute(small, 'sweep', upward)  12.3 us
    ppermute x1, waiting for transfers between devices, shards(): after = lax.ppermute(packet, 'sweep', downward)  7.2 us
    all_to_all x3, waiting for transfers between devices, exchange(): gathered = lax.all_to_all(spread, 'plane', 0, 0)  6.91 us
  transfers between devices with their start and end apart: 11, of which 4 were waited for; matrix products, arithmetic and copies ran while one was open for 0% of the time, Pallas kernels for 1%

profile of v1, /device:TPU:0, one launch (start us, length us, event | category | flops | bytes accessed | tf_op | source)
XLA Modules:
  0.0 179.5 jit_solution(7354845593552992702)
XLA Ops:
  4.6 1.7 first_fronts.1
  6.4 5.2 %all-to-all-start = ((bf16[8,8,16,128]{3,2,1,0:T(8,128)(2,1)}), bf16[8,8,16,128]{3,2,1,0:T(8,128)(2,1)S(1)}, u32[]{:S(2)}, u32[]{:S(2)}) async-start(bf16[8,8,16,128]{3,2,1,0:T(8,128)(2,1)} %get-tuple-element.24), calls=%async_computation | async-start | bytes 524288 | tf_op jit(solution)/shard_map/all_to_all | solution.py:299
  11.5 1.3 collective-permute-start
  12.8 7.2 %collective-permute-done.after = f32[40,1024]{1,0:T(8,128)S(1)} collective-permute-done((f32[40,1024]{1,0:T(8,128)S(1)}, f32[40,1024]{1,0:T(8,128)S(1)}, u32[]{:S(2)}, u32[]{:S(2)}) %collective-permute-start) | collective-permute-done | bytes 163872 | tf_op jit(solution)/shard_map/ppermute | solution.py:320
  20.1 5.8 %copy-done = bf16[2,2,512,4096]{3,2,1,0:T(8,128)(2,1)S(1)} copy-done((bf16[2,2,512,4096]{3,2,1,0:T(8,128)(2,1)S(1)}, bf16[2,2,512,4096]{3,2,1,0:T(8,128)(2,1)}, u32[]{:S(2)}) %copy-start) | copy-done | bytes 16777240
  27.4 3.3 %forward_section_0.1 = (f32[2,16,1024]{2,1,0:T(8,128)S(1)}, bf16[24,16,128]{2,1,0:T(8,128)(2,1)S(1)}) custom-call(s32[4]{0:T(128)S(1)} %copy-done.8, bf16[8,8,16,128]{3,2,1,0:T(8,128)(2,1)S(1)} %all-to-all-done.gathered, bf16[2,2,512,4096]{3,2,1,0:T(8,128)(2,1)S(1)} %copy-done, f32[2,16,1024]{2,1,0:T(8,128)S(1)} %bitcast.6, ...), custom_call_target="tpu_custom_call" | custom-call | tf_op jit(solution)/shard_map/forward_section_0/pallas_call | solution.py:258
  30.8 1.6 collective-permute-start.1
  32.3 2.2 %collective-permute-done.1.incoming = bf16[24,16,128]{2,1,0:T(8,128)(2,1)S(1)} collective-permute-done((bf16[24,16,128]{2,1,0:T(8,128)(2,1)S(1)}, bf16[24,16,128]{2,1,0:T(8,128)(2,1)S(1)}, u32[]{:S(2)}, u32[]{:S(2)}) %collective-permute-start.1) | collective-permute-done | bytes 98336 | tf_op jit(solution)/shard_map/ppermute | solution.py:339
  34.6 10.6 %all_to_all.40.gathered = bf16[8,8,16,128]{3,2,1,0:T(8,128)(2,1)S(1)} all-to-all(bf16[8,8,16,128]{3,2,1,0:T(8,128)(2,1)S(1)} %broadcast_in_dim.21), channel_id=1, replica_groups=mesh['sweep'=4,'plane'=8] {'plane'}, dimensions={0} | all-to-all | bytes 524288 | tf_op jit(solution)/shard_map/all_to_all | solution.py:299
  46.5 9.3 %all_to_all.41.gathered = bf16[8,8,16,128]{3,2,1,0:T(8,128)(2,1)S(1)} all-to-all(bf16[8,8,16,128]{3,2,1,0:T(8,128)(2,1)S(1)} %broadcast_in_dim.22), channel_id=1, replica_groups=mesh['sweep'=4,'plane'=8] {'plane'}, dimensions={0} | all-to-all | bytes 524288 | tf_op jit(solution)/shard_map/all_to_all | solution.py:299
  58.0 3.4 %all-to-all-start.3 = ((bf16[8,8,16,128]{3,2,1,0:T(8,128)(2,1)}), bf16[8,8,16,128]{3,2,1,0:T(8,128)(2,1)S(1)}, u32[]{:S(2)}, u32[]{:S(2)}) async-start(bf16[8,8,16,128]{3,2,1,0:T(8,128)(2,1)} %broadcast_in_dim.23), calls=%async_computation.3 | async-start | bytes 524288 | tf_op jit(solution)/shard_map/all_to_all | solution.py:299
  61.4 12.3 %collective-permute-start.4 = (f32[8,1024]{1,0:T(8,128)S(1)}, f32[8,1024]{1,0:T(8,128)S(1)}, u32[]{:S(2)}, u32[]{:S(2)}) collective-permute-start(f32[8,1024]{1,0:T(8,128)S(1)} %get-tuple-element.25.small), channel_id=1, source_target_pairs={{0,8},{8,16},{16,24},{1,9},{9,17},{17,25},{2,10},{10,18},{18,26},{... | collective-permute-start | bytes 98312 | tf_op jit(solution)/shard_map/ppermute | solution.py:321
  73.7 5.8 %copy-done.2 = bf16[2,2,512,4096]{3,2,1,0:T(8,128)(2,1)S(1)} copy-done((bf16[2,2,512,4096]{3,2,1,0:T(8,128)(2,1)S(1)}, bf16[2,2,512,4096]{3,2,1,0:T(8,128)(2,1)}, u32[]{:S(2)}) %copy-start.2) | copy-done | bytes 16777240
  79.5 1.3 forward_section_3.1
  80.7 4.1 %all-to-all-start.4 = ((bf16[8,8,16,128]{3,2,1,0:T(8,128)(2,1)}), bf16[8,8,16,128]{3,2,1,0:T(8,128)(2,1)S(1)}, u32[]{:S(2)}, u32[]{:S(2)}) async-start(bf16[8,8,16,128]{3,2,1,0:T(8,128)(2,1)} %get-tuple-element.34), calls=%async_computation.4 | async-start | bytes 524288 | tf_op jit(solution)/shard_map/all_to_all | solution.py:299
  84.9 6.9 %all-to-all-done.4.gathered = bf16[8,8,16,128]{3,2,1,0:T(8,128)(2,1)S(1)} async-done(((bf16[8,8,16,128]{3,2,1,0:T(8,128)(2,1)}), bf16[8,8,16,128]{3,2,1,0:T(8,128)(2,1)S(1)}, u32[]{:S(2)}, u32[]{:S(2)}) %all-to-all-start.4) | async-done | bytes 262176 | tf_op jit(solution)/shard_map/all_to_all | solution.py:299
  91.8 5.8 %copy-done.3 = bf16[2,2,512,4096]{3,2,1,0:T(8,128)(2,1)S(1)} copy-done((bf16[2,2,512,4096]{3,2,1,0:T(8,128)(2,1)S(1)}, bf16[2,2,512,4096]{3,2,1,0:T(8,128)(2,1)}, u32[]{:S(2)}) %copy-start.3) | copy-done | bytes 16777240
  99.0 9.6 %all_to_all.42.gathered = bf16[8,8,16,128]{3,2,1,0:T(8,128)(2,1)S(1)} all-to-all(bf16[8,8,16,128]{3,2,1,0:T(8,128)(2,1)S(1)} %broadcast_in_dim.24), channel_id=1, replica_groups=mesh['sweep'=4,'plane'=8] {'plane'}, dimensions={0} | all-to-all | bytes 524288 | tf_op jit(solution)/shard_map/all_to_all | solution.py:299
  108.6 5.8 %copy-done.4 = bf16[2,2,512,4096]{3,2,1,0:T(8,128)(2,1)S(1)} copy-done((bf16[2,2,512,4096]{3,2,1,0:T(8,128)(2,1)S(1)}, bf16[2,2,512,4096]{3,2,1,0:T(8,128)(2,1)}, u32[]{:S(2)}) %copy-start.4) | copy-done | bytes 16777240
  115.8 9.6 %all_to_all.43.gathered = bf16[8,8,16,128]{3,2,1,0:T(8,128)(2,1)S(1)} all-to-all(bf16[8,8,16,128]{3,2,1,0:T(8,128)(2,1)S(1)} %broadcast_in_dim.25), channel_id=1, replica_groups=mesh['sweep'=4,'plane'=8] {'plane'}, dimensions={0} | all-to-all | bytes 524288 | tf_op jit(solution)/shard_map/all_to_all | solution.py:299
  126.2 1.3 collective-permute-start.7
  127.5 38.6 %collective-permute-done.7.incoming = bf16[24,16,128]{2,1,0:T(8,128)(2,1)S(1)} collective-permute-done((bf16[24,16,128]{2,1,0:T(8,128)(2,1)S(1)}, bf16[24,16,128]{2,1,0:T(8,128)(2,1)S(1)}, u32[]{:S(2)}, u32[]{:S(2)}) %collective-permute-start.7) | collective-permute-done | bytes 98336 | tf_op jit(solution)/shard_map/ppermute | solution.py:354
  166.2 9.3 %all_to_all.44.gathered = bf16[8,8,16,128]{3,2,1,0:T(8,128)(2,1)S(1)} all-to-all(bf16[8,8,16,128]{3,2,1,0:T(8,128)(2,1)S(1)} %broadcast_in_dim.26), channel_id=1, replica_groups=mesh['sweep'=4,'plane'=8] {'plane'}, dimensions={0} | all-to-all | bytes 524288 | tf_op jit(solution)/shard_map/all_to_all | solution.py:299
  175.6 3.9 %backward_section_0.1 = (f32[2,16,1024]{2,1,0:T(8,128)}, bf16[24,16,128]{2,1,0:T(8,128)(2,1)}) custom-call(s32[4]{0:T(128)S(1)} %copy-done.9, bf16[8,8,16,128]{3,2,1,0:T(8,128)(2,1)S(1)} %all_to_all.44.gathered, bf16[2,2,512,4096]{3,2,1,0:T(8,128)(2,1)S(1)} %bitcast.4, f32[8,1024]{1,0:T(8,128)S(1)} %get-tuple-element.25.small, ...), custom_call_target="tpu_custom_call" | custom-call | tf_op jit(solution)/shard_map/backward_section_0/pallas_call | solution.py:258
  (65 shorter events, 13.4 us)
Async XLA Ops:
  0.0 45.1 %copy-start.7 = (f32[2,2,8,1024]{3,2,1,0:T(8,128)S(1)}, f32[2,2,8,1024]{3,2,1,0:T(8,128)}, u32[]{:S(2)}) copy-start(f32[2,2,8,1024]{3,2,1,0:T(8,128)} %param.7) | copy-start | bytes 393220
  0.0 45.1 %copy-start.9 = (s32[4]{0:T(128)S(1)}, s32[4]{0:T(128)}, u32[]{:S(2)}) copy-start(s32[4]{0:T(128)} %layers.15) | copy-start | bytes 52
  0.9 0.9 copy-start.5
  6.4 13.7 %all-to-all-start = ((bf16[8,8,16,128]{3,2,1,0:T(8,128)(2,1)}), bf16[8,8,16,128]{3,2,1,0:T(8,128)(2,1)S(1)}, u32[]{:S(2)}, u32[]{:S(2)}) async-start(bf16[8,8,16,128]{3,2,1,0:T(8,128)(2,1)} %get-tuple-element.24), calls=%async_computation | async-start | bytes 524288 | tf_op jit(solution)/shard_map/all_to_all | solution.py:299
  11.5 8.5 %collective-permute-start = (f32[40,1024]{1,0:T(8,128)S(1)}, f32[40,1024]{1,0:T(8,128)S(1)}, u32[]{:S(2)}, u32[]{:S(2)}) collective-permute-start(f32[40,1024]{1,0:T(8,128)S(1)} %get-tuple-element.27), channel_id=1, source_target_pairs={{8,0},{16,8},{24,16},{9,1},{17,9},{25,17},{10,2},{18,10},{26,18},{... | collective-permute-start | bytes 491528 | tf_op jit(solution)/shard_map/ppermute | solution.py:320
  20.1 5.8 %copy-start = (bf16[2,2,512,4096]{3,2,1,0:T(8,128)(2,1)S(1)}, bf16[2,2,512,4096]{3,2,1,0:T(8,128)(2,1)}, u32[]{:S(2)}) copy-start(bf16[2,2,512,4096]{3,2,1,0:T(8,128)(2,1)} %inverse.15) | copy-start | bytes 50331652
  25.8 0.9 copy-start.6
  27.4 17.7 %copy-start.1 = (bf16[2,2,512,4096]{3,2,1,0:T(8,128)(2,1)S(1)}, bf16[2,2,512,4096]{3,2,1,0:T(8,128)(2,1)}, u32[]{:S(2)}) copy-start(bf16[2,2,512,4096]{3,2,1,0:T(8,128)(2,1)} %inverse.15) | copy-start | bytes 50331652
  30.8 3.8 %collective-permute-start.1 = (bf16[24,16,128]{2,1,0:T(8,128)(2,1)S(1)}, bf16[24,16,128]{2,1,0:T(8,128)(2,1)S(1)}, u32[]{:S(2)}, u32[]{:S(2)}) collective-permute-start(bf16[24,16,128]{2,1,0:T(8,128)(2,1)S(1)} %get-tuple-element.28), channel_id=1, source_target_pairs={{0,8},{1,9},{2,10},{3,11},{4,12},{5,13},{6,14},{7,15}} | collective-permute-start | bytes 294920 | tf_op jit(solution)/shard_map/ppermute | solution.py:339
  45.7 0.7 collective-permute-start.2
  56.6 0.7 collective-permute-start.3
  58.0 15.7 %all-to-all-start.3 = ((bf16[8,8,16,128]{3,2,1,0:T(8,128)(2,1)}), bf16[8,8,16,128]{3,2,1,0:T(8,128)(2,1)S(1)}, u32[]{:S(2)}, u32[]{:S(2)}) async-start(bf16[8,8,16,128]{3,2,1,0:T(8,128)(2,1)} %broadcast_in_dim.23), calls=%async_computation.3 | async-start | bytes 524288 | tf_op jit(solution)/shard_map/all_to_all | solution.py:299
  61.4 23.4 %collective-permute-start.4 = (f32[8,1024]{1,0:T(8,128)S(1)}, f32[8,1024]{1,0:T(8,128)S(1)}, u32[]{:S(2)}, u32[]{:S(2)}) collective-permute-start(f32[8,1024]{1,0:T(8,128)S(1)} %get-tuple-element.25.small), channel_id=1, source_target_pairs={{0,8},{8,16},{16,24},{1,9},{9,17},{17,25},{2,10},{10,18},{18,26},{... | collective-permute-start | bytes 98312 | tf_op jit(solution)/shard_map/ppermute | solution.py:321
  73.7 5.8 %copy-start.2 = (bf16[2,2,512,4096]{3,2,1,0:T(8,128)(2,1)S(1)}, bf16[2,2,512,4096]{3,2,1,0:T(8,128)(2,1)}, u32[]{:S(2)}) copy-start(bf16[2,2,512,4096]{3,2,1,0:T(8,128)(2,1)} %inverse.15) | copy-start | bytes 50331652
  80.7 11.0 %all-to-all-start.4 = ((bf16[8,8,16,128]{3,2,1,0:T(8,128)(2,1)}), bf16[8,8,16,128]{3,2,1,0:T(8,128)(2,1)S(1)}, u32[]{:S(2)}, u32[]{:S(2)}) async-start(bf16[8,8,16,128]{3,2,1,0:T(8,128)(2,1)} %get-tuple-element.34), calls=%async_computation.4 | async-start | bytes 524288 | tf_op jit(solution)/shard_map/all_to_all | solution.py:299
  91.8 5.8 %copy-start.3 = (bf16[2,2,512,4096]{3,2,1,0:T(8,128)(2,1)S(1)}, bf16[2,2,512,4096]{3,2,1,0:T(8,128)(2,1)}, u32[]{:S(2)}) copy-start(bf16[2,2,512,4096]{3,2,1,0:T(8,128)(2,1)} %inverse.15) | copy-start | bytes 50331652
  97.5 27.9 %slice-start = ((s8[16777216]{0:T(1024)(128)(4,1)}), s8[4194304]{0:T(1024)(128)(4,1)S(1)}, s32[]{:S(2)}) async-start(s8[16777216]{0:T(1024)(128)(4,1)} %bitcast.3), calls=%async_computation.8 | async-start | bytes 8388608
  97.5 27.9 %slice-start.1 = ((s8[16777216]{0:T(1024)(128)(4,1)}), s8[4194304]{0:T(1024)(128)(4,1)S(1)}, s32[]{:S(2)}) async-start(s8[16777216]{0:T(1024)(128)(4,1)} %bitcast.3), calls=%async_computation.9 | async-start | bytes 8388608
  98.1 0.8 collective-permute-start.5
  108.6 5.8 %copy-start.4 = (bf16[2,2,512,4096]{3,2,1,0:T(8,128)(2,1)S(1)}, bf16[2,2,512,4096]{3,2,1,0:T(8,128)(2,1)}, u32[]{:S(2)}) copy-start(bf16[2,2,512,4096]{3,2,1,0:T(8,128)(2,1)} %inverse.15) | copy-start | bytes 50331652
  114.4 11.1 %slice-start.2 = ((s8[16777216]{0:T(1024)(128)(4,1)}), s8[4194304]{0:T(1024)(128)(4,1)S(1)}, s32[]{:S(2)}) async-start(s8[16777216]{0:T(1024)(128)(4,1)} %bitcast.3), calls=%async_computation.10 | async-start | bytes 8388608
  114.4 11.1 %slice-start.3 = ((s8[16777216]{0:T(1024)(128)(4,1)}), s8[4194304]{0:T(1024)(128)(4,1)S(1)}, s32[]{:S(2)}) async-start(s8[16777216]{0:T(1024)(128)(4,1)} %bitcast.3), calls=%async_computation.11 | async-start | bytes 8388608
  114.9 0.8 collective-permute-start.6
  126.2 39.9 %collective-permute-start.7 = (bf16[24,16,128]{2,1,0:T(8,128)(2,1)S(1)}, bf16[24,16,128]{2,1,0:T(8,128)(2,1)S(1)}, u32[]{:S(2)}, u32[]{:S(2)}) collective-permute-start(bf16[24,16,128]{2,1,0:T(8,128)(2,1)S(1)} %get-tuple-element.40), channel_id=1, source_target_pairs={{8,0},{9,1},{10,2},{11,3},{12,4},{13,5},{14,6},{15,7}} | collective-permute-start | bytes 294920 | tf_op jit(solution)/shard_map/ppermute | solution.py:354
  (5 other events, 3.4 us)

commit v2 on v1

v2 whole, which is shorter than its diff:
```python
import functools

import jax
import jax.numpy as jnp
from jax import lax
from jax.experimental import pallas as pl
from jax.experimental.pallas import tpu as pltpu
from jax.sharding import PartitionSpec as P

LANES = 128
CORES = 2
ISC, FWD, BWD, PICK = 0, 2, 4, 6
F32, BF16 = jnp.float32, jnp.bfloat16


def split(field):
    return [field[:, at:at + LANES] for at in range(0, field.shape[1], LANES)]


def gather_lanes(chunks, index, beyond=None):
    result = []
    for place, part in enumerate(split(index)):
        part = jnp.broadcast_to(part, chunks[0].shape)
        lane, chunk = part & (LANES - 1), part >> (LANES.bit_length() - 1)
        total = jnp.zeros(chunks[0].shape, F32) if beyond is None else beyond[place]
        for number, source in enumerate(chunks):
            found = jnp.take_along_axis(source, lane, axis=1, mode="promise_in_bounds")
            total = jnp.where(chunk == number, found, total)
        result.append(total)
    return result


def scaled(row, chunks):
    return [part * chunk for part, chunk in zip(split(row), chunks)]


def minus(left, right):
    return [a - b for a, b in zip(left, right)]


def choose(flag, left, right):
    return [jnp.where(flag, a, b) for a, b in zip(left, right)]


def rounded(chunks):
    return [c.astype(BF16).astype(F32) for c in chunks]


def row_of(ref, at):
    return ref[at:at + 1, :]


def picks(ref, at, width):
    return ref[at:at + 1, :width].astype(jnp.int32)


def forward_front(rhs_a, rhs_b, small, incoming, width):
    first = rhs_a if incoming is None else minus(rhs_a, scaled(row_of(small, FWD), incoming))
    second = minus(rhs_b, scaled(row_of(small, FWD + 1), scaled(row_of(small, ISC), first)))
    return (
        gather_lanes(rounded(first), picks(small, PICK, width))
        + gather_lanes(rounded(second), picks(small, PICK + 1, width))
    )


def backward_front(small, incoming, second_fwd, both, width):
    z = scaled(row_of(small, BWD + 1), incoming)
    local = minus(second_fwd, scaled(row_of(small, ISC + 1), z))
    first = scaled(row_of(small, BWD), choose(both, local, incoming))
    return (
        gather_lanes(rounded(first), picks(small, PICK, width))
        + gather_lanes(rounded(z), picks(small, PICK + 1, width))
    )


def write_front(ref, chunks):
    for at, chunk in enumerate(chunks):
        ref[at] = chunk.astype(BF16)
    for at in range(len(chunks), ref.shape[0]):
        ref[at] = jnp.zeros(ref.shape[1:], BF16)


def write_field(ref, chunks):
    for at, chunk in enumerate(chunks):
        ref[:, at * LANES:(at + 1) * LANES] = chunk


def sources(blocks, planes):
    if len(blocks) == 1:
        return [range(blocks[0].shape[0])]
    chips = planes // CORES
    own = lax.axis_index("plane")
    chip, core = own // CORES, lax.rem(own, CORES)
    behind = [lax.rem(chip - step + chips, chips) * CORES for step in range(chips)]
    return [[b + core for b in behind], [b + (CORES - 1 - core) for b in behind]]


def solve(blocks, planes, inverse, stacked, solved, layer):
    for gathered, owners in zip(blocks, sources(blocks, planes)):
        per_layer = gathered.shape[1] // 2
        half = gathered.shape[2] // 2
        for block, owner in enumerate(owners):
            for i in range(per_layer):
                at = pl.multiple_of((owner * per_layer + i) * LANES, LANES)
                piece = gathered[block, layer * per_layer + i]
                wide = piece.astype(F32)
                turned = jnp.concatenate([-wide[half:], wide[:half]], axis=0)
                stacked[0, :, pl.ds(at, LANES)] = piece
                stacked[1, :, pl.ds(at, LANES)] = turned.astype(BF16)
    dims = (((1,), (1,)), ((), ()))
    out = lax.dot_general(inverse[layer, 0], stacked[0], dims, preferred_element_type=F32)
    out = out + lax.dot_general(inverse[layer, 1], stacked[1], dims, preferred_element_type=F32)
    rows = out.shape[0]
    if rows % LANES:
        out = jnp.concatenate([out, jnp.zeros((-rows % LANES, out.shape[1]), F32)], axis=0)
    solved[layer] = out.T


def places(picked, cells):
    rows = picked.shape[1]
    column = jnp.broadcast_to(picked.astype(F32), (8, rows)).T[:, 0:1].astype(jnp.int32)
    cell = lax.broadcasted_iota(jnp.int32, (rows, cells), 1)
    row = lax.broadcasted_iota(jnp.int32, (rows, cells), 0)
    return jnp.max(jnp.where(column == cell, row, -1), axis=0, keepdims=True)


def first_kernel(
    width, rhs_in, isc_in, fwd_in, bwd_in, picked_in, packet, small, place, front,
    rhs, isc, fwd, bwd, picked, sems,
):
    pairs = ((rhs_in, rhs), (isc_in, isc), (fwd_in, fwd), (bwd_in, bwd), (picked_in, picked))
    copies = [pltpu.make_async_copy(a, b, sems.at[i]) for i, (a, b) in enumerate(pairs)]
    for copy in copies:
        copy.start()
    for copy in copies:
        copy.wait()
    cells = rhs.shape[-1]
    count = rhs.shape[1]
    small[ISC:ISC + 2, :] = isc[...]
    small[FWD:FWD + 2, :] = fwd[...]
    small[BWD:BWD + 2, :] = bwd[...]
    small[PICK:PICK + 2, :] = jnp.full((2, cells), -1, F32)
    small[PICK:PICK + 2, :width] = picked[...].astype(F32)
    packet[0:count, :] = rhs[0]
    packet[count:2 * count, :] = rhs[1]
    packet[2 * count:, :] = small[...]
    for layer in range(2):
        place[layer:layer + 1, :] = places(picked[layer:layer + 1, :], cells)
    write_front(front, forward_front(split(rhs[0]), split(rhs[1]), small, None, width))


def forward_kernel(step, sections, planes, width, blocks, layers, inverse, packet, place, *rest):
    gathered, rest = rest[:blocks], rest[blocks:]
    if step:
        incoming, *rest = rest
    if step < sections - 1:
        after, *rest = rest
    kept, front, *rest = rest
    if step < sections - 1:
        field, *rest = rest
    stacked, solved = rest
    own = lax.axis_index("sweep")
    cells = packet.shape[-1]
    rows = kept.shape[1]
    small = packet.at[2 * rows:]

    @pl.when(own == step)
    def _():
        both = layers[own] == 2
        solve(gathered, planes, inverse, stacked, solved, 0)

        @pl.when(both)
        def _():
            solve(gathered, planes, inverse, stacked, solved, 1)

        rhs_a, rhs_b = split(packet[0:rows, :]), split(packet[rows:2 * rows, :])
        first_res = rhs_a
        if step:
            first_res = minus(rhs_a, scaled(row_of(small, FWD), split(incoming[...])))
        first = gather_lanes(
            split(solved[0]), place[0:1, :], scaled(row_of(small, ISC), first_res)
        )
        second_res = minus(rhs_b, scaled(row_of(small, FWD + 1), first))
        second = gather_lanes(
            split(solved[1]), place[1:2, :], scaled(row_of(small, ISC + 1), second_res)
        )
        write_field(kept.at[0], first)
        write_field(kept.at[1], second)
        if step < sections - 1:
            outgoing = choose(both, second, first)
            write_field(field, outgoing)
            ahead = after.at[2 * rows:]
            write_front(front, forward_front(
                split(after[0:rows, :]), split(after[rows:2 * rows, :]), ahead, outgoing, width
            ))
        else:
            z = scaled(row_of(small, BWD), choose(both, second, [jnp.zeros_like(c) for c in first]))
            write_front(front, gather_lanes(rounded(z), picks(small, PICK, width)))


def backward_kernel(step, sections, planes, width, blocks, layers, inverse, small, place, *rest):
    gathered, rest = rest[:blocks], rest[blocks:]
    kept, *rest = rest
    last = step == sections - 1
    if not last:
        incoming, before, *rest = rest
    if step:
        behind, held, *rest = rest
    result, *rest = rest
    if step:
        front, field, *rest = rest
    stacked, solved = rest
    own = lax.axis_index("sweep")

    if not last:
        @pl.when(own != step)
        def _():
            result[...] = before[...]

    @pl.when(own == step)
    def _():
        both = layers[own] == 2

        def first_solve():
            solve(gathered, planes, inverse, stacked, solved, 0)

        if last:
            pl.when(both)(first_solve)
        else:
            first_solve()

            @pl.when(both)
            def _():
                solve(gathered, planes, inverse, stacked, solved, 1)

        first_fwd, second_fwd = split(kept[0]), split(kept[1])
        zero = [jnp.zeros_like(c) for c in first_fwd]
        if last:
            second, arriving = second_fwd, zero
        else:
            arriving = split(incoming[...])
            z = scaled(row_of(small, BWD + 1), arriving)
            local = scaled(row_of(small, ISC + 1), z)
            second = minus(second_fwd, gather_lanes(split(solved[1]), place[1:2, :], local))
        following = choose(both, second, arriving)
        z = scaled(row_of(small, BWD), following)
        local = scaled(row_of(small, ISC), z)
        change = gather_lanes(split(solved[0]), place[0:1, :], local)
        if last:
            change = choose(both, change, zero)
        first = minus(first_fwd, change)
        write_field(result.at[0], first)
        write_field(result.at[1], choose(both, second, zero))
        if step:
            write_field(field, first)
            write_front(front, backward_front(
                behind, first, split(held[...]), layers[own - 1] == 2, width
            ))


def whole(space=pltpu.VMEM):
    return pl.BlockSpec(memory_space=space)


def call(kernel, operands, outs, scratch, name, space=pltpu.VMEM):
    specs = [whole(pltpu.SMEM if o.ndim == 1 else space) for o in operands]
    return pl.pallas_call(
        kernel,
        in_specs=specs,
        out_specs=[whole()] * len(outs),
        out_shape=[jax.ShapeDtypeStruct(s, t) for s, t in outs],
        scratch_shapes=scratch,
        compiler_params=pltpu.CompilerParams(vmem_limit_bytes=8 * 2**20),
        name=name,
    )(*operands)


def shards(
    rhs_field,
    front_inverse,
    interior_scale,
    forward_coupling,
    backward_coupling,
    front_cells,
    section_layers,
):
    sections, planes = lax.axis_size("sweep"), lax.axis_size("plane")
    layer_slots, parts, columns, cells = rhs_field.shape
    rows = parts * columns
    owned, order = front_inverse.shape[2:]
    width = -(-owned // LANES) * LANES
    per_layer = width // LANES
    chips = planes // CORES
    direct = planes == chips * CORES and chips <= 4 and owned == width

    rhs = rhs_field.reshape(layer_slots, rows, cells)
    picked = jnp.pad(front_cells, ((0, 0), (0, width - owned)), constant_values=-1)
    inverse = pltpu.with_memory_space_constraint(front_inverse, pltpu.VMEM)

    front_shape = ((2 * per_layer, rows, LANES), BF16)
    field_shape = ((rows, cells), F32)
    layers_shape = ((layer_slots, rows, cells), F32)
    scratch = [
        pltpu.VMEM((2, rows, order), BF16),
        pltpu.VMEM((2, rows, width), F32),
    ]

    def send(block, start, stop, chip_step=0, other_core=False):
        route = []
        for own in range(planes):
            chip, core = own // CORES, own % CORES
            chip = (chip + chip_step) % chips
            core = CORES - 1 - core if other_core else core
            route.append((start * planes + own, stop * planes + chip * CORES + core))
        return lax.ppermute(block, ("sweep", "plane"), route)

    def pass_on(block, start, stop):
        return lax.ppermute(block, "sweep", [(start, stop)])

    def exchange(front, start, stop):
        if not direct:
            if start != stop:
                front = pass_on(front, start, stop)
            gathered = lax.all_gather(front, "plane")
            if owned != width:
                gathered = gathered.reshape(planes, 2, per_layer, rows, LANES)
                gathered = gathered.transpose(1, 3, 0, 2, 4).reshape(2, rows, planes, width)
                gathered = gathered[..., :owned].reshape(2, rows, order // LANES, LANES)
                gathered = gathered.transpose(0, 2, 1, 3)
                gathered = gathered.reshape(1, 2 * order // LANES, rows, LANES)
            return [gathered]
        mine = [
            front if start == stop and not step else send(front, start, stop, step)
            for step in range(chips)
        ]
        mine = jnp.stack(mine)
        return [mine, send(mine, stop, stop, other_core=True)]

    packet, small, place, front = call(
        functools.partial(first_kernel, width),
        [rhs, interior_scale, forward_coupling, backward_coupling, picked],
        [((2 * rows + 8, cells), F32), ((8, cells), F32), ((2, cells), jnp.int32), front_shape],
        [
            pltpu.VMEM(rhs.shape, F32),
            pltpu.VMEM(interior_scale.shape, F32),
            pltpu.VMEM(forward_coupling.shape, F32),
            pltpu.VMEM(backward_coupling.shape, F32),
            pltpu.VMEM(picked.shape, jnp.int32),
            pltpu.SemaphoreType.DMA((5,)),
        ],
        "first_fronts",
        pltpu.HBM,
    )
    gathered = exchange(front, 0, 0)
    after = lax.ppermute(packet, "sweep", [(i + 1, i) for i in range(sections - 1)])
    behind = lax.ppermute(small, "sweep", [(i, i + 1) for i in range(sections - 1)])

    kept, held = [], [None]
    for step in range(sections):
        final = step == sections - 1
        extra = ([held[step]] if step else []) + ([] if final else [after])
        outs = call(
            functools.partial(forward_kernel, step, sections, planes, width, len(gathered)),
            [section_layers, inverse, packet, place, *gathered, *extra],
            [layers_shape, front_shape] + ([] if final else [field_shape]),
            scratch,
            f"forward_section_{step}",
        )
        kept.append(outs[0])
        gathered = exchange(outs[1], step, step if final else step + 1)
        if not final:
            held.append(pass_on(outs[2], step, step + 1))

    result = incoming = None
    for step in reversed(range(sections)):
        extra = ([] if result is None else [incoming, result]) + ([behind, held[step]] if step else [])
        outs = call(
            functools.partial(backward_kernel, step, sections, planes, width, len(gathered)),
            [section_layers, inverse, small, place, *gathered, kept[step], *extra],
            [layers_shape] + ([front_shape, field_shape] if step else []),
            scratch,
            f"backward_section_{step}",
        )
        result = outs[0]
        if step:
            gathered = exchange(outs[1], step, step - 1)
            incoming = pass_on(outs[2], step, step - 1)
    return result.reshape(rhs_field.shape)


def solution(mesh):
    in_specs = (
        P("sweep", None, None, "plane"),
        P("sweep", None, "plane", None),
        P("sweep", "plane"),
        P("sweep", "plane"),
        P("sweep", "plane"),
        P("sweep", "plane"),
        P(),
    )
    out_specs = P("sweep", None, None, "plane")
    return jax.shard_map(shards, mesh=mesh, in_specs=in_specs, out_specs=out_specs, check_vma=False)
```

time: 180 us -> 187 us (1.039)
  blocking collectives: 48.5 us -> 0 us
  starting transfers between devices: 32 us -> 72.9 us
  waiting for transfers between devices: 55 us -> 84.8 us
  local copies, waits for them, and re-layouts: 30.2 us -> 10.1 us
  Pallas kernels: 13.4 us -> 17.2 us
    ppermute x8 -> x46, starting transfers between devices: 19.3 us -> 72.9 us  [the longest x38 41.5 us: send(): return lax.ppermute(block, ('sweep', 'plane'), route)]
    all_to_all x5 -> x0, blocking collectives: 48.5 us -> none  [exchange(): gathered = lax.all_to_all(spread, 'plane', 0, 0)]
    ppermute x8 -> x46, waiting for transfers between devices: 48.1 us -> 84.8 us  [the longest x38 76.2 us: send(): return lax.ppermute(block, ('sweep', 'plane'), route)]
    unnamed x36 -> x18, local copies, waits for them, and re-layouts: 28.3 us -> 10.1 us
    all_to_all x3 -> x0, starting transfers between devices: 12.7 us -> none  [exchange(): gathered = lax.all_to_all(spread, 'plane', 0, 0)]
    all_to_all x3 -> x0, waiting for transfers between devices: 6.91 us -> none  [exchange(): gathered = lax.all_to_all(spread, 'plane', 0, 0)]
    pallas_call x9, Pallas kernels: 13.4 us -> 17.2 us  [call(): pl.pallas_call(kernel, in_specs=specs, out_specs=[whole()] * len(outs), o...]
  transfers between devices with their start and end apart: 11 -> 46, of which waited for: 4 -> 11; matrix products, arithmetic and copies ran while one was open for 0% -> 0% of each run, Pallas kernels for 1% -> 0%
where the time goes in v2:
time: 187 us; the launch traced here: 186 us
  waiting for transfers between devices  84.8 us (45%)
  starting transfers between devices  72.9 us (39%)
  Pallas kernels  17.2 us (9%)
  local copies, waits for them, and re-layouts  10.1 us (5%)
    ppermute x38, waiting for transfers between devices, send(): return lax.ppermute(block, ('sweep', 'plane'), route)  76.2 us
    ppermute x38, starting transfers between devices, send(): return lax.ppermute(block, ('sweep', 'plane'), route)  41.5 us
    ppermute x1, starting transfers between devices, shards(): lax.ppermute(small, 'sweep', [(i, i + 1) for i in range(sections - 1)])  20.4 us
    pallas_call x9, Pallas kernels, call(): pl.pallas_call(kernel, in_specs=specs, out_specs=[whole()] * len(outs), o...  17.2 us
    unnamed x18, local copies, waits for them, and re-layouts  10.1 us
    ppermute x6, starting transfers between devices, pass_on(): return lax.ppermute(block, 'sweep', [(start, stop)])  9.65 us
    ppermute x6, waiting for transfers between devices, pass_on(): return lax.ppermute(block, 'sweep', [(start, stop)])  7.09 us
  transfers between devices with their start and end apart: 46, of which 11 were waited for; matrix products, arithmetic and copies ran while one was open for 0% of the time, Pallas kernels for 0%

profile of v2, /device:TPU:0, one launch (start us, length us, event | category | flops | bytes accessed | tf_op | source)
XLA Modules:
  0.0 185.9 jit_solution(3927674396539247648)
XLA Ops:
  3.7 1.5 first_fronts.1
  5.2 5.8 %collective-permute-start.2 = (bf16[8,16,128]{2,1,0:T(8,128)(2,1)S(1)}, bf16[8,16,128]{2,1,0:T(8,128)(2,1)S(1)}, u32[]{:S(2)}, u32[]{:S(2)}) collective-permute-start(bf16[8,16,128]{2,1,0:T(8,128)(2,1)S(1)} %get-tuple-element.32), channel_id=1, source_target_pairs={{0,6},{1,7},{2,0},{3,1},{4,2},{5,3},{6,4},{7,5}} | collective-permute-start | bytes 98312 | tf_op jit(solution)/shard_map/ppermute | solution.py:315
  11.0 2.4 %collective-permute-start.1 = (bf16[8,16,128]{2,1,0:T(8,128)(2,1)S(1)}, bf16[8,16,128]{2,1,0:T(8,128)(2,1)S(1)}, u32[]{:S(2)}, u32[]{:S(2)}) collective-permute-start(bf16[8,16,128]{2,1,0:T(8,128)(2,1)S(1)} %get-tuple-element.32), channel_id=1, source_target_pairs={{0,4},{1,5},{2,6},{3,7},{4,0},{5,1},{6,2},{7,3}} | collective-permute-start | bytes 98312 | tf_op jit(solution)/shard_map/ppermute | solution.py:315
  13.4 2.5 %collective-permute-start = (bf16[8,16,128]{2,1,0:T(8,128)(2,1)S(1)}, bf16[8,16,128]{2,1,0:T(8,128)(2,1)S(1)}, u32[]{:S(2)}, u32[]{:S(2)}) collective-permute-start(bf16[8,16,128]{2,1,0:T(8,128)(2,1)S(1)} %get-tuple-element.32), channel_id=1, source_target_pairs={{0,2},{1,3},{2,4},{3,5},{4,6},{5,7},{6,0},{7,1}} | collective-permute-start | bytes 98312 | tf_op jit(solution)/shard_map/ppermute | solution.py:315
  15.9 1.3 collective-permute-start.4
  17.2 2.9 %collective-permute-done = bf16[8,16,128]{2,1,0:T(8,128)(2,1)S(1)} collective-permute-done((bf16[8,16,128]{2,1,0:T(8,128)(2,1)S(1)}, bf16[8,16,128]{2,1,0:T(8,128)(2,1)S(1)}, u32[]{:S(2)}, u32[]{:S(2)}) %collective-permute-start) | collective-permute-done | bytes 32800 | tf_op jit(solution)/shard_map/ppermute | solution.py:315
  20.1 1.9 %collective-permute-start.3 = (bf16[4,8,16,128]{3,2,1,0:T(8,128)(2,1)S(1)}, bf16[4,8,16,128]{3,2,1,0:T(8,128)(2,1)S(1)}, u32[]{:S(2)}, u32[]{:S(2)}) collective-permute-start(bf16[4,8,16,128]{3,2,1,0:T(8,128)(2,1)S(1)} %pad_maximum_fusion.rest_0_), channel_id=1, source_target_pairs={{0,1},{1,0},{2,3},{3,2},{4,5},{5,4},{6,7},{7,6}} | collective-permute-start | bytes 393224 | tf_op jit(solution)/shard_map/ppermute | solution.py:315
  22.1 1.3 collective-permute-done.3.rest_1_
  23.4 5.8 %copy-done = bf16[2,2,512,4096]{3,2,1,0:T(8,128)(2,1)S(1)} copy-done((bf16[2,2,512,4096]{3,2,1,0:T(8,128)(2,1)S(1)}, bf16[2,2,512,4096]{3,2,1,0:T(8,128)(2,1)}, u32[]{:S(2)}) %copy-start) | copy-done | bytes 16777240
  29.8 5.7 %forward_section_0.1 = (f32[2,16,1024]{2,1,0:T(8,128)S(1)}, bf16[8,16,128]{2,1,0:T(8,128)(2,1)S(1)}, f32[16,1024]{1,0:T(8,128)S(1)}) custom-call(s32[4]{0:T(128)S(1)} %copy-done.3, bf16[2,2,512,4096]{3,2,1,0:T(8,128)(2,1)S(1)} %copy-done, f32[40,1024]{1,0:T(8,128)S(1)} %get-tuple-element.31.packet, s32[2,1024]{1,0:T(2,128)S(1)} %get-tuple-element.30.place, ...), custom_call_target="tpu_custom_call" | custom-call | tf_op jit(solution)/shard_map/forward_section_0/pallas_call | solution.py:267
  41.0 1.3 collective-permute-done.5
  43.0 5.7 %collective-permute-start.10 = (f32[16,1024]{1,0:T(8,128)S(1)}, f32[16,1024]{1,0:T(8,128)S(1)}, u32[]{:S(2)}, u32[]{:S(2)}) collective-permute-start(f32[16,1024]{1,0:T(8,128)S(1)} %get-tuple-element.34), channel_id=1, source_target_pairs={{0,8},{1,9},{2,10},{3,11},{4,12},{5,13},{6,14},{7,15}} | collective-permute-start | bytes 196616 | tf_op jit(solution)/shard_map/ppermute | solution.py:318
  48.7 2.0 %collective-permute-done.10.rest_2_.rest_6_ = f32[16,1024]{1,0:T(8,128)S(1)} collective-permute-done((f32[16,1024]{1,0:T(8,128)S(1)}, f32[16,1024]{1,0:T(8,128)S(1)}, u32[]{:S(2)}, u32[]{:S(2)}) %collective-permute-start.10) | collective-permute-done | bytes 65568 | tf_op jit(solution)/shard_map/ppermute | solution.py:318
  63.6 20.4 %collective-permute-start.27 = (f32[8,1024]{1,0:T(8,128)S(1)}, f32[8,1024]{1,0:T(8,128)S(1)}, u32[]{:S(2)}, u32[]{:S(2)}) collective-permute-start(f32[8,1024]{1,0:T(8,128)S(1)} %get-tuple-element.29.small), channel_id=1, source_target_pairs={{0,8},{8,16},{16,24},{1,9},{9,17},{17,25},{2,10},{10,18},{18,26},{... | collective-permute-start | bytes 98312 | tf_op jit(solution)/shard_map/ppermute | solution.py:356
  84.0 1.6 collective-permute-done.27.rest_3_.rest_5_
  95.8 1.3 collective-permute-start.43
  97.1 1.3 collective-permute-start.42
  101.0 66.5 %collective-permute-done.43 = bf16[8,16,128]{2,1,0:T(8,128)(2,1)S(1)} collective-permute-done((bf16[8,16,128]{2,1,0:T(8,128)(2,1)S(1)}, bf16[8,16,128]{2,1,0:T(8,128)(2,1)S(1)}, u32[]{:S(2)}, u32[]{:S(2)}) %collective-permute-start.43) | collective-permute-done | bytes 32800 | tf_op jit(solution)/shard_map/ppermute | solution.py:315
  167.5 1.3 collective-permute-done.42
  168.8 2.2 %collective-permute-done.41 = bf16[8,16,128]{2,1,0:T(8,128)(2,1)S(1)} collective-permute-done((bf16[8,16,128]{2,1,0:T(8,128)(2,1)S(1)}, bf16[8,16,128]{2,1,0:T(8,128)(2,1)S(1)}, u32[]{:S(2)}, u32[]{:S(2)}) %collective-permute-start.41) | collective-permute-done | bytes 32800 | tf_op jit(solution)/shard_map/ppermute | solution.py:315
  171.4 1.9 %collective-permute-start.44 = (bf16[4,8,16,128]{3,2,1,0:T(8,128)(2,1)S(1)}, bf16[4,8,16,128]{3,2,1,0:T(8,128)(2,1)S(1)}, u32[]{:S(2)}, u32[]{:S(2)}) collective-permute-start(bf16[4,8,16,128]{3,2,1,0:T(8,128)(2,1)S(1)} %pad_maximum_fusion.7.rest_0_), channel_id=1, source_target_pairs={{0,1},{1,0},{2,3},{3,2},{4,5},{5,4},{6,7},{7,6}} | collective-permute-start | bytes 393224 | tf_op jit(solution)/shard_map/ppermute | solution.py:315
  173.3 1.3 collective-permute-start.45
  174.6 5.1 %collective-permute-done.45.rest_3_ = f32[16,1024]{1,0:T(8,128)S(1)} collective-permute-done((f32[16,1024]{1,0:T(8,128)S(1)}, f32[16,1024]{1,0:T(8,128)S(1)}, u32[]{:S(2)}, u32[]{:S(2)}) %collective-permute-start.45) | collective-permute-done | bytes 65568 | tf_op jit(solution)/shard_map/ppermute | solution.py:318
  179.7 6.3 %backward_section_0.1 = f32[2,16,1024]{2,1,0:T(8,128)} custom-call(s32[4]{0:T(128)S(1)} %copy-done.4, bf16[2,2,512,4096]{3,2,1,0:T(8,128)(2,1)S(1)} %copy-done.1, f32[8,1024]{1,0:T(8,128)S(1)} %get-tuple-element.29.small, s32[2,1024]{1,0:T(2,128)S(1)} %get-tuple-element.30.place, bf16[4,8,16,128]{3,2,1,0:T(8,128)(2,1)S(1)} %pad_maximum_fusion.7.rest_0_, ...), custom_call_target="tpu_custom_call" | custom-call | tf_op jit(solution)/shard_map/backward_section_0/pallas_call | solution.py:267
  (103 shorter events, 36.0 us)
Async XLA Ops:
  5.2 12.0 %collective-permute-start.2 = (bf16[8,16,128]{2,1,0:T(8,128)(2,1)S(1)}, bf16[8,16,128]{2,1,0:T(8,128)(2,1)S(1)}, u32[]{:S(2)}, u32[]{:S(2)}) collective-permute-start(bf16[8,16,128]{2,1,0:T(8,128)(2,1)S(1)} %get-tuple-element.32), channel_id=1, source_target_pairs={{0,6},{1,7},{2,0},{3,1},{4,2},{5,3},{6,4},{7,5}} | collective-permute-start | bytes 98312 | tf_op jit(solution)/shard_map/ppermute | solution.py:315
  11.0 6.2 %collective-permute-start.1 = (bf16[8,16,128]{2,1,0:T(8,128)(2,1)S(1)}, bf16[8,16,128]{2,1,0:T(8,128)(2,1)S(1)}, u32[]{:S(2)}, u32[]{:S(2)}) collective-permute-start(bf16[8,16,128]{2,1,0:T(8,128)(2,1)S(1)} %get-tuple-element.32), channel_id=1, source_target_pairs={{0,4},{1,5},{2,6},{3,7},{4,0},{5,1},{6,2},{7,3}} | collective-permute-start | bytes 98312 | tf_op jit(solution)/shard_map/ppermute | solution.py:315
  13.4 6.7 %collective-permute-start = (bf16[8,16,128]{2,1,0:T(8,128)(2,1)S(1)}, bf16[8,16,128]{2,1,0:T(8,128)(2,1)S(1)}, u32[]{:S(2)}, u32[]{:S(2)}) collective-permute-start(bf16[8,16,128]{2,1,0:T(8,128)(2,1)S(1)} %get-tuple-element.32), channel_id=1, source_target_pairs={{0,2},{1,3},{2,4},{3,5},{4,6},{5,7},{6,0},{7,1}} | collective-permute-start | bytes 98312 | tf_op jit(solution)/shard_map/ppermute | solution.py:315
  15.9 7.5 %collective-permute-start.4 = (f32[40,1024]{1,0:T(8,128)S(1)}, f32[40,1024]{1,0:T(8,128)S(1)}, u32[]{:S(2)}, u32[]{:S(2)}) collective-permute-start(f32[40,1024]{1,0:T(8,128)S(1)} %get-tuple-element.31.packet), channel_id=1, source_target_pairs={{8,0},{16,8},{24,16},{9,1},{17,9},{25,17},{10,2},{18,10},{26,18},{... | collective-permute-start | bytes 491528 | tf_op jit(solution)/shard_map/ppermute | solution.py:355
  20.1 3.2 %collective-permute-start.3 = (bf16[4,8,16,128]{3,2,1,0:T(8,128)(2,1)S(1)}, bf16[4,8,16,128]{3,2,1,0:T(8,128)(2,1)S(1)}, u32[]{:S(2)}, u32[]{:S(2)}) collective-permute-start(bf16[4,8,16,128]{3,2,1,0:T(8,128)(2,1)S(1)} %pad_maximum_fusion.rest_0_), channel_id=1, source_target_pairs={{0,1},{1,0},{2,3},{3,2},{4,5},{5,4},{6,7},{7,6}} | collective-permute-start | bytes 393224 | tf_op jit(solution)/shard_map/ppermute | solution.py:315
  35.6 5.2 %collective-permute-start.8 = (bf16[8,16,128]{2,1,0:T(8,128)(2,1)S(1)}, bf16[8,16,128]{2,1,0:T(8,128)(2,1)S(1)}, u32[]{:S(2)}, u32[]{:S(2)}) collective-permute-start(bf16[8,16,128]{2,1,0:T(8,128)(2,1)S(1)} %get-tuple-element.33), channel_id=1, source_target_pairs={{0,14},{1,15},{2,8},{3,9},{4,10},{5,11},{6,12},{7,13}} | collective-permute-start | bytes 98312 | tf_op jit(solution)/shard_map/ppermute | solution.py:315
  36.9 3.9 %collective-permute-start.7 = (bf16[8,16,128]{2,1,0:T(8,128)(2,1)S(1)}, bf16[8,16,128]{2,1,0:T(8,128)(2,1)S(1)}, u32[]{:S(2)}, u32[]{:S(2)}) collective-permute-start(bf16[8,16,128]{2,1,0:T(8,128)(2,1)S(1)} %get-tuple-element.33), channel_id=1, source_target_pairs={{0,12},{1,13},{2,14},{3,15},{4,8},{5,9},{6,10},{7,11}} | collective-permute-start | bytes 98312 | tf_op jit(solution)/shard_map/ppermute | solution.py:315
  38.1 2.9 %collective-permute-start.6 = (bf16[8,16,128]{2,1,0:T(8,128)(2,1)S(1)}, bf16[8,16,128]{2,1,0:T(8,128)(2,1)S(1)}, u32[]{:S(2)}, u32[]{:S(2)}) collective-permute-start(bf16[8,16,128]{2,1,0:T(8,128)(2,1)S(1)} %get-tuple-element.33), channel_id=1, source_target_pairs={{0,10},{1,11},{2,12},{3,13},{4,14},{5,15},{6,8},{7,9}} | collective-permute-start | bytes 98312 | tf_op jit(solution)/shard_map/ppermute | solution.py:315
  39.4 2.9 %collective-permute-start.5 = (bf16[8,16,128]{2,1,0:T(8,128)(2,1)S(1)}, bf16[8,16,128]{2,1,0:T(8,128)(2,1)S(1)}, u32[]{:S(2)}, u32[]{:S(2)}) collective-permute-start(bf16[8,16,128]{2,1,0:T(8,128)(2,1)S(1)} %get-tuple-element.33), channel_id=1, source_target_pairs={{0,8},{1,9},{2,10},{3,11},{4,12},{5,13},{6,14},{7,15}} | collective-permute-start | bytes 98312 | tf_op jit(solution)/shard_map/ppermute | solution.py:315
  42.4 8.4 %collective-permute-start.9 = (bf16[4,8,16,128]{3,2,1,0:T(8,128)(2,1)S(1)}, bf16[4,8,16,128]{3,2,1,0:T(8,128)(2,1)S(1)}, u32[]{:S(2)}, u32[]{:S(2)}) collective-permute-start(bf16[4,8,16,128]{3,2,1,0:T(8,128)(2,1)S(1)} %pad_maximum_fusion.1.rest_0_), channel_id=1, source_target_pairs={{8,9},{9,8},{10,11},{11,10},{12,13},{13,12},{14,15},{15,14}} | collective-permute-start | bytes 393224 | tf_op jit(solution)/shard_map/ppermute | solution.py:315
  43.0 7.7 %collective-permute-start.10 = (f32[16,1024]{1,0:T(8,128)S(1)}, f32[16,1024]{1,0:T(8,128)S(1)}, u32[]{:S(2)}, u32[]{:S(2)}) collective-permute-start(f32[16,1024]{1,0:T(8,128)S(1)} %get-tuple-element.34), channel_id=1, source_target_pairs={{0,8},{1,9},{2,10},{3,11},{4,12},{5,13},{6,14},{7,15}} | collective-permute-start | bytes 196616 | tf_op jit(solution)/shard_map/ppermute | solution.py:318
  51.3 2.7 %collective-permute-start.14 = (bf16[8,16,128]{2,1,0:T(8,128)(2,1)S(1)}, bf16[8,16,128]{2,1,0:T(8,128)(2,1)S(1)}, u32[]{:S(2)}, u32[]{:S(2)}) collective-permute-start(bf16[8,16,128]{2,1,0:T(8,128)(2,1)S(1)} %get-tuple-element.35), channel_id=1, source_target_pairs={{8,22},{9,23},{10,16},{11,17},{12,18},{13,19},{14,20},{15,21}} | collective-permute-start | bytes 98312 | tf_op jit(solution)/shard_map/ppermute | solution.py:315
  52.0 2.0 %collective-permute-start.13 = (bf16[8,16,128]{2,1,0:T(8,128)(2,1)S(1)}, bf16[8,16,128]{2,1,0:T(8,128)(2,1)S(1)}, u32[]{:S(2)}, u32[]{:S(2)}) collective-permute-start(bf16[8,16,128]{2,1,0:T(8,128)(2,1)S(1)} %get-tuple-element.35), channel_id=1, source_target_pairs={{8,20},{9,21},{10,22},{11,23},{12,16},{13,17},{14,18},{15,19}} | collective-permute-start | bytes 98312 | tf_op jit(solution)/shard_map/ppermute | solution.py:315
  56.2 2.7 %collective-permute-start.20 = (bf16[8,16,128]{2,1,0:T(8,128)(2,1)S(1)}, bf16[8,16,128]{2,1,0:T(8,128)(2,1)S(1)}, u32[]{:S(2)}, u32[]{:S(2)}) collective-permute-start(bf16[8,16,128]{2,1,0:T(8,128)(2,1)S(1)} %get-tuple-element.37), channel_id=1, source_target_pairs={{16,30},{17,31},{18,24},{19,25},{20,26},{21,27},{22,28},{23,29}} | collective-permute-start | bytes 98312 | tf_op jit(solution)/shard_map/ppermute | solution.py:315
  62.9 22.7 %collective-permute-start.26 = (bf16[4,8,16,128]{3,2,1,0:T(8,128)(2,1)S(1)}, bf16[4,8,16,128]{3,2,1,0:T(8,128)(2,1)S(1)}, u32[]{:S(2)}, u32[]{:S(2)}) collective-permute-start(bf16[4,8,16,128]{3,2,1,0:T(8,128)(2,1)S(1)} %pad_maximum_fusion.4.rest_0_), channel_id=1, source_target_pairs={{24,25},{25,24},{26,27},{27,26},{28,29},{29,28},{30,31},{31,30}} | collective-permute-start | bytes 393224 | tf_op jit(solution)/shard_map/ppermute | solution.py:315
  63.6 22.0 %collective-permute-start.27 = (f32[8,1024]{1,0:T(8,128)S(1)}, f32[8,1024]{1,0:T(8,128)S(1)}, u32[]{:S(2)}, u32[]{:S(2)}) collective-permute-start(f32[8,1024]{1,0:T(8,128)S(1)} %get-tuple-element.29.small), channel_id=1, source_target_pairs={{0,8},{8,16},{16,24},{1,9},{9,17},{17,25},{2,10},{10,18},{18,26},{... | collective-permute-start | bytes 98312 | tf_op jit(solution)/shard_map/ppermute | solution.py:356
  86.2 2.7 %collective-permute-start.31 = (bf16[8,16,128]{2,1,0:T(8,128)(2,1)S(1)}, bf16[8,16,128]{2,1,0:T(8,128)(2,1)S(1)}, u32[]{:S(2)}, u32[]{:S(2)}) collective-permute-start(bf16[8,16,128]{2,1,0:T(8,128)(2,1)S(1)} %get-tuple-element.41), channel_id=1, source_target_pairs={{24,22},{25,23},{26,16},{27,17},{28,18},{29,19},{30,20},{31,21}} | collective-permute-start | bytes 98312 | tf_op jit(solution)/shard_map/ppermute | solution.py:315
  90.9 2.7 %collective-permute-start.37 = (bf16[8,16,128]{2,1,0:T(8,128)(2,1)S(1)}, bf16[8,16,128]{2,1,0:T(8,128)(2,1)S(1)}, u32[]{:S(2)}, u32[]{:S(2)}) collective-permute-start(bf16[8,16,128]{2,1,0:T(8,128)(2,1)S(1)} %get-tuple-element.45), channel_id=1, source_target_pairs={{16,14},{17,15},{18,8},{19,9},{20,10},{21,11},{22,12},{23,13}} | collective-permute-start | bytes 98312 | tf_op jit(solution)/shard_map/ppermute | solution.py:315
  95.8 71.7 %collective-permute-start.43 = (bf16[8,16,128]{2,1,0:T(8,128)(2,1)S(1)}, bf16[8,16,128]{2,1,0:T(8,128)(2,1)S(1)}, u32[]{:S(2)}, u32[]{:S(2)}) collective-permute-start(bf16[8,16,128]{2,1,0:T(8,128)(2,1)S(1)} %get-tuple-element.49), channel_id=1, source_target_pairs={{8,6},{9,7},{10,0},{11,1},{12,2},{13,3},{14,4},{15,5}} | collective-permute-start | bytes 98312 | tf_op jit(solution)/shard_map/ppermute | solution.py:315
  97.1 71.7 %collective-permute-start.42 = (bf16[8,16,128]{2,1,0:T(8,128)(2,1)S(1)}, bf16[8,16,128]{2,1,0:T(8,128)(2,1)S(1)}, u32[]{:S(2)}, u32[]{:S(2)}) collective-permute-start(bf16[8,16,128]{2,1,0:T(8,128)(2,1)S(1)} %get-tuple-element.49), channel_id=1, source_target_pairs={{8,4},{9,5},{10,6},{11,7},{12,0},{13,1},{14,2},{15,3}} | collective-permute-start | bytes 98312 | tf_op jit(solution)/shard_map/ppermute | solution.py:315
  98.4 72.6 %collective-permute-start.41 = (bf16[8,16,128]{2,1,0:T(8,128)(2,1)S(1)}, bf16[8,16,128]{2,1,0:T(8,128)(2,1)S(1)}, u32[]{:S(2)}, u32[]{:S(2)}) collective-permute-start(bf16[8,16,128]{2,1,0:T(8,128)(2,1)S(1)} %get-tuple-element.49), channel_id=1, source_target_pairs={{8,2},{9,3},{10,4},{11,5},{12,6},{13,7},{14,0},{15,1}} | collective-permute-start | bytes 98312 | tf_op jit(solution)/shard_map/ppermute | solution.py:315
  99.7 71.6 %collective-permute-start.40 = (bf16[8,16,128]{2,1,0:T(8,128)(2,1)S(1)}, bf16[8,16,128]{2,1,0:T(8,128)(2,1)S(1)}, u32[]{:S(2)}, u32[]{:S(2)}) collective-permute-start(bf16[8,16,128]{2,1,0:T(8,128)(2,1)S(1)} %get-tuple-element.49), channel_id=1, source_target_pairs={{8,0},{9,1},{10,2},{11,3},{12,4},{13,5},{14,6},{15,7}} | collective-permute-start | bytes 98312 | tf_op jit(solution)/shard_map/ppermute | solution.py:315
  171.4 8.3 %collective-permute-start.44 = (bf16[4,8,16,128]{3,2,1,0:T(8,128)(2,1)S(1)}, bf16[4,8,16,128]{3,2,1,0:T(8,128)(2,1)S(1)}, u32[]{:S(2)}, u32[]{:S(2)}) collective-permute-start(bf16[4,8,16,128]{3,2,1,0:T(8,128)(2,1)S(1)} %pad_maximum_fusion.7.rest_0_), channel_id=1, source_target_pairs={{0,1},{1,0},{2,3},{3,2},{4,5},{5,4},{6,7},{7,6}} | collective-permute-start | bytes 393224 | tf_op jit(solution)/shard_map/ppermute | solution.py:315
  173.3 6.4 %collective-permute-start.45 = (f32[16,1024]{1,0:T(8,128)S(1)}, f32[16,1024]{1,0:T(8,128)S(1)}, u32[]{:S(2)}, u32[]{:S(2)}) collective-permute-start(f32[16,1024]{1,0:T(8,128)S(1)} %get-tuple-element.51), channel_id=1, source_target_pairs={{8,0},{9,1},{10,2},{11,3},{12,4},{13,5},{14,6},{15,7}} | collective-permute-start | bytes 196616 | tf_op jit(solution)/shard_map/ppermute | solution.py:318
  (31 other events, 108.3 us)

commit v3 on v2

v3 whole, which is shorter than its diff:
```python
import functools

import jax
import jax.numpy as jnp
from jax import lax
from jax.experimental import pallas as pl
from jax.experimental.pallas import tpu as pltpu
from jax.sharding import PartitionSpec as P

LANES = 128
CORES = 2
ISC, FWD, BWD, PICK = 0, 2, 4, 6
F32, BF16 = jnp.float32, jnp.bfloat16


def split(field):
    return [field[:, at:at + LANES] for at in range(0, field.shape[1], LANES)]


def gather_lanes(chunks, index, beyond=None):
    result = []
    for place, part in enumerate(split(index)):
        part = jnp.broadcast_to(part, chunks[0].shape)
        lane, chunk = part & (LANES - 1), part >> (LANES.bit_length() - 1)
        total = jnp.zeros(chunks[0].shape, F32) if beyond is None else beyond[place]
        for number, source in enumerate(chunks):
            found = jnp.take_along_axis(source, lane, axis=1, mode="promise_in_bounds")
            total = jnp.where(chunk == number, found, total)
        result.append(total)
    return result


def scaled(row, chunks):
    return [part * chunk for part, chunk in zip(split(row), chunks)]


def minus(left, right):
    return [a - b for a, b in zip(left, right)]


def choose(flag, left, right):
    return [jnp.where(flag, a, b) for a, b in zip(left, right)]


def rounded(chunks):
    return [c.astype(BF16).astype(F32) for c in chunks]


def row_of(ref, at):
    return ref[at:at + 1, :]


def picks(ref, at, width):
    return ref[at:at + 1, :width].astype(jnp.int32)


def forward_front(rhs_a, rhs_b, small, incoming, width):
    first = rhs_a if incoming is None else minus(rhs_a, scaled(row_of(small, FWD), incoming))
    second = minus(rhs_b, scaled(row_of(small, FWD + 1), scaled(row_of(small, ISC), first)))
    return (
        gather_lanes(rounded(first), picks(small, PICK, width))
        + gather_lanes(rounded(second), picks(small, PICK + 1, width))
    )


def backward_front(small, incoming, second_fwd, both, width):
    z = scaled(row_of(small, BWD + 1), incoming)
    local = minus(second_fwd, scaled(row_of(small, ISC + 1), z))
    first = scaled(row_of(small, BWD), choose(both, local, incoming))
    return (
        gather_lanes(rounded(first), picks(small, PICK, width))
        + gather_lanes(rounded(z), picks(small, PICK + 1, width))
    )


def write_front(ref, chunks, field=()):
    high = [c.astype(BF16) for c in field]
    low = [(c - h.astype(F32)).astype(BF16) for c, h in zip(field, high)]
    for at, chunk in enumerate(chunks + high + low):
        ref[at] = chunk.astype(BF16)


def read_field(packet, count):
    start = packet.shape[0] - 2 * count
    return [
        packet[start + i].astype(F32) + packet[start + count + i].astype(F32)
        for i in range(count)
    ]


def write_field(ref, chunks):
    for at, chunk in enumerate(chunks):
        ref[:, at * LANES:(at + 1) * LANES] = chunk


def owner_of(place, planes):
    if isinstance(place, int):
        return place
    step, other = place
    chips = planes // CORES
    own = lax.axis_index("plane")
    chip, core = own // CORES, lax.rem(own, CORES)
    chip = lax.rem(chip - step + chips, chips) if step else chip
    return chip * CORES + (CORES - 1 - core if other else core)


def stack_fronts(blocks, owners, planes, per_layer, stacked, layer):
    for ref, places in zip(blocks, owners):
        for number, place in enumerate(places):
            owner = owner_of(place, planes)
            for i in range(per_layer):
                at = pl.multiple_of((owner * per_layer + i) * LANES, LANES)
                slot = layer * per_layer + i
                piece = ref[slot] if len(ref.shape) == 3 else ref[number, slot]
                half = piece.shape[0] // 2
                wide = piece.astype(F32)
                turned = jnp.concatenate([-wide[half:], wide[:half]], axis=0)
                stacked[0, :, pl.ds(at, LANES)] = piece
                stacked[1, :, pl.ds(at, LANES)] = turned.astype(BF16)


def product(matrix, columns):
    return lax.dot_general(
        matrix, columns, (((1,), (1,)), ((), ())), preferred_element_type=F32
    )


def store_solved(solved, layer, out):
    rows = out.shape[0]
    if rows % LANES:
        out = jnp.concatenate([out, jnp.zeros((-rows % LANES, out.shape[1]), F32)], axis=0)
    solved[layer] = out.T


def solve(inverse, stacked, solved, layer):
    out = product(inverse[layer, 0], stacked[0]) + product(inverse[layer, 1], stacked[1])
    store_solved(solved, layer, out)


def places(picked, cells):
    rows = picked.shape[1]
    column = jnp.broadcast_to(picked.astype(F32), (8, rows)).T[:, 0:1].astype(jnp.int32)
    cell = lax.broadcasted_iota(jnp.int32, (rows, cells), 1)
    row = lax.broadcasted_iota(jnp.int32, (rows, cells), 0)
    return jnp.max(jnp.where(column == cell, row, -1), axis=0, keepdims=True)


def first_kernel(
    width, rhs_in, isc_in, fwd_in, bwd_in, picked_in, packet, small, place, front,
    rhs, isc, fwd, bwd, picked, sems,
):
    pairs = ((rhs_in, rhs), (isc_in, isc), (fwd_in, fwd), (bwd_in, bwd), (picked_in, picked))
    copies = [pltpu.make_async_copy(a, b, sems.at[i]) for i, (a, b) in enumerate(pairs)]
    for copy in copies:
        copy.start()
    for copy in copies:
        copy.wait()
    cells = rhs.shape[-1]
    count = rhs.shape[1]
    small[ISC:ISC + 2, :] = isc[...]
    small[FWD:FWD + 2, :] = fwd[...]
    small[BWD:BWD + 2, :] = bwd[...]
    small[PICK:PICK + 2, :] = jnp.full((2, cells), -1, F32)
    small[PICK:PICK + 2, :width] = picked[...].astype(F32)
    packet[0:count, :] = rhs[0]
    packet[count:2 * count, :] = rhs[1]
    packet[2 * count:, :] = small[...]
    for layer in range(2):
        place[layer:layer + 1, :] = places(picked[layer:layer + 1, :], cells)
    write_front(front, forward_front(split(rhs[0]), split(rhs[1]), small, None, width))


def forward_kernel(
    step, sections, planes, width, per_layer, owners, layers, inverse, packet, place, *rest
):
    blocks, rest = rest[:len(owners)], rest[len(owners):]
    final = step == sections - 1
    if step:
        incoming, *rest = rest
    if not final:
        after, *rest = rest
    kept, front, *rest = rest
    if not final:
        outgoing_packet, *rest = rest
    if step:
        resident, (stacked, solved) = inverse, rest
    else:
        resident, stacked, solved, kept_sum, sems = rest
    own = lax.axis_index("sweep")
    cells = packet.shape[-1]
    count = cells // LANES
    rows = kept.shape[1]
    order = inverse.shape[-1]
    small = packet.at[2 * rows:]
    mine = own == step
    both = layers[step] == 2

    def fill(layer):
        stack_fronts(blocks, owners, planes, per_layer, stacked, layer)

    if step:
        @pl.when(mine)
        def _():
            fill(0)
            solve(resident, stacked, solved, 0)

        @pl.when(mine & both)
        def _():
            fill(1)
            solve(resident, stacked, solved, 1)
    else:
        cuts = 2 if order % (2 * LANES) == 0 else 1
        depth = order // cuts
        copies = {}
        for layer in range(2):
            for cut in range(cuts):
                for part in range(2):
                    piece = (layer, part, slice(None), pl.ds(cut * depth, depth))
                    copies[layer, cut, part] = pltpu.make_async_copy(
                        inverse.at[piece], resident.at[piece], sems.at[len(copies)]
                    )
        for copy in copies.values():
            copy.start()
        for layer in range(2):
            needed = mine if layer == 0 else mine & both

            @pl.when(needed)
            def _():
                fill(layer)

            for cut in range(cuts):
                for part in range(2):
                    copies[layer, cut, part].wait()

                @pl.when(needed)
                def _():
                    columns = pl.ds(cut * depth, depth)
                    out = product(resident[layer, 0, :, columns], stacked[0, :, columns])
                    out = out + product(resident[layer, 1, :, columns], stacked[1, :, columns])
                    if cut == cuts - 1:
                        if cut:
                            out = out + kept_sum[...]
                        store_solved(solved, layer, out)
                    else:
                        kept_sum[...] = out

    @pl.when(mine)
    def _():
        rhs_a, rhs_b = split(packet[0:rows, :]), split(packet[rows:2 * rows, :])
        first_res = rhs_a
        if step:
            first_res = minus(rhs_a, scaled(row_of(small, FWD), read_field(incoming, count)))
        first = gather_lanes(
            split(solved[0]), place[0:1, :], scaled(row_of(small, ISC), first_res)
        )
        second_res = minus(rhs_b, scaled(row_of(small, FWD + 1), first))
        second = gather_lanes(
            split(solved[1]), place[1:2, :], scaled(row_of(small, ISC + 1), second_res)
        )
        if final:
            z = scaled(row_of(small, BWD), choose(both, second, [jnp.zeros_like(c) for c in first]))
            write_front(front, gather_lanes(rounded(z), picks(small, PICK, width)))
        else:
            outgoing = choose(both, second, first)
            ahead = after.at[2 * rows:]
            chunks = forward_front(
                split(after[0:rows, :]), split(after[rows:2 * rows, :]), ahead, outgoing, width
            )
            write_front(front, chunks)
            write_front(outgoing_packet, chunks, outgoing)
        write_field(kept.at[0], first)
        write_field(kept.at[1], second)


def backward_kernel(
    step, sections, planes, width, per_layer, owners, layers, inverse, small, place, *rest
):
    blocks, rest = rest[:len(owners)], rest[len(owners):]
    kept, *rest = rest
    last = step == sections - 1
    if not last:
        incoming, before, *rest = rest
    if step:
        behind, *rest = rest
        held, *rest = rest
    result, *rest = rest
    if step:
        front, outgoing_packet, *rest = rest
    stacked, solved = rest
    own = lax.axis_index("sweep")
    count = kept.shape[-1] // LANES
    mine = own == step
    both = layers[step] == 2

    def whole_solve(layer):
        stack_fronts(blocks, owners, planes, per_layer, stacked, layer)
        solve(inverse, stacked, solved, layer)

    if not last:
        @pl.when(own != step)
        def _():
            result[...] = before[...]

        @pl.when(mine & both)
        def _():
            whole_solve(1)

    @pl.when(mine & both if last else mine)
    def _():
        whole_solve(0)

    @pl.when(mine)
    def _():
        first_fwd, second_fwd = split(kept[0]), split(kept[1])
        zero = [jnp.zeros_like(c) for c in first_fwd]
        if last:
            second, arriving = second_fwd, zero
        else:
            arriving = read_field(incoming, count)
            z = scaled(row_of(small, BWD + 1), arriving)
            local = scaled(row_of(small, ISC + 1), z)
            second = minus(second_fwd, gather_lanes(split(solved[1]), place[1:2, :], local))
        following = choose(both, second, arriving)
        z = scaled(row_of(small, BWD), following)
        local = scaled(row_of(small, ISC), z)
        change = gather_lanes(split(solved[0]), place[0:1, :], local)
        if last:
            change = choose(both, change, zero)
        first = minus(first_fwd, change)
        if step:
            chunks = backward_front(
                behind, first, read_field(held, count), layers[step - 1] == 2, width
            )
            write_front(front, chunks)
            write_front(outgoing_packet, chunks, first)
        write_field(result.at[0], first)
        write_field(result.at[1], choose(both, second, zero))


def whole(space=pltpu.VMEM):
    return pl.BlockSpec(memory_space=space)


def call(kernel, operands, outs, scratch, name, spaces=()):
    specs = [whole(pltpu.SMEM if o.ndim == 1 else pltpu.VMEM) for o in operands]
    for at, space in spaces:
        specs[at] = whole(space)
    return pl.pallas_call(
        kernel,
        in_specs=specs,
        out_specs=[whole()] * len(outs),
        out_shape=[jax.ShapeDtypeStruct(*o) if isinstance(o, tuple) else o for o in outs],
        scratch_shapes=scratch,
        compiler_params=pltpu.CompilerParams(vmem_limit_bytes=8 * 2**20),
        name=name,
    )(*operands)


def in_hbm(array):
    return pltpu.with_memory_space_constraint(array, pltpu.HBM)


def shards(
    rhs_field,
    front_inverse,
    interior_scale,
    forward_coupling,
    backward_coupling,
    front_cells,
    section_layers,
):
    sections, planes = lax.axis_size("sweep"), lax.axis_size("plane")
    layer_slots, parts, columns, cells = rhs_field.shape
    rows = parts * columns
    owned, order = front_inverse.shape[2:]
    width = -(-owned // LANES) * LANES
    per_layer = width // LANES
    chips = planes // CORES
    direct = planes == chips * CORES and chips <= 4 and owned == width

    rhs = rhs_field.reshape(layer_slots, rows, cells)
    picked = jnp.pad(front_cells, ((0, 0), (0, width - owned)), constant_values=-1)
    layers = section_layers

    half_shape = ((per_layer, rows, LANES), BF16)
    front_shape = ((2 * per_layer, rows, LANES), BF16)
    packet_shape = ((2 * per_layer + 2 * (cells // LANES), rows, LANES), BF16)
    layers_shape = ((layer_slots, rows, cells), F32)
    scratch = [
        pltpu.VMEM((2, rows, order), BF16),
        pltpu.VMEM((2, rows, width), F32),
    ]

    def send(block, start, stop, chip_step=0, other_core=False):
        route = []
        for own in range(planes):
            chip, core = own // CORES, own % CORES
            chip = (chip + chip_step) % chips
            core = CORES - 1 - core if other_core else core
            route.append((start * planes + own, stop * planes + chip * CORES + core))
        return lax.ppermute(block, ("sweep", "plane"), route)

    def everywhere(front):
        slots = front.shape[0] // per_layer
        gathered = lax.all_gather(front, "plane")
        if owned != width:
            gathered = gathered.reshape(planes, slots, per_layer, rows, LANES)
            gathered = gathered.transpose(1, 3, 0, 2, 4).reshape(slots, rows, planes, width)
            gathered = gathered[..., :owned].reshape(slots, rows, order // LANES, LANES)
            gathered = gathered.transpose(0, 2, 1, 3)
            gathered = gathered.reshape(slots * order // LANES, rows, LANES)
            return [gathered], [[0]], order // LANES
        return [gathered], [list(range(planes))], per_layer

    def within(front, section):
        if not direct:
            return everywhere(front)
        mine = [front] + [send(front, section, section, s) for s in range(1, chips)]
        swapped = send(jnp.stack(mine), section, section, other_core=True)
        owners = [[(s, False)] for s in range(chips)] + [[(s, True) for s in range(chips)]]
        return mine + [swapped], owners, per_layer

    def between(front, packet, start, stop):
        if not direct:
            packet = lax.ppermute(packet, "sweep", [(start, stop)])
            return *everywhere(packet[:2 * per_layer]), packet
        other = send(front, start, stop, other_core=True)
        across = [send(front, start, stop, s) for s in range(1, chips)]
        packet = send(packet, start, stop)
        relayed = [send(other, stop, stop, s) for s in range(1, chips)]
        owners = [[(0, True)], [(0, False)]]
        owners += [[(s, False)] for s in range(1, chips)] + [[(s, True)] for s in range(1, chips)]
        return [other, packet] + across + relayed, owners, per_layer, packet

    packet, small, place, front = call(
        functools.partial(first_kernel, width),
        [in_hbm(a) for a in (rhs, interior_scale, forward_coupling, backward_coupling, picked)],
        [((2 * rows + 8, cells), F32), ((8, cells), F32), ((2, cells), jnp.int32), front_shape],
        [
            pltpu.VMEM(rhs.shape, F32),
            pltpu.VMEM(interior_scale.shape, F32),
            pltpu.VMEM(forward_coupling.shape, F32),
            pltpu.VMEM(backward_coupling.shape, F32),
            pltpu.VMEM(picked.shape, jnp.int32),
            pltpu.SemaphoreType.DMA((5,)),
        ],
        "first_fronts",
        [(i, pltpu.HBM) for i in range(5)],
    )
    gathered, owners, slots = within(front, 0)
    after = lax.ppermute(packet, "sweep", [(i + 1, i) for i in range(sections - 1)])
    behind = lax.ppermute(small, "sweep", [(i, i + 1) for i in range(sections - 1)])

    inverse = in_hbm(front_inverse)
    kept, held = [], [None]
    for step in range(sections):
        final = step == sections - 1
        extra = ([held[step]] if step else []) + ([] if final else [after])
        outs = [layers_shape, half_shape if final else front_shape]
        outs += [] if final else [packet_shape]
        outs += [] if step else [pltpu.VMEM(front_inverse.shape, BF16)]
        room = [] if step else [
            pltpu.VMEM((owned, rows), F32), pltpu.SemaphoreType.DMA((8,))
        ]
        outs = call(
            functools.partial(
                forward_kernel, step, sections, planes, width, slots, owners
            ),
            [layers, inverse, packet, place, *gathered, *extra],
            outs,
            scratch + room,
            f"forward_section_{step}",
            [] if step else [(1, pltpu.HBM)],
        )
        if not step:
            inverse = outs[-1]
        kept.append(outs[0])
        if final:
            gathered, owners, slots = within(outs[1], step)
        else:
            gathered, owners, slots, incoming = between(outs[1], outs[2], step, step + 1)
            held.append(incoming)

    result = incoming = None
    for step in reversed(range(sections)):
        extra = ([] if result is None else [incoming, result]) + ([behind, held[step]] if step else [])
        outs = call(
            functools.partial(
                backward_kernel, step, sections, planes, width, slots, owners
            ),
            [layers, inverse, small, place, *gathered, kept[step], *extra],
            [layers_shape] + ([front_shape, packet_shape] if step else []),
            scratch,
            f"backward_section_{step}",
        )
        result = outs[0]
        if step:
            gathered, owners, slots, incoming = between(outs[1], outs[2], step, step - 1)
    return result.reshape(rhs_field.shape)


def solution(mesh):
    in_specs = (
        P("sweep", None, None, "plane"),
        P("sweep", None, "plane", None),
        P("sweep", "plane"),
        P("sweep", "plane"),
        P("sweep", "plane"),
        P("sweep", "plane"),
        P(),
    )
    out_specs = P("sweep", None, None, "plane")
    return jax.shard_map(shards, mesh=mesh, in_specs=in_specs, out_specs=out_specs, check_vma=False)
```

time: 187 us -> 238 us (1.27)
  starting transfers between devices: 72.9 us -> 175 us
  waiting for transfers between devices: 84.8 us -> 43.4 us
  local copies, waits for them, and re-layouts: 10.1 us -> 0.66 us
    ppermute x38 -> x56, starting transfers between devices: 41.5 us -> 164 us  [send(): return lax.ppermute(block, ('sweep', 'plane'), route)]
    ppermute x38 -> x56, waiting for transfers between devices: 76.2 us -> 39.1 us  [send(): return lax.ppermute(block, ('sweep', 'plane'), route)]
    ppermute x1, starting transfers between devices: 20.4 us -> 7.64 us  [shards(): lax.ppermute(small, 'sweep', [(i, i + 1) for i in range(sections - 1)])]
    ppermute x6 -> x0, starting transfers between devices: 9.65 us -> none  [pass_on(): return lax.ppermute(block, 'sweep', [(start, stop)])]
    unnamed x18 -> x4, local copies, waits for them, and re-layouts: 10.1 us -> 0.66 us
    ppermute x6 -> x0, waiting for transfers between devices: 7.09 us -> none  [pass_on(): return lax.ppermute(block, 'sweep', [(start, stop)])]
    ppermute x1, waiting for transfers between devices: 0.01 us -> 2.73 us  [shards(): lax.ppermute(packet, 'sweep', [(i + 1, i) for i in range(sections - 1)])]
  transfers between devices with their start and end apart: 46 -> 58, of which waited for: 11 -> 6; matrix products, arithmetic and copies ran while one was open for 0% -> 0% of each run, Pallas kernels for 0% -> 0%
where the time goes in v3:
time: 238 us; the launch traced here: 237 us
  starting transfers between devices  175 us (74%)
  waiting for transfers between devices  43.4 us (18%)
  Pallas kernels  16.5 us (7%)
    ppermute x56, starting transfers between devices, send(): return lax.ppermute(block, ('sweep', 'plane'), route)  164 us
    ppermute x56, waiting for transfers between devices, send(): return lax.ppermute(block, ('sweep', 'plane'), route)  39.1 us
    pallas_call x9, Pallas kernels, call(): pl.pallas_call(kernel, in_specs=specs, out_specs=[whole()] * len(outs), o...  16.5 us
    ppermute x1, starting transfers between devices, shards(): lax.ppermute(small, 'sweep', [(i, i + 1) for i in range(sections - 1)])  7.64 us
  transfers between devices with their start and end apart: 58, of which 6 were waited for; matrix products, arithmetic and copies ran while one was open for 0% of the time, Pallas kernels for 0%

profile of v3, /device:TPU:0, one launch (start us, length us, event | category | flops | bytes accessed | tf_op | source)
XLA Modules:
  0.0 236.8 jit_solution(17701674474938748120)
XLA Ops:
  0.0 2.2 first_fronts.1
  2.2 5.8 %collective-permute-start.2 = (bf16[8,16,128]{2,1,0:T(8,128)(2,1)S(1)}, bf16[8,16,128]{2,1,0:T(8,128)(2,1)S(1)}, u32[]{:S(2)}, u32[]{:S(2)}) collective-permute-start(bf16[8,16,128]{2,1,0:T(8,128)(2,1)S(1)} %get-tuple-element.32.rest_0_), channel_id=1, source_target_pairs={{0,6},{1,7},{2,0},{3,1},{4,2},{5,3},{6,4},{7,5}} | collective-permute-start | bytes 98312 | tf_op jit(solution)/shard_map/ppermute | solution.py:401
  8.0 2.4 %collective-permute-start.1 = (bf16[8,16,128]{2,1,0:T(8,128)(2,1)S(1)}, bf16[8,16,128]{2,1,0:T(8,128)(2,1)S(1)}, u32[]{:S(2)}, u32[]{:S(2)}) collective-permute-start(bf16[8,16,128]{2,1,0:T(8,128)(2,1)S(1)} %get-tuple-element.32.rest_0_), channel_id=1, source_target_pairs={{0,4},{1,5},{2,6},{3,7},{4,0},{5,1},{6,2},{7,3}} | collective-permute-start | bytes 98312 | tf_op jit(solution)/shard_map/ppermute | solution.py:401
  10.4 2.5 %collective-permute-start = (bf16[8,16,128]{2,1,0:T(8,128)(2,1)S(1)}, bf16[8,16,128]{2,1,0:T(8,128)(2,1)S(1)}, u32[]{:S(2)}, u32[]{:S(2)}) collective-permute-start(bf16[8,16,128]{2,1,0:T(8,128)(2,1)S(1)} %get-tuple-element.32.rest_0_), channel_id=1, source_target_pairs={{0,2},{1,3},{2,4},{3,5},{4,6},{5,7},{6,0},{7,1}} | collective-permute-start | bytes 98312 | tf_op jit(solution)/shard_map/ppermute | solution.py:401
  12.9 3.2 %collective-permute-start.4 = (f32[40,1024]{1,0:T(8,128)S(1)}, f32[40,1024]{1,0:T(8,128)S(1)}, u32[]{:S(2)}, u32[]{:S(2)}) collective-permute-start(f32[40,1024]{1,0:T(8,128)S(1)} %get-tuple-element.30.packet), channel_id=1, source_target_pairs={{8,0},{16,8},{24,16},{9,1},{17,9},{25,17},{10,2},{18,10},{26,18},{... | collective-permute-start | bytes 491528 | tf_op jit(solution)/shard_map/ppermute | solution.py:451
  20.4 2.7 %collective-permute-done.4.rest_5_.rest_9_ = f32[40,1024]{1,0:T(8,128)S(1)} collective-permute-done((f32[40,1024]{1,0:T(8,128)S(1)}, f32[40,1024]{1,0:T(8,128)S(1)}, u32[]{:S(2)}, u32[]{:S(2)}) %collective-permute-start.4) | collective-permute-done | bytes 163872 | tf_op jit(solution)/shard_map/ppermute | solution.py:451
  23.8 6.9 %forward_section_0.1 = (f32[2,16,1024]{2,1,0:T(8,128)S(1)}, bf16[8,16,128]{2,1,0:T(8,128)(2,1)S(1)}, bf16[24,16,128]{2,1,0:T(8,128)(2,1)S(1)}, bf16[2,2,512,4096]{3,2,1,0:T(8,128)(2,1)S(1)}) custom-call(s32[4]{0:T(128)S(1)} %copy-done, bf16[2,2,512,4096]{3,2,1,0:T(8,128)(2,1)} %inverse.1, f32[40,1024]{1,0:T(8,128)S(1)} %get-tuple-element.30.packet, ...), custom_call_target="tpu_custom_call" | custom-call | tf_op jit(solution)/shard_map/forward_section_0/pallas_call | solution.py:348
  30.7 3.0 %collective-permute-start.6 = (bf16[24,16,128]{2,1,0:T(8,128)(2,1)S(1)}, bf16[24,16,128]{2,1,0:T(8,128)(2,1)S(1)}, u32[]{:S(2)}, u32[]{:S(2)}) collective-permute-start(bf16[24,16,128]{2,1,0:T(8,128)(2,1)S(1)} %get-tuple-element.36), channel_id=1, source_target_pairs={{0,8},{1,9},{2,10},{3,11},{4,12},{5,13},{6,14},{7,15}} | collective-permute-start | bytes 294920 | tf_op jit(solution)/shard_map/ppermute | solution.py:401
  35.0 3.1 %collective-permute-start.9 = (bf16[8,16,128]{2,1,0:T(8,128)(2,1)S(1)}, bf16[8,16,128]{2,1,0:T(8,128)(2,1)S(1)}, u32[]{:S(2)}, u32[]{:S(2)}) collective-permute-start(bf16[8,16,128]{2,1,0:T(8,128)(2,1)S(1)} %get-tuple-element.35), channel_id=1, source_target_pairs={{0,14},{1,15},{2,8},{3,9},{4,10},{5,11},{6,12},{7,13}} | collective-permute-start | bytes 98312 | tf_op jit(solution)/shard_map/ppermute | solution.py:401
  50.9 34.7 %collective-permute-start.25 = (bf16[8,16,128]{2,1,0:T(8,128)(2,1)S(1)}, bf16[8,16,128]{2,1,0:T(8,128)(2,1)S(1)}, u32[]{:S(2)}, u32[]{:S(2)}) collective-permute-start(bf16[8,16,128]{2,1,0:T(8,128)(2,1)S(1)} %get-tuple-element.39), channel_id=1, source_target_pairs={{16,30},{17,31},{18,24},{19,25},{20,26},{21,27},{22,28},{23,29}} | collective-permute-start | bytes 98312 | tf_op jit(solution)/shard_map/ppermute | solution.py:401
  85.6 6.4 %collective-permute-start.24 = (bf16[8,16,128]{2,1,0:T(8,128)(2,1)S(1)}, bf16[8,16,128]{2,1,0:T(8,128)(2,1)S(1)}, u32[]{:S(2)}, u32[]{:S(2)}) collective-permute-start(bf16[8,16,128]{2,1,0:T(8,128)(2,1)S(1)} %get-tuple-element.39), channel_id=1, source_target_pairs={{16,28},{17,29},{18,30},{19,31},{20,24},{21,25},{22,26},{23,27}} | collective-permute-start | bytes 98312 | tf_op jit(solution)/shard_map/ppermute | solution.py:401
  97.4 29.7 %collective-permute-start.32 = (bf16[4,4,16,128]{3,2,1,0:T(8,128)(2,1)S(1)}, bf16[4,4,16,128]{3,2,1,0:T(8,128)(2,1)S(1)}, u32[]{:S(2)}, u32[]{:S(2)}) collective-permute-start(bf16[4,4,16,128]{3,2,1,0:T(8,128)(2,1)S(1)} %pad_maximum_fusion.1), channel_id=1, source_target_pairs={{24,25},{25,24},{26,27},{27,26},{28,29},{29,28},{30,31},{31,30}} | collective-permute-start | bytes 196616 | tf_op jit(solution)/shard_map/ppermute | solution.py:401
  127.0 7.6 %collective-permute-start.33 = (f32[8,1024]{1,0:T(8,128)S(1)}, f32[8,1024]{1,0:T(8,128)S(1)}, u32[]{:S(2)}, u32[]{:S(2)}) collective-permute-start(f32[8,1024]{1,0:T(8,128)S(1)} %get-tuple-element.34.small), channel_id=1, source_target_pairs={{0,8},{8,16},{16,24},{1,9},{9,17},{17,25},{2,10},{10,18},{18,26},{... | collective-permute-start | bytes 98312 | tf_op jit(solution)/shard_map/ppermute | solution.py:452
  136.8 7.5 %collective-permute-start.35 = (bf16[24,16,128]{2,1,0:T(8,128)(2,1)S(1)}, bf16[24,16,128]{2,1,0:T(8,128)(2,1)S(1)}, u32[]{:S(2)}, u32[]{:S(2)}) collective-permute-start(bf16[24,16,128]{2,1,0:T(8,128)(2,1)S(1)} %get-tuple-element.44), channel_id=1, source_target_pairs={{24,16},{25,17},{26,18},{27,19},{28,20},{29,21},{30,22},{31,23}} | collective-permute-start | bytes 294920 | tf_op jit(solution)/shard_map/ppermute | solution.py:401
  144.3 7.0 %collective-permute-start.34 = (bf16[8,16,128]{2,1,0:T(8,128)(2,1)S(1)}, bf16[8,16,128]{2,1,0:T(8,128)(2,1)S(1)}, u32[]{:S(2)}, u32[]{:S(2)}) collective-permute-start(bf16[8,16,128]{2,1,0:T(8,128)(2,1)S(1)} %get-tuple-element.43), channel_id=1, source_target_pairs={{24,17},{25,16},{26,19},{27,18},{28,21},{29,20},{30,23},{31,22}} | collective-permute-start | bytes 98312 | tf_op jit(solution)/shard_map/ppermute | solution.py:401
  151.3 7.0 %collective-permute-start.38 = (bf16[8,16,128]{2,1,0:T(8,128)(2,1)S(1)}, bf16[8,16,128]{2,1,0:T(8,128)(2,1)S(1)}, u32[]{:S(2)}, u32[]{:S(2)}) collective-permute-start(bf16[8,16,128]{2,1,0:T(8,128)(2,1)S(1)} %get-tuple-element.43), channel_id=1, source_target_pairs={{24,22},{25,23},{26,16},{27,17},{28,18},{29,19},{30,20},{31,21}} | collective-permute-start | bytes 98312 | tf_op jit(solution)/shard_map/ppermute | solution.py:401
  158.4 7.0 %collective-permute-start.37 = (bf16[8,16,128]{2,1,0:T(8,128)(2,1)S(1)}, bf16[8,16,128]{2,1,0:T(8,128)(2,1)S(1)}, u32[]{:S(2)}, u32[]{:S(2)}) collective-permute-start(bf16[8,16,128]{2,1,0:T(8,128)(2,1)S(1)} %get-tuple-element.43), channel_id=1, source_target_pairs={{24,20},{25,21},{26,22},{27,23},{28,16},{29,17},{30,18},{31,19}} | collective-permute-start | bytes 98312 | tf_op jit(solution)/shard_map/ppermute | solution.py:401
  165.4 7.0 %collective-permute-start.36 = (bf16[8,16,128]{2,1,0:T(8,128)(2,1)S(1)}, bf16[8,16,128]{2,1,0:T(8,128)(2,1)S(1)}, u32[]{:S(2)}, u32[]{:S(2)}) collective-permute-start(bf16[8,16,128]{2,1,0:T(8,128)(2,1)S(1)} %get-tuple-element.43), channel_id=1, source_target_pairs={{24,18},{25,19},{26,20},{27,21},{28,22},{29,23},{30,16},{31,17}} | collective-permute-start | bytes 98312 | tf_op jit(solution)/shard_map/ppermute | solution.py:401
  187.8 32.7 %collective-permute-done.50.rest_0_ = bf16[8,16,128]{2,1,0:T(8,128)(2,1)S(1)} collective-permute-done((bf16[8,16,128]{2,1,0:T(8,128)(2,1)S(1)}, bf16[8,16,128]{2,1,0:T(8,128)(2,1)S(1)}, u32[]{:S(2)}, u32[]{:S(2)}) %collective-permute-start.50) | collective-permute-done | bytes 32800 | tf_op jit(solution)/shard_map/ppermute | solution.py:401
  220.5 1.9 collective-permute-start.57
  222.5 3.8 %collective-permute-start.56 = (bf16[8,16,128]{2,1,0:T(8,128)(2,1)S(1)}, bf16[8,16,128]{2,1,0:T(8,128)(2,1)S(1)}, u32[]{:S(2)}, u32[]{:S(2)}) collective-permute-start(bf16[8,16,128]{2,1,0:T(8,128)(2,1)S(1)} %collective-permute-done.50.rest_0_), channel_id=1, source_target_pairs={{0,4},{1,5},{2,6},{3,7},{4,0},{5,1},{6,2},{7,3}} | collective-permute-start | bytes 98312 | tf_op jit(solution)/shard_map/ppermute | solution.py:401
  226.2 2.7 %collective-permute-start.55 = (bf16[8,16,128]{2,1,0:T(8,128)(2,1)S(1)}, bf16[8,16,128]{2,1,0:T(8,128)(2,1)S(1)}, u32[]{:S(2)}, u32[]{:S(2)}) collective-permute-start(bf16[8,16,128]{2,1,0:T(8,128)(2,1)S(1)} %collective-permute-done.50.rest_0_), channel_id=1, source_target_pairs={{0,2},{1,3},{2,4},{3,5},{4,6},{5,7},{6,0},{7,1}} | collective-permute-start | bytes 98312 | tf_op jit(solution)/shard_map/ppermute | solution.py:401
  229.0 4.0 %collective-permute-done.55.rest_5_ = bf16[8,16,128]{2,1,0:T(8,128)(2,1)S(1)} collective-permute-done((bf16[8,16,128]{2,1,0:T(8,128)(2,1)S(1)}, bf16[8,16,128]{2,1,0:T(8,128)(2,1)S(1)}, u32[]{:S(2)}, u32[]{:S(2)}) %collective-permute-start.55) | collective-permute-done | bytes 32800 | tf_op jit(solution)/shard_map/ppermute | solution.py:401
  233.0 3.8 %backward_section_0.1 = f32[2,16,1024]{2,1,0:T(8,128)} custom-call(s32[4]{0:T(128)S(1)} %copy-done.1, bf16[2,2,512,4096]{3,2,1,0:T(8,128)(2,1)S(1)} %get-tuple-element.33.inverse, f32[8,1024]{1,0:T(8,128)S(1)} %get-tuple-element.34.small, s32[2,1024]{1,0:T(2,128)S(1)} %get-tuple-element.31.place, bf16[8,16,128]{2,1,0:T(8,128)(2,1)S(1)} %collective-permute-done.50.rest_0_, ...), custom_call_target="tpu_custom_call" | custom-call | tf_op jit(solution)/shard_map/backward_section_0/pallas_call | solution.py:348
  (107 shorter events, 41.4 us)
Async XLA Ops:
  2.2 13.9 %collective-permute-start.2 = (bf16[8,16,128]{2,1,0:T(8,128)(2,1)S(1)}, bf16[8,16,128]{2,1,0:T(8,128)(2,1)S(1)}, u32[]{:S(2)}, u32[]{:S(2)}) collective-permute-start(bf16[8,16,128]{2,1,0:T(8,128)(2,1)S(1)} %get-tuple-element.32.rest_0_), channel_id=1, source_target_pairs={{0,6},{1,7},{2,0},{3,1},{4,2},{5,3},{6,4},{7,5}} | collective-permute-start | bytes 98312 | tf_op jit(solution)/shard_map/ppermute | solution.py:401
  8.0 8.1 %collective-permute-start.1 = (bf16[8,16,128]{2,1,0:T(8,128)(2,1)S(1)}, bf16[8,16,128]{2,1,0:T(8,128)(2,1)S(1)}, u32[]{:S(2)}, u32[]{:S(2)}) collective-permute-start(bf16[8,16,128]{2,1,0:T(8,128)(2,1)S(1)} %get-tuple-element.32.rest_0_), channel_id=1, source_target_pairs={{0,4},{1,5},{2,6},{3,7},{4,0},{5,1},{6,2},{7,3}} | collective-permute-start | bytes 98312 | tf_op jit(solution)/shard_map/ppermute | solution.py:401
  10.4 6.7 %collective-permute-start = (bf16[8,16,128]{2,1,0:T(8,128)(2,1)S(1)}, bf16[8,16,128]{2,1,0:T(8,128)(2,1)S(1)}, u32[]{:S(2)}, u32[]{:S(2)}) collective-permute-start(bf16[8,16,128]{2,1,0:T(8,128)(2,1)S(1)} %get-tuple-element.32.rest_0_), channel_id=1, source_target_pairs={{0,2},{1,3},{2,4},{3,5},{4,6},{5,7},{6,0},{7,1}} | collective-permute-start | bytes 98312 | tf_op jit(solution)/shard_map/ppermute | solution.py:401
  12.9 10.2 %collective-permute-start.4 = (f32[40,1024]{1,0:T(8,128)S(1)}, f32[40,1024]{1,0:T(8,128)S(1)}, u32[]{:S(2)}, u32[]{:S(2)}) collective-permute-start(f32[40,1024]{1,0:T(8,128)S(1)} %get-tuple-element.30.packet), channel_id=1, source_target_pairs={{8,0},{16,8},{24,16},{9,1},{17,9},{25,17},{10,2},{18,10},{26,18},{... | collective-permute-start | bytes 491528 | tf_op jit(solution)/shard_map/ppermute | solution.py:451
  30.7 12.1 %collective-permute-start.6 = (bf16[24,16,128]{2,1,0:T(8,128)(2,1)S(1)}, bf16[24,16,128]{2,1,0:T(8,128)(2,1)S(1)}, u32[]{:S(2)}, u32[]{:S(2)}) collective-permute-start(bf16[24,16,128]{2,1,0:T(8,128)(2,1)S(1)} %get-tuple-element.36), channel_id=1, source_target_pairs={{0,8},{1,9},{2,10},{3,11},{4,12},{5,13},{6,14},{7,15}} | collective-permute-start | bytes 294920 | tf_op jit(solution)/shard_map/ppermute | solution.py:401
  33.7 7.0 %collective-permute-start.5 = (bf16[8,16,128]{2,1,0:T(8,128)(2,1)S(1)}, bf16[8,16,128]{2,1,0:T(8,128)(2,1)S(1)}, u32[]{:S(2)}, u32[]{:S(2)}) collective-permute-start(bf16[8,16,128]{2,1,0:T(8,128)(2,1)S(1)} %get-tuple-element.35), channel_id=1, source_target_pairs={{0,9},{1,8},{2,11},{3,10},{4,13},{5,12},{6,15},{7,14}} | collective-permute-start | bytes 98312 | tf_op jit(solution)/shard_map/ppermute | solution.py:401
  49.6 45.1 %collective-permute-start.22 = (bf16[24,16,128]{2,1,0:T(8,128)(2,1)S(1)}, bf16[24,16,128]{2,1,0:T(8,128)(2,1)S(1)}, u32[]{:S(2)}, u32[]{:S(2)}) collective-permute-start(bf16[24,16,128]{2,1,0:T(8,128)(2,1)S(1)} %get-tuple-element.40), channel_id=1, source_target_pairs={{16,24},{17,25},{18,26},{19,27},{20,28},{21,29},{22,30},{23,31}} | collective-permute-start | bytes 294920 | tf_op jit(solution)/shard_map/ppermute | solution.py:401
  50.3 42.4 %collective-permute-start.21 = (bf16[8,16,128]{2,1,0:T(8,128)(2,1)S(1)}, bf16[8,16,128]{2,1,0:T(8,128)(2,1)S(1)}, u32[]{:S(2)}, u32[]{:S(2)}) collective-permute-start(bf16[8,16,128]{2,1,0:T(8,128)(2,1)S(1)} %get-tuple-element.39), channel_id=1, source_target_pairs={{16,25},{17,24},{18,27},{19,26},{20,29},{21,28},{22,31},{23,30}} | collective-permute-start | bytes 98312 | tf_op jit(solution)/shard_map/ppermute | solution.py:401
  50.9 42.4 %collective-permute-start.25 = (bf16[8,16,128]{2,1,0:T(8,128)(2,1)S(1)}, bf16[8,16,128]{2,1,0:T(8,128)(2,1)S(1)}, u32[]{:S(2)}, u32[]{:S(2)}) collective-permute-start(bf16[8,16,128]{2,1,0:T(8,128)(2,1)S(1)} %get-tuple-element.39), channel_id=1, source_target_pairs={{16,30},{17,31},{18,24},{19,25},{20,26},{21,27},{22,28},{23,29}} | collective-permute-start | bytes 98312 | tf_op jit(solution)/shard_map/ppermute | solution.py:401
  85.6 8.4 %collective-permute-start.24 = (bf16[8,16,128]{2,1,0:T(8,128)(2,1)S(1)}, bf16[8,16,128]{2,1,0:T(8,128)(2,1)S(1)}, u32[]{:S(2)}, u32[]{:S(2)}) collective-permute-start(bf16[8,16,128]{2,1,0:T(8,128)(2,1)S(1)} %get-tuple-element.39), channel_id=1, source_target_pairs={{16,28},{17,29},{18,30},{19,31},{20,24},{21,25},{22,26},{23,27}} | collective-permute-start | bytes 98312 | tf_op jit(solution)/shard_map/ppermute | solution.py:401
  97.4 38.9 %collective-permute-start.32 = (bf16[4,4,16,128]{3,2,1,0:T(8,128)(2,1)S(1)}, bf16[4,4,16,128]{3,2,1,0:T(8,128)(2,1)S(1)}, u32[]{:S(2)}, u32[]{:S(2)}) collective-permute-start(bf16[4,4,16,128]{3,2,1,0:T(8,128)(2,1)S(1)} %pad_maximum_fusion.1), channel_id=1, source_target_pairs={{24,25},{25,24},{26,27},{27,26},{28,29},{29,28},{30,31},{31,30}} | collective-permute-start | bytes 196616 | tf_op jit(solution)/shard_map/ppermute | solution.py:401
  127.0 9.2 %collective-permute-start.33 = (f32[8,1024]{1,0:T(8,128)S(1)}, f32[8,1024]{1,0:T(8,128)S(1)}, u32[]{:S(2)}, u32[]{:S(2)}) collective-permute-start(f32[8,1024]{1,0:T(8,128)S(1)} %get-tuple-element.34.small), channel_id=1, source_target_pairs={{0,8},{8,16},{16,24},{1,9},{9,17},{17,25},{2,10},{10,18},{18,26},{... | collective-permute-start | bytes 98312 | tf_op jit(solution)/shard_map/ppermute | solution.py:452
  136.8 37.6 %collective-permute-start.35 = (bf16[24,16,128]{2,1,0:T(8,128)(2,1)S(1)}, bf16[24,16,128]{2,1,0:T(8,128)(2,1)S(1)}, u32[]{:S(2)}, u32[]{:S(2)}) collective-permute-start(bf16[24,16,128]{2,1,0:T(8,128)(2,1)S(1)} %get-tuple-element.44), channel_id=1, source_target_pairs={{24,16},{25,17},{26,18},{27,19},{28,20},{29,21},{30,22},{31,23}} | collective-permute-start | bytes 294920 | tf_op jit(solution)/shard_map/ppermute | solution.py:401
  144.3 28.1 %collective-permute-start.34 = (bf16[8,16,128]{2,1,0:T(8,128)(2,1)S(1)}, bf16[8,16,128]{2,1,0:T(8,128)(2,1)S(1)}, u32[]{:S(2)}, u32[]{:S(2)}) collective-permute-start(bf16[8,16,128]{2,1,0:T(8,128)(2,1)S(1)} %get-tuple-element.43), channel_id=1, source_target_pairs={{24,17},{25,16},{26,19},{27,18},{28,21},{29,20},{30,23},{31,22}} | collective-permute-start | bytes 98312 | tf_op jit(solution)/shard_map/ppermute | solution.py:401
  151.3 21.7 %collective-permute-start.38 = (bf16[8,16,128]{2,1,0:T(8,128)(2,1)S(1)}, bf16[8,16,128]{2,1,0:T(8,128)(2,1)S(1)}, u32[]{:S(2)}, u32[]{:S(2)}) collective-permute-start(bf16[8,16,128]{2,1,0:T(8,128)(2,1)S(1)} %get-tuple-element.43), channel_id=1, source_target_pairs={{24,22},{25,23},{26,16},{27,17},{28,18},{29,19},{30,20},{31,21}} | collective-permute-start | bytes 98312 | tf_op jit(solution)/shard_map/ppermute | solution.py:401
  158.4 15.4 %collective-permute-start.37 = (bf16[8,16,128]{2,1,0:T(8,128)(2,1)S(1)}, bf16[8,16,128]{2,1,0:T(8,128)(2,1)S(1)}, u32[]{:S(2)}, u32[]{:S(2)}) collective-permute-start(bf16[8,16,128]{2,1,0:T(8,128)(2,1)S(1)} %get-tuple-element.43), channel_id=1, source_target_pairs={{24,20},{25,21},{26,22},{27,23},{28,16},{29,17},{30,18},{31,19}} | collective-permute-start | bytes 98312 | tf_op jit(solution)/shard_map/ppermute | solution.py:401
  165.4 9.1 %collective-permute-start.36 = (bf16[8,16,128]{2,1,0:T(8,128)(2,1)S(1)}, bf16[8,16,128]{2,1,0:T(8,128)(2,1)S(1)}, u32[]{:S(2)}, u32[]{:S(2)}) collective-permute-start(bf16[8,16,128]{2,1,0:T(8,128)(2,1)S(1)} %get-tuple-element.43), channel_id=1, source_target_pairs={{24,18},{25,19},{26,20},{27,21},{28,22},{29,23},{30,16},{31,17}} | collective-permute-start | bytes 98312 | tf_op jit(solution)/shard_map/ppermute | solution.py:401
  181.3 51.6 %collective-permute-start.51 = (bf16[24,16,128]{2,1,0:T(8,128)(2,1)S(1)}, bf16[24,16,128]{2,1,0:T(8,128)(2,1)S(1)}, u32[]{:S(2)}, u32[]{:S(2)}) collective-permute-start(bf16[24,16,128]{2,1,0:T(8,128)(2,1)S(1)} %get-tuple-element.52), channel_id=1, source_target_pairs={{8,0},{9,1},{10,2},{11,3},{12,4},{13,5},{14,6},{15,7}} | collective-permute-start | bytes 294920 | tf_op jit(solution)/shard_map/ppermute | solution.py:401
  182.6 37.9 %collective-permute-start.50 = (bf16[8,16,128]{2,1,0:T(8,128)(2,1)S(1)}, bf16[8,16,128]{2,1,0:T(8,128)(2,1)S(1)}, u32[]{:S(2)}, u32[]{:S(2)}) collective-permute-start(bf16[8,16,128]{2,1,0:T(8,128)(2,1)S(1)} %get-tuple-element.51), channel_id=1, source_target_pairs={{8,1},{9,0},{10,3},{11,2},{12,5},{13,4},{14,7},{15,6}} | collective-permute-start | bytes 98312 | tf_op jit(solution)/shard_map/ppermute | solution.py:401
  183.9 38.5 %collective-permute-start.54 = (bf16[8,16,128]{2,1,0:T(8,128)(2,1)S(1)}, bf16[8,16,128]{2,1,0:T(8,128)(2,1)S(1)}, u32[]{:S(2)}, u32[]{:S(2)}) collective-permute-start(bf16[8,16,128]{2,1,0:T(8,128)(2,1)S(1)} %get-tuple-element.51), channel_id=1, source_target_pairs={{8,6},{9,7},{10,0},{11,1},{12,2},{13,3},{14,4},{15,5}} | collective-permute-start | bytes 98312 | tf_op jit(solution)/shard_map/ppermute | solution.py:401
  185.2 41.0 %collective-permute-start.53 = (bf16[8,16,128]{2,1,0:T(8,128)(2,1)S(1)}, bf16[8,16,128]{2,1,0:T(8,128)(2,1)S(1)}, u32[]{:S(2)}, u32[]{:S(2)}) collective-permute-start(bf16[8,16,128]{2,1,0:T(8,128)(2,1)S(1)} %get-tuple-element.51), channel_id=1, source_target_pairs={{8,4},{9,5},{10,6},{11,7},{12,0},{13,1},{14,2},{15,3}} | collective-permute-start | bytes 98312 | tf_op jit(solution)/shard_map/ppermute | solution.py:401
  186.5 42.4 %collective-permute-start.52 = (bf16[8,16,128]{2,1,0:T(8,128)(2,1)S(1)}, bf16[8,16,128]{2,1,0:T(8,128)(2,1)S(1)}, u32[]{:S(2)}, u32[]{:S(2)}) collective-permute-start(bf16[8,16,128]{2,1,0:T(8,128)(2,1)S(1)} %get-tuple-element.51), channel_id=1, source_target_pairs={{8,2},{9,3},{10,4},{11,5},{12,6},{13,7},{14,0},{15,1}} | collective-permute-start | bytes 98312 | tf_op jit(solution)/shard_map/ppermute | solution.py:401
  220.5 8.5 %collective-permute-start.57 = (bf16[8,16,128]{2,1,0:T(8,128)(2,1)S(1)}, bf16[8,16,128]{2,1,0:T(8,128)(2,1)S(1)}, u32[]{:S(2)}, u32[]{:S(2)}) collective-permute-start(bf16[8,16,128]{2,1,0:T(8,128)(2,1)S(1)} %collective-permute-done.50.rest_0_), channel_id=1, source_target_pairs={{0,6},{1,7},{2,0},{3,1},{4,2},{5,3},{6,4},{7,5}} | collective-permute-start | bytes 98312 | tf_op jit(solution)/shard_map/ppermute | solution.py:401
  226.2 6.7 %collective-permute-start.55 = (bf16[8,16,128]{2,1,0:T(8,128)(2,1)S(1)}, bf16[8,16,128]{2,1,0:T(8,128)(2,1)S(1)}, u32[]{:S(2)}, u32[]{:S(2)}) collective-permute-start(bf16[8,16,128]{2,1,0:T(8,128)(2,1)S(1)} %collective-permute-done.50.rest_0_), channel_id=1, source_target_pairs={{0,2},{1,3},{2,4},{3,5},{4,6},{5,7},{6,0},{7,1}} | collective-permute-start | bytes 98312 | tf_op jit(solution)/shard_map/ppermute | solution.py:401
  (36 other events, 110.2 us)

commit v4 on v3

--- a/solution.py
+++ b/solution.py
@@ -97,11 +97,7 @@
     if isinstance(place, int):
         return place
     step, other = place
-    chips = planes // CORES
-    own = lax.axis_index("plane")
-    chip, core = own // CORES, lax.rem(own, CORES)
-    chip = lax.rem(chip - step + chips, chips) if step else chip
-    return chip * CORES + (CORES - 1 - core if other else core)
+    return lax.bitwise_xor(lax.axis_index("plane"), step * CORES + int(other))
 
 
 def stack_fronts(blocks, owners, planes, per_layer, stacked, layer):
@@ -376,7 +372,7 @@
     width = -(-owned // LANES) * LANES
     per_layer = width // LANES
     chips = planes // CORES
-    direct = planes == chips * CORES and chips <= 4 and owned == width
+    direct = planes in (2, 4, 8) and owned == width
 
     rhs = rhs_field.reshape(layer_slots, rows, cells)
     picked = jnp.pad(front_cells, ((0, 0), (0, width - owned)), constant_values=-1)
@@ -391,13 +387,12 @@
         pltpu.VMEM((2, rows, width), F32),
     ]
 
-    def send(block, start, stop, chip_step=0, other_core=False):
-        route = []
-        for own in range(planes):
-            chip, core = own // CORES, own % CORES
-            chip = (chip + chip_step) % chips
-            core = CORES - 1 - core if other_core else core
-            route.append((start * planes + own, stop * planes + chip * CORES + core))
+    def send(block, start, stop, step=0, other_core=False):
+        flip = step * CORES + int(other_core)
+        pairs = [(start, stop)] if start is not None else [(i, i) for i in range(sections)]
+        route = [
+            (i * planes + own, j * planes + (own ^ flip)) for i, j in pairs for own in range(planes)
+        ]
         return lax.ppermute(block, ("sweep", "plane"), route)
 
     def everywhere(front):
@@ -412,11 +407,11 @@
             return [gathered], [[0]], order // LANES
         return [gathered], [list(range(planes))], per_layer
 
-    def within(front, section):
+    def within(front):
         if not direct:
             return everywhere(front)
-        mine = [front] + [send(front, section, section, s) for s in range(1, chips)]
-        swapped = send(jnp.stack(mine), section, section, other_core=True)
+        mine = [front] + [send(front, None, None, s) for s in range(1, chips)]
+        swapped = send(jnp.stack(mine), None, None, other_core=True)
         owners = [[(s, False)] for s in range(chips)] + [[(s, True) for s in range(chips)]]
         return mine + [swapped], owners, per_layer
 
@@ -424,13 +419,12 @@
         if not direct:
             packet = lax.ppermute(packet, "sweep", [(start, stop)])
             return *everywhere(packet[:2 * per_layer]), packet
-        other = send(front, start, stop, other_core=True)
-        across = [send(front, start, stop, s) for s in range(1, chips)]
         packet = send(packet, start, stop)
-        relayed = [send(other, stop, stop, s) for s in range(1, chips)]
-        owners = [[(0, True)], [(0, False)]]
-        owners += [[(s, False)] for s in range(1, chips)] + [[(s, True)] for s in range(1, chips)]
-        return [other, packet] + across + relayed, owners, per_layer, packet
+        mine = [packet] + [send(front, start, stop, s) for s in range(1, chips)]
+        swapped = jnp.stack([packet[:2 * per_layer]] + mine[1:])
+        swapped = send(swapped, None, None, other_core=True)
+        owners = [[(s, False)] for s in range(chips)] + [[(s, True) for s in range(chips)]]
+        return mine + [swapped], owners, per_layer, packet
 
     packet, small, place, front = call(
         functools.partial(first_kernel, width),
@@ -447,7 +441,7 @@
         "first_fronts",
         [(i, pltpu.HBM) for i in range(5)],
     )
-    gathered, owners, slots = within(front, 0)
+    gathered, owners, slots = within(front)
     after = lax.ppermute(packet, "sweep", [(i + 1, i) for i in range(sections - 1)])
     behind = lax.ppermute(small, "sweep", [(i, i + 1) for i in range(sections - 1)])
 
@@ -476,9 +470,9 @@
             inverse = outs[-1]
         kept.append(outs[0])
         if final:
-            gathered, owners, slots = within(outs[1], step)
+            gathered, owners, slots = within(outs[1])
         else:
-            gathered, owners, slots, incoming = between(outs[1], outs[2], step, step + 1)
+            gathered, owners, slots, incoming = between(*outs[1:3], step, step + 1)
             held.append(incoming)
 
     result = incoming = None
@@ -495,7 +489,7 @@
         )
         result = outs[0]
         if step:
-            gathered, owners, slots, incoming = between(outs[1], outs[2], step, step - 1)
+            gathered, owners, slots, incoming = between(*outs[1:3], step, step - 1)
     return result.reshape(rhs_field.shape)
 
 

time: 238 us -> 129 us (0.54)
  starting transfers between devices: 175 us -> 47.3 us
  waiting for transfers between devices: 43.4 us -> 63 us
    ppermute x56 -> x38, starting transfers between devices: 164 us -> 34.1 us  [send(): return lax.ppermute(block, ('sweep', 'plane'), route)]
    ppermute x56 -> x38, waiting for transfers between devices: 39.1 us -> 59.4 us  [send(): return lax.ppermute(block, ('sweep', 'plane'), route)]
    ppermute x1, starting transfers between devices: 7.64 us -> 11.9 us  [shards(): lax.ppermute(small, 'sweep', [(i, i + 1) for i in range(sections - 1)])]
  transfers between devices with their start and end apart: 58 -> 40, of which waited for: 6 -> 19; matrix products, arithmetic and copies ran while one was open for 0% -> 0% of each run, Pallas kernels for 0% -> 0%
where the time goes in v4:
time: 129 us; the launch traced here: 128 us
  waiting for transfers between devices  63 us (49%)
  starting transfers between devices  47.3 us (37%)
  Pallas kernels  16.7 us (13%)
    ppermute x38, waiting for transfers between devices, send(): return lax.ppermute(block, ('sweep', 'plane'), route)  59.4 us
    ppermute x38, starting transfers between devices, send(): return lax.ppermute(block, ('sweep', 'plane'), route)  34.1 us
    pallas_call x9, Pallas kernels, call(): pl.pallas_call(kernel, in_specs=specs, out_specs=[whole()] * len(outs), o...  16.7 us
    ppermute x1, starting transfers between devices, shards(): lax.ppermute(small, 'sweep', [(i, i + 1) for i in range(sections - 1)])  11.9 us
  transfers between devices with their start and end apart: 40, of which 19 were waited for; matrix products, arithmetic and copies ran while one was open for 0% of the time, Pallas kernels for 0%

profile of v4, /device:TPU:0, one launch (start us, length us, event | category | flops | bytes accessed | tf_op | source)
XLA Modules:
  0.0 128.4 jit_solution(11304723675298847627)
XLA Ops:
  0.0 2.2 %first_fronts.1 = (f32[40,1024]{1,0:T(8,128)S(1)}, f32[8,1024]{1,0:T(8,128)S(1)}, s32[2,1024]{1,0:T(2,128)S(1)}, bf16[8,16,128]{2,1,0:T(8,128)(2,1)S(1)}) custom-call(f32[2,16,1024]{2,1,0:T(8,128)} %bitcast.66, f32[2,1024]{1,0:T(2,128)} %isc_in.1, f32[2,1024]{1,0:T(2,128)} %fwd_in.1, f32[2,1024]{1,0:T(2,128)} %bwd_in.1, s32[2,512]{1,0:T(2,128)} %picked_in.1), custom_call_target="tpu_custom_call" | custom-call | tf_op jit(solution)/shard_map/first_fronts/pallas_call | solution.py:344
  2.2 4.0 %collective-permute-start.2 = (bf16[8,16,128]{2,1,0:T(8,128)(2,1)S(1)}, bf16[8,16,128]{2,1,0:T(8,128)(2,1)S(1)}, u32[]{:S(2)}, u32[]{:S(2)}) collective-permute-start(bf16[8,16,128]{2,1,0:T(8,128)(2,1)S(1)} %get-tuple-element.32.rest_0_), channel_id=1, source_target_pairs={{0,6},{1,7},{2,4},{3,5},{4,2},{5,3},{6,0},{7,1},{8,14},{9,15},{10,... | collective-permute-start | bytes 98312 | tf_op jit(solution)/shard_map/ppermute | solution.py:396
  8.1 2.0 %collective-permute-done.1.rest_2_ = bf16[8,16,128]{2,1,0:T(8,128)(2,1)S(1)} collective-permute-done((bf16[8,16,128]{2,1,0:T(8,128)(2,1)S(1)}, bf16[8,16,128]{2,1,0:T(8,128)(2,1)S(1)}, u32[]{:S(2)}, u32[]{:S(2)}) %collective-permute-start.1) | collective-permute-done | bytes 32800 | tf_op jit(solution)/shard_map/ppermute | solution.py:396
  10.7 1.3 %collective-permute-done.3.rest_4_ = bf16[4,8,16,128]{3,2,1,0:T(8,128)(2,1)S(1)} collective-permute-done((bf16[4,8,16,128]{3,2,1,0:T(8,128)(2,1)S(1)}, bf16[4,8,16,128]{3,2,1,0:T(8,128)(2,1)S(1)}, u32[]{:S(2)}, u32[]{:S(2)}) %collective-permute-start.3) | collective-permute-done | bytes 131104 | tf_op jit(solution)/shard_map/ppermute | solution.py:396
  12.0 2.0 %collective-permute-done.4.rest_5_.rest_6_ = f32[40,1024]{1,0:T(8,128)S(1)} collective-permute-done((f32[40,1024]{1,0:T(8,128)S(1)}, f32[40,1024]{1,0:T(8,128)S(1)}, u32[]{:S(2)}, u32[]{:S(2)}) %collective-permute-start.4) | collective-permute-done | bytes 163872 | tf_op jit(solution)/shard_map/ppermute | solution.py:445
  14.7 6.9 %forward_section_0.1 = (f32[2,16,1024]{2,1,0:T(8,128)S(1)}, bf16[8,16,128]{2,1,0:T(8,128)(2,1)S(1)}, bf16[24,16,128]{2,1,0:T(8,128)(2,1)S(1)}, bf16[2,2,512,4096]{3,2,1,0:T(8,128)(2,1)S(1)}) custom-call(s32[4]{0:T(128)S(1)} %copy-done, bf16[2,2,512,4096]{3,2,1,0:T(8,128)(2,1)} %inverse.1, f32[40,1024]{1,0:T(8,128)S(1)} %get-tuple-element.30.packet, ...), custom_call_target="tpu_custom_call" | custom-call | tf_op jit(solution)/shard_map/forward_section_0/pallas_call | solution.py:344
  21.6 3.4 %collective-permute-start.5 = (bf16[24,16,128]{2,1,0:T(8,128)(2,1)S(1)}, bf16[24,16,128]{2,1,0:T(8,128)(2,1)S(1)}, u32[]{:S(2)}, u32[]{:S(2)}) collective-permute-start(bf16[24,16,128]{2,1,0:T(8,128)(2,1)S(1)} %get-tuple-element.35), channel_id=1, source_target_pairs={{0,8},{1,9},{2,10},{3,11},{4,12},{5,13},{6,14},{7,15}} | collective-permute-start | bytes 294920 | tf_op jit(solution)/shard_map/ppermute | solution.py:396
  25.1 3.2 %collective-permute-start.8 = (bf16[8,16,128]{2,1,0:T(8,128)(2,1)S(1)}, bf16[8,16,128]{2,1,0:T(8,128)(2,1)S(1)}, u32[]{:S(2)}, u32[]{:S(2)}) collective-permute-start(bf16[8,16,128]{2,1,0:T(8,128)(2,1)S(1)} %get-tuple-element.36), channel_id=1, source_target_pairs={{0,14},{1,15},{2,12},{3,13},{4,10},{5,11},{6,8},{7,9}} | collective-permute-start | bytes 98312 | tf_op jit(solution)/shard_map/ppermute | solution.py:396
  28.2 1.3 %collective-permute-start.7 = (bf16[8,16,128]{2,1,0:T(8,128)(2,1)S(1)}, bf16[8,16,128]{2,1,0:T(8,128)(2,1)S(1)}, u32[]{:S(2)}, u32[]{:S(2)}) collective-permute-start(bf16[8,16,128]{2,1,0:T(8,128)(2,1)S(1)} %get-tuple-element.36), channel_id=1, source_target_pairs={{0,12},{1,13},{2,14},{3,15},{4,8},{5,9},{6,10},{7,11}} | collective-permute-start | bytes 98312 | tf_op jit(solution)/shard_map/ppermute | solution.py:396
  29.5 1.3 %collective-permute-start.6 = (bf16[8,16,128]{2,1,0:T(8,128)(2,1)S(1)}, bf16[8,16,128]{2,1,0:T(8,128)(2,1)S(1)}, u32[]{:S(2)}, u32[]{:S(2)}) collective-permute-start(bf16[8,16,128]{2,1,0:T(8,128)(2,1)S(1)} %get-tuple-element.36), channel_id=1, source_target_pairs={{0,10},{1,11},{2,8},{3,9},{4,14},{5,15},{6,12},{7,13}} | collective-permute-start | bytes 98312 | tf_op jit(solution)/shard_map/ppermute | solution.py:396
  31.1 1.3 %collective-permute-done.6.rest_1_ = bf16[8,16,128]{2,1,0:T(8,128)(2,1)S(1)} collective-permute-done((bf16[8,16,128]{2,1,0:T(8,128)(2,1)S(1)}, bf16[8,16,128]{2,1,0:T(8,128)(2,1)S(1)}, u32[]{:S(2)}, u32[]{:S(2)}) %collective-permute-start.6) | collective-permute-done | bytes 32800 | tf_op jit(solution)/shard_map/ppermute | solution.py:396
  32.5 1.3 %collective-permute-done.9.rest_4_ = bf16[4,8,16,128]{3,2,1,0:T(8,128)(2,1)S(1)} collective-permute-done((bf16[4,8,16,128]{3,2,1,0:T(8,128)(2,1)S(1)}, bf16[4,8,16,128]{3,2,1,0:T(8,128)(2,1)S(1)}, u32[]{:S(2)}, u32[]{:S(2)}) %collective-permute-start.9) | collective-permute-done | bytes 131104 | tf_op jit(solution)/shard_map/ppermute | solution.py:396
  44.7 1.5 %collective-permute-start.21 = (bf16[4,16,128]{2,1,0:T(8,128)(2,1)S(1)}, bf16[4,16,128]{2,1,0:T(8,128)(2,1)S(1)}, u32[]{:S(2)}, u32[]{:S(2)}) collective-permute-start(bf16[4,16,128]{2,1,0:T(8,128)(2,1)S(1)} %get-tuple-element.41.rest_0_), channel_id=1, source_target_pairs={{0,4},{1,5},{2,6},{3,7},{4,0},{5,1},{6,2},{7,3},{8,12},{9,13},{10,... | collective-permute-start | bytes 49160 | tf_op jit(solution)/shard_map/ppermute | solution.py:396
  46.2 1.5 %collective-permute-start.20 = (bf16[4,16,128]{2,1,0:T(8,128)(2,1)S(1)}, bf16[4,16,128]{2,1,0:T(8,128)(2,1)S(1)}, u32[]{:S(2)}, u32[]{:S(2)}) collective-permute-start(bf16[4,16,128]{2,1,0:T(8,128)(2,1)S(1)} %get-tuple-element.41.rest_0_), channel_id=1, source_target_pairs={{0,2},{1,3},{2,0},{3,1},{4,6},{5,7},{6,4},{7,5},{8,10},{9,11},{10,... | collective-permute-start | bytes 49160 | tf_op jit(solution)/shard_map/ppermute | solution.py:396
  50.0 11.9 %collective-permute-start.24 = (f32[8,1024]{1,0:T(8,128)S(1)}, f32[8,1024]{1,0:T(8,128)S(1)}, u32[]{:S(2)}, u32[]{:S(2)}) collective-permute-start(f32[8,1024]{1,0:T(8,128)S(1)} %get-tuple-element.34.small), channel_id=1, source_target_pairs={{0,8},{8,16},{16,24},{1,9},{9,17},{17,25},{2,10},{10,18},{18,26},{... | collective-permute-start | bytes 98312 | tf_op jit(solution)/shard_map/ppermute | solution.py:446
  62.0 1.6 %collective-permute-done.24.rest_6_.rest_8_ = f32[8,1024]{1,0:T(8,128)S(1)} collective-permute-done((f32[8,1024]{1,0:T(8,128)S(1)}, f32[8,1024]{1,0:T(8,128)S(1)}, u32[]{:S(2)}, u32[]{:S(2)}) %collective-permute-start.24) | collective-permute-done | bytes 32800 | tf_op jit(solution)/shard_map/ppermute | solution.py:446
  67.0 1.3 %collective-permute-done.29.rest_4_ = bf16[4,8,16,128]{3,2,1,0:T(8,128)(2,1)S(1)} collective-permute-done((bf16[4,8,16,128]{3,2,1,0:T(8,128)(2,1)S(1)}, bf16[4,8,16,128]{3,2,1,0:T(8,128)(2,1)S(1)}, u32[]{:S(2)}, u32[]{:S(2)}) %collective-permute-start.29) | collective-permute-done | bytes 131104 | tf_op jit(solution)/shard_map/ppermute | solution.py:396
  73.9 1.3 %collective-permute-start.35 = (bf16[24,16,128]{2,1,0:T(8,128)(2,1)S(1)}, bf16[24,16,128]{2,1,0:T(8,128)(2,1)S(1)}, u32[]{:S(2)}, u32[]{:S(2)}) collective-permute-start(bf16[24,16,128]{2,1,0:T(8,128)(2,1)S(1)} %get-tuple-element.51), channel_id=1, source_target_pairs={{8,0},{9,1},{10,2},{11,3},{12,4},{13,5},{14,6},{15,7}} | collective-permute-start | bytes 294920 | tf_op jit(solution)/shard_map/ppermute | solution.py:396
  75.2 1.3 %collective-permute-start.38 = (bf16[8,16,128]{2,1,0:T(8,128)(2,1)S(1)}, bf16[8,16,128]{2,1,0:T(8,128)(2,1)S(1)}, u32[]{:S(2)}, u32[]{:S(2)}) collective-permute-start(bf16[8,16,128]{2,1,0:T(8,128)(2,1)S(1)} %get-tuple-element.52), channel_id=1, source_target_pairs={{8,6},{9,7},{10,4},{11,5},{12,2},{13,3},{14,0},{15,1}} | collective-permute-start | bytes 98312 | tf_op jit(solution)/shard_map/ppermute | solution.py:396
  76.5 1.3 %collective-permute-start.37 = (bf16[8,16,128]{2,1,0:T(8,128)(2,1)S(1)}, bf16[8,16,128]{2,1,0:T(8,128)(2,1)S(1)}, u32[]{:S(2)}, u32[]{:S(2)}) collective-permute-start(bf16[8,16,128]{2,1,0:T(8,128)(2,1)S(1)} %get-tuple-element.52), channel_id=1, source_target_pairs={{8,4},{9,5},{10,6},{11,7},{12,0},{13,1},{14,2},{15,3}} | collective-permute-start | bytes 98312 | tf_op jit(solution)/shard_map/ppermute | solution.py:396
  77.8 1.3 %collective-permute-start.36 = (bf16[8,16,128]{2,1,0:T(8,128)(2,1)S(1)}, bf16[8,16,128]{2,1,0:T(8,128)(2,1)S(1)}, u32[]{:S(2)}, u32[]{:S(2)}) collective-permute-start(bf16[8,16,128]{2,1,0:T(8,128)(2,1)S(1)} %get-tuple-element.52), channel_id=1, source_target_pairs={{8,2},{9,3},{10,0},{11,1},{12,6},{13,7},{14,4},{15,5}} | collective-permute-start | bytes 98312 | tf_op jit(solution)/shard_map/ppermute | solution.py:396
  79.1 41.8 %collective-permute-done.35.rest_0_.rest_6_ = bf16[24,16,128]{2,1,0:T(8,128)(2,1)S(1)} collective-permute-done((bf16[24,16,128]{2,1,0:T(8,128)(2,1)S(1)}, bf16[24,16,128]{2,1,0:T(8,128)(2,1)S(1)}, u32[]{:S(2)}, u32[]{:S(2)}) %collective-permute-start.35) | collective-permute-done | bytes 98336 | tf_op jit(solution)/shard_map/ppermute | solution.py:396
  123.3 1.3 %collective-permute-done.39.rest_4_ = bf16[4,8,16,128]{3,2,1,0:T(8,128)(2,1)S(1)} collective-permute-done((bf16[4,8,16,128]{3,2,1,0:T(8,128)(2,1)S(1)}, bf16[4,8,16,128]{3,2,1,0:T(8,128)(2,1)S(1)}, u32[]{:S(2)}, u32[]{:S(2)}) %collective-permute-start.39) | collective-permute-done | bytes 131104 | tf_op jit(solution)/shard_map/ppermute | solution.py:396
  124.6 3.8 %backward_section_0.1 = f32[2,16,1024]{2,1,0:T(8,128)} custom-call(s32[4]{0:T(128)S(1)} %copy-done.1, bf16[2,2,512,4096]{3,2,1,0:T(8,128)(2,1)S(1)} %get-tuple-element.33.inverse, f32[8,1024]{1,0:T(8,128)S(1)} %get-tuple-element.34.small, s32[2,1024]{1,0:T(2,128)S(1)} %get-tuple-element.31.place, ...), custom_call_target="tpu_custom_call" | custom-call | tf_op jit(solution)/shard_map/backward_section_0/pallas_call | solution.py:344
  (83 shorter events, 27.8 us)
Async XLA Ops:
  2.2 5.9 %collective-permute-start.2 = (bf16[8,16,128]{2,1,0:T(8,128)(2,1)S(1)}, bf16[8,16,128]{2,1,0:T(8,128)(2,1)S(1)}, u32[]{:S(2)}, u32[]{:S(2)}) collective-permute-start(bf16[8,16,128]{2,1,0:T(8,128)(2,1)S(1)} %get-tuple-element.32.rest_0_), channel_id=1, source_target_pairs={{0,6},{1,7},{2,4},{3,5},{4,2},{5,3},{6,0},{7,1},{8,14},{9,15},{10,... | collective-permute-start | bytes 98312 | tf_op jit(solution)/shard_map/ppermute | solution.py:396
  6.2 3.9 %collective-permute-start.1 = (bf16[8,16,128]{2,1,0:T(8,128)(2,1)S(1)}, bf16[8,16,128]{2,1,0:T(8,128)(2,1)S(1)}, u32[]{:S(2)}, u32[]{:S(2)}) collective-permute-start(bf16[8,16,128]{2,1,0:T(8,128)(2,1)S(1)} %get-tuple-element.32.rest_0_), channel_id=1, source_target_pairs={{0,4},{1,5},{2,6},{3,7},{4,0},{5,1},{6,2},{7,3},{8,12},{9,13},{10,... | collective-permute-start | bytes 98312 | tf_op jit(solution)/shard_map/ppermute | solution.py:396
  6.7 3.9 %collective-permute-start = (bf16[8,16,128]{2,1,0:T(8,128)(2,1)S(1)}, bf16[8,16,128]{2,1,0:T(8,128)(2,1)S(1)}, u32[]{:S(2)}, u32[]{:S(2)}) collective-permute-start(bf16[8,16,128]{2,1,0:T(8,128)(2,1)S(1)} %get-tuple-element.32.rest_0_), channel_id=1, source_target_pairs={{0,2},{1,3},{2,0},{3,1},{4,6},{5,7},{6,4},{7,5},{8,10},{9,11},{10,... | collective-permute-start | bytes 98312 | tf_op jit(solution)/shard_map/ppermute | solution.py:396
  6.8 7.3 %collective-permute-start.4 = (f32[40,1024]{1,0:T(8,128)S(1)}, f32[40,1024]{1,0:T(8,128)S(1)}, u32[]{:S(2)}, u32[]{:S(2)}) collective-permute-start(f32[40,1024]{1,0:T(8,128)S(1)} %get-tuple-element.30.packet), channel_id=1, source_target_pairs={{8,0},{16,8},{24,16},{9,1},{17,9},{25,17},{10,2},{18,10},{26,18},{... | collective-permute-start | bytes 491528 | tf_op jit(solution)/shard_map/ppermute | solution.py:445
  21.6 9.2 %collective-permute-start.5 = (bf16[24,16,128]{2,1,0:T(8,128)(2,1)S(1)}, bf16[24,16,128]{2,1,0:T(8,128)(2,1)S(1)}, u32[]{:S(2)}, u32[]{:S(2)}) collective-permute-start(bf16[24,16,128]{2,1,0:T(8,128)(2,1)S(1)} %get-tuple-element.35), channel_id=1, source_target_pairs={{0,8},{1,9},{2,10},{3,11},{4,12},{5,13},{6,14},{7,15}} | collective-permute-start | bytes 294920 | tf_op jit(solution)/shard_map/ppermute | solution.py:396
  25.1 5.8 %collective-permute-start.8 = (bf16[8,16,128]{2,1,0:T(8,128)(2,1)S(1)}, bf16[8,16,128]{2,1,0:T(8,128)(2,1)S(1)}, u32[]{:S(2)}, u32[]{:S(2)}) collective-permute-start(bf16[8,16,128]{2,1,0:T(8,128)(2,1)S(1)} %get-tuple-element.36), channel_id=1, source_target_pairs={{0,14},{1,15},{2,12},{3,13},{4,10},{5,11},{6,8},{7,9}} | collective-permute-start | bytes 98312 | tf_op jit(solution)/shard_map/ppermute | solution.py:396
  28.2 2.9 %collective-permute-start.7 = (bf16[8,16,128]{2,1,0:T(8,128)(2,1)S(1)}, bf16[8,16,128]{2,1,0:T(8,128)(2,1)S(1)}, u32[]{:S(2)}, u32[]{:S(2)}) collective-permute-start(bf16[8,16,128]{2,1,0:T(8,128)(2,1)S(1)} %get-tuple-element.36), channel_id=1, source_target_pairs={{0,12},{1,13},{2,14},{3,15},{4,8},{5,9},{6,10},{7,11}} | collective-permute-start | bytes 98312 | tf_op jit(solution)/shard_map/ppermute | solution.py:396
  29.5 2.9 %collective-permute-start.6 = (bf16[8,16,128]{2,1,0:T(8,128)(2,1)S(1)}, bf16[8,16,128]{2,1,0:T(8,128)(2,1)S(1)}, u32[]{:S(2)}, u32[]{:S(2)}) collective-permute-start(bf16[8,16,128]{2,1,0:T(8,128)(2,1)S(1)} %get-tuple-element.36), channel_id=1, source_target_pairs={{0,10},{1,11},{2,8},{3,9},{4,14},{5,15},{6,12},{7,13}} | collective-permute-start | bytes 98312 | tf_op jit(solution)/shard_map/ppermute | solution.py:396
  34.4 2.7 %collective-permute-start.10 = (bf16[24,16,128]{2,1,0:T(8,128)(2,1)S(1)}, bf16[24,16,128]{2,1,0:T(8,128)(2,1)S(1)}, u32[]{:S(2)}, u32[]{:S(2)}) collective-permute-start(bf16[24,16,128]{2,1,0:T(8,128)(2,1)S(1)} %get-tuple-element.37), channel_id=1, source_target_pairs={{8,16},{9,17},{10,18},{11,19},{12,20},{13,21},{14,22},{15,23}} | collective-permute-start | bytes 294920 | tf_op jit(solution)/shard_map/ppermute | solution.py:396
  35.1 2.0 %collective-permute-start.13 = (bf16[8,16,128]{2,1,0:T(8,128)(2,1)S(1)}, bf16[8,16,128]{2,1,0:T(8,128)(2,1)S(1)}, u32[]{:S(2)}, u32[]{:S(2)}) collective-permute-start(bf16[8,16,128]{2,1,0:T(8,128)(2,1)S(1)} %get-tuple-element.38), channel_id=1, source_target_pairs={{8,22},{9,23},{10,20},{11,21},{12,18},{13,19},{14,16},{15,17}} | collective-permute-start | bytes 98312 | tf_op jit(solution)/shard_map/ppermute | solution.py:396
  39.4 2.7 %collective-permute-start.15 = (bf16[24,16,128]{2,1,0:T(8,128)(2,1)S(1)}, bf16[24,16,128]{2,1,0:T(8,128)(2,1)S(1)}, u32[]{:S(2)}, u32[]{:S(2)}) collective-permute-start(bf16[24,16,128]{2,1,0:T(8,128)(2,1)S(1)} %get-tuple-element.39), channel_id=1, source_target_pairs={{16,24},{17,25},{18,26},{19,27},{20,28},{21,29},{22,30},{23,31}} | collective-permute-start | bytes 294920 | tf_op jit(solution)/shard_map/ppermute | solution.py:396
  40.0 2.0 %collective-permute-start.18 = (bf16[8,16,128]{2,1,0:T(8,128)(2,1)S(1)}, bf16[8,16,128]{2,1,0:T(8,128)(2,1)S(1)}, u32[]{:S(2)}, u32[]{:S(2)}) collective-permute-start(bf16[8,16,128]{2,1,0:T(8,128)(2,1)S(1)} %get-tuple-element.40), channel_id=1, source_target_pairs={{16,30},{17,31},{18,28},{19,29},{20,26},{21,27},{22,24},{23,25}} | collective-permute-start | bytes 98312 | tf_op jit(solution)/shard_map/ppermute | solution.py:396
  44.1 4.7 %collective-permute-start.22 = (bf16[4,16,128]{2,1,0:T(8,128)(2,1)S(1)}, bf16[4,16,128]{2,1,0:T(8,128)(2,1)S(1)}, u32[]{:S(2)}, u32[]{:S(2)}) collective-permute-start(bf16[4,16,128]{2,1,0:T(8,128)(2,1)S(1)} %get-tuple-element.41.rest_0_), channel_id=1, source_target_pairs={{0,6},{1,7},{2,4},{3,5},{4,2},{5,3},{6,0},{7,1},{8,14},{9,15},{10,... | collective-permute-start | bytes 49160 | tf_op jit(solution)/shard_map/ppermute | solution.py:396
  44.7 4.1 %collective-permute-start.21 = (bf16[4,16,128]{2,1,0:T(8,128)(2,1)S(1)}, bf16[4,16,128]{2,1,0:T(8,128)(2,1)S(1)}, u32[]{:S(2)}, u32[]{:S(2)}) collective-permute-start(bf16[4,16,128]{2,1,0:T(8,128)(2,1)S(1)} %get-tuple-element.41.rest_0_), channel_id=1, source_target_pairs={{0,4},{1,5},{2,6},{3,7},{4,0},{5,1},{6,2},{7,3},{8,12},{9,13},{10,... | collective-permute-start | bytes 49160 | tf_op jit(solution)/shard_map/ppermute | solution.py:396
  46.2 3.7 %collective-permute-start.20 = (bf16[4,16,128]{2,1,0:T(8,128)(2,1)S(1)}, bf16[4,16,128]{2,1,0:T(8,128)(2,1)S(1)}, u32[]{:S(2)}, u32[]{:S(2)}) collective-permute-start(bf16[4,16,128]{2,1,0:T(8,128)(2,1)S(1)} %get-tuple-element.41.rest_0_), channel_id=1, source_target_pairs={{0,2},{1,3},{2,0},{3,1},{4,6},{5,7},{6,4},{7,5},{8,10},{9,11},{10,... | collective-permute-start | bytes 49160 | tf_op jit(solution)/shard_map/ppermute | solution.py:396
  50.0 13.6 %collective-permute-start.23 = (bf16[4,4,16,128]{3,2,1,0:T(8,128)(2,1)S(1)}, bf16[4,4,16,128]{3,2,1,0:T(8,128)(2,1)S(1)}, u32[]{:S(2)}, u32[]{:S(2)}) collective-permute-start(bf16[4,4,16,128]{3,2,1,0:T(8,128)(2,1)S(1)} %pad_maximum_fusion.7), channel_id=1, source_target_pairs={{0,1},{1,0},{2,3},{3,2},{4,5},{5,4},{6,7},{7,6},{8,9},{9,8},{10,11... | collective-permute-start | bytes 196616 | tf_op jit(solution)/shard_map/ppermute | solution.py:396
  50.0 13.5 %collective-permute-start.24 = (f32[8,1024]{1,0:T(8,128)S(1)}, f32[8,1024]{1,0:T(8,128)S(1)}, u32[]{:S(2)}, u32[]{:S(2)}) collective-permute-start(f32[8,1024]{1,0:T(8,128)S(1)} %get-tuple-element.34.small), channel_id=1, source_target_pairs={{0,8},{8,16},{16,24},{1,9},{9,17},{17,25},{2,10},{10,18},{18,26},{... | collective-permute-start | bytes 98312 | tf_op jit(solution)/shard_map/ppermute | solution.py:446
  64.1 2.7 %collective-permute-start.25 = (bf16[24,16,128]{2,1,0:T(8,128)(2,1)S(1)}, bf16[24,16,128]{2,1,0:T(8,128)(2,1)S(1)}, u32[]{:S(2)}, u32[]{:S(2)}) collective-permute-start(bf16[24,16,128]{2,1,0:T(8,128)(2,1)S(1)} %get-tuple-element.43), channel_id=1, source_target_pairs={{24,16},{25,17},{26,18},{27,19},{28,20},{29,21},{30,22},{31,23}} | collective-permute-start | bytes 294920 | tf_op jit(solution)/shard_map/ppermute | solution.py:396
  64.8 2.0 %collective-permute-start.28 = (bf16[8,16,128]{2,1,0:T(8,128)(2,1)S(1)}, bf16[8,16,128]{2,1,0:T(8,128)(2,1)S(1)}, u32[]{:S(2)}, u32[]{:S(2)}) collective-permute-start(bf16[8,16,128]{2,1,0:T(8,128)(2,1)S(1)} %get-tuple-element.44), channel_id=1, source_target_pairs={{24,22},{25,23},{26,20},{27,21},{28,18},{29,19},{30,16},{31,17}} | collective-permute-start | bytes 98312 | tf_op jit(solution)/shard_map/ppermute | solution.py:396
  68.9 2.7 %collective-permute-start.30 = (bf16[24,16,128]{2,1,0:T(8,128)(2,1)S(1)}, bf16[24,16,128]{2,1,0:T(8,128)(2,1)S(1)}, u32[]{:S(2)}, u32[]{:S(2)}) collective-permute-start(bf16[24,16,128]{2,1,0:T(8,128)(2,1)S(1)} %get-tuple-element.47), channel_id=1, source_target_pairs={{16,8},{17,9},{18,10},{19,11},{20,12},{21,13},{22,14},{23,15}} | collective-permute-start | bytes 294920 | tf_op jit(solution)/shard_map/ppermute | solution.py:396
  73.9 47.0 %collective-permute-start.35 = (bf16[24,16,128]{2,1,0:T(8,128)(2,1)S(1)}, bf16[24,16,128]{2,1,0:T(8,128)(2,1)S(1)}, u32[]{:S(2)}, u32[]{:S(2)}) collective-permute-start(bf16[24,16,128]{2,1,0:T(8,128)(2,1)S(1)} %get-tuple-element.51), channel_id=1, source_target_pairs={{8,0},{9,1},{10,2},{11,3},{12,4},{13,5},{14,6},{15,7}} | collective-permute-start | bytes 294920 | tf_op jit(solution)/shard_map/ppermute | solution.py:396
  75.2 46.1 %collective-permute-start.38 = (bf16[8,16,128]{2,1,0:T(8,128)(2,1)S(1)}, bf16[8,16,128]{2,1,0:T(8,128)(2,1)S(1)}, u32[]{:S(2)}, u32[]{:S(2)}) collective-permute-start(bf16[8,16,128]{2,1,0:T(8,128)(2,1)S(1)} %get-tuple-element.52), channel_id=1, source_target_pairs={{8,6},{9,7},{10,4},{11,5},{12,2},{13,3},{14,0},{15,1}} | collective-permute-start | bytes 98312 | tf_op jit(solution)/shard_map/ppermute | solution.py:396
  76.5 45.4 %collective-permute-start.37 = (bf16[8,16,128]{2,1,0:T(8,128)(2,1)S(1)}, bf16[8,16,128]{2,1,0:T(8,128)(2,1)S(1)}, u32[]{:S(2)}, u32[]{:S(2)}) collective-permute-start(bf16[8,16,128]{2,1,0:T(8,128)(2,1)S(1)} %get-tuple-element.52), channel_id=1, source_target_pairs={{8,4},{9,5},{10,6},{11,7},{12,0},{13,1},{14,2},{15,3}} | collective-permute-start | bytes 98312 | tf_op jit(solution)/shard_map/ppermute | solution.py:396
  77.8 45.4 %collective-permute-start.36 = (bf16[8,16,128]{2,1,0:T(8,128)(2,1)S(1)}, bf16[8,16,128]{2,1,0:T(8,128)(2,1)S(1)}, u32[]{:S(2)}, u32[]{:S(2)}) collective-permute-start(bf16[8,16,128]{2,1,0:T(8,128)(2,1)S(1)} %get-tuple-element.52), channel_id=1, source_target_pairs={{8,2},{9,3},{10,0},{11,1},{12,6},{13,7},{14,4},{15,5}} | collective-permute-start | bytes 98312 | tf_op jit(solution)/shard_map/ppermute | solution.py:396
  (18 other events, 54.8 us)

commit v5 on v4

--- a/solution.py
+++ b/solution.py
@@ -142,13 +142,15 @@
 
 
 def first_kernel(
-    width, rhs_in, isc_in, fwd_in, bwd_in, picked_in, packet, small, place, front,
-    rhs, isc, fwd, bwd, picked, sems,
+    width, layers, rhs_in, isc_in, fwd_in, bwd_in, picked_in, packet, small, place, front,
+    layers_out, rhs, isc, fwd, bwd, picked, sems,
 ):
     pairs = ((rhs_in, rhs), (isc_in, isc), (fwd_in, fwd), (bwd_in, bwd), (picked_in, picked))
     copies = [pltpu.make_async_copy(a, b, sems.at[i]) for i, (a, b) in enumerate(pairs)]
     for copy in copies:
         copy.start()
+    for at in range(layers.shape[0]):
+        layers_out[at] = layers[at]
     for copy in copies:
         copy.wait()
     cells = rhs.shape[-1]
@@ -175,6 +177,8 @@
         incoming, *rest = rest
     if not final:
         after, *rest = rest
+    if not step:
+        _, *rest = rest
     kept, front, *rest = rest
     if not final:
         outgoing_packet, *rest = rest
@@ -338,14 +342,15 @@
 
 
 def call(kernel, operands, outs, scratch, name, spaces=()):
+    outs = [jax.ShapeDtypeStruct(*o) if isinstance(o, tuple) else o for o in outs]
     specs = [whole(pltpu.SMEM if o.ndim == 1 else pltpu.VMEM) for o in operands]
     for at, space in spaces:
         specs[at] = whole(space)
     return pl.pallas_call(
         kernel,
         in_specs=specs,
-        out_specs=[whole()] * len(outs),
-        out_shape=[jax.ShapeDtypeStruct(*o) if isinstance(o, tuple) else o for o in outs],
+        out_specs=[whole(pltpu.SMEM if len(o.shape) == 1 else pltpu.VMEM) for o in outs],
+        out_shape=outs,
         scratch_shapes=scratch,
         compiler_params=pltpu.CompilerParams(vmem_limit_bytes=8 * 2**20),
         name=name,
@@ -376,7 +381,6 @@
 
     rhs = rhs_field.reshape(layer_slots, rows, cells)
     picked = jnp.pad(front_cells, ((0, 0), (0, width - owned)), constant_values=-1)
-    layers = section_layers
 
     half_shape = ((per_layer, rows, LANES), BF16)
     front_shape = ((2 * per_layer, rows, LANES), BF16)
@@ -387,11 +391,11 @@
         pltpu.VMEM((2, rows, width), F32),
     ]
 
-    def send(block, start, stop, step=0, other_core=False):
+    def send(block, shift, step=0, other_core=False):
         flip = step * CORES + int(other_core)
-        pairs = [(start, stop)] if start is not None else [(i, i) for i in range(sections)]
         route = [
-            (i * planes + own, j * planes + (own ^ flip)) for i, j in pairs for own in range(planes)
+            (i * planes + own, (i + shift) % sections * planes + (own ^ flip))
+            for i in range(sections) for own in range(planes)
         ]
         return lax.ppermute(block, ("sweep", "plane"), route)
 
@@ -407,29 +411,37 @@
             return [gathered], [[0]], order // LANES
         return [gathered], [list(range(planes))], per_layer
 
+    def swap(mine):
+        mine = [m[:2 * per_layer] for m in mine]
+        owners = [[(s, False)] for s in range(chips)] + [[(s, True) for s in range(chips)]]
+        return send(jnp.stack(mine), 0, other_core=True), owners
+
     def within(front):
         if not direct:
             return everywhere(front)
-        mine = [front] + [send(front, None, None, s) for s in range(1, chips)]
-        swapped = send(jnp.stack(mine), None, None, other_core=True)
-        owners = [[(s, False)] for s in range(chips)] + [[(s, True) for s in range(chips)]]
+        mine = [front] + [send(front, 0, s) for s in range(1, chips)]
+        swapped, owners = swap(mine)
         return mine + [swapped], owners, per_layer
 
-    def between(front, packet, start, stop):
+    def between(front, packet, shift):
+        packet = send(packet, shift)
         if not direct:
-            packet = lax.ppermute(packet, "sweep", [(start, stop)])
             return *everywhere(packet[:2 * per_layer]), packet
-        packet = send(packet, start, stop)
-        mine = [packet] + [send(front, start, stop, s) for s in range(1, chips)]
-        swapped = jnp.stack([packet[:2 * per_layer]] + mine[1:])
-        swapped = send(swapped, None, None, other_core=True)
-        owners = [[(s, False)] for s in range(chips)] + [[(s, True) for s in range(chips)]]
+        mine = [packet] + [send(front, shift, s) for s in range(1, chips)]
+        swapped, owners = swap(mine)
         return mine + [swapped], owners, per_layer, packet
 
-    packet, small, place, front = call(
+    packet, small, place, front, layers = call(
         functools.partial(first_kernel, width),
-        [in_hbm(a) for a in (rhs, interior_scale, forward_coupling, backward_coupling, picked)],
-        [((2 * rows + 8, cells), F32), ((8, cells), F32), ((2, cells), jnp.int32), front_shape],
+        [section_layers]
+        + [in_hbm(a) for a in (rhs, interior_scale, forward_coupling, backward_coupling, picked)],
+        [
+            ((2 * rows + 8, cells), F32),
+            ((8, cells), F32),
+            ((2, cells), jnp.int32),
+            front_shape,
+            (section_layers.shape, jnp.int32),
+        ],
         [
             pltpu.VMEM(rhs.shape, F32),
             pltpu.VMEM(interior_scale.shape, F32),
@@ -439,17 +451,17 @@
             pltpu.SemaphoreType.DMA((5,)),
         ],
         "first_fronts",
-        [(i, pltpu.HBM) for i in range(5)],
+        [(i, pltpu.HBM) for i in range(1, 6)],
     )
     gathered, owners, slots = within(front)
-    after = lax.ppermute(packet, "sweep", [(i + 1, i) for i in range(sections - 1)])
-    behind = lax.ppermute(small, "sweep", [(i, i + 1) for i in range(sections - 1)])
+    after, behind = send(packet, -1), send(small, 1)
 
     inverse = in_hbm(front_inverse)
     kept, held = [], [None]
     for step in range(sections):
         final = step == sections - 1
         extra = ([held[step]] if step else []) + ([] if final else [after])
+        extra += [] if step else [behind]
         outs = [layers_shape, half_shape if final else front_shape]
         outs += [] if final else [packet_shape]
         outs += [] if step else [pltpu.VMEM(front_inverse.shape, BF16)]
@@ -472,7 +484,7 @@
         if final:
             gathered, owners, slots = within(outs[1])
         else:
-            gathered, owners, slots, incoming = between(*outs[1:3], step, step + 1)
+            gathered, owners, slots, incoming = between(*outs[1:3], 1)
             held.append(incoming)
 
     result = incoming = None
@@ -489,7 +501,7 @@
         )
         result = outs[0]
         if step:
-            gathered, owners, slots, incoming = between(*outs[1:3], step, step - 1)
+            gathered, owners, slots, incoming = between(*outs[1:3], -1)
     return result.reshape(rhs_field.shape)
 
 

time: 129 us -> 133 us (1.031)
  starting transfers between devices: 47.3 us -> 67.6 us
  waiting for transfers between devices: 63 us -> 47.8 us
    ppermute x38 -> x40, starting transfers between devices: 34.1 us -> 67.6 us  [send(): return lax.ppermute(block, ('sweep', 'plane'), route)]
    ppermute x2 -> x0, starting transfers between devices: 13.2 us -> none  [the longest x1 11.9 us: shards(): lax.ppermute(small, 'sweep', [(i, i + 1) for i in range(sections - 1)])]
    ppermute x38 -> x40, waiting for transfers between devices: 59.4 us -> 47.8 us  [send(): return lax.ppermute(block, ('sweep', 'plane'), route)]
    ppermute x2 -> x0, waiting for transfers between devices: 3.62 us -> none  [the longest x1 2.05 us: shards(): lax.ppermute(packet, 'sweep', [(i + 1, i) for i in range(sections - 1)])]
  transfers between devices with their start and end apart: 40 -> 40, of which waited for: 19 -> 28; matrix products, arithmetic and copies ran while one was open for 0% -> 0% of each run, Pallas kernels for 0% -> 0%
where the time goes in v5:
time: 133 us; the launch traced here: 134 us
  starting transfers between devices  67.6 us (51%)
  waiting for transfers between devices  47.8 us (36%)
  Pallas kernels  17.2 us (13%)
    ppermute x40, starting transfers between devices, send(): return lax.ppermute(block, ('sweep', 'plane'), route)  67.6 us
    ppermute x40, waiting for transfers between devices, send(): return lax.ppermute(block, ('sweep', 'plane'), route)  47.8 us
    pallas_call x9, Pallas kernels, call(): pl.pallas_call(kernel, in_specs=specs, out_specs=[whole(pltpu.SMEM if len...  17.2 us
  transfers between devices with their start and end apart: 40, of which 28 were waited for; matrix products, arithmetic and copies ran while one was open for 0% of the time, Pallas kernels for 0%

profile of v5, /device:TPU:0, one launch (start us, length us, event | category | flops | bytes accessed | tf_op | source)
XLA Modules:
  0.0 133.7 jit_solution(14910993457180539606)
XLA Ops:
  0.7 2.7 %first_fronts.1 = (f32[40,1024]{1,0:T(8,128)S(1)}, f32[8,1024]{1,0:T(8,128)S(1)}, s32[2,1024]{1,0:T(2,128)S(1)}, bf16[8,16,128]{2,1,0:T(8,128)(2,1)S(1)}, s32[4]{0:T(128)S(1)}) custom-call(s32[4]{0:T(128)S(1)} %copy-done, f32[2,16,1024]{2,1,0:T(8,128)} %bitcast.66, f32[2,1024]{1,0:T(2,128)} %isc_in.1, f32[2,1024]{1,0:T(2,128)} %fwd_in.1, f32[2,1024]{1,0:T(2,128)} %bwd_in.1, ...), custom_call_target="tpu_custom_call" | custom-call | tf_op jit(solution)/shard_map/first_fronts/pallas_call | solution.py:349
  3.4 4.0 %collective-permute-start.2 = (bf16[8,16,128]{2,1,0:T(8,128)(2,1)S(1)}, bf16[8,16,128]{2,1,0:T(8,128)(2,1)S(1)}, u32[]{:S(2)}, u32[]{:S(2)}) collective-permute-start(bf16[8,16,128]{2,1,0:T(8,128)(2,1)S(1)} %get-tuple-element.34.rest_0_), channel_id=1, source_target_pairs={{0,6},{1,7},{2,4},{3,5},{4,2},{5,3},{6,0},{7,1},{8,14},{9,15},{10,... | collective-permute-start | bytes 98312 | tf_op jit(solution)/shard_map/ppermute | solution.py:400
  8.0 4.0 %collective-permute-start.4 = (f32[40,1024]{1,0:T(8,128)S(1)}, f32[40,1024]{1,0:T(8,128)S(1)}, u32[]{:S(2)}, u32[]{:S(2)}) collective-permute-start(f32[40,1024]{1,0:T(8,128)S(1)} %get-tuple-element.32.packet), channel_id=1, source_target_pairs={{0,24},{1,25},{2,26},{3,27},{4,28},{5,29},{6,30},{7,31},{8,0},{9,1... | collective-permute-start | bytes 491528 | tf_op jit(solution)/shard_map/ppermute | solution.py:400
  13.5 4.4 %collective-permute-done.5.rest_6_.rest_8_ = f32[8,1024]{1,0:T(8,128)S(1)} collective-permute-done((f32[8,1024]{1,0:T(8,128)S(1)}, f32[8,1024]{1,0:T(8,128)S(1)}, u32[]{:S(2)}, u32[]{:S(2)}) %collective-permute-start.5) | collective-permute-done | bytes 32800 | tf_op jit(solution)/shard_map/ppermute | solution.py:400
  17.9 6.9 %forward_section_0.1 = (f32[2,16,1024]{2,1,0:T(8,128)S(1)}, bf16[8,16,128]{2,1,0:T(8,128)(2,1)S(1)}, bf16[24,16,128]{2,1,0:T(8,128)(2,1)S(1)}, bf16[2,2,512,4096]{3,2,1,0:T(8,128)(2,1)S(1)}) custom-call(s32[4]{0:T(128)S(1)} %get-tuple-element.31.layers, bf16[2,2,512,4096]{3,2,1,0:T(8,128)(2,1)} %inverse.1, f32[40,1024]{1,0:T(8,128)S(1)} %get-tuple-element.32.packet, ...), custom_call_target="tpu_custom_call" | custom-call | tf_op jit(solution)/shard_map/forward_section_0/pallas_call | solution.py:349
  24.9 3.1 %collective-permute-start.9 = (bf16[8,16,128]{2,1,0:T(8,128)(2,1)S(1)}, bf16[8,16,128]{2,1,0:T(8,128)(2,1)S(1)}, u32[]{:S(2)}, u32[]{:S(2)}) collective-permute-start(bf16[8,16,128]{2,1,0:T(8,128)(2,1)S(1)} %get-tuple-element.38), channel_id=1, source_target_pairs={{0,14},{1,15},{2,12},{3,13},{4,10},{5,11},{6,8},{7,9},{8,22},{9,23... | collective-permute-start | bytes 98312 | tf_op jit(solution)/shard_map/ppermute | solution.py:400
  29.4 2.2 %collective-permute-start.7 = (bf16[8,16,128]{2,1,0:T(8,128)(2,1)S(1)}, bf16[8,16,128]{2,1,0:T(8,128)(2,1)S(1)}, u32[]{:S(2)}, u32[]{:S(2)}) collective-permute-start(bf16[8,16,128]{2,1,0:T(8,128)(2,1)S(1)} %get-tuple-element.38), channel_id=1, source_target_pairs={{0,10},{1,11},{2,8},{3,9},{4,14},{5,15},{6,12},{7,13},{8,18},{9,19... | collective-permute-start | bytes 98312 | tf_op jit(solution)/shard_map/ppermute | solution.py:400
  31.6 2.2 %collective-permute-done.9.rest_3_ = bf16[8,16,128]{2,1,0:T(8,128)(2,1)S(1)} collective-permute-done((bf16[8,16,128]{2,1,0:T(8,128)(2,1)S(1)}, bf16[8,16,128]{2,1,0:T(8,128)(2,1)S(1)}, u32[]{:S(2)}, u32[]{:S(2)}) %collective-permute-start.9) | collective-permute-done | bytes 32800 | tf_op jit(solution)/shard_map/ppermute | solution.py:400
  38.1 5.6 %collective-permute-start.11 = (bf16[24,16,128]{2,1,0:T(8,128)(2,1)S(1)}, bf16[24,16,128]{2,1,0:T(8,128)(2,1)S(1)}, u32[]{:S(2)}, u32[]{:S(2)}) collective-permute-start(bf16[24,16,128]{2,1,0:T(8,128)(2,1)S(1)} %get-tuple-element.39), channel_id=1, source_target_pairs={{0,8},{1,9},{2,10},{3,11},{4,12},{5,13},{6,14},{7,15},{8,16},{9,17... | collective-permute-start | bytes 294920 | tf_op jit(solution)/shard_map/ppermute | solution.py:400
  44.9 2.0 %collective-permute-done.11.rest_0_.rest_5_.rest_9_ = bf16[24,16,128]{2,1,0:T(8,128)(2,1)S(1)} collective-permute-done((bf16[24,16,128]{2,1,0:T(8,128)(2,1)S(1)}, bf16[24,16,128]{2,1,0:T(8,128)(2,1)S(1)}, u32[]{:S(2)}, u32[]{:S(2)}) %collective-permute-start.11) | collective-permute-done | bytes 98336 | tf_op jit(solution)/shard_map/ppermute | solution.py:400
  46.8 4.8 %collective-permute-done.14.rest_3_ = bf16[8,16,128]{2,1,0:T(8,128)(2,1)S(1)} collective-permute-done((bf16[8,16,128]{2,1,0:T(8,128)(2,1)S(1)}, bf16[8,16,128]{2,1,0:T(8,128)(2,1)S(1)}, u32[]{:S(2)}, u32[]{:S(2)}) %collective-permute-start.14) | collective-permute-done | bytes 32800 | tf_op jit(solution)/shard_map/ppermute | solution.py:400
  54.3 9.3 %collective-permute-start.19 = (bf16[8,16,128]{2,1,0:T(8,128)(2,1)S(1)}, bf16[8,16,128]{2,1,0:T(8,128)(2,1)S(1)}, u32[]{:S(2)}, u32[]{:S(2)}) collective-permute-start(bf16[8,16,128]{2,1,0:T(8,128)(2,1)S(1)} %get-tuple-element.42), channel_id=1, source_target_pairs={{0,14},{1,15},{2,12},{3,13},{4,10},{5,11},{6,8},{7,9},{8,22},{9,23... | collective-permute-start | bytes 98312 | tf_op jit(solution)/shard_map/ppermute | solution.py:400
  65.2 5.0 %collective-permute-done.18.rest_2_ = bf16[8,16,128]{2,1,0:T(8,128)(2,1)S(1)} collective-permute-done((bf16[8,16,128]{2,1,0:T(8,128)(2,1)S(1)}, bf16[8,16,128]{2,1,0:T(8,128)(2,1)S(1)}, u32[]{:S(2)}, u32[]{:S(2)}) %collective-permute-start.18) | collective-permute-done | bytes 32800 | tf_op jit(solution)/shard_map/ppermute | solution.py:400
  72.2 1.9 %collective-permute-start.23 = (bf16[4,16,128]{2,1,0:T(8,128)(2,1)S(1)}, bf16[4,16,128]{2,1,0:T(8,128)(2,1)S(1)}, u32[]{:S(2)}, u32[]{:S(2)}) collective-permute-start(bf16[4,16,128]{2,1,0:T(8,128)(2,1)S(1)} %get-tuple-element.43.rest_0_), channel_id=1, source_target_pairs={{0,6},{1,7},{2,4},{3,5},{4,2},{5,3},{6,0},{7,1},{8,14},{9,15},{10,... | collective-permute-start | bytes 49160 | tf_op jit(solution)/shard_map/ppermute | solution.py:400
  80.2 4.8 %collective-permute-start.25 = (bf16[24,16,128]{2,1,0:T(8,128)(2,1)S(1)}, bf16[24,16,128]{2,1,0:T(8,128)(2,1)S(1)}, u32[]{:S(2)}, u32[]{:S(2)}) collective-permute-start(bf16[24,16,128]{2,1,0:T(8,128)(2,1)S(1)} %get-tuple-element.45), channel_id=1, source_target_pairs={{0,24},{1,25},{2,26},{3,27},{4,28},{5,29},{6,30},{7,31},{8,0},{9,1... | collective-permute-start | bytes 294920 | tf_op jit(solution)/shard_map/ppermute | solution.py:400
  85.0 1.9 %collective-permute-start.28 = (bf16[8,16,128]{2,1,0:T(8,128)(2,1)S(1)}, bf16[8,16,128]{2,1,0:T(8,128)(2,1)S(1)}, u32[]{:S(2)}, u32[]{:S(2)}) collective-permute-start(bf16[8,16,128]{2,1,0:T(8,128)(2,1)S(1)} %get-tuple-element.46), channel_id=1, source_target_pairs={{0,30},{1,31},{2,28},{3,29},{4,26},{5,27},{6,24},{7,25},{8,6},{9,7... | collective-permute-start | bytes 98312 | tf_op jit(solution)/shard_map/ppermute | solution.py:400
  87.5 3.5 %collective-permute-done.28.rest_3_ = bf16[8,16,128]{2,1,0:T(8,128)(2,1)S(1)} collective-permute-done((bf16[8,16,128]{2,1,0:T(8,128)(2,1)S(1)}, bf16[8,16,128]{2,1,0:T(8,128)(2,1)S(1)}, u32[]{:S(2)}, u32[]{:S(2)}) %collective-permute-start.28) | collective-permute-done | bytes 32800 | tf_op jit(solution)/shard_map/ppermute | solution.py:400
  93.8 3.2 %collective-permute-start.30 = (bf16[24,16,128]{2,1,0:T(8,128)(2,1)S(1)}, bf16[24,16,128]{2,1,0:T(8,128)(2,1)S(1)}, u32[]{:S(2)}, u32[]{:S(2)}) collective-permute-start(bf16[24,16,128]{2,1,0:T(8,128)(2,1)S(1)} %get-tuple-element.49), channel_id=1, source_target_pairs={{0,24},{1,25},{2,26},{3,27},{4,28},{5,29},{6,30},{7,31},{8,0},{9,1... | collective-permute-start | bytes 294920 | tf_op jit(solution)/shard_map/ppermute | solution.py:400
  97.0 7.7 %collective-permute-start.33 = (bf16[8,16,128]{2,1,0:T(8,128)(2,1)S(1)}, bf16[8,16,128]{2,1,0:T(8,128)(2,1)S(1)}, u32[]{:S(2)}, u32[]{:S(2)}) collective-permute-start(bf16[8,16,128]{2,1,0:T(8,128)(2,1)S(1)} %get-tuple-element.50), channel_id=1, source_target_pairs={{0,30},{1,31},{2,28},{3,29},{4,26},{5,27},{6,24},{7,25},{8,6},{9,7... | collective-permute-start | bytes 98312 | tf_op jit(solution)/shard_map/ppermute | solution.py:400
  106.3 3.1 %collective-permute-done.32.rest_2_ = bf16[8,16,128]{2,1,0:T(8,128)(2,1)S(1)} collective-permute-done((bf16[8,16,128]{2,1,0:T(8,128)(2,1)S(1)}, bf16[8,16,128]{2,1,0:T(8,128)(2,1)S(1)}, u32[]{:S(2)}, u32[]{:S(2)}) %collective-permute-start.32) | collective-permute-done | bytes 32800 | tf_op jit(solution)/shard_map/ppermute | solution.py:400
  112.0 2.3 %collective-permute-start.35 = (bf16[24,16,128]{2,1,0:T(8,128)(2,1)S(1)}, bf16[24,16,128]{2,1,0:T(8,128)(2,1)S(1)}, u32[]{:S(2)}, u32[]{:S(2)}) collective-permute-start(bf16[24,16,128]{2,1,0:T(8,128)(2,1)S(1)} %get-tuple-element.53), channel_id=1, source_target_pairs={{0,24},{1,25},{2,26},{3,27},{4,28},{5,29},{6,30},{7,31},{8,0},{9,1... | collective-permute-start | bytes 294920 | tf_op jit(solution)/shard_map/ppermute | solution.py:400
  115.3 8.3 %collective-permute-start.37 = (bf16[8,16,128]{2,1,0:T(8,128)(2,1)S(1)}, bf16[8,16,128]{2,1,0:T(8,128)(2,1)S(1)}, u32[]{:S(2)}, u32[]{:S(2)}) collective-permute-start(bf16[8,16,128]{2,1,0:T(8,128)(2,1)S(1)} %get-tuple-element.54), channel_id=1, source_target_pairs={{0,28},{1,29},{2,30},{3,31},{4,24},{5,25},{6,26},{7,27},{8,4},{9,5... | collective-permute-start | bytes 98312 | tf_op jit(solution)/shard_map/ppermute | solution.py:400
  125.2 3.2 %collective-permute-done.36.rest_1_ = bf16[8,16,128]{2,1,0:T(8,128)(2,1)S(1)} collective-permute-done((bf16[8,16,128]{2,1,0:T(8,128)(2,1)S(1)}, bf16[8,16,128]{2,1,0:T(8,128)(2,1)S(1)}, u32[]{:S(2)}, u32[]{:S(2)}) %collective-permute-start.36) | collective-permute-done | bytes 32800 | tf_op jit(solution)/shard_map/ppermute | solution.py:400
  129.9 3.8 %backward_section_0.1 = f32[2,16,1024]{2,1,0:T(8,128)} custom-call(s32[4]{0:T(128)S(1)} %get-tuple-element.31.layers, bf16[2,2,512,4096]{3,2,1,0:T(8,128)(2,1)S(1)} %get-tuple-element.36.inverse, f32[8,1024]{1,0:T(8,128)S(1)} %get-tuple-element.35.small, s32[2,1024]{1,0:T(2,128)S(1)} %get-tuple-element.33.place, ...), custom_call_target="tpu_custom_call" | custom-call | tf_op jit(solution)/shard_map/backward_section_0/pallas_call | solution.py:349
  (81 shorter events, 33.6 us)
Async XLA Ops:
  3.4 8.6 %collective-permute-start.2 = (bf16[8,16,128]{2,1,0:T(8,128)(2,1)S(1)}, bf16[8,16,128]{2,1,0:T(8,128)(2,1)S(1)}, u32[]{:S(2)}, u32[]{:S(2)}) collective-permute-start(bf16[8,16,128]{2,1,0:T(8,128)(2,1)S(1)} %get-tuple-element.34.rest_0_), channel_id=1, source_target_pairs={{0,6},{1,7},{2,4},{3,5},{4,2},{5,3},{6,0},{7,1},{8,14},{9,15},{10,... | collective-permute-start | bytes 98312 | tf_op jit(solution)/shard_map/ppermute | solution.py:400
  8.0 9.9 %collective-permute-start.4 = (f32[40,1024]{1,0:T(8,128)S(1)}, f32[40,1024]{1,0:T(8,128)S(1)}, u32[]{:S(2)}, u32[]{:S(2)}) collective-permute-start(f32[40,1024]{1,0:T(8,128)S(1)} %get-tuple-element.32.packet), channel_id=1, source_target_pairs={{0,24},{1,25},{2,26},{3,27},{4,28},{5,29},{6,30},{7,31},{8,0},{9,1... | collective-permute-start | bytes 491528 | tf_op jit(solution)/shard_map/ppermute | solution.py:400
  12.1 5.8 %collective-permute-start.3 = (bf16[4,8,16,128]{3,2,1,0:T(8,128)(2,1)S(1)}, bf16[4,8,16,128]{3,2,1,0:T(8,128)(2,1)S(1)}, u32[]{:S(2)}, u32[]{:S(2)}) collective-permute-start(bf16[4,8,16,128]{3,2,1,0:T(8,128)(2,1)S(1)} %pad_maximum_fusion), channel_id=1, source_target_pairs={{0,1},{1,0},{2,3},{3,2},{4,5},{5,4},{6,7},{7,6},{8,9},{9,8},{10,11... | collective-permute-start | bytes 393224 | tf_op jit(solution)/shard_map/ppermute | solution.py:400
  12.1 5.8 %collective-permute-start.5 = (f32[8,1024]{1,0:T(8,128)S(1)}, f32[8,1024]{1,0:T(8,128)S(1)}, u32[]{:S(2)}, u32[]{:S(2)}) collective-permute-start(f32[8,1024]{1,0:T(8,128)S(1)} %get-tuple-element.35.small), channel_id=1, source_target_pairs={{0,8},{1,9},{2,10},{3,11},{4,12},{5,13},{6,14},{7,15},{8,16},{9,17... | collective-permute-start | bytes 98312 | tf_op jit(solution)/shard_map/ppermute | solution.py:400
  24.8 6.8 %collective-permute-start.6 = (bf16[24,16,128]{2,1,0:T(8,128)(2,1)S(1)}, bf16[24,16,128]{2,1,0:T(8,128)(2,1)S(1)}, u32[]{:S(2)}, u32[]{:S(2)}) collective-permute-start(bf16[24,16,128]{2,1,0:T(8,128)(2,1)S(1)} %get-tuple-element.37), channel_id=1, source_target_pairs={{0,8},{1,9},{2,10},{3,11},{4,12},{5,13},{6,14},{7,15},{8,16},{9,17... | collective-permute-start | bytes 294920 | tf_op jit(solution)/shard_map/ppermute | solution.py:400
  24.9 9.0 %collective-permute-start.9 = (bf16[8,16,128]{2,1,0:T(8,128)(2,1)S(1)}, bf16[8,16,128]{2,1,0:T(8,128)(2,1)S(1)}, u32[]{:S(2)}, u32[]{:S(2)}) collective-permute-start(bf16[8,16,128]{2,1,0:T(8,128)(2,1)S(1)} %get-tuple-element.38), channel_id=1, source_target_pairs={{0,14},{1,15},{2,12},{3,13},{4,10},{5,11},{6,8},{7,9},{8,22},{9,23... | collective-permute-start | bytes 98312 | tf_op jit(solution)/shard_map/ppermute | solution.py:400
  28.0 6.6 %collective-permute-start.8 = (bf16[8,16,128]{2,1,0:T(8,128)(2,1)S(1)}, bf16[8,16,128]{2,1,0:T(8,128)(2,1)S(1)}, u32[]{:S(2)}, u32[]{:S(2)}) collective-permute-start(bf16[8,16,128]{2,1,0:T(8,128)(2,1)S(1)} %get-tuple-element.38), channel_id=1, source_target_pairs={{0,12},{1,13},{2,14},{3,15},{4,8},{5,9},{6,10},{7,11},{8,20},{9,21... | collective-permute-start | bytes 98312 | tf_op jit(solution)/shard_map/ppermute | solution.py:400
  29.4 6.6 %collective-permute-start.7 = (bf16[8,16,128]{2,1,0:T(8,128)(2,1)S(1)}, bf16[8,16,128]{2,1,0:T(8,128)(2,1)S(1)}, u32[]{:S(2)}, u32[]{:S(2)}) collective-permute-start(bf16[8,16,128]{2,1,0:T(8,128)(2,1)S(1)} %get-tuple-element.38), channel_id=1, source_target_pairs={{0,10},{1,11},{2,8},{3,9},{4,14},{5,15},{6,12},{7,13},{8,18},{9,19... | collective-permute-start | bytes 98312 | tf_op jit(solution)/shard_map/ppermute | solution.py:400
  38.1 8.8 %collective-permute-start.11 = (bf16[24,16,128]{2,1,0:T(8,128)(2,1)S(1)}, bf16[24,16,128]{2,1,0:T(8,128)(2,1)S(1)}, u32[]{:S(2)}, u32[]{:S(2)}) collective-permute-start(bf16[24,16,128]{2,1,0:T(8,128)(2,1)S(1)} %get-tuple-element.39), channel_id=1, source_target_pairs={{0,8},{1,9},{2,10},{3,11},{4,12},{5,13},{6,14},{7,15},{8,16},{9,17... | collective-permute-start | bytes 294920 | tf_op jit(solution)/shard_map/ppermute | solution.py:400
  43.7 7.9 %collective-permute-start.14 = (bf16[8,16,128]{2,1,0:T(8,128)(2,1)S(1)}, bf16[8,16,128]{2,1,0:T(8,128)(2,1)S(1)}, u32[]{:S(2)}, u32[]{:S(2)}) collective-permute-start(bf16[8,16,128]{2,1,0:T(8,128)(2,1)S(1)} %get-tuple-element.40), channel_id=1, source_target_pairs={{0,14},{1,15},{2,12},{3,13},{4,10},{5,11},{6,8},{7,9},{8,22},{9,23... | collective-permute-start | bytes 98312 | tf_op jit(solution)/shard_map/ppermute | solution.py:400
  44.7 6.9 %collective-permute-start.13 = (bf16[8,16,128]{2,1,0:T(8,128)(2,1)S(1)}, bf16[8,16,128]{2,1,0:T(8,128)(2,1)S(1)}, u32[]{:S(2)}, u32[]{:S(2)}) collective-permute-start(bf16[8,16,128]{2,1,0:T(8,128)(2,1)S(1)} %get-tuple-element.40), channel_id=1, source_target_pairs={{0,12},{1,13},{2,14},{3,15},{4,8},{5,9},{6,10},{7,11},{8,20},{9,21... | collective-permute-start | bytes 98312 | tf_op jit(solution)/shard_map/ppermute | solution.py:400
  44.8 7.2 %collective-permute-start.12 = (bf16[8,16,128]{2,1,0:T(8,128)(2,1)S(1)}, bf16[8,16,128]{2,1,0:T(8,128)(2,1)S(1)}, u32[]{:S(2)}, u32[]{:S(2)}) collective-permute-start(bf16[8,16,128]{2,1,0:T(8,128)(2,1)S(1)} %get-tuple-element.40), channel_id=1, source_target_pairs={{0,10},{1,11},{2,8},{3,9},{4,14},{5,15},{6,12},{7,13},{8,18},{9,19... | collective-permute-start | bytes 98312 | tf_op jit(solution)/shard_map/ppermute | solution.py:400
  54.1 9.6 %collective-permute-start.16 = (bf16[24,16,128]{2,1,0:T(8,128)(2,1)S(1)}, bf16[24,16,128]{2,1,0:T(8,128)(2,1)S(1)}, u32[]{:S(2)}, u32[]{:S(2)}) collective-permute-start(bf16[24,16,128]{2,1,0:T(8,128)(2,1)S(1)} %get-tuple-element.41), channel_id=1, source_target_pairs={{0,8},{1,9},{2,10},{3,11},{4,12},{5,13},{6,14},{7,15},{8,16},{9,17... | collective-permute-start | bytes 294920 | tf_op jit(solution)/shard_map/ppermute | solution.py:400
  54.3 10.9 %collective-permute-start.19 = (bf16[8,16,128]{2,1,0:T(8,128)(2,1)S(1)}, bf16[8,16,128]{2,1,0:T(8,128)(2,1)S(1)}, u32[]{:S(2)}, u32[]{:S(2)}) collective-permute-start(bf16[8,16,128]{2,1,0:T(8,128)(2,1)S(1)} %get-tuple-element.42), channel_id=1, source_target_pairs={{0,14},{1,15},{2,12},{3,13},{4,10},{5,11},{6,8},{7,9},{8,22},{9,23... | collective-permute-start | bytes 98312 | tf_op jit(solution)/shard_map/ppermute | solution.py:400
  63.6 6.6 %collective-permute-start.18 = (bf16[8,16,128]{2,1,0:T(8,128)(2,1)S(1)}, bf16[8,16,128]{2,1,0:T(8,128)(2,1)S(1)}, u32[]{:S(2)}, u32[]{:S(2)}) collective-permute-start(bf16[8,16,128]{2,1,0:T(8,128)(2,1)S(1)} %get-tuple-element.42), channel_id=1, source_target_pairs={{0,12},{1,13},{2,14},{3,15},{4,8},{5,9},{6,10},{7,11},{8,20},{9,21... | collective-permute-start | bytes 98312 | tf_op jit(solution)/shard_map/ppermute | solution.py:400
  63.6 6.6 %collective-permute-start.17 = (bf16[8,16,128]{2,1,0:T(8,128)(2,1)S(1)}, bf16[8,16,128]{2,1,0:T(8,128)(2,1)S(1)}, u32[]{:S(2)}, u32[]{:S(2)}) collective-permute-start(bf16[8,16,128]{2,1,0:T(8,128)(2,1)S(1)} %get-tuple-element.42), channel_id=1, source_target_pairs={{0,10},{1,11},{2,8},{3,9},{4,14},{5,15},{6,12},{7,13},{8,18},{9,19... | collective-permute-start | bytes 98312 | tf_op jit(solution)/shard_map/ppermute | solution.py:400
  80.2 7.3 %collective-permute-start.25 = (bf16[24,16,128]{2,1,0:T(8,128)(2,1)S(1)}, bf16[24,16,128]{2,1,0:T(8,128)(2,1)S(1)}, u32[]{:S(2)}, u32[]{:S(2)}) collective-permute-start(bf16[24,16,128]{2,1,0:T(8,128)(2,1)S(1)} %get-tuple-element.45), channel_id=1, source_target_pairs={{0,24},{1,25},{2,26},{3,27},{4,28},{5,29},{6,30},{7,31},{8,0},{9,1... | collective-permute-start | bytes 294920 | tf_op jit(solution)/shard_map/ppermute | solution.py:400
  85.0 6.1 %collective-permute-start.28 = (bf16[8,16,128]{2,1,0:T(8,128)(2,1)S(1)}, bf16[8,16,128]{2,1,0:T(8,128)(2,1)S(1)}, u32[]{:S(2)}, u32[]{:S(2)}) collective-permute-start(bf16[8,16,128]{2,1,0:T(8,128)(2,1)S(1)} %get-tuple-element.46), channel_id=1, source_target_pairs={{0,30},{1,31},{2,28},{3,29},{4,26},{5,27},{6,24},{7,25},{8,6},{9,7... | collective-permute-start | bytes 98312 | tf_op jit(solution)/shard_map/ppermute | solution.py:400
  93.8 11.9 %collective-permute-start.30 = (bf16[24,16,128]{2,1,0:T(8,128)(2,1)S(1)}, bf16[24,16,128]{2,1,0:T(8,128)(2,1)S(1)}, u32[]{:S(2)}, u32[]{:S(2)}) collective-permute-start(bf16[24,16,128]{2,1,0:T(8,128)(2,1)S(1)} %get-tuple-element.49), channel_id=1, source_target_pairs={{0,24},{1,25},{2,26},{3,27},{4,28},{5,29},{6,30},{7,31},{8,0},{9,1... | collective-permute-start | bytes 294920 | tf_op jit(solution)/shard_map/ppermute | solution.py:400
  97.0 9.4 %collective-permute-start.33 = (bf16[8,16,128]{2,1,0:T(8,128)(2,1)S(1)}, bf16[8,16,128]{2,1,0:T(8,128)(2,1)S(1)}, u32[]{:S(2)}, u32[]{:S(2)}) collective-permute-start(bf16[8,16,128]{2,1,0:T(8,128)(2,1)S(1)} %get-tuple-element.50), channel_id=1, source_target_pairs={{0,30},{1,31},{2,28},{3,29},{4,26},{5,27},{6,24},{7,25},{8,6},{9,7... | collective-permute-start | bytes 98312 | tf_op jit(solution)/shard_map/ppermute | solution.py:400
  104.7 5.1 %collective-permute-start.31 = (bf16[8,16,128]{2,1,0:T(8,128)(2,1)S(1)}, bf16[8,16,128]{2,1,0:T(8,128)(2,1)S(1)}, u32[]{:S(2)}, u32[]{:S(2)}) collective-permute-start(bf16[8,16,128]{2,1,0:T(8,128)(2,1)S(1)} %get-tuple-element.50), channel_id=1, source_target_pairs={{0,26},{1,27},{2,24},{3,25},{4,30},{5,31},{6,28},{7,29},{8,2},{9,3... | collective-permute-start | bytes 98312 | tf_op jit(solution)/shard_map/ppermute | solution.py:400
  112.0 11.6 %collective-permute-start.35 = (bf16[24,16,128]{2,1,0:T(8,128)(2,1)S(1)}, bf16[24,16,128]{2,1,0:T(8,128)(2,1)S(1)}, u32[]{:S(2)}, u32[]{:S(2)}) collective-permute-start(bf16[24,16,128]{2,1,0:T(8,128)(2,1)S(1)} %get-tuple-element.53), channel_id=1, source_target_pairs={{0,24},{1,25},{2,26},{3,27},{4,28},{5,29},{6,30},{7,31},{8,0},{9,1... | collective-permute-start | bytes 294920 | tf_op jit(solution)/shard_map/ppermute | solution.py:400
  114.3 10.6 %collective-permute-start.38 = (bf16[8,16,128]{2,1,0:T(8,128)(2,1)S(1)}, bf16[8,16,128]{2,1,0:T(8,128)(2,1)S(1)}, u32[]{:S(2)}, u32[]{:S(2)}) collective-permute-start(bf16[8,16,128]{2,1,0:T(8,128)(2,1)S(1)} %get-tuple-element.54), channel_id=1, source_target_pairs={{0,30},{1,31},{2,28},{3,29},{4,26},{5,27},{6,24},{7,25},{8,6},{9,7... | collective-permute-start | bytes 98312 | tf_op jit(solution)/shard_map/ppermute | solution.py:400
  115.3 9.9 %collective-permute-start.37 = (bf16[8,16,128]{2,1,0:T(8,128)(2,1)S(1)}, bf16[8,16,128]{2,1,0:T(8,128)(2,1)S(1)}, u32[]{:S(2)}, u32[]{:S(2)}) collective-permute-start(bf16[8,16,128]{2,1,0:T(8,128)(2,1)S(1)} %get-tuple-element.54), channel_id=1, source_target_pairs={{0,28},{1,29},{2,30},{3,31},{4,24},{5,25},{6,26},{7,27},{8,4},{9,5... | collective-permute-start | bytes 98312 | tf_op jit(solution)/shard_map/ppermute | solution.py:400
  (17 other events, 50.7 us)

commit v6 on v4

--- a/solution.py
+++ b/solution.py
@@ -96,8 +96,8 @@
 def owner_of(place, planes):
     if isinstance(place, int):
         return place
-    step, other = place
-    return lax.bitwise_xor(lax.axis_index("plane"), step * CORES + int(other))
+    own = lax.axis_index("plane")
+    return lax.bitwise_xor(own, jnp.where(lax.rem(own, CORES) == 0, place[0], place[1]))
 
 
 def stack_fronts(blocks, owners, planes, per_layer, stacked, layer):
@@ -129,7 +129,7 @@
 
 
 def solve(inverse, stacked, solved, layer):
-    out = product(inverse[layer, 0], stacked[0]) + product(inverse[layer, 1], stacked[1])
+    out = product(inverse[0], stacked[0]) + product(inverse[1], stacked[1])
     store_solved(solved, layer, out)
 
 
@@ -142,17 +142,23 @@
 
 
 def first_kernel(
-    width, rhs_in, isc_in, fwd_in, bwd_in, picked_in, packet, small, place, front,
-    rhs, isc, fwd, bwd, picked, sems,
+    width, layers_in, rhs_in, isc_in, fwd_in, bwd_in, picked_in, inverse, packet, place, front,
+    layers, first_inverse, rhs, isc, fwd, bwd, picked, sems, load_sem,
 ):
-    pairs = ((rhs_in, rhs), (isc_in, isc), (fwd_in, fwd), (bwd_in, bwd), (picked_in, picked))
+    pairs = (
+        (rhs_in, rhs), (isc_in, isc), (fwd_in, fwd), (bwd_in, bwd), (picked_in, picked),
+        (layers_in, layers),
+    )
     copies = [pltpu.make_async_copy(a, b, sems.at[i]) for i, (a, b) in enumerate(pairs)]
+    load = pltpu.make_async_copy(inverse.at[0], first_inverse, load_sem.at[0])
     for copy in copies:
         copy.start()
+    load.start()
     for copy in copies:
         copy.wait()
     cells = rhs.shape[-1]
     count = rhs.shape[1]
+    small = packet.at[2 * count:]
     small[ISC:ISC + 2, :] = isc[...]
     small[FWD:FWD + 2, :] = fwd[...]
     small[BWD:BWD + 2, :] = bwd[...]
@@ -160,14 +166,15 @@
     small[PICK:PICK + 2, :width] = picked[...].astype(F32)
     packet[0:count, :] = rhs[0]
     packet[count:2 * count, :] = rhs[1]
-    packet[2 * count:, :] = small[...]
     for layer in range(2):
         place[layer:layer + 1, :] = places(picked[layer:layer + 1, :], cells)
     write_front(front, forward_front(split(rhs[0]), split(rhs[1]), small, None, width))
+    load.wait()
 
 
 def forward_kernel(
-    step, sections, planes, width, per_layer, owners, layers, inverse, packet, place, *rest
+    step, sections, planes, width, per_layer, owners, layers, first_inverse, inverse, packet,
+    place, *rest
 ):
     blocks, rest = rest[:len(owners)], rest[len(owners):]
     final = step == sections - 1
@@ -175,70 +182,41 @@
         incoming, *rest = rest
     if not final:
         after, *rest = rest
+    if not step:
+        _, *rest = rest
     kept, front, *rest = rest
     if not final:
         outgoing_packet, *rest = rest
-    if step:
-        resident, (stacked, solved) = inverse, rest
+    if not step:
+        second_inverse, stacked, solved, sems = rest
     else:
-        resident, stacked, solved, kept_sum, sems = rest
+        second_inverse, (stacked, solved) = inverse, rest
     own = lax.axis_index("sweep")
     cells = packet.shape[-1]
     count = cells // LANES
     rows = kept.shape[1]
-    order = inverse.shape[-1]
     small = packet.at[2 * rows:]
     mine = own == step
     both = layers[step] == 2
-
-    def fill(layer):
+    load = None
+    if not step:
+        load = pltpu.make_async_copy(inverse.at[1], second_inverse, sems.at[0])
+        load.start()
+
+    def whole_solve(layer, matrices):
         stack_fronts(blocks, owners, planes, per_layer, stacked, layer)
-
-    if step:
-        @pl.when(mine)
-        def _():
-            fill(0)
-            solve(resident, stacked, solved, 0)
-
-        @pl.when(mine & both)
-        def _():
-            fill(1)
-            solve(resident, stacked, solved, 1)
-    else:
-        cuts = 2 if order % (2 * LANES) == 0 else 1
-        depth = order // cuts
-        copies = {}
-        for layer in range(2):
-            for cut in range(cuts):
-                for part in range(2):
-                    piece = (layer, part, slice(None), pl.ds(cut * depth, depth))
-                    copies[layer, cut, part] = pltpu.make_async_copy(
-                        inverse.at[piece], resident.at[piece], sems.at[len(copies)]
-                    )
-        for copy in copies.values():
-            copy.start()
-        for layer in range(2):
-            needed = mine if layer == 0 else mine & both
-
-            @pl.when(needed)
-            def _():
-                fill(layer)
-
-            for cut in range(cuts):
-                for part in range(2):
-                    copies[layer, cut, part].wait()
-
-                @pl.when(needed)
-                def _():
-                    columns = pl.ds(cut * depth, depth)
-                    out = product(resident[layer, 0, :, columns], stacked[0, :, columns])
-                    out = out + product(resident[layer, 1, :, columns], stacked[1, :, columns])
-                    if cut == cuts - 1:
-                        if cut:
-                            out = out + kept_sum[...]
-                        store_solved(solved, layer, out)
-                    else:
-                        kept_sum[...] = out
+        solve(matrices, stacked, solved, layer)
+
+    @pl.when(mine)
+    def _():
+        whole_solve(0, first_inverse)
+
+    if load is not None:
+        load.wait()
+
+    @pl.when(mine & both)
+    def _():
+        whole_solve(1, second_inverse)
 
     @pl.when(mine)
     def _():
@@ -269,7 +247,8 @@
 
 
 def backward_kernel(
-    step, sections, planes, width, per_layer, owners, layers, inverse, small, place, *rest
+    step, sections, planes, width, per_layer, owners, layers, first_inverse, second_inverse,
+    packet, place, *rest
 ):
     blocks, rest = rest[:len(owners)], rest[len(owners):]
     kept, *rest = rest
@@ -285,12 +264,13 @@
     stacked, solved = rest
     own = lax.axis_index("sweep")
     count = kept.shape[-1] // LANES
+    small = packet.at[2 * kept.shape[1]:]
     mine = own == step
     both = layers[step] == 2
 
     def whole_solve(layer):
         stack_fronts(blocks, owners, planes, per_layer, stacked, layer)
-        solve(inverse, stacked, solved, layer)
+        solve((first_inverse, second_inverse)[layer], stacked, solved, layer)
 
     if not last:
         @pl.when(own != step)
@@ -325,7 +305,8 @@
         first = minus(first_fwd, change)
         if step:
             chunks = backward_front(
-                behind, first, read_field(held, count), layers[step - 1] == 2, width
+                behind.at[2 * kept.shape[1]:], first, read_field(held, count),
+                layers[step - 1] == 2, width
             )
             write_front(front, chunks)
             write_front(outgoing_packet, chunks, first)
@@ -337,15 +318,16 @@
     return pl.BlockSpec(memory_space=space)
 
 
-def call(kernel, operands, outs, scratch, name, spaces=()):
+def call(kernel, operands, outs, scratch, name, in_place=()):
+    outs = [jax.ShapeDtypeStruct(*o) if isinstance(o, tuple) else o for o in outs]
     specs = [whole(pltpu.SMEM if o.ndim == 1 else pltpu.VMEM) for o in operands]
-    for at, space in spaces:
-        specs[at] = whole(space)
+    for at in in_place:
+        specs[at] = whole(pltpu.HBM)
     return pl.pallas_call(
         kernel,
         in_specs=specs,
-        out_specs=[whole()] * len(outs),
-        out_shape=[jax.ShapeDtypeStruct(*o) if isinstance(o, tuple) else o for o in outs],
+        out_specs=[whole(pltpu.SMEM if len(o.shape) == 1 else pltpu.VMEM) for o in outs],
+        out_shape=outs,
         scratch_shapes=scratch,
         compiler_params=pltpu.CompilerParams(vmem_limit_bytes=8 * 2**20),
         name=name,
@@ -387,11 +369,11 @@
         pltpu.VMEM((2, rows, width), F32),
     ]
 
-    def send(block, start, stop, step=0, other_core=False):
-        flip = step * CORES + int(other_core)
-        pairs = [(start, stop)] if start is not None else [(i, i) for i in range(sections)]
+    def send(block, pair, *flips):
+        pairs = [pair] if pair else [(i, i) for i in range(sections)]
         route = [
-            (i * planes + own, j * planes + (own ^ flip)) for i, j in pairs for own in range(planes)
+            (i * planes + own, j * planes + (own ^ flips[own % CORES % len(flips)]))
+            for i, j in pairs for own in range(planes)
         ]
         return lax.ppermute(block, ("sweep", "plane"), route)
 
@@ -407,64 +389,71 @@
             return [gathered], [[0]], order // LANES
         return [gathered], [list(range(planes))], per_layer
 
+    def spread(front, straight, pair):
+        blocks, owners = [straight], [[(0, 0)]]
+        for step in [1] if chips == 2 else range(3, chips):
+            blocks.append(send(front, pair, CORES * step))
+            owners.append([(CORES * step, CORES * step)])
+        if chips == 4:
+            both = jnp.stack([front, send(front, None, 1)])
+            blocks.append(send(both, pair, CORES, 2 * CORES))
+            owners += [[(CORES + core, 2 * CORES + core) for core in range(CORES)]]
+        short = [b[:2 * per_layer] if b.ndim == 3 else b for b in blocks]
+        mine = jnp.concatenate([b[None] if b.ndim == 3 else b for b in short])
+        blocks.append(send(mine, None, 1))
+        owners.append([(one ^ 1, zero ^ 1) for places in owners for zero, one in places])
+        return blocks, owners, per_layer
+
     def within(front):
-        if not direct:
-            return everywhere(front)
-        mine = [front] + [send(front, None, None, s) for s in range(1, chips)]
-        swapped = send(jnp.stack(mine), None, None, other_core=True)
-        owners = [[(s, False)] for s in range(chips)] + [[(s, True) for s in range(chips)]]
-        return mine + [swapped], owners, per_layer
+        return spread(front, front, None) if direct else everywhere(front)
 
     def between(front, packet, start, stop):
         if not direct:
             packet = lax.ppermute(packet, "sweep", [(start, stop)])
             return *everywhere(packet[:2 * per_layer]), packet
-        packet = send(packet, start, stop)
-        mine = [packet] + [send(front, start, stop, s) for s in range(1, chips)]
-        swapped = jnp.stack([packet[:2 * per_layer]] + mine[1:])
-        swapped = send(swapped, None, None, other_core=True)
-        owners = [[(s, False)] for s in range(chips)] + [[(s, True) for s in range(chips)]]
-        return mine + [swapped], owners, per_layer, packet
-
-    packet, small, place, front = call(
+        packet = send(packet, (start, stop), 0)
+        return *spread(front, packet, (start, stop)), packet
+
+    inverse = in_hbm(front_inverse)
+    half_inverse = pltpu.VMEM(front_inverse.shape[1:], BF16)
+    coefficients = (interior_scale, forward_coupling, backward_coupling)
+    operands = [section_layers, rhs, *coefficients, picked]
+    packet, place, front, layers, first_inverse = call(
         functools.partial(first_kernel, width),
-        [in_hbm(a) for a in (rhs, interior_scale, forward_coupling, backward_coupling, picked)],
-        [((2 * rows + 8, cells), F32), ((8, cells), F32), ((2, cells), jnp.int32), front_shape],
+        [in_hbm(a) for a in operands] + [inverse],
         [
-            pltpu.VMEM(rhs.shape, F32),
-            pltpu.VMEM(interior_scale.shape, F32),
-            pltpu.VMEM(forward_coupling.shape, F32),
-            pltpu.VMEM(backward_coupling.shape, F32),
-            pltpu.VMEM(picked.shape, jnp.int32),
-            pltpu.SemaphoreType.DMA((5,)),
+            ((2 * rows + 8, cells), F32),
+            ((2, cells), jnp.int32),
+            front_shape,
+            (section_layers.shape, jnp.int32),
+            half_inverse,
         ],
+        [pltpu.VMEM(a.shape, a.dtype) for a in operands[1:]]
+        + [pltpu.SemaphoreType.DMA((6,)), pltpu.SemaphoreType.DMA((1,))],
         "first_fronts",
-        [(i, pltpu.HBM) for i in range(5)],
+        range(7),
     )
     gathered, owners, slots = within(front)
     after = lax.ppermute(packet, "sweep", [(i + 1, i) for i in range(sections - 1)])
-    behind = lax.ppermute(small, "sweep", [(i, i + 1) for i in range(sections - 1)])
-
-    inverse = in_hbm(front_inverse)
+    behind = lax.ppermute(packet, "sweep", [(i, i + 1) for i in range(sections - 1)])
+
     kept, held = [], [None]
     for step in range(sections):
         final = step == sections - 1
         extra = ([held[step]] if step else []) + ([] if final else [after])
+        extra += [] if step else [behind]
         outs = [layers_shape, half_shape if final else front_shape]
         outs += [] if final else [packet_shape]
-        outs += [] if step else [pltpu.VMEM(front_inverse.shape, BF16)]
-        room = [] if step else [
-            pltpu.VMEM((owned, rows), F32), pltpu.SemaphoreType.DMA((8,))
-        ]
+        outs += [] if step else [half_inverse]
         outs = call(
             functools.partial(
                 forward_kernel, step, sections, planes, width, slots, owners
             ),
-            [layers, inverse, packet, place, *gathered, *extra],
+            [layers, first_inverse, inverse, packet, place, *gathered, *extra],
             outs,
-            scratch + room,
+            scratch + ([] if step else [pltpu.SemaphoreType.DMA((1,))]),
             f"forward_section_{step}",
-            [] if step else [(1, pltpu.HBM)],
+            [] if step else [2],
         )
         if not step:
             inverse = outs[-1]
@@ -472,7 +461,7 @@
         if final:
             gathered, owners, slots = within(outs[1])
         else:
-            gathered, owners, slots, incoming = between(*outs[1:3], step, step + 1)
+            gathered, owners, slots, incoming = between(outs[1], outs[2], step, step + 1)
             held.append(incoming)
 
     result = incoming = None
@@ -482,14 +471,14 @@
             functools.partial(
                 backward_kernel, step, sections, planes, width, slots, owners
             ),
-            [layers, inverse, small, place, *gathered, kept[step], *extra],
+            [layers, first_inverse, inverse, packet, place, *gathered, kept[step], *extra],
             [layers_shape] + ([front_shape, packet_shape] if step else []),
             scratch,
             f"backward_section_{step}",
         )
         result = outs[0]
         if step:
-            gathered, owners, slots, incoming = between(*outs[1:3], step, step - 1)
+            gathered, owners, slots, incoming = between(outs[1], outs[2], step, step - 1)
     return result.reshape(rhs_field.shape)
 
 

time: 129 us -> 128 us (level)
  starting transfers between devices: 47.3 us -> 32 us
  waiting for transfers between devices: 63 us -> 73.8 us
  Pallas kernels: 16.7 us -> 20.9 us
    ppermute x38, waiting for transfers between devices: 59.4 us -> 67.9 us  [send(): return lax.ppermute(block, ('sweep', 'plane'), route)]
    ppermute x1, starting transfers between devices: 11.9 us -> 3.48 us  [shards(): lax.ppermute(packet, 'sweep', [(i, i + 1) for i in range(sections - 1)])]
    ppermute x38, starting transfers between devices: 34.1 us -> 27.2 us  [send(): return lax.ppermute(block, ('sweep', 'plane'), route)]
    pallas_call x9, Pallas kernels: 16.7 us -> 20.9 us  [call(): pl.pallas_call(kernel, in_specs=specs, out_specs=[whole(pltpu.SMEM if len...]
    ppermute x1, waiting for transfers between devices: 2.05 us -> 4.12 us  [shards(): lax.ppermute(packet, 'sweep', [(i + 1, i) for i in range(sections - 1)])]
  transfers between devices with their start and end apart: 40 -> 40, of which waited for: 19 -> 16; matrix products, arithmetic and copies ran while one was open for 0% -> 0% of each run, Pallas kernels for 0% -> 0%
where the time goes in v6:
time: 128 us; the launch traced here: 127 us
  waiting for transfers between devices  73.8 us (58%)
  starting transfers between devices  32 us (25%)
  Pallas kernels  20.9 us (16%)
    ppermute x38, waiting for transfers between devices, send(): return lax.ppermute(block, ('sweep', 'plane'), route)  67.9 us
    ppermute x38, starting transfers between devices, send(): return lax.ppermute(block, ('sweep', 'plane'), route)  27.2 us
    pallas_call x9, Pallas kernels, call(): pl.pallas_call(kernel, in_specs=specs, out_specs=[whole(pltpu.SMEM if len...  20.9 us
    ppermute x1, waiting for transfers between devices, shards(): lax.ppermute(packet, 'sweep', [(i + 1, i) for i in range(sections - 1)])  4.12 us
    ppermute x1, starting transfers between devices, shards(): lax.ppermute(packet, 'sweep', [(i, i + 1) for i in range(sections - 1)])  3.48 us
  transfers between devices with their start and end apart: 40, of which 16 were waited for; matrix products, arithmetic and copies ran while one was open for 0% of the time, Pallas kernels for 0%

profile of v6, /device:TPU:0, one launch (start us, length us, event | category | flops | bytes accessed | tf_op | source)
XLA Modules:
  0.0 127.4 jit_solution(16996946959999163208)
XLA Ops:
  0.0 4.2 %first_fronts.1 = (f32[40,1024]{1,0:T(8,128)S(1)}, s32[2,1024]{1,0:T(2,128)S(1)}, bf16[8,16,128]{2,1,0:T(8,128)(2,1)S(1)}, s32[4]{0:T(128)S(1)}, bf16[2,512,4096]{2,1,0:T(8,128)(2,1)S(1)}) custom-call(s32[4]{0:T(128)} %layers_in.1, f32[2,16,1024]{2,1,0:T(8,128)} %bitcast.56, f32[2,1024]{1,0:T(2,128)} %isc_in.1, f32[2,1024]{1,0:T(2,128)} %fwd_in.1, ...), custom_call_target="tpu_custom_call" | custom-call | tf_op jit(solution)/shard_map/first_fronts/pallas_call | solution.py:326
  5.6 2.9 %collective-permute-start.2 = (bf16[2,8,16,128]{3,2,1,0:T(8,128)(2,1)S(1)}, bf16[2,8,16,128]{3,2,1,0:T(8,128)(2,1)S(1)}, u32[]{:S(2)}, u32[]{:S(2)}) collective-permute-start(bf16[2,8,16,128]{3,2,1,0:T(8,128)(2,1)S(1)} %pad_maximum_fusion.7), channel_id=1, source_target_pairs={{0,2},{1,5},{2,0},{3,7},{4,6},{5,1},{6,4},{7,3},{8,10},{9,13},{10,... | collective-permute-start | bytes 196616 | tf_op jit(solution)/shard_map/ppermute | solution.py:378
  8.5 1.5 %collective-permute-start = (bf16[8,16,128]{2,1,0:T(8,128)(2,1)S(1)}, bf16[8,16,128]{2,1,0:T(8,128)(2,1)S(1)}, u32[]{:S(2)}, u32[]{:S(2)}) collective-permute-start(bf16[8,16,128]{2,1,0:T(8,128)(2,1)S(1)} %get-tuple-element.35.rest_0_), channel_id=1, source_target_pairs={{0,6},{1,7},{2,4},{3,5},{4,2},{5,3},{6,0},{7,1},{8,14},{9,15},{10,... | collective-permute-start | bytes 98312 | tf_op jit(solution)/shard_map/ppermute | solution.py:378
  10.0 3.5 %collective-permute-start.5 = (f32[40,1024]{1,0:T(8,128)S(1)}, f32[40,1024]{1,0:T(8,128)S(1)}, u32[]{:S(2)}, u32[]{:S(2)}) collective-permute-start(f32[40,1024]{1,0:T(8,128)S(1)} %get-tuple-element.33.packet), channel_id=1, source_target_pairs={{0,8},{8,16},{16,24},{1,9},{9,17},{17,25},{2,10},{10,18},{18,26},{... | collective-permute-start | bytes 491528 | tf_op jit(solution)/shard_map/ppermute | solution.py:438
  13.5 1.3 %collective-permute-start.4 = (f32[40,1024]{1,0:T(8,128)S(1)}, f32[40,1024]{1,0:T(8,128)S(1)}, u32[]{:S(2)}, u32[]{:S(2)}) collective-permute-start(f32[40,1024]{1,0:T(8,128)S(1)} %get-tuple-element.33.packet), channel_id=1, source_target_pairs={{8,0},{16,8},{24,16},{9,1},{17,9},{25,17},{10,2},{18,10},{26,18},{... | collective-permute-start | bytes 491528 | tf_op jit(solution)/shard_map/ppermute | solution.py:437
  14.9 1.7 %collective-permute-done.5.rest_5_.rest_7_ = f32[40,1024]{1,0:T(8,128)S(1)} collective-permute-done((f32[40,1024]{1,0:T(8,128)S(1)}, f32[40,1024]{1,0:T(8,128)S(1)}, u32[]{:S(2)}, u32[]{:S(2)}) %collective-permute-start.5) | collective-permute-done | bytes 163872 | tf_op jit(solution)/shard_map/ppermute | solution.py:438
  16.6 4.1 %collective-permute-done.4.rest_4_.rest_5_ = f32[40,1024]{1,0:T(8,128)S(1)} collective-permute-done((f32[40,1024]{1,0:T(8,128)S(1)}, f32[40,1024]{1,0:T(8,128)S(1)}, u32[]{:S(2)}, u32[]{:S(2)}) %collective-permute-start.4) | collective-permute-done | bytes 163872 | tf_op jit(solution)/shard_map/ppermute | solution.py:437
  20.7 6.7 %forward_section_0.1 = (f32[2,16,1024]{2,1,0:T(8,128)S(1)}, bf16[8,16,128]{2,1,0:T(8,128)(2,1)S(1)}, bf16[24,16,128]{2,1,0:T(8,128)(2,1)S(1)}, bf16[2,512,4096]{2,1,0:T(8,128)(2,1)S(1)}) custom-call(s32[4]{0:T(128)S(1)} %get-tuple-element.31.layers, bf16[2,512,4096]{2,1,0:T(8,128)(2,1)S(1)} %get-tuple-element.32.first_inverse, ...), custom_call_target="tpu_custom_call" | custom-call | tf_op jit(solution)/shard_map/forward_section_0/pallas_call | solution.py:326
  27.5 1.6 %collective-permute-start.7 = (bf16[8,16,128]{2,1,0:T(8,128)(2,1)S(1)}, bf16[8,16,128]{2,1,0:T(8,128)(2,1)S(1)}, u32[]{:S(2)}, u32[]{:S(2)}) collective-permute-start(bf16[8,16,128]{2,1,0:T(8,128)(2,1)S(1)} %get-tuple-element.38), channel_id=1, source_target_pairs={{0,14},{1,15},{2,12},{3,13},{4,10},{5,11},{6,8},{7,9}} | collective-permute-start | bytes 98312 | tf_op jit(solution)/shard_map/ppermute | solution.py:378
  29.1 1.3 %collective-permute-start.6 = (bf16[24,16,128]{2,1,0:T(8,128)(2,1)S(1)}, bf16[24,16,128]{2,1,0:T(8,128)(2,1)S(1)}, u32[]{:S(2)}, u32[]{:S(2)}) collective-permute-start(bf16[24,16,128]{2,1,0:T(8,128)(2,1)S(1)} %get-tuple-element.37), channel_id=1, source_target_pairs={{0,8},{1,9},{2,10},{3,11},{4,12},{5,13},{6,14},{7,15}} | collective-permute-start | bytes 294920 | tf_op jit(solution)/shard_map/ppermute | solution.py:378
  30.5 1.3 %collective-permute-start.9 = (bf16[2,8,16,128]{3,2,1,0:T(8,128)(2,1)S(1)}, bf16[2,8,16,128]{3,2,1,0:T(8,128)(2,1)S(1)}, u32[]{:S(2)}, u32[]{:S(2)}) collective-permute-start(bf16[2,8,16,128]{3,2,1,0:T(8,128)(2,1)S(1)} %pad_maximum_fusion.8), channel_id=1, source_target_pairs={{0,10},{1,13},{2,8},{3,15},{4,14},{5,9},{6,12},{7,11}} | collective-permute-start | bytes 196616 | tf_op jit(solution)/shard_map/ppermute | solution.py:378
  31.8 1.8 %collective-permute-done.6.rest_0_.rest_4_.rest_8_ = bf16[24,16,128]{2,1,0:T(8,128)(2,1)S(1)} collective-permute-done((bf16[24,16,128]{2,1,0:T(8,128)(2,1)S(1)}, bf16[24,16,128]{2,1,0:T(8,128)(2,1)S(1)}, u32[]{:S(2)}, u32[]{:S(2)}) %collective-permute-start.6) | collective-permute-done | bytes 98336 | tf_op jit(solution)/shard_map/ppermute | solution.py:378
  34.6 1.3 %collective-permute-done.10.rest_3_ = bf16[4,8,16,128]{3,2,1,0:T(8,128)(2,1)S(1)} collective-permute-done((bf16[4,8,16,128]{3,2,1,0:T(8,128)(2,1)S(1)}, bf16[4,8,16,128]{3,2,1,0:T(8,128)(2,1)S(1)}, u32[]{:S(2)}, u32[]{:S(2)}) %collective-permute-start.10) | collective-permute-done | bytes 131104 | tf_op jit(solution)/shard_map/ppermute | solution.py:378
  46.8 1.5 %collective-permute-start.23 = (bf16[2,4,16,128]{3,2,1,0:T(8,128)(2,1)S(1)}, bf16[2,4,16,128]{3,2,1,0:T(8,128)(2,1)S(1)}, u32[]{:S(2)}, u32[]{:S(2)}) collective-permute-start(bf16[2,4,16,128]{3,2,1,0:T(8,128)(2,1)S(1)} %pad_maximum_fusion.15), channel_id=1, source_target_pairs={{0,2},{1,5},{2,0},{3,7},{4,6},{5,1},{6,4},{7,3},{8,10},{9,13},{10,... | collective-permute-start | bytes 98312 | tf_op jit(solution)/shard_map/ppermute | solution.py:378
  48.3 1.5 %collective-permute-start.21 = (bf16[4,16,128]{2,1,0:T(8,128)(2,1)S(1)}, bf16[4,16,128]{2,1,0:T(8,128)(2,1)S(1)}, u32[]{:S(2)}, u32[]{:S(2)}) collective-permute-start(bf16[4,16,128]{2,1,0:T(8,128)(2,1)S(1)} %get-tuple-element.43.rest_0_), channel_id=1, source_target_pairs={{0,6},{1,7},{2,4},{3,5},{4,2},{5,3},{6,0},{7,1},{8,14},{9,15},{10,... | collective-permute-start | bytes 49160 | tf_op jit(solution)/shard_map/ppermute | solution.py:378
  49.7 3.2 %collective-permute-done.21.rest_1_ = bf16[4,16,128]{2,1,0:T(8,128)(2,1)S(1)} collective-permute-done((bf16[4,16,128]{2,1,0:T(8,128)(2,1)S(1)}, bf16[4,16,128]{2,1,0:T(8,128)(2,1)S(1)}, u32[]{:S(2)}, u32[]{:S(2)}) %collective-permute-start.21) | collective-permute-done | bytes 16416 | tf_op jit(solution)/shard_map/ppermute | solution.py:378
  53.0 1.2 collective-permute-done.24.rest_3_
  64.1 1.3 %collective-permute-start.36 = (bf16[8,16,128]{2,1,0:T(8,128)(2,1)S(1)}, bf16[8,16,128]{2,1,0:T(8,128)(2,1)S(1)}, u32[]{:S(2)}, u32[]{:S(2)}) collective-permute-start(bf16[8,16,128]{2,1,0:T(8,128)(2,1)S(1)} %get-tuple-element.54), channel_id=1, source_target_pairs={{8,6},{9,7},{10,4},{11,5},{12,2},{13,3},{14,0},{15,1}} | collective-permute-start | bytes 98312 | tf_op jit(solution)/shard_map/ppermute | solution.py:378
  65.4 1.3 %collective-permute-start.35 = (bf16[24,16,128]{2,1,0:T(8,128)(2,1)S(1)}, bf16[24,16,128]{2,1,0:T(8,128)(2,1)S(1)}, u32[]{:S(2)}, u32[]{:S(2)}) collective-permute-start(bf16[24,16,128]{2,1,0:T(8,128)(2,1)S(1)} %get-tuple-element.53), channel_id=1, source_target_pairs={{8,0},{9,1},{10,2},{11,3},{12,4},{13,5},{14,6},{15,7}} | collective-permute-start | bytes 294920 | tf_op jit(solution)/shard_map/ppermute | solution.py:378
  66.7 1.3 %collective-permute-start.38 = (bf16[2,8,16,128]{3,2,1,0:T(8,128)(2,1)S(1)}, bf16[2,8,16,128]{3,2,1,0:T(8,128)(2,1)S(1)}, u32[]{:S(2)}, u32[]{:S(2)}) collective-permute-start(bf16[2,8,16,128]{3,2,1,0:T(8,128)(2,1)S(1)} %pad_maximum_fusion.14), channel_id=1, source_target_pairs={{8,2},{9,5},{10,0},{11,7},{12,6},{13,1},{14,4},{15,3}} | collective-permute-start | bytes 196616 | tf_op jit(solution)/shard_map/ppermute | solution.py:378
  68.0 49.8 %collective-permute-done.35.rest_0_.rest_5_ = bf16[24,16,128]{2,1,0:T(8,128)(2,1)S(1)} collective-permute-done((bf16[24,16,128]{2,1,0:T(8,128)(2,1)S(1)}, bf16[24,16,128]{2,1,0:T(8,128)(2,1)S(1)}, u32[]{:S(2)}, u32[]{:S(2)}) %collective-permute-start.35) | collective-permute-done | bytes 98336 | tf_op jit(solution)/shard_map/ppermute | solution.py:378
  117.8 2.0 %collective-permute-done.38.rest_2_ = bf16[2,8,16,128]{3,2,1,0:T(8,128)(2,1)S(1)} collective-permute-done((bf16[2,8,16,128]{3,2,1,0:T(8,128)(2,1)S(1)}, bf16[2,8,16,128]{3,2,1,0:T(8,128)(2,1)S(1)}, u32[]{:S(2)}, u32[]{:S(2)}) %collective-permute-start.38) | collective-permute-done | bytes 65568 | tf_op jit(solution)/shard_map/ppermute | solution.py:378
  119.9 1.3 %collective-permute-done.39.rest_3_ = bf16[4,8,16,128]{3,2,1,0:T(8,128)(2,1)S(1)} collective-permute-done((bf16[4,8,16,128]{3,2,1,0:T(8,128)(2,1)S(1)}, bf16[4,8,16,128]{3,2,1,0:T(8,128)(2,1)S(1)}, u32[]{:S(2)}, u32[]{:S(2)}) %collective-permute-start.39) | collective-permute-done | bytes 131104 | tf_op jit(solution)/shard_map/ppermute | solution.py:378
  121.2 6.2 %backward_section_0.1 = f32[2,16,1024]{2,1,0:T(8,128)} custom-call(s32[4]{0:T(128)S(1)} %get-tuple-element.31.layers, bf16[2,512,4096]{2,1,0:T(8,128)(2,1)S(1)} %get-tuple-element.32.first_inverse, bf16[2,512,4096]{2,1,0:T(8,128)(2,1)S(1)} %get-tuple-element.36.inverse.second_inverse, f32[40,1024]{1,0:T(8,128)S(1)} %get-tuple-element.33.packet, ...), custom_call_target="tpu_custom_call" | custom-call | tf_op jit(solution)/shard_map/backward_section_0/pallas_call | solution.py:326
  (87 shorter events, 23.1 us)
Async XLA Ops:
  5.6 9.2 %collective-permute-start.2 = (bf16[2,8,16,128]{3,2,1,0:T(8,128)(2,1)S(1)}, bf16[2,8,16,128]{3,2,1,0:T(8,128)(2,1)S(1)}, u32[]{:S(2)}, u32[]{:S(2)}) collective-permute-start(bf16[2,8,16,128]{3,2,1,0:T(8,128)(2,1)S(1)} %pad_maximum_fusion.7), channel_id=1, source_target_pairs={{0,2},{1,5},{2,0},{3,7},{4,6},{5,1},{6,4},{7,3},{8,10},{9,13},{10,... | collective-permute-start | bytes 196616 | tf_op jit(solution)/shard_map/ppermute | solution.py:378
  8.5 6.3 %collective-permute-start = (bf16[8,16,128]{2,1,0:T(8,128)(2,1)S(1)}, bf16[8,16,128]{2,1,0:T(8,128)(2,1)S(1)}, u32[]{:S(2)}, u32[]{:S(2)}) collective-permute-start(bf16[8,16,128]{2,1,0:T(8,128)(2,1)S(1)} %get-tuple-element.35.rest_0_), channel_id=1, source_target_pairs={{0,6},{1,7},{2,4},{3,5},{4,2},{5,3},{6,0},{7,1},{8,14},{9,15},{10,... | collective-permute-start | bytes 98312 | tf_op jit(solution)/shard_map/ppermute | solution.py:378
  10.0 6.6 %collective-permute-start.5 = (f32[40,1024]{1,0:T(8,128)S(1)}, f32[40,1024]{1,0:T(8,128)S(1)}, u32[]{:S(2)}, u32[]{:S(2)}) collective-permute-start(f32[40,1024]{1,0:T(8,128)S(1)} %get-tuple-element.33.packet), channel_id=1, source_target_pairs={{0,8},{8,16},{16,24},{1,9},{9,17},{17,25},{2,10},{10,18},{18,26},{... | collective-permute-start | bytes 491528 | tf_op jit(solution)/shard_map/ppermute | solution.py:438
  13.5 7.2 %collective-permute-start.4 = (f32[40,1024]{1,0:T(8,128)S(1)}, f32[40,1024]{1,0:T(8,128)S(1)}, u32[]{:S(2)}, u32[]{:S(2)}) collective-permute-start(f32[40,1024]{1,0:T(8,128)S(1)} %get-tuple-element.33.packet), channel_id=1, source_target_pairs={{8,0},{16,8},{24,16},{9,1},{17,9},{25,17},{10,2},{18,10},{26,18},{... | collective-permute-start | bytes 491528 | tf_op jit(solution)/shard_map/ppermute | solution.py:437
  14.8 5.9 %collective-permute-start.3 = (bf16[4,8,16,128]{3,2,1,0:T(8,128)(2,1)S(1)}, bf16[4,8,16,128]{3,2,1,0:T(8,128)(2,1)S(1)}, u32[]{:S(2)}, u32[]{:S(2)}) collective-permute-start(bf16[4,8,16,128]{3,2,1,0:T(8,128)(2,1)S(1)} %pad_maximum_fusion), channel_id=1, source_target_pairs={{0,1},{1,0},{2,3},{3,2},{4,5},{5,4},{6,7},{7,6},{8,9},{9,8},{10,11... | collective-permute-start | bytes 393224 | tf_op jit(solution)/shard_map/ppermute | solution.py:378
  27.4 3.0 %collective-permute-start.8 = (bf16[8,16,128]{2,1,0:T(8,128)(2,1)S(1)}, bf16[8,16,128]{2,1,0:T(8,128)(2,1)S(1)}, u32[]{:S(2)}, u32[]{:S(2)}) collective-permute-start(bf16[8,16,128]{2,1,0:T(8,128)(2,1)S(1)} %get-tuple-element.38), channel_id=1, source_target_pairs={{0,1},{1,0},{2,3},{3,2},{4,5},{5,4},{6,7},{7,6},{8,9},{9,8},{10,11... | collective-permute-start | bytes 98312 | tf_op jit(solution)/shard_map/ppermute | solution.py:378
  27.5 6.0 %collective-permute-start.7 = (bf16[8,16,128]{2,1,0:T(8,128)(2,1)S(1)}, bf16[8,16,128]{2,1,0:T(8,128)(2,1)S(1)}, u32[]{:S(2)}, u32[]{:S(2)}) collective-permute-start(bf16[8,16,128]{2,1,0:T(8,128)(2,1)S(1)} %get-tuple-element.38), channel_id=1, source_target_pairs={{0,14},{1,15},{2,12},{3,13},{4,10},{5,11},{6,8},{7,9}} | collective-permute-start | bytes 98312 | tf_op jit(solution)/shard_map/ppermute | solution.py:378
  29.1 4.4 %collective-permute-start.6 = (bf16[24,16,128]{2,1,0:T(8,128)(2,1)S(1)}, bf16[24,16,128]{2,1,0:T(8,128)(2,1)S(1)}, u32[]{:S(2)}, u32[]{:S(2)}) collective-permute-start(bf16[24,16,128]{2,1,0:T(8,128)(2,1)S(1)} %get-tuple-element.37), channel_id=1, source_target_pairs={{0,8},{1,9},{2,10},{3,11},{4,12},{5,13},{6,14},{7,15}} | collective-permute-start | bytes 294920 | tf_op jit(solution)/shard_map/ppermute | solution.py:378
  30.5 4.1 %collective-permute-start.9 = (bf16[2,8,16,128]{3,2,1,0:T(8,128)(2,1)S(1)}, bf16[2,8,16,128]{3,2,1,0:T(8,128)(2,1)S(1)}, u32[]{:S(2)}, u32[]{:S(2)}) collective-permute-start(bf16[2,8,16,128]{3,2,1,0:T(8,128)(2,1)S(1)} %pad_maximum_fusion.8), channel_id=1, source_target_pairs={{0,10},{1,13},{2,8},{3,15},{4,14},{5,9},{6,12},{7,11}} | collective-permute-start | bytes 196616 | tf_op jit(solution)/shard_map/ppermute | solution.py:378
  36.5 1.6 %collective-permute-start.13 = (bf16[8,16,128]{2,1,0:T(8,128)(2,1)S(1)}, bf16[8,16,128]{2,1,0:T(8,128)(2,1)S(1)}, u32[]{:S(2)}, u32[]{:S(2)}) collective-permute-start(bf16[8,16,128]{2,1,0:T(8,128)(2,1)S(1)} %get-tuple-element.40), channel_id=1, source_target_pairs={{0,1},{1,0},{2,3},{3,2},{4,5},{5,4},{6,7},{7,6},{8,9},{9,8},{10,11... | collective-permute-start | bytes 98312 | tf_op jit(solution)/shard_map/ppermute | solution.py:378
  36.7 2.1 %collective-permute-start.12 = (bf16[8,16,128]{2,1,0:T(8,128)(2,1)S(1)}, bf16[8,16,128]{2,1,0:T(8,128)(2,1)S(1)}, u32[]{:S(2)}, u32[]{:S(2)}) collective-permute-start(bf16[8,16,128]{2,1,0:T(8,128)(2,1)S(1)} %get-tuple-element.40), channel_id=1, source_target_pairs={{8,22},{9,23},{10,20},{11,21},{12,18},{13,19},{14,16},{15,17}} | collective-permute-start | bytes 98312 | tf_op jit(solution)/shard_map/ppermute | solution.py:378
  38.8 1.4 %collective-permute-start.15 = (bf16[4,8,16,128]{3,2,1,0:T(8,128)(2,1)S(1)}, bf16[4,8,16,128]{3,2,1,0:T(8,128)(2,1)S(1)}, u32[]{:S(2)}, u32[]{:S(2)}) collective-permute-start(bf16[4,8,16,128]{3,2,1,0:T(8,128)(2,1)S(1)} %pad_maximum_fusion.2), channel_id=1, source_target_pairs={{0,1},{1,0},{2,3},{3,2},{4,5},{5,4},{6,7},{7,6},{8,9},{9,8},{10,11... | collective-permute-start | bytes 393224 | tf_op jit(solution)/shard_map/ppermute | solution.py:378
  41.0 1.8 %collective-permute-start.18 = (bf16[8,16,128]{2,1,0:T(8,128)(2,1)S(1)}, bf16[8,16,128]{2,1,0:T(8,128)(2,1)S(1)}, u32[]{:S(2)}, u32[]{:S(2)}) collective-permute-start(bf16[8,16,128]{2,1,0:T(8,128)(2,1)S(1)} %get-tuple-element.42), channel_id=1, source_target_pairs={{0,1},{1,0},{2,3},{3,2},{4,5},{5,4},{6,7},{7,6},{8,9},{9,8},{10,11... | collective-permute-start | bytes 98312 | tf_op jit(solution)/shard_map/ppermute | solution.py:378
  41.4 2.1 %collective-permute-start.17 = (bf16[8,16,128]{2,1,0:T(8,128)(2,1)S(1)}, bf16[8,16,128]{2,1,0:T(8,128)(2,1)S(1)}, u32[]{:S(2)}, u32[]{:S(2)}) collective-permute-start(bf16[8,16,128]{2,1,0:T(8,128)(2,1)S(1)} %get-tuple-element.42), channel_id=1, source_target_pairs={{16,30},{17,31},{18,28},{19,29},{20,26},{21,27},{22,24},{23,25}} | collective-permute-start | bytes 98312 | tf_op jit(solution)/shard_map/ppermute | solution.py:378
  46.8 6.1 %collective-permute-start.23 = (bf16[2,4,16,128]{3,2,1,0:T(8,128)(2,1)S(1)}, bf16[2,4,16,128]{3,2,1,0:T(8,128)(2,1)S(1)}, u32[]{:S(2)}, u32[]{:S(2)}) collective-permute-start(bf16[2,4,16,128]{3,2,1,0:T(8,128)(2,1)S(1)} %pad_maximum_fusion.15), channel_id=1, source_target_pairs={{0,2},{1,5},{2,0},{3,7},{4,6},{5,1},{6,4},{7,3},{8,10},{9,13},{10,... | collective-permute-start | bytes 98312 | tf_op jit(solution)/shard_map/ppermute | solution.py:378
  48.3 4.6 %collective-permute-start.21 = (bf16[4,16,128]{2,1,0:T(8,128)(2,1)S(1)}, bf16[4,16,128]{2,1,0:T(8,128)(2,1)S(1)}, u32[]{:S(2)}, u32[]{:S(2)}) collective-permute-start(bf16[4,16,128]{2,1,0:T(8,128)(2,1)S(1)} %get-tuple-element.43.rest_0_), channel_id=1, source_target_pairs={{0,6},{1,7},{2,4},{3,5},{4,2},{5,3},{6,0},{7,1},{8,14},{9,15},{10,... | collective-permute-start | bytes 49160 | tf_op jit(solution)/shard_map/ppermute | solution.py:378
  54.8 1.6 %collective-permute-start.27 = (bf16[8,16,128]{2,1,0:T(8,128)(2,1)S(1)}, bf16[8,16,128]{2,1,0:T(8,128)(2,1)S(1)}, u32[]{:S(2)}, u32[]{:S(2)}) collective-permute-start(bf16[8,16,128]{2,1,0:T(8,128)(2,1)S(1)} %get-tuple-element.46), channel_id=1, source_target_pairs={{0,1},{1,0},{2,3},{3,2},{4,5},{5,4},{6,7},{7,6},{8,9},{9,8},{10,11... | collective-permute-start | bytes 98312 | tf_op jit(solution)/shard_map/ppermute | solution.py:378
  55.0 2.1 %collective-permute-start.26 = (bf16[8,16,128]{2,1,0:T(8,128)(2,1)S(1)}, bf16[8,16,128]{2,1,0:T(8,128)(2,1)S(1)}, u32[]{:S(2)}, u32[]{:S(2)}) collective-permute-start(bf16[8,16,128]{2,1,0:T(8,128)(2,1)S(1)} %get-tuple-element.46), channel_id=1, source_target_pairs={{24,22},{25,23},{26,20},{27,21},{28,18},{29,19},{30,16},{31,17}} | collective-permute-start | bytes 98312 | tf_op jit(solution)/shard_map/ppermute | solution.py:378
  59.1 1.8 %collective-permute-start.32 = (bf16[8,16,128]{2,1,0:T(8,128)(2,1)S(1)}, bf16[8,16,128]{2,1,0:T(8,128)(2,1)S(1)}, u32[]{:S(2)}, u32[]{:S(2)}) collective-permute-start(bf16[8,16,128]{2,1,0:T(8,128)(2,1)S(1)} %get-tuple-element.50), channel_id=1, source_target_pairs={{0,1},{1,0},{2,3},{3,2},{4,5},{5,4},{6,7},{7,6},{8,9},{9,8},{10,11... | collective-permute-start | bytes 98312 | tf_op jit(solution)/shard_map/ppermute | solution.py:378
  59.5 2.1 %collective-permute-start.31 = (bf16[8,16,128]{2,1,0:T(8,128)(2,1)S(1)}, bf16[8,16,128]{2,1,0:T(8,128)(2,1)S(1)}, u32[]{:S(2)}, u32[]{:S(2)}) collective-permute-start(bf16[8,16,128]{2,1,0:T(8,128)(2,1)S(1)} %get-tuple-element.50), channel_id=1, source_target_pairs={{16,14},{17,15},{18,12},{19,13},{20,10},{21,11},{22,8},{23,9}} | collective-permute-start | bytes 98312 | tf_op jit(solution)/shard_map/ppermute | solution.py:378
  63.9 2.8 %collective-permute-start.37 = (bf16[8,16,128]{2,1,0:T(8,128)(2,1)S(1)}, bf16[8,16,128]{2,1,0:T(8,128)(2,1)S(1)}, u32[]{:S(2)}, u32[]{:S(2)}) collective-permute-start(bf16[8,16,128]{2,1,0:T(8,128)(2,1)S(1)} %get-tuple-element.54), channel_id=1, source_target_pairs={{0,1},{1,0},{2,3},{3,2},{4,5},{5,4},{6,7},{7,6},{8,9},{9,8},{10,11... | collective-permute-start | bytes 98312 | tf_op jit(solution)/shard_map/ppermute | solution.py:378
  64.1 53.7 %collective-permute-start.36 = (bf16[8,16,128]{2,1,0:T(8,128)(2,1)S(1)}, bf16[8,16,128]{2,1,0:T(8,128)(2,1)S(1)}, u32[]{:S(2)}, u32[]{:S(2)}) collective-permute-start(bf16[8,16,128]{2,1,0:T(8,128)(2,1)S(1)} %get-tuple-element.54), channel_id=1, source_target_pairs={{8,6},{9,7},{10,4},{11,5},{12,2},{13,3},{14,0},{15,1}} | collective-permute-start | bytes 98312 | tf_op jit(solution)/shard_map/ppermute | solution.py:378
  65.4 52.4 %collective-permute-start.35 = (bf16[24,16,128]{2,1,0:T(8,128)(2,1)S(1)}, bf16[24,16,128]{2,1,0:T(8,128)(2,1)S(1)}, u32[]{:S(2)}, u32[]{:S(2)}) collective-permute-start(bf16[24,16,128]{2,1,0:T(8,128)(2,1)S(1)} %get-tuple-element.53), channel_id=1, source_target_pairs={{8,0},{9,1},{10,2},{11,3},{12,4},{13,5},{14,6},{15,7}} | collective-permute-start | bytes 294920 | tf_op jit(solution)/shard_map/ppermute | solution.py:378
  66.7 53.1 %collective-permute-start.38 = (bf16[2,8,16,128]{3,2,1,0:T(8,128)(2,1)S(1)}, bf16[2,8,16,128]{3,2,1,0:T(8,128)(2,1)S(1)}, u32[]{:S(2)}, u32[]{:S(2)}) collective-permute-start(bf16[2,8,16,128]{3,2,1,0:T(8,128)(2,1)S(1)} %pad_maximum_fusion.14), channel_id=1, source_target_pairs={{8,2},{9,5},{10,0},{11,7},{12,6},{13,1},{14,4},{15,3}} | collective-permute-start | bytes 196616 | tf_op jit(solution)/shard_map/ppermute | solution.py:378
  (16 other events, 19.4 us)

commit v7 on v6

--- a/solution.py
+++ b/solution.py
@@ -10,6 +10,7 @@
 LANES = 128
 CORES = 2
 ISC, FWD, BWD, PICK = 0, 2, 4, 6
+SLOPE, TURN, FOLD, CELL, NEEDS = 0, 1, 2, 3, 8
 F32, BF16 = jnp.float32, jnp.bfloat16
 
 
@@ -54,23 +55,37 @@
     return ref[at:at + 1, :width].astype(jnp.int32)
 
 
-def forward_front(rhs_a, rhs_b, small, incoming, width):
-    first = rhs_a if incoming is None else minus(rhs_a, scaled(row_of(small, FWD), incoming))
-    second = minus(rhs_b, scaled(row_of(small, FWD + 1), scaled(row_of(small, ISC), first)))
-    return (
-        gather_lanes(rounded(first), picks(small, PICK, width))
-        + gather_lanes(rounded(second), picks(small, PICK + 1, width))
-    )
-
-
-def backward_front(small, incoming, second_fwd, both, width):
-    z = scaled(row_of(small, BWD + 1), incoming)
-    local = minus(second_fwd, scaled(row_of(small, ISC + 1), z))
-    first = scaled(row_of(small, BWD), choose(both, local, incoming))
-    return (
-        gather_lanes(rounded(first), picks(small, PICK, width))
-        + gather_lanes(rounded(z), picks(small, PICK + 1, width))
-    )
+def halves(row):
+    chunks = split(row)
+    return chunks[:len(chunks) // 2], chunks[len(chunks) // 2:]
+
+
+def times(left, right):
+    return [a * b for a, b in zip(left, right)]
+
+
+def plus(left, right):
+    return [a + b for a, b in zip(left, right)]
+
+
+def gathered_at(needs, field):
+    cells = needs[CELL:CELL + 1, :].astype(jnp.int32)
+    half = cells.shape[1] // 2
+    return gather_lanes(field, cells[:, :half]), gather_lanes(field, cells[:, half:])
+
+
+def forward_front(base, needs, incoming):
+    (base_a, base_b), (slope_a, slope_b) = halves(base[...]), halves(row_of(needs, SLOPE))
+    at_a, at_b = gathered_at(needs, incoming)
+    return minus(base_a, times(slope_a, at_a)) + plus(base_b, times(slope_b, at_b))
+
+
+def backward_front(needs, incoming, second_fwd, both):
+    (turn_a, turn_b), (fold, _) = halves(row_of(needs, TURN)), halves(row_of(needs, FOLD))
+    at_a, at_b = gathered_at(needs, incoming)
+    second_a, _ = gathered_at(needs, second_fwd)
+    following = choose(both, minus(second_a, times(fold, at_a)), at_a)
+    return times(turn_a, following) + times(turn_b, at_b)
 
 
 def write_front(ref, chunks, field=()):
@@ -142,33 +157,60 @@
 
 
 def first_kernel(
-    width, layers_in, rhs_in, isc_in, fwd_in, bwd_in, picked_in, inverse, packet, place, front,
-    layers, first_inverse, rhs, isc, fwd, bwd, picked, sems, load_sem,
+    width, layers_in, rhs_in, isc_in, fwd_in, bwd_in, picked_in, local, ahead, back, place, front,
+    layers, rhs, isc, fwd, bwd, picked, sems,
 ):
     pairs = (
         (rhs_in, rhs), (isc_in, isc), (fwd_in, fwd), (bwd_in, bwd), (picked_in, picked),
         (layers_in, layers),
     )
     copies = [pltpu.make_async_copy(a, b, sems.at[i]) for i, (a, b) in enumerate(pairs)]
-    load = pltpu.make_async_copy(inverse.at[0], first_inverse, load_sem.at[0])
     for copy in copies:
         copy.start()
-    load.start()
     for copy in copies:
         copy.wait()
     cells = rhs.shape[-1]
     count = rhs.shape[1]
-    small = packet.at[2 * count:]
+    small = local.at[2 * count:]
     small[ISC:ISC + 2, :] = isc[...]
     small[FWD:FWD + 2, :] = fwd[...]
     small[BWD:BWD + 2, :] = bwd[...]
     small[PICK:PICK + 2, :] = jnp.full((2, cells), -1, F32)
     small[PICK:PICK + 2, :width] = picked[...].astype(F32)
-    packet[0:count, :] = rhs[0]
-    packet[count:2 * count, :] = rhs[1]
+    local[0:count, :] = rhs[0]
+    local[count:2 * count, :] = rhs[1]
+
+    at_a, at_b = picked[0:1, :], picked[1:2, :]
+    isc_a, isc_b, fwd_a, fwd_b, bwd_a, bwd_b = (
+        split(jnp.broadcast_to(row_of(small, at), (8, cells))) for at in range(PICK)
+    )
+    base_a = gather_lanes(split(rhs[0]), at_a)
+    fed = times(fwd_b, isc_a)
+    base_b = gather_lanes(
+        minus(split(rhs[1]), [f[0:1] * r for f, r in zip(fed, split(rhs[0]))]), at_b
+    )
+    write_front(front, base_a + base_b)
+    zero = [jnp.zeros((8, LANES), F32)] * (width // LANES)
+    rows = {
+        SLOPE: gather_lanes(fwd_a, at_a) + gather_lanes(times(fed, fwd_a), at_b),
+        TURN: gather_lanes(bwd_a, at_a) + gather_lanes(bwd_b, at_b),
+        FOLD: gather_lanes(times(isc_b, bwd_b), at_a) + zero,
+        CELL: split(at_a.astype(F32)) + split(at_b.astype(F32)),
+    }
+    back[...] = jnp.zeros(back.shape, F32)
+    for at, chunks in rows.items():
+        for i, chunk in enumerate(chunks):
+            back[at:at + 1, i * LANES:(i + 1) * LANES] = chunk[0:1]
+    write_field(ahead.at[0:count], base_a + base_b)
+    ahead[count:, :] = back[...]
     for layer in range(2):
         place[layer:layer + 1, :] = places(picked[layer:layer + 1, :], cells)
-    write_front(front, forward_front(split(rhs[0]), split(rhs[1]), small, None, width))
+
+
+def load_kernel(inverse, _, loaded, done, sem):
+    load = pltpu.make_async_copy(inverse.at[0], loaded, sem.at[0])
+    load.start()
+    done[...] = jnp.zeros(done.shape, F32)
     load.wait()
 
 
@@ -182,8 +224,6 @@
         incoming, *rest = rest
     if not final:
         after, *rest = rest
-    if not step:
-        _, *rest = rest
     kept, front, *rest = rest
     if not final:
         outgoing_packet, *rest = rest
@@ -236,10 +276,7 @@
             write_front(front, gather_lanes(rounded(z), picks(small, PICK, width)))
         else:
             outgoing = choose(both, second, first)
-            ahead = after.at[2 * rows:]
-            chunks = forward_front(
-                split(after[0:rows, :]), split(after[rows:2 * rows, :]), ahead, outgoing, width
-            )
+            chunks = forward_front(after.at[0:rows], after.at[rows:], outgoing)
             write_front(front, chunks)
             write_front(outgoing_packet, chunks, outgoing)
         write_field(kept.at[0], first)
@@ -305,8 +342,7 @@
         first = minus(first_fwd, change)
         if step:
             chunks = backward_front(
-                behind.at[2 * kept.shape[1]:], first, read_field(held, count),
-                layers[step - 1] == 2, width
+                behind, first, read_field(held, count), layers[step - 1] == 2
             )
             write_front(front, chunks)
             write_front(outgoing_packet, chunks, first)
@@ -389,23 +425,26 @@
             return [gathered], [[0]], order // LANES
         return [gathered], [list(range(planes))], per_layer
 
-    def spread(front, straight, pair):
-        blocks, owners = [straight], [[(0, 0)]]
+    def spread(front, straight, pair, beside=None):
+        blocks, owners, tokens = [straight], [[(0, 0)]], []
         for step in [1] if chips == 2 else range(3, chips):
             blocks.append(send(front, pair, CORES * step))
             owners.append([(CORES * step, CORES * step)])
         if chips == 4:
             both = jnp.stack([front, send(front, None, 1)])
+            tokens = beside(both) if beside else []
             blocks.append(send(both, pair, CORES, 2 * CORES))
             owners += [[(CORES + core, 2 * CORES + core) for core in range(CORES)]]
         short = [b[:2 * per_layer] if b.ndim == 3 else b for b in blocks]
         mine = jnp.concatenate([b[None] if b.ndim == 3 else b for b in short])
+        for token in tokens:
+            mine = mine + jnp.minimum(jnp.abs(token), 0).astype(BF16)
         blocks.append(send(mine, None, 1))
         owners.append([(one ^ 1, zero ^ 1) for places in owners for zero, one in places])
         return blocks, owners, per_layer
 
-    def within(front):
-        return spread(front, front, None) if direct else everywhere(front)
+    def within(front, beside=None):
+        return spread(front, front, None, beside) if direct else everywhere(front)
 
     def between(front, packet, start, stop):
         if not direct:
@@ -418,30 +457,52 @@
     half_inverse = pltpu.VMEM(front_inverse.shape[1:], BF16)
     coefficients = (interior_scale, forward_coupling, backward_coupling)
     operands = [section_layers, rhs, *coefficients, picked]
-    packet, place, front, layers, first_inverse = call(
+    local, ahead, back, place, front, layers = call(
         functools.partial(first_kernel, width),
-        [in_hbm(a) for a in operands] + [inverse],
+        [in_hbm(a) for a in operands],
         [
             ((2 * rows + 8, cells), F32),
+            ((rows + NEEDS, 2 * width), F32),
+            ((NEEDS, 2 * width), F32),
             ((2, cells), jnp.int32),
             front_shape,
             (section_layers.shape, jnp.int32),
-            half_inverse,
         ],
-        [pltpu.VMEM(a.shape, a.dtype) for a in operands[1:]]
-        + [pltpu.SemaphoreType.DMA((6,)), pltpu.SemaphoreType.DMA((1,))],
+        [pltpu.VMEM(a.shape, a.dtype) for a in operands[1:]] + [pltpu.SemaphoreType.DMA((6,))],
         "first_fronts",
-        range(7),
+        range(6),
     )
-    gathered, owners, slots = within(front)
-    after = lax.ppermute(packet, "sweep", [(i + 1, i) for i in range(sections - 1)])
-    behind = lax.ppermute(packet, "sweep", [(i, i + 1) for i in range(sections - 1)])
+    after = lax.ppermute(ahead, "sweep", [(i + 1, i) for i in range(sections - 1)])
+    behind = lax.ppermute(back, "sweep", [(i, i + 1) for i in range(sections - 1)])
+
+    def load(token):
+        return call(
+            load_kernel,
+            [inverse, token],
+            [half_inverse, ((8, LANES), F32)],
+            [pltpu.SemaphoreType.DMA((1,))],
+            "load_first",
+            [0],
+        )
+
+    if chips == 4 and direct:
+        loaded = []
+
+        def beside(both):
+            loaded.extend(load(both))
+            token = loaded[1][0, 0]
+            return [after[0, 0], token, jnp.min(jnp.abs(behind - token))]
+
+        gathered, owners, slots = within(front, beside)
+        first_inverse = loaded[0]
+    else:
+        gathered, owners, slots = within(front)
+        first_inverse = load(front)[0]
 
     kept, held = [], [None]
     for step in range(sections):
         final = step == sections - 1
         extra = ([held[step]] if step else []) + ([] if final else [after])
-        extra += [] if step else [behind]
         outs = [layers_shape, half_shape if final else front_shape]
         outs += [] if final else [packet_shape]
         outs += [] if step else [half_inverse]
@@ -449,7 +510,7 @@
             functools.partial(
                 forward_kernel, step, sections, planes, width, slots, owners
             ),
-            [layers, first_inverse, inverse, packet, place, *gathered, *extra],
+            [layers, first_inverse, inverse, local, place, *gathered, *extra],
             outs,
             scratch + ([] if step else [pltpu.SemaphoreType.DMA((1,))]),
             f"forward_section_{step}",
@@ -471,7 +532,7 @@
             functools.partial(
                 backward_kernel, step, sections, planes, width, slots, owners
             ),
-            [layers, first_inverse, inverse, packet, place, *gathered, kept[step], *extra],
+            [layers, first_inverse, inverse, local, place, *gathered, kept[step], *extra],
             [layers_shape] + ([front_shape, packet_shape] if step else []),
             scratch,
             f"backward_section_{step}",

time: 128 us -> 138 us (1.078)
  local copies, waits for them, and re-layouts: 0.02 us -> 7.71 us
  starting transfers between devices: 32 us -> 35.7 us
  Pallas kernels: 20.9 us -> 18 us
  between operations: 0.57 us -> 2.64 us
  waiting for transfers between devices: 73.8 us -> 72.2 us
    unnamed x0 -> x6, local copies, waits for them, and re-layouts: none -> 6.67 us
    ppermute x2, waiting for transfers between devices: 5.82 us -> 0.01 us  [the longest x1 0.01 us: shards(): lax.ppermute(back, 'sweep', [(i, i + 1) for i in range(sections - 1)])]
    ppermute x38, waiting for transfers between devices: 67.9 us -> 72.2 us  [send(): return lax.ppermute(block, ('sweep', 'plane'), route)]
    ppermute x38, starting transfers between devices: 27.2 us -> 31 us  [send(): return lax.ppermute(block, ('sweep', 'plane'), route)]
    pallas_call x9 -> x10, Pallas kernels: 20.9 us -> 18 us  [call(): pl.pallas_call(kernel, in_specs=specs, out_specs=[whole(pltpu.SMEM if len...]
  transfers between devices with their start and end apart: 40 -> 40, of which waited for: 16 -> 14; matrix products, arithmetic and copies ran while one was open for 0% -> 2% of each run, Pallas kernels for 0% -> 2%
where the time goes in v7:
time: 138 us
  waiting for transfers between devices  72.2 us (52%)
  starting transfers between devices  35.7 us (26%)
  Pallas kernels  18 us (13%)
  local copies, waits for them, and re-layouts  7.71 us (6%)
  between operations  2.64 us (2%)
  other arithmetic  1.53 us (1%)
    ppermute x38, waiting for transfers between devices, send(): return lax.ppermute(block, ('sweep', 'plane'), route)  72.2 us
    ppermute x38, starting transfers between devices, send(): return lax.ppermute(block, ('sweep', 'plane'), route)  31 us
    pallas_call x10, Pallas kernels, call(): pl.pallas_call(kernel, in_specs=specs, out_specs=[whole(pltpu.SMEM if len...  18 us
    unnamed x6, local copies, waits for them, and re-layouts  6.67 us
    ppermute x1, starting transfers between devices, shards(): lax.ppermute(back, 'sweep', [(i, i + 1) for i in range(sections - 1)])  3.47 us
  transfers between devices with their start and end apart: 40, of which 14 were waited for; matrix products, arithmetic and copies ran while one was open for 2% of the time, Pallas kernels for 2%

profile of v7, /device:TPU:0, one launch (start us, length us, event | category | flops | bytes accessed | tf_op | source)
XLA Modules:
  0.0 137.8 jit_solution(2180558227969718306)
XLA Ops:
  0.0 2.4 %first_fronts.1 = (f32[40,1024]{1,0:T(8,128)S(1)}, f32[24,1024]{1,0:T(8,128)S(1)}, f32[8,1024]{1,0:T(8,128)S(1)}, s32[2,1024]{1,0:T(2,128)S(1)}, bf16[8,16,128]{2,1,0:T(8,128)(2,1)S(1)}, /*index=5*/s32[4]{0:T(128)S(1)}) custom-call(s32[4]{0:T(128)} %layers_in.1, f32[2,16,1024]{2,1,0:T(8,128)} %bitcast.58, f32[2,1024]{1,0:T(2,128)} %isc_in.1, ...), custom_call_target="tpu_custom_call" | custom-call | tf_op jit(solution)/shard_map/first_fronts/pallas_call | solution.py:362
  2.9 3.5 %collective-permute-start.1 = (bf16[8,16,128]{2,1,0:T(8,128)(2,1)S(1)}, bf16[8,16,128]{2,1,0:T(8,128)(2,1)S(1)}, u32[]{:S(2)}, u32[]{:S(2)}) collective-permute-start(bf16[8,16,128]{2,1,0:T(8,128)(2,1)S(1)} %get-tuple-element.35.rest_0_), channel_id=1, source_target_pairs={{0,6},{1,7},{2,4},{3,5},{4,2},{5,3},{6,0},{7,1},{8,14},{9,15},{10,... | collective-permute-start | bytes 98312 | tf_op jit(solution)/shard_map/ppermute | solution.py:414
  6.5 3.5 %collective-permute-start.4 = (f32[8,1024]{1,0:T(8,128)S(1)}, f32[8,1024]{1,0:T(8,128)S(1)}, u32[]{:S(2)}, u32[]{:S(2)}) collective-permute-start(f32[8,1024]{1,0:T(8,128)S(1)} %get-tuple-element.41), channel_id=1, source_target_pairs={{0,8},{8,16},{16,24},{1,9},{9,17},{17,25},{2,10},{10,18},{18,26},{... | collective-permute-start | bytes 98312 | tf_op jit(solution)/shard_map/ppermute | solution.py:476
  9.9 1.3 collective-permute-start.3
  11.9 3.4 %load_first.1 = (bf16[2,512,4096]{2,1,0:T(8,128)(2,1)S(1)}, f32[8,128]{1,0:T(8,128)S(1)}) custom-call(bf16[2,2,512,4096]{3,2,1,0:T(8,128)(2,1)} %inverse.3, bf16[2,8,16,128]{3,2,1,0:T(8,128)(2,1)S(1)} %pad_maximum_fusion.6._), custom_call_target="tpu_custom_call" | custom-call | tf_op jit(solution)/shard_map/load_first/pallas_call | solution.py:362
  15.3 3.3 %copy-done = bf16[2,512,4096]{2,1,0:T(8,128)(2,1)} copy-done((bf16[2,512,4096]{2,1,0:T(8,128)(2,1)}, bf16[2,512,4096]{2,1,0:T(8,128)(2,1)S(1)}, u32[]{:S(2)}) %copy-start) | copy-done | bytes 8388632
  19.1 1.3 abs_reduce_fusion
  23.1 1.3 collective-permute-done.5.rest_3_
  24.4 3.4 %copy-done.1 = bf16[2,512,4096]{2,1,0:T(8,128)(2,1)S(1)} copy-done((bf16[2,512,4096]{2,1,0:T(8,128)(2,1)S(1)}, bf16[2,512,4096]{2,1,0:T(8,128)(2,1)}, u32[]{:S(2)}) %copy-start.1) | copy-done | bytes 8388632
  27.8 4.6 %forward_section_0.1 = (f32[2,16,1024]{2,1,0:T(8,128)S(1)}, bf16[8,16,128]{2,1,0:T(8,128)(2,1)S(1)}, bf16[24,16,128]{2,1,0:T(8,128)(2,1)S(1)}, bf16[2,512,4096]{2,1,0:T(8,128)(2,1)S(1)}) custom-call(s32[4]{0:T(128)S(1)} %get-tuple-element.34.layers, bf16[2,512,4096]{2,1,0:T(8,128)(2,1)S(1)} %copy-done.1, bf16[2,2,512,4096]{3,2,1,0:T(8,128)(2,1)} %inverse.3, ...), custom_call_target="tpu_custom_call" | custom-call | tf_op jit(solution)/shard_map/forward_section_0/pallas_call | solution.py:362
  32.7 5.1 %collective-permute-start.7 = (bf16[8,16,128]{2,1,0:T(8,128)(2,1)S(1)}, bf16[8,16,128]{2,1,0:T(8,128)(2,1)S(1)}, u32[]{:S(2)}, u32[]{:S(2)}) collective-permute-start(bf16[8,16,128]{2,1,0:T(8,128)(2,1)S(1)} %get-tuple-element.44), channel_id=1, source_target_pairs={{0,14},{1,15},{2,12},{3,13},{4,10},{5,11},{6,8},{7,9}} | collective-permute-start | bytes 98312 | tf_op jit(solution)/shard_map/ppermute | solution.py:414
  37.8 1.3 collective-permute-start.6
  39.1 1.3 collective-permute-start.9
  40.4 1.7 %collective-permute-done.6.rest_0_.rest_4_.rest_8_ = bf16[24,16,128]{2,1,0:T(8,128)(2,1)S(1)} collective-permute-done((bf16[24,16,128]{2,1,0:T(8,128)(2,1)S(1)}, bf16[24,16,128]{2,1,0:T(8,128)(2,1)S(1)}, u32[]{:S(2)}, u32[]{:S(2)}) %collective-permute-start.6) | collective-permute-done | bytes 98336 | tf_op jit(solution)/shard_map/ppermute | solution.py:414
  43.1 1.3 collective-permute-done.10.rest_3_
  52.2 1.2 collective-permute-done.20.rest_3_
  55.9 2.4 %collective-permute-start.21 = (bf16[4,16,128]{2,1,0:T(8,128)(2,1)S(1)}, bf16[4,16,128]{2,1,0:T(8,128)(2,1)S(1)}, u32[]{:S(2)}, u32[]{:S(2)}) collective-permute-start(bf16[4,16,128]{2,1,0:T(8,128)(2,1)S(1)} %get-tuple-element.49.rest_0_), channel_id=1, source_target_pairs={{0,6},{1,7},{2,4},{3,5},{4,2},{5,3},{6,0},{7,1},{8,14},{9,15},{10,... | collective-permute-start | bytes 49160 | tf_op jit(solution)/shard_map/ppermute | solution.py:414
  58.2 2.3 %collective-permute-done.21.rest_1_ = bf16[4,16,128]{2,1,0:T(8,128)(2,1)S(1)} collective-permute-done((bf16[4,16,128]{2,1,0:T(8,128)(2,1)S(1)}, bf16[4,16,128]{2,1,0:T(8,128)(2,1)S(1)}, u32[]{:S(2)}, u32[]{:S(2)}) %collective-permute-start.21) | collective-permute-done | bytes 16416 | tf_op jit(solution)/shard_map/ppermute | solution.py:414
  60.6 1.2 collective-permute-done.24.rest_3_
  71.7 1.3 collective-permute-start.36
  73.0 1.3 collective-permute-start.35
  74.3 1.3 collective-permute-start.38
  75.6 55.8 %collective-permute-done.35.rest_0_.rest_5_ = bf16[24,16,128]{2,1,0:T(8,128)(2,1)S(1)} collective-permute-done((bf16[24,16,128]{2,1,0:T(8,128)(2,1)S(1)}, bf16[24,16,128]{2,1,0:T(8,128)(2,1)S(1)}, u32[]{:S(2)}, u32[]{:S(2)}) %collective-permute-start.35) | collective-permute-done | bytes 98336 | tf_op jit(solution)/shard_map/ppermute | solution.py:414
  134.0 3.8 %backward_section_0.1 = f32[2,16,1024]{2,1,0:T(8,128)} custom-call(s32[4]{0:T(128)S(1)} %get-tuple-element.34.layers, bf16[2,512,4096]{2,1,0:T(8,128)(2,1)S(1)} %copy-done.2, bf16[2,512,4096]{2,1,0:T(8,128)(2,1)S(1)} %get-tuple-element.42.inverse.second_inverse, f32[40,1024]{1,0:T(8,128)S(1)} %get-tuple-element.37.packet, ...), custom_call_target="tpu_custom_call" | custom-call | tf_op jit(solution)/shard_map/backward_section_0/pallas_call | solution.py:362
  (97 shorter events, 25.8 us)
Async XLA Ops:
  2.4 8.8 %collective-permute-start = (bf16[8,16,128]{2,1,0:T(8,128)(2,1)S(1)}, bf16[8,16,128]{2,1,0:T(8,128)(2,1)S(1)}, u32[]{:S(2)}, u32[]{:S(2)}) collective-permute-start(bf16[8,16,128]{2,1,0:T(8,128)(2,1)S(1)} %get-tuple-element.35.rest_0_), channel_id=1, source_target_pairs={{0,1},{1,0},{2,3},{3,2},{4,5},{5,4},{6,7},{7,6},{8,9},{9,8},{10,11... | collective-permute-start | bytes 98312 | tf_op jit(solution)/shard_map/ppermute | solution.py:414
  2.9 20.0 %collective-permute-start.1 = (bf16[8,16,128]{2,1,0:T(8,128)(2,1)S(1)}, bf16[8,16,128]{2,1,0:T(8,128)(2,1)S(1)}, u32[]{:S(2)}, u32[]{:S(2)}) collective-permute-start(bf16[8,16,128]{2,1,0:T(8,128)(2,1)S(1)} %get-tuple-element.35.rest_0_), channel_id=1, source_target_pairs={{0,6},{1,7},{2,4},{3,5},{4,2},{5,3},{6,0},{7,1},{8,14},{9,15},{10,... | collective-permute-start | bytes 98312 | tf_op jit(solution)/shard_map/ppermute | solution.py:414
  6.5 12.6 %collective-permute-start.4 = (f32[8,1024]{1,0:T(8,128)S(1)}, f32[8,1024]{1,0:T(8,128)S(1)}, u32[]{:S(2)}, u32[]{:S(2)}) collective-permute-start(f32[8,1024]{1,0:T(8,128)S(1)} %get-tuple-element.41), channel_id=1, source_target_pairs={{0,8},{8,16},{16,24},{1,9},{9,17},{17,25},{2,10},{10,18},{18,26},{... | collective-permute-start | bytes 98312 | tf_op jit(solution)/shard_map/ppermute | solution.py:476
  9.9 11.8 %collective-permute-start.3 = (f32[24,1024]{1,0:T(8,128)S(1)}, f32[24,1024]{1,0:T(8,128)S(1)}, u32[]{:S(2)}, u32[]{:S(2)}) collective-permute-start(f32[24,1024]{1,0:T(8,128)S(1)} %get-tuple-element.39), channel_id=1, source_target_pairs={{8,0},{16,8},{24,16},{9,1},{17,9},{25,17},{10,2},{18,10},{26,18},{... | collective-permute-start | bytes 294920 | tf_op jit(solution)/shard_map/ppermute | solution.py:475
  11.3 11.7 %collective-permute-start.2 = (bf16[2,8,16,128]{3,2,1,0:T(8,128)(2,1)S(1)}, bf16[2,8,16,128]{3,2,1,0:T(8,128)(2,1)S(1)}, u32[]{:S(2)}, u32[]{:S(2)}) collective-permute-start(bf16[2,8,16,128]{3,2,1,0:T(8,128)(2,1)S(1)} %pad_maximum_fusion.6._), channel_id=1, source_target_pairs={{0,2},{1,5},{2,0},{3,7},{4,6},{5,1},{6,4},{7,3},{8,10},{9,13},{10,... | collective-permute-start | bytes 196616 | tf_op jit(solution)/shard_map/ppermute | solution.py:414
  32.4 6.6 %collective-permute-start.8 = (bf16[8,16,128]{2,1,0:T(8,128)(2,1)S(1)}, bf16[8,16,128]{2,1,0:T(8,128)(2,1)S(1)}, u32[]{:S(2)}, u32[]{:S(2)}) collective-permute-start(bf16[8,16,128]{2,1,0:T(8,128)(2,1)S(1)} %get-tuple-element.44), channel_id=1, source_target_pairs={{0,1},{1,0},{2,3},{3,2},{4,5},{5,4},{6,7},{7,6},{8,9},{9,8},{10,11... | collective-permute-start | bytes 98312 | tf_op jit(solution)/shard_map/ppermute | solution.py:414
  32.7 9.5 %collective-permute-start.7 = (bf16[8,16,128]{2,1,0:T(8,128)(2,1)S(1)}, bf16[8,16,128]{2,1,0:T(8,128)(2,1)S(1)}, u32[]{:S(2)}, u32[]{:S(2)}) collective-permute-start(bf16[8,16,128]{2,1,0:T(8,128)(2,1)S(1)} %get-tuple-element.44), channel_id=1, source_target_pairs={{0,14},{1,15},{2,12},{3,13},{4,10},{5,11},{6,8},{7,9}} | collective-permute-start | bytes 98312 | tf_op jit(solution)/shard_map/ppermute | solution.py:414
  37.8 4.4 %collective-permute-start.6 = (bf16[24,16,128]{2,1,0:T(8,128)(2,1)S(1)}, bf16[24,16,128]{2,1,0:T(8,128)(2,1)S(1)}, u32[]{:S(2)}, u32[]{:S(2)}) collective-permute-start(bf16[24,16,128]{2,1,0:T(8,128)(2,1)S(1)} %get-tuple-element.43), channel_id=1, source_target_pairs={{0,8},{1,9},{2,10},{3,11},{4,12},{5,13},{6,14},{7,15}} | collective-permute-start | bytes 294920 | tf_op jit(solution)/shard_map/ppermute | solution.py:414
  39.1 3.9 %collective-permute-start.9 = (bf16[2,8,16,128]{3,2,1,0:T(8,128)(2,1)S(1)}, bf16[2,8,16,128]{3,2,1,0:T(8,128)(2,1)S(1)}, u32[]{:S(2)}, u32[]{:S(2)}) collective-permute-start(bf16[2,8,16,128]{3,2,1,0:T(8,128)(2,1)S(1)} %pad_maximum_fusion.7), channel_id=1, source_target_pairs={{0,10},{1,13},{2,8},{3,15},{4,14},{5,9},{6,12},{7,11}} | collective-permute-start | bytes 196616 | tf_op jit(solution)/shard_map/ppermute | solution.py:414
  45.0 1.6 %collective-permute-start.13 = (bf16[8,16,128]{2,1,0:T(8,128)(2,1)S(1)}, bf16[8,16,128]{2,1,0:T(8,128)(2,1)S(1)}, u32[]{:S(2)}, u32[]{:S(2)}) collective-permute-start(bf16[8,16,128]{2,1,0:T(8,128)(2,1)S(1)} %get-tuple-element.46), channel_id=1, source_target_pairs={{0,1},{1,0},{2,3},{3,2},{4,5},{5,4},{6,7},{7,6},{8,9},{9,8},{10,11... | collective-permute-start | bytes 98312 | tf_op jit(solution)/shard_map/ppermute | solution.py:414
  45.2 2.1 %collective-permute-start.12 = (bf16[8,16,128]{2,1,0:T(8,128)(2,1)S(1)}, bf16[8,16,128]{2,1,0:T(8,128)(2,1)S(1)}, u32[]{:S(2)}, u32[]{:S(2)}) collective-permute-start(bf16[8,16,128]{2,1,0:T(8,128)(2,1)S(1)} %get-tuple-element.46), channel_id=1, source_target_pairs={{8,22},{9,23},{10,20},{11,21},{12,18},{13,19},{14,16},{15,17}} | collective-permute-start | bytes 98312 | tf_op jit(solution)/shard_map/ppermute | solution.py:414
  47.3 1.4 %collective-permute-start.15 = (bf16[4,8,16,128]{3,2,1,0:T(8,128)(2,1)S(1)}, bf16[4,8,16,128]{3,2,1,0:T(8,128)(2,1)S(1)}, u32[]{:S(2)}, u32[]{:S(2)}) collective-permute-start(bf16[4,8,16,128]{3,2,1,0:T(8,128)(2,1)S(1)} %pad_maximum_fusion.1), channel_id=1, source_target_pairs={{0,1},{1,0},{2,3},{3,2},{4,5},{5,4},{6,7},{7,6},{8,9},{9,8},{10,11... | collective-permute-start | bytes 393224 | tf_op jit(solution)/shard_map/ppermute | solution.py:414
  49.5 1.8 %collective-permute-start.18 = (bf16[8,16,128]{2,1,0:T(8,128)(2,1)S(1)}, bf16[8,16,128]{2,1,0:T(8,128)(2,1)S(1)}, u32[]{:S(2)}, u32[]{:S(2)}) collective-permute-start(bf16[8,16,128]{2,1,0:T(8,128)(2,1)S(1)} %get-tuple-element.48), channel_id=1, source_target_pairs={{0,1},{1,0},{2,3},{3,2},{4,5},{5,4},{6,7},{7,6},{8,9},{9,8},{10,11... | collective-permute-start | bytes 98312 | tf_op jit(solution)/shard_map/ppermute | solution.py:414
  49.9 2.1 %collective-permute-start.17 = (bf16[8,16,128]{2,1,0:T(8,128)(2,1)S(1)}, bf16[8,16,128]{2,1,0:T(8,128)(2,1)S(1)}, u32[]{:S(2)}, u32[]{:S(2)}) collective-permute-start(bf16[8,16,128]{2,1,0:T(8,128)(2,1)S(1)} %get-tuple-element.48), channel_id=1, source_target_pairs={{16,30},{17,31},{18,28},{19,29},{20,26},{21,27},{22,24},{23,25}} | collective-permute-start | bytes 98312 | tf_op jit(solution)/shard_map/ppermute | solution.py:414
  55.3 5.3 %collective-permute-start.23 = (bf16[2,4,16,128]{3,2,1,0:T(8,128)(2,1)S(1)}, bf16[2,4,16,128]{3,2,1,0:T(8,128)(2,1)S(1)}, u32[]{:S(2)}, u32[]{:S(2)}) collective-permute-start(bf16[2,4,16,128]{3,2,1,0:T(8,128)(2,1)S(1)} %pad_maximum_fusion.14), channel_id=1, source_target_pairs={{0,2},{1,5},{2,0},{3,7},{4,6},{5,1},{6,4},{7,3},{8,10},{9,13},{10,... | collective-permute-start | bytes 98312 | tf_op jit(solution)/shard_map/ppermute | solution.py:414
  55.9 4.6 %collective-permute-start.21 = (bf16[4,16,128]{2,1,0:T(8,128)(2,1)S(1)}, bf16[4,16,128]{2,1,0:T(8,128)(2,1)S(1)}, u32[]{:S(2)}, u32[]{:S(2)}) collective-permute-start(bf16[4,16,128]{2,1,0:T(8,128)(2,1)S(1)} %get-tuple-element.49.rest_0_), channel_id=1, source_target_pairs={{0,6},{1,7},{2,4},{3,5},{4,2},{5,3},{6,0},{7,1},{8,14},{9,15},{10,... | collective-permute-start | bytes 49160 | tf_op jit(solution)/shard_map/ppermute | solution.py:414
  62.4 1.6 %collective-permute-start.27 = (bf16[8,16,128]{2,1,0:T(8,128)(2,1)S(1)}, bf16[8,16,128]{2,1,0:T(8,128)(2,1)S(1)}, u32[]{:S(2)}, u32[]{:S(2)}) collective-permute-start(bf16[8,16,128]{2,1,0:T(8,128)(2,1)S(1)} %get-tuple-element.52), channel_id=1, source_target_pairs={{0,1},{1,0},{2,3},{3,2},{4,5},{5,4},{6,7},{7,6},{8,9},{9,8},{10,11... | collective-permute-start | bytes 98312 | tf_op jit(solution)/shard_map/ppermute | solution.py:414
  62.7 2.1 %collective-permute-start.26 = (bf16[8,16,128]{2,1,0:T(8,128)(2,1)S(1)}, bf16[8,16,128]{2,1,0:T(8,128)(2,1)S(1)}, u32[]{:S(2)}, u32[]{:S(2)}) collective-permute-start(bf16[8,16,128]{2,1,0:T(8,128)(2,1)S(1)} %get-tuple-element.52), channel_id=1, source_target_pairs={{24,22},{25,23},{26,20},{27,21},{28,18},{29,19},{30,16},{31,17}} | collective-permute-start | bytes 98312 | tf_op jit(solution)/shard_map/ppermute | solution.py:414
  66.7 1.8 %collective-permute-start.32 = (bf16[8,16,128]{2,1,0:T(8,128)(2,1)S(1)}, bf16[8,16,128]{2,1,0:T(8,128)(2,1)S(1)}, u32[]{:S(2)}, u32[]{:S(2)}) collective-permute-start(bf16[8,16,128]{2,1,0:T(8,128)(2,1)S(1)} %get-tuple-element.56), channel_id=1, source_target_pairs={{0,1},{1,0},{2,3},{3,2},{4,5},{5,4},{6,7},{7,6},{8,9},{9,8},{10,11... | collective-permute-start | bytes 98312 | tf_op jit(solution)/shard_map/ppermute | solution.py:414
  67.2 2.1 %collective-permute-start.31 = (bf16[8,16,128]{2,1,0:T(8,128)(2,1)S(1)}, bf16[8,16,128]{2,1,0:T(8,128)(2,1)S(1)}, u32[]{:S(2)}, u32[]{:S(2)}) collective-permute-start(bf16[8,16,128]{2,1,0:T(8,128)(2,1)S(1)} %get-tuple-element.56), channel_id=1, source_target_pairs={{16,14},{17,15},{18,12},{19,13},{20,10},{21,11},{22,8},{23,9}} | collective-permute-start | bytes 98312 | tf_op jit(solution)/shard_map/ppermute | solution.py:414
  71.5 2.8 %collective-permute-start.37 = (bf16[8,16,128]{2,1,0:T(8,128)(2,1)S(1)}, bf16[8,16,128]{2,1,0:T(8,128)(2,1)S(1)}, u32[]{:S(2)}, u32[]{:S(2)}) collective-permute-start(bf16[8,16,128]{2,1,0:T(8,128)(2,1)S(1)} %get-tuple-element.60), channel_id=1, source_target_pairs={{0,1},{1,0},{2,3},{3,2},{4,5},{5,4},{6,7},{7,6},{8,9},{9,8},{10,11... | collective-permute-start | bytes 98312 | tf_op jit(solution)/shard_map/ppermute | solution.py:414
  71.7 59.7 %collective-permute-start.36 = (bf16[8,16,128]{2,1,0:T(8,128)(2,1)S(1)}, bf16[8,16,128]{2,1,0:T(8,128)(2,1)S(1)}, u32[]{:S(2)}, u32[]{:S(2)}) collective-permute-start(bf16[8,16,128]{2,1,0:T(8,128)(2,1)S(1)} %get-tuple-element.60), channel_id=1, source_target_pairs={{8,6},{9,7},{10,4},{11,5},{12,2},{13,3},{14,0},{15,1}} | collective-permute-start | bytes 98312 | tf_op jit(solution)/shard_map/ppermute | solution.py:414
  73.0 58.4 %collective-permute-start.35 = (bf16[24,16,128]{2,1,0:T(8,128)(2,1)S(1)}, bf16[24,16,128]{2,1,0:T(8,128)(2,1)S(1)}, u32[]{:S(2)}, u32[]{:S(2)}) collective-permute-start(bf16[24,16,128]{2,1,0:T(8,128)(2,1)S(1)} %get-tuple-element.59), channel_id=1, source_target_pairs={{8,0},{9,1},{10,2},{11,3},{12,4},{13,5},{14,6},{15,7}} | collective-permute-start | bytes 294920 | tf_op jit(solution)/shard_map/ppermute | solution.py:414
  74.3 58.3 %collective-permute-start.38 = (bf16[2,8,16,128]{3,2,1,0:T(8,128)(2,1)S(1)}, bf16[2,8,16,128]{3,2,1,0:T(8,128)(2,1)S(1)}, u32[]{:S(2)}, u32[]{:S(2)}) collective-permute-start(bf16[2,8,16,128]{3,2,1,0:T(8,128)(2,1)S(1)} %pad_maximum_fusion.13), channel_id=1, source_target_pairs={{8,2},{9,5},{10,0},{11,7},{12,6},{13,1},{14,4},{15,3}} | collective-permute-start | bytes 196616 | tf_op jit(solution)/shard_map/ppermute | solution.py:414
  (19 other events, 42.7 us)

commit v8 on v7

--- a/solution.py
+++ b/solution.py
@@ -157,7 +157,7 @@
 
 
 def first_kernel(
-    width, layers_in, rhs_in, isc_in, fwd_in, bwd_in, picked_in, local, ahead, back, place, front,
+    width, layers_in, rhs_in, isc_in, fwd_in, bwd_in, picked_in, local, ahead, place, front,
     layers, rhs, isc, fwd, bwd, picked, sems,
 ):
     pairs = (
@@ -197,21 +197,29 @@
         FOLD: gather_lanes(times(isc_b, bwd_b), at_a) + zero,
         CELL: split(at_a.astype(F32)) + split(at_b.astype(F32)),
     }
-    back[...] = jnp.zeros(back.shape, F32)
+    ahead[count:, :] = jnp.zeros((NEEDS, ahead.shape[1]), F32)
     for at, chunks in rows.items():
         for i, chunk in enumerate(chunks):
-            back[at:at + 1, i * LANES:(i + 1) * LANES] = chunk[0:1]
+            ahead[count + at:count + at + 1, i * LANES:(i + 1) * LANES] = chunk[0:1]
     write_field(ahead.at[0:count], base_a + base_b)
-    ahead[count:, :] = back[...]
     for layer in range(2):
         place[layer:layer + 1, :] = places(picked[layer:layer + 1, :], cells)
 
 
-def load_kernel(inverse, _, loaded, done, sem):
+def load_kernel(inverse, loaded, done, sem):
     load = pltpu.make_async_copy(inverse.at[0], loaded, sem.at[0])
     load.start()
     done[...] = jnp.zeros(done.shape, F32)
     load.wait()
+
+
+def join_kernel(*refs):
+    *blocks, _, _, joined = refs
+    at = 0
+    for block in blocks:
+        for piece in [block] if len(block.shape) == 3 else [block.at[i] for i in range(block.shape[0])]:
+            joined[at] = piece[...]
+            at += 1
 
 
 def forward_kernel(
@@ -227,7 +235,9 @@
     kept, front, *rest = rest
     if not final:
         outgoing_packet, *rest = rest
-    if not step:
+    if step == 0:
+        stacked, solved, sems, second_inverse = rest
+    elif step == 1:
         second_inverse, stacked, solved, sems = rest
     else:
         second_inverse, (stacked, solved) = inverse, rest
@@ -238,10 +248,11 @@
     small = packet.at[2 * rows:]
     mine = own == step
     both = layers[step] == 2
-    load = None
-    if not step:
-        load = pltpu.make_async_copy(inverse.at[1], second_inverse, sems.at[0])
-        load.start()
+    loads = [mine, step == 1][step] if step < 2 else False
+    load = pltpu.make_async_copy(inverse.at[1], second_inverse, sems.at[0]) if step < 2 else None
+
+    if step < 2:
+        pl.when(loads)(load.start)
 
     def whole_solve(layer, matrices):
         stack_fronts(blocks, owners, planes, per_layer, stacked, layer)
@@ -251,8 +262,8 @@
     def _():
         whole_solve(0, first_inverse)
 
-    if load is not None:
-        load.wait()
+    if step < 2:
+        pl.when(loads)(load.wait)
 
     @pl.when(mine & both)
     def _():
@@ -342,7 +353,7 @@
         first = minus(first_fwd, change)
         if step:
             chunks = backward_front(
-                behind, first, read_field(held, count), layers[step - 1] == 2
+                behind.at[kept.shape[1]:], first, read_field(held, count), layers[step - 1] == 2
             )
             write_front(front, chunks)
             write_front(outgoing_packet, chunks, first)
@@ -354,7 +365,7 @@
     return pl.BlockSpec(memory_space=space)
 
 
-def call(kernel, operands, outs, scratch, name, in_place=()):
+def call(kernel, operands, outs, scratch, name, in_place=(), more_vmem=0):
     outs = [jax.ShapeDtypeStruct(*o) if isinstance(o, tuple) else o for o in outs]
     specs = [whole(pltpu.SMEM if o.ndim == 1 else pltpu.VMEM) for o in operands]
     for at in in_place:
@@ -365,7 +376,7 @@
         out_specs=[whole(pltpu.SMEM if len(o.shape) == 1 else pltpu.VMEM) for o in outs],
         out_shape=outs,
         scratch_shapes=scratch,
-        compiler_params=pltpu.CompilerParams(vmem_limit_bytes=8 * 2**20),
+        compiler_params=pltpu.CompilerParams(vmem_limit_bytes=8 * 2**20 + more_vmem),
         name=name,
     )(*operands)
 
@@ -405,11 +416,10 @@
         pltpu.VMEM((2, rows, width), F32),
     ]
 
-    def send(block, pair, *flips):
-        pairs = [pair] if pair else [(i, i) for i in range(sections)]
+    def send(block, shift, *flips):
         route = [
-            (i * planes + own, j * planes + (own ^ flips[own % CORES % len(flips)]))
-            for i, j in pairs for own in range(planes)
+            (i * planes + own, (i + shift) % sections * planes + (own ^ flips[own % len(flips)]))
+            for i in range(sections) for own in range(planes)
         ]
         return lax.ppermute(block, ("sweep", "plane"), route)
 
@@ -425,45 +435,44 @@
             return [gathered], [[0]], order // LANES
         return [gathered], [list(range(planes))], per_layer
 
-    def spread(front, straight, pair, beside=None):
-        blocks, owners, tokens = [straight], [[(0, 0)]], []
+    def spread(front, straight, shift, join=None):
+        blocks, owners = [straight], [[(0, 0)]]
         for step in [1] if chips == 2 else range(3, chips):
-            blocks.append(send(front, pair, CORES * step))
+            blocks.append(send(front, shift, CORES * step))
             owners.append([(CORES * step, CORES * step)])
         if chips == 4:
-            both = jnp.stack([front, send(front, None, 1)])
-            tokens = beside(both) if beside else []
-            blocks.append(send(both, pair, CORES, 2 * CORES))
+            both = jnp.stack([front, send(front, 0, 1)])
+            blocks.append(send(both, shift, CORES, 2 * CORES))
             owners += [[(CORES + core, 2 * CORES + core) for core in range(CORES)]]
-        short = [b[:2 * per_layer] if b.ndim == 3 else b for b in blocks]
-        mine = jnp.concatenate([b[None] if b.ndim == 3 else b for b in short])
-        for token in tokens:
-            mine = mine + jnp.minimum(jnp.abs(token), 0).astype(BF16)
-        blocks.append(send(mine, None, 1))
+        if join:
+            mine = join(blocks)
+        else:
+            short = [b[:2 * per_layer] if b.ndim == 3 else b for b in blocks]
+            mine = jnp.concatenate([b[None] if b.ndim == 3 else b for b in short])
+        blocks.append(send(mine, 0, 1))
         owners.append([(one ^ 1, zero ^ 1) for places in owners for zero, one in places])
         return blocks, owners, per_layer
 
-    def within(front, beside=None):
-        return spread(front, front, None, beside) if direct else everywhere(front)
+    def within(front, join=None):
+        return spread(front, front, 0, join) if direct else everywhere(front)
 
     def between(front, packet, start, stop):
         if not direct:
             packet = lax.ppermute(packet, "sweep", [(start, stop)])
             return *everywhere(packet[:2 * per_layer]), packet
-        packet = send(packet, (start, stop), 0)
-        return *spread(front, packet, (start, stop)), packet
+        packet = send(packet, stop - start, 0)
+        return *spread(front, packet, stop - start), packet
 
     inverse = in_hbm(front_inverse)
     half_inverse = pltpu.VMEM(front_inverse.shape[1:], BF16)
     coefficients = (interior_scale, forward_coupling, backward_coupling)
     operands = [section_layers, rhs, *coefficients, picked]
-    local, ahead, back, place, front, layers = call(
+    local, ahead, place, front, layers = call(
         functools.partial(first_kernel, width),
         [in_hbm(a) for a in operands],
         [
             ((2 * rows + 8, cells), F32),
             ((rows + NEEDS, 2 * width), F32),
-            ((NEEDS, 2 * width), F32),
             ((2, cells), jnp.int32),
             front_shape,
             (section_layers.shape, jnp.int32),
@@ -473,31 +482,20 @@
         range(6),
     )
     after = lax.ppermute(ahead, "sweep", [(i + 1, i) for i in range(sections - 1)])
-    behind = lax.ppermute(back, "sweep", [(i, i + 1) for i in range(sections - 1)])
-
-    def load(token):
-        return call(
-            load_kernel,
-            [inverse, token],
-            [half_inverse, ((8, LANES), F32)],
-            [pltpu.SemaphoreType.DMA((1,))],
-            "load_first",
-            [0],
-        )
-
-    if chips == 4 and direct:
-        loaded = []
-
-        def beside(both):
-            loaded.extend(load(both))
-            token = loaded[1][0, 0]
-            return [after[0, 0], token, jnp.min(jnp.abs(behind - token))]
-
-        gathered, owners, slots = within(front, beside)
-        first_inverse = loaded[0]
-    else:
-        gathered, owners, slots = within(front)
-        first_inverse = load(front)[0]
+    first_inverse, token = call(
+        load_kernel,
+        [inverse],
+        [half_inverse, ((8, LANES), F32)],
+        [pltpu.SemaphoreType.DMA((1,))],
+        "load_first",
+        [0],
+    )
+
+    def join(blocks):
+        shape = (sum(b.shape[0] if b.ndim == 4 else 1 for b in blocks), *front_shape[0])
+        return call(join_kernel, [*blocks, after, token], [(shape, BF16)], [], "join")[0]
+
+    gathered, owners, slots = within(front, join)
 
     kept, held = [], [None]
     for step in range(sections):
@@ -505,21 +503,24 @@
         extra = ([held[step]] if step else []) + ([] if final else [after])
         outs = [layers_shape, half_shape if final else front_shape]
         outs += [] if final else [packet_shape]
-        outs += [] if step else [half_inverse]
+        outs += [half_inverse] if step == 1 else []
+        room = [pltpu.SemaphoreType.DMA((1,))] if step < 2 else []
         outs = call(
             functools.partial(
                 forward_kernel, step, sections, planes, width, slots, owners
             ),
             [layers, first_inverse, inverse, local, place, *gathered, *extra],
             outs,
-            scratch + ([] if step else [pltpu.SemaphoreType.DMA((1,))]),
+            scratch + room + ([] if step else [half_inverse]),
             f"forward_section_{step}",
-            [] if step else [2],
+            [2] if step < 2 else [],
+            0 if step else front_inverse.size,
         )
-        if not step:
+        if step == 1:
             inverse = outs[-1]
         kept.append(outs[0])
         if final:
+            behind = lax.ppermute(ahead, "sweep", [(i, i + 1) for i in range(sections - 1)])
             gathered, owners, slots = within(outs[1])
         else:
             gathered, owners, slots, incoming = between(outs[1], outs[2], step, step + 1)

time: 138 us -> 123 us (0.89)
  waiting for transfers between devices: 72.2 us -> 50.2 us
  Pallas kernels: 18 us -> 27.9 us
  starting transfers between devices: 35.7 us -> 45.4 us
  local copies, waits for them, and re-layouts: 7.71 us -> 0.02 us
  between operations: 2.64 us -> 0.29 us
    ppermute x38, waiting for transfers between devices: 72.2 us -> 49.6 us  [send(): return lax.ppermute(block, ('sweep', 'plane'), route)]
    ppermute x38, starting transfers between devices: 31 us -> 42.2 us  [send(): return lax.ppermute(block, ('sweep', 'plane'), route)]
    pallas_call x10 -> x11, Pallas kernels: 18 us -> 27.9 us  [call(): pl.pallas_call(kernel, in_specs=specs, out_specs=[whole(pltpu.SMEM if len...]
    unnamed x6 -> x0, local copies, waits for them, and re-layouts: 6.67 us -> none
    ppermute x1, starting transfers between devices: 3.47 us -> 1.97 us  [shards(): lax.ppermute(ahead, 'sweep', [(i, i + 1) for i in range(sections - 1)])]
  transfers between devices with their start and end apart: 40 -> 40, of which waited for: 14 -> 24; matrix products, arithmetic and copies ran while one was open for 2% -> 0% of each run, Pallas kernels for 2% -> 3%
where the time goes in v8:
time: 123 us; the launch traced here: 124 us
  waiting for transfers between devices  50.2 us (41%)
  starting transfers between devices  45.4 us (37%)
  Pallas kernels  27.9 us (23%)
    ppermute x38, waiting for transfers between devices, send(): return lax.ppermute(block, ('sweep', 'plane'), route)  49.6 us
    ppermute x38, starting transfers between devices, send(): return lax.ppermute(block, ('sweep', 'plane'), route)  42.2 us
    pallas_call x11, Pallas kernels, call(): pl.pallas_call(kernel, in_specs=specs, out_specs=[whole(pltpu.SMEM if len...  27.9 us
  transfers between devices with their start and end apart: 40, of which 24 were waited for; matrix products, arithmetic and copies ran while one was open for 0% of the time, Pallas kernels for 3%

profile of v8, /device:TPU:0, one launch (start us, length us, event | category | flops | bytes accessed | tf_op | source)
XLA Modules:
  0.0 124.0 jit_solution(4379765536766624919)
XLA Ops:
  0.0 2.4 %first_fronts.1 = (f32[40,1024]{1,0:T(8,128)S(1)}, f32[24,1024]{1,0:T(8,128)S(1)}, s32[2,1024]{1,0:T(2,128)S(1)}, bf16[8,16,128]{2,1,0:T(8,128)(2,1)S(1)}, s32[4]{0:T(128)S(1)}) custom-call(s32[4]{0:T(128)} %layers_in.1, f32[2,16,1024]{2,1,0:T(8,128)} %bitcast.53, f32[2,1024]{1,0:T(2,128)} %isc_in.1, f32[2,1024]{1,0:T(2,128)} %fwd_in.1, f32[2,1024]{1,0:T(2,128)} %bwd_in.1, ...), custom_call_target="tpu_custom_call" | custom-call | tf_op jit(solution)/shard_map/first_fronts/pallas_call | solution.py:373
  4.2 2.6 %collective-permute-start.2 = (bf16[2,8,16,128]{3,2,1,0:T(8,128)(2,1)S(1)}, bf16[2,8,16,128]{3,2,1,0:T(8,128)(2,1)S(1)}, u32[]{:S(2)}, u32[]{:S(2)}) collective-permute-start(bf16[2,8,16,128]{3,2,1,0:T(8,128)(2,1)S(1)} %pad_maximum_fusion.6), channel_id=1, source_target_pairs={{0,2},{1,5},{2,0},{3,7},{4,6},{5,1},{6,4},{7,3},{8,10},{9,13},{10,... | collective-permute-start | bytes 196616 | tf_op jit(solution)/shard_map/ppermute | solution.py:424
  6.8 1.5 %collective-permute-start = (bf16[8,16,128]{2,1,0:T(8,128)(2,1)S(1)}, bf16[8,16,128]{2,1,0:T(8,128)(2,1)S(1)}, u32[]{:S(2)}, u32[]{:S(2)}) collective-permute-start(bf16[8,16,128]{2,1,0:T(8,128)(2,1)S(1)} %get-tuple-element.37.refs_0_.rest_0_), channel_id=1, source_target_pairs={{0,6},{1,7},{2,4},{3,5},{4,2},{5,3},{6,0},{7,1},{8,14},{9,15},{10,... | collective-permute-start | bytes 98312 | tf_op jit(solution)/shard_map/ppermute | solution.py:424
  8.3 3.4 %load_first.1 = (bf16[2,512,4096]{2,1,0:T(8,128)(2,1)S(1)}, f32[8,128]{1,0:T(8,128)S(1)}) custom-call(bf16[2,2,512,4096]{3,2,1,0:T(8,128)(2,1)} %inverse.5), custom_call_target="tpu_custom_call" | custom-call | tf_op jit(solution)/shard_map/load_first/pallas_call | solution.py:373
  13.2 9.0 %forward_section_0.1 = (f32[2,16,1024]{2,1,0:T(8,128)S(1)}, bf16[8,16,128]{2,1,0:T(8,128)(2,1)S(1)}, bf16[24,16,128]{2,1,0:T(8,128)(2,1)S(1)}) custom-call(s32[4]{0:T(128)S(1)} %get-tuple-element.33.layers, bf16[2,512,4096]{2,1,0:T(8,128)(2,1)S(1)} %get-tuple-element.34.first_inverse, bf16[2,2,512,4096]{3,2,1,0:T(8,128)(2,1)} %inverse.5, ...), custom_call_target="tpu_custom_call" | custom-call | tf_op jit(solution)/shard_map/forward_section_0/pallas_call | solution.py:373
  23.5 8.1 %collective-permute-done.5.rest_0_.rest_4_.rest_8_ = bf16[24,16,128]{2,1,0:T(8,128)(2,1)S(1)} collective-permute-done((bf16[24,16,128]{2,1,0:T(8,128)(2,1)S(1)}, bf16[24,16,128]{2,1,0:T(8,128)(2,1)S(1)}, u32[]{:S(2)}, u32[]{:S(2)}) %collective-permute-start.5) | collective-permute-done | bytes 98336 | tf_op jit(solution)/shard_map/ppermute | solution.py:424
  31.7 1.4 %collective-permute-done.8.rest_2_ = bf16[2,8,16,128]{3,2,1,0:T(8,128)(2,1)S(1)} collective-permute-done((bf16[2,8,16,128]{3,2,1,0:T(8,128)(2,1)S(1)}, bf16[2,8,16,128]{3,2,1,0:T(8,128)(2,1)S(1)}, u32[]{:S(2)}, u32[]{:S(2)}) %collective-permute-start.8) | collective-permute-done | bytes 65568 | tf_op jit(solution)/shard_map/ppermute | solution.py:424
  33.2 1.3 %collective-permute-done.9.rest_3_ = bf16[4,8,16,128]{3,2,1,0:T(8,128)(2,1)S(1)} collective-permute-done((bf16[4,8,16,128]{3,2,1,0:T(8,128)(2,1)S(1)}, bf16[4,8,16,128]{3,2,1,0:T(8,128)(2,1)S(1)}, u32[]{:S(2)}, u32[]{:S(2)}) %collective-permute-start.9) | collective-permute-done | bytes 131104 | tf_op jit(solution)/shard_map/ppermute | solution.py:424
  34.6 3.9 %forward_section_1.1 = (f32[2,16,1024]{2,1,0:T(8,128)S(1)}, bf16[8,16,128]{2,1,0:T(8,128)(2,1)S(1)}, bf16[24,16,128]{2,1,0:T(8,128)(2,1)S(1)}, bf16[2,512,4096]{2,1,0:T(8,128)(2,1)S(1)}) custom-call(s32[4]{0:T(128)S(1)} %get-tuple-element.33.layers, bf16[2,512,4096]{2,1,0:T(8,128)(2,1)S(1)} %get-tuple-element.34.first_inverse, ...), custom_call_target="tpu_custom_call" | custom-call | tf_op jit(solution)/shard_map/forward_section_1/pallas_call | solution.py:373
  40.0 1.9 %collective-permute-start.13 = (bf16[2,8,16,128]{3,2,1,0:T(8,128)(2,1)S(1)}, bf16[2,8,16,128]{3,2,1,0:T(8,128)(2,1)S(1)}, u32[]{:S(2)}, u32[]{:S(2)}) collective-permute-start(bf16[2,8,16,128]{3,2,1,0:T(8,128)(2,1)S(1)} %pad_maximum_fusion.8), channel_id=1, source_target_pairs={{0,10},{1,13},{2,8},{3,15},{4,14},{5,9},{6,12},{7,11},{8,18},{9,21... | collective-permute-start | bytes 196616 | tf_op jit(solution)/shard_map/ppermute | solution.py:424
  41.9 5.9 %collective-permute-done.10.rest_0_.rest_4_.rest_8_ = bf16[24,16,128]{2,1,0:T(8,128)(2,1)S(1)} collective-permute-done((bf16[24,16,128]{2,1,0:T(8,128)(2,1)S(1)}, bf16[24,16,128]{2,1,0:T(8,128)(2,1)S(1)}, u32[]{:S(2)}, u32[]{:S(2)}) %collective-permute-start.10) | collective-permute-done | bytes 98336 | tf_op jit(solution)/shard_map/ppermute | solution.py:424
  48.7 1.3 %collective-permute-done.14.rest_3_ = bf16[4,8,16,128]{3,2,1,0:T(8,128)(2,1)S(1)} collective-permute-done((bf16[4,8,16,128]{3,2,1,0:T(8,128)(2,1)S(1)}, bf16[4,8,16,128]{3,2,1,0:T(8,128)(2,1)S(1)}, u32[]{:S(2)}, u32[]{:S(2)}) %collective-permute-start.14) | collective-permute-done | bytes 131104 | tf_op jit(solution)/shard_map/ppermute | solution.py:424
  51.0 4.9 %collective-permute-start.15 = (bf16[24,16,128]{2,1,0:T(8,128)(2,1)S(1)}, bf16[24,16,128]{2,1,0:T(8,128)(2,1)S(1)}, u32[]{:S(2)}, u32[]{:S(2)}) collective-permute-start(bf16[24,16,128]{2,1,0:T(8,128)(2,1)S(1)} %get-tuple-element.45), channel_id=1, source_target_pairs={{0,8},{1,9},{2,10},{3,11},{4,12},{5,13},{6,14},{7,15},{8,16},{9,17... | collective-permute-start | bytes 294920 | tf_op jit(solution)/shard_map/ppermute | solution.py:424
  56.3 3.5 %collective-permute-done.15.rest_0_.rest_4_.rest_6_ = bf16[24,16,128]{2,1,0:T(8,128)(2,1)S(1)} collective-permute-done((bf16[24,16,128]{2,1,0:T(8,128)(2,1)S(1)}, bf16[24,16,128]{2,1,0:T(8,128)(2,1)S(1)}, u32[]{:S(2)}, u32[]{:S(2)}) %collective-permute-start.15) | collective-permute-done | bytes 98336 | tf_op jit(solution)/shard_map/ppermute | solution.py:424
  59.7 3.2 %collective-permute-done.18.rest_2_ = bf16[2,8,16,128]{3,2,1,0:T(8,128)(2,1)S(1)} collective-permute-done((bf16[2,8,16,128]{3,2,1,0:T(8,128)(2,1)S(1)}, bf16[2,8,16,128]{3,2,1,0:T(8,128)(2,1)S(1)}, u32[]{:S(2)}, u32[]{:S(2)}) %collective-permute-start.18) | collective-permute-done | bytes 65568 | tf_op jit(solution)/shard_map/ppermute | solution.py:424
  68.3 2.0 %collective-permute-start.24 = (f32[24,1024]{1,0:T(8,128)S(1)}, f32[24,1024]{1,0:T(8,128)S(1)}, u32[]{:S(2)}, u32[]{:S(2)}) collective-permute-start(f32[24,1024]{1,0:T(8,128)S(1)} %get-tuple-element.38), channel_id=1, source_target_pairs={{0,8},{8,16},{16,24},{1,9},{9,17},{17,25},{2,10},{10,18},{18,26},{... | collective-permute-start | bytes 294920 | tf_op jit(solution)/shard_map/ppermute | solution.py:523
  70.3 1.5 %collective-permute-done.20.rest_1_ = bf16[4,16,128]{2,1,0:T(8,128)(2,1)S(1)} collective-permute-done((bf16[4,16,128]{2,1,0:T(8,128)(2,1)S(1)}, bf16[4,16,128]{2,1,0:T(8,128)(2,1)S(1)}, u32[]{:S(2)}, u32[]{:S(2)}) %collective-permute-start.20) | collective-permute-done | bytes 16416 | tf_op jit(solution)/shard_map/ppermute | solution.py:424
  73.8 10.6 %collective-permute-start.26 = (bf16[8,16,128]{2,1,0:T(8,128)(2,1)S(1)}, bf16[8,16,128]{2,1,0:T(8,128)(2,1)S(1)}, u32[]{:S(2)}, u32[]{:S(2)}) collective-permute-start(bf16[8,16,128]{2,1,0:T(8,128)(2,1)S(1)} %get-tuple-element.50), channel_id=1, source_target_pairs={{0,30},{1,31},{2,28},{3,29},{4,26},{5,27},{6,24},{7,25},{8,6},{9,7... | collective-permute-start | bytes 98312 | tf_op jit(solution)/shard_map/ppermute | solution.py:424
  85.4 4.6 %collective-permute-done.25.rest_0_.rest_5_ = bf16[24,16,128]{2,1,0:T(8,128)(2,1)S(1)} collective-permute-done((bf16[24,16,128]{2,1,0:T(8,128)(2,1)S(1)}, bf16[24,16,128]{2,1,0:T(8,128)(2,1)S(1)}, u32[]{:S(2)}, u32[]{:S(2)}) %collective-permute-start.25) | collective-permute-done | bytes 98336 | tf_op jit(solution)/shard_map/ppermute | solution.py:424
  93.5 3.8 %collective-permute-start.31 = (bf16[8,16,128]{2,1,0:T(8,128)(2,1)S(1)}, bf16[8,16,128]{2,1,0:T(8,128)(2,1)S(1)}, u32[]{:S(2)}, u32[]{:S(2)}) collective-permute-start(bf16[8,16,128]{2,1,0:T(8,128)(2,1)S(1)} %get-tuple-element.54), channel_id=1, source_target_pairs={{0,30},{1,31},{2,28},{3,29},{4,26},{5,27},{6,24},{7,25},{8,6},{9,7... | collective-permute-start | bytes 98312 | tf_op jit(solution)/shard_map/ppermute | solution.py:424
  98.7 4.0 %collective-permute-done.30.rest_0_.rest_5_ = bf16[24,16,128]{2,1,0:T(8,128)(2,1)S(1)} collective-permute-done((bf16[24,16,128]{2,1,0:T(8,128)(2,1)S(1)}, bf16[24,16,128]{2,1,0:T(8,128)(2,1)S(1)}, u32[]{:S(2)}, u32[]{:S(2)}) %collective-permute-start.30) | collective-permute-done | bytes 98336 | tf_op jit(solution)/shard_map/ppermute | solution.py:424
  105.6 4.0 %collective-permute-start.36 = (bf16[8,16,128]{2,1,0:T(8,128)(2,1)S(1)}, bf16[8,16,128]{2,1,0:T(8,128)(2,1)S(1)}, u32[]{:S(2)}, u32[]{:S(2)}) collective-permute-start(bf16[8,16,128]{2,1,0:T(8,128)(2,1)S(1)} %get-tuple-element.58), channel_id=1, source_target_pairs={{0,30},{1,31},{2,28},{3,29},{4,26},{5,27},{6,24},{7,25},{8,6},{9,7... | collective-permute-start | bytes 98312 | tf_op jit(solution)/shard_map/ppermute | solution.py:424
  109.7 4.3 %collective-permute-start.38 = (bf16[2,8,16,128]{3,2,1,0:T(8,128)(2,1)S(1)}, bf16[2,8,16,128]{3,2,1,0:T(8,128)(2,1)S(1)}, u32[]{:S(2)}, u32[]{:S(2)}) collective-permute-start(bf16[2,8,16,128]{3,2,1,0:T(8,128)(2,1)S(1)} %pad_maximum_fusion.13), channel_id=1, source_target_pairs={{0,26},{1,29},{2,24},{3,31},{4,30},{5,25},{6,28},{7,27},{8,2},{9,5... | collective-permute-start | bytes 196616 | tf_op jit(solution)/shard_map/ppermute | solution.py:424
  117.9 6.2 %backward_section_0.1 = f32[2,16,1024]{2,1,0:T(8,128)} custom-call(s32[4]{0:T(128)S(1)} %get-tuple-element.33.layers, bf16[2,512,4096]{2,1,0:T(8,128)(2,1)S(1)} %get-tuple-element.34.first_inverse, bf16[2,512,4096]{2,1,0:T(8,128)(2,1)S(1)} %get-tuple-element.42.inverse.second_inverse, f32[40,1024]{1,0:T(8,128)S(1)} %get-tuple-element.35.packet, ...), custom_call_target="tpu_custom_call" | custom-call | tf_op jit(solution)/shard_map/backward_section_0/pallas_call | solution.py:373
  (88 shorter events, 28.5 us)
Async XLA Ops:
  2.9 8.8 %collective-permute-start.3 = (f32[24,1024]{1,0:T(8,128)S(1)}, f32[24,1024]{1,0:T(8,128)S(1)}, u32[]{:S(2)}, u32[]{:S(2)}) collective-permute-start(f32[24,1024]{1,0:T(8,128)S(1)} %get-tuple-element.38), channel_id=1, source_target_pairs={{8,0},{16,8},{24,16},{9,1},{17,9},{25,17},{10,2},{18,10},{26,18},{... | collective-permute-start | bytes 294920 | tf_op jit(solution)/shard_map/ppermute | solution.py:484
  4.2 7.5 %collective-permute-start.2 = (bf16[2,8,16,128]{3,2,1,0:T(8,128)(2,1)S(1)}, bf16[2,8,16,128]{3,2,1,0:T(8,128)(2,1)S(1)}, u32[]{:S(2)}, u32[]{:S(2)}) collective-permute-start(bf16[2,8,16,128]{3,2,1,0:T(8,128)(2,1)S(1)} %pad_maximum_fusion.6), channel_id=1, source_target_pairs={{0,2},{1,5},{2,0},{3,7},{4,6},{5,1},{6,4},{7,3},{8,10},{9,13},{10,... | collective-permute-start | bytes 196616 | tf_op jit(solution)/shard_map/ppermute | solution.py:424
  6.8 4.9 %collective-permute-start = (bf16[8,16,128]{2,1,0:T(8,128)(2,1)S(1)}, bf16[8,16,128]{2,1,0:T(8,128)(2,1)S(1)}, u32[]{:S(2)}, u32[]{:S(2)}) collective-permute-start(bf16[8,16,128]{2,1,0:T(8,128)(2,1)S(1)} %get-tuple-element.37.refs_0_.rest_0_), channel_id=1, source_target_pairs={{0,6},{1,7},{2,4},{3,5},{4,2},{5,3},{6,0},{7,1},{8,14},{9,15},{10,... | collective-permute-start | bytes 98312 | tf_op jit(solution)/shard_map/ppermute | solution.py:424
  22.4 9.3 %collective-permute-start.6 = (bf16[8,16,128]{2,1,0:T(8,128)(2,1)S(1)}, bf16[8,16,128]{2,1,0:T(8,128)(2,1)S(1)}, u32[]{:S(2)}, u32[]{:S(2)}) collective-permute-start(bf16[8,16,128]{2,1,0:T(8,128)(2,1)S(1)} %get-tuple-element.41), channel_id=1, source_target_pairs={{0,14},{1,15},{2,12},{3,13},{4,10},{5,11},{6,8},{7,9},{8,22},{9,23... | collective-permute-start | bytes 98312 | tf_op jit(solution)/shard_map/ppermute | solution.py:424
  22.4 9.3 %collective-permute-start.5 = (bf16[24,16,128]{2,1,0:T(8,128)(2,1)S(1)}, bf16[24,16,128]{2,1,0:T(8,128)(2,1)S(1)}, u32[]{:S(2)}, u32[]{:S(2)}) collective-permute-start(bf16[24,16,128]{2,1,0:T(8,128)(2,1)S(1)} %get-tuple-element.40), channel_id=1, source_target_pairs={{0,8},{1,9},{2,10},{3,11},{4,12},{5,13},{6,14},{7,15},{8,16},{9,17... | collective-permute-start | bytes 294920 | tf_op jit(solution)/shard_map/ppermute | solution.py:424
  23.5 9.7 %collective-permute-start.8 = (bf16[2,8,16,128]{3,2,1,0:T(8,128)(2,1)S(1)}, bf16[2,8,16,128]{3,2,1,0:T(8,128)(2,1)S(1)}, u32[]{:S(2)}, u32[]{:S(2)}) collective-permute-start(bf16[2,8,16,128]{3,2,1,0:T(8,128)(2,1)S(1)} %pad_maximum_fusion.7), channel_id=1, source_target_pairs={{0,10},{1,13},{2,8},{3,15},{4,14},{5,9},{6,12},{7,11},{8,18},{9,21... | collective-permute-start | bytes 196616 | tf_op jit(solution)/shard_map/ppermute | solution.py:424
  38.7 9.1 %collective-permute-start.11 = (bf16[8,16,128]{2,1,0:T(8,128)(2,1)S(1)}, bf16[8,16,128]{2,1,0:T(8,128)(2,1)S(1)}, u32[]{:S(2)}, u32[]{:S(2)}) collective-permute-start(bf16[8,16,128]{2,1,0:T(8,128)(2,1)S(1)} %get-tuple-element.44), channel_id=1, source_target_pairs={{0,14},{1,15},{2,12},{3,13},{4,10},{5,11},{6,8},{7,9},{8,22},{9,23... | collective-permute-start | bytes 98312 | tf_op jit(solution)/shard_map/ppermute | solution.py:424
  38.7 9.1 %collective-permute-start.10 = (bf16[24,16,128]{2,1,0:T(8,128)(2,1)S(1)}, bf16[24,16,128]{2,1,0:T(8,128)(2,1)S(1)}, u32[]{:S(2)}, u32[]{:S(2)}) collective-permute-start(bf16[24,16,128]{2,1,0:T(8,128)(2,1)S(1)} %get-tuple-element.43), channel_id=1, source_target_pairs={{0,8},{1,9},{2,10},{3,11},{4,12},{5,13},{6,14},{7,15},{8,16},{9,17... | collective-permute-start | bytes 294920 | tf_op jit(solution)/shard_map/ppermute | solution.py:424
  40.0 8.6 %collective-permute-start.13 = (bf16[2,8,16,128]{3,2,1,0:T(8,128)(2,1)S(1)}, bf16[2,8,16,128]{3,2,1,0:T(8,128)(2,1)S(1)}, u32[]{:S(2)}, u32[]{:S(2)}) collective-permute-start(bf16[2,8,16,128]{3,2,1,0:T(8,128)(2,1)S(1)} %pad_maximum_fusion.8), channel_id=1, source_target_pairs={{0,10},{1,13},{2,8},{3,15},{4,14},{5,9},{6,12},{7,11},{8,18},{9,21... | collective-permute-start | bytes 196616 | tf_op jit(solution)/shard_map/ppermute | solution.py:424
  50.8 5.1 %collective-permute-start.17 = (bf16[8,16,128]{2,1,0:T(8,128)(2,1)S(1)}, bf16[8,16,128]{2,1,0:T(8,128)(2,1)S(1)}, u32[]{:S(2)}, u32[]{:S(2)}) collective-permute-start(bf16[8,16,128]{2,1,0:T(8,128)(2,1)S(1)} %get-tuple-element.46), channel_id=1, source_target_pairs={{0,1},{1,0},{2,3},{3,2},{4,5},{5,4},{6,7},{7,6},{8,9},{9,8},{10,11... | collective-permute-start | bytes 98312 | tf_op jit(solution)/shard_map/ppermute | solution.py:424
  51.0 8.7 %collective-permute-start.16 = (bf16[8,16,128]{2,1,0:T(8,128)(2,1)S(1)}, bf16[8,16,128]{2,1,0:T(8,128)(2,1)S(1)}, u32[]{:S(2)}, u32[]{:S(2)}) collective-permute-start(bf16[8,16,128]{2,1,0:T(8,128)(2,1)S(1)} %get-tuple-element.46), channel_id=1, source_target_pairs={{0,14},{1,15},{2,12},{3,13},{4,10},{5,11},{6,8},{7,9},{8,22},{9,23... | collective-permute-start | bytes 98312 | tf_op jit(solution)/shard_map/ppermute | solution.py:424
  51.0 8.7 %collective-permute-start.15 = (bf16[24,16,128]{2,1,0:T(8,128)(2,1)S(1)}, bf16[24,16,128]{2,1,0:T(8,128)(2,1)S(1)}, u32[]{:S(2)}, u32[]{:S(2)}) collective-permute-start(bf16[24,16,128]{2,1,0:T(8,128)(2,1)S(1)} %get-tuple-element.45), channel_id=1, source_target_pairs={{0,8},{1,9},{2,10},{3,11},{4,12},{5,13},{6,14},{7,15},{8,16},{9,17... | collective-permute-start | bytes 294920 | tf_op jit(solution)/shard_map/ppermute | solution.py:424
  55.9 7.0 %collective-permute-start.18 = (bf16[2,8,16,128]{3,2,1,0:T(8,128)(2,1)S(1)}, bf16[2,8,16,128]{3,2,1,0:T(8,128)(2,1)S(1)}, u32[]{:S(2)}, u32[]{:S(2)}) collective-permute-start(bf16[2,8,16,128]{3,2,1,0:T(8,128)(2,1)S(1)} %pad_maximum_fusion.9), channel_id=1, source_target_pairs={{0,10},{1,13},{2,8},{3,15},{4,14},{5,9},{6,12},{7,11},{8,18},{9,21... | collective-permute-start | bytes 196616 | tf_op jit(solution)/shard_map/ppermute | solution.py:424
  66.2 5.5 %collective-permute-start.22 = (bf16[2,4,16,128]{3,2,1,0:T(8,128)(2,1)S(1)}, bf16[2,4,16,128]{3,2,1,0:T(8,128)(2,1)S(1)}, u32[]{:S(2)}, u32[]{:S(2)}) collective-permute-start(bf16[2,4,16,128]{3,2,1,0:T(8,128)(2,1)S(1)} %pad_maximum_fusion.14), channel_id=1, source_target_pairs={{0,2},{1,5},{2,0},{3,7},{4,6},{5,1},{6,4},{7,3},{8,10},{9,13},{10,... | collective-permute-start | bytes 98312 | tf_op jit(solution)/shard_map/ppermute | solution.py:424
  73.6 10.8 %collective-permute-start.27 = (bf16[8,16,128]{2,1,0:T(8,128)(2,1)S(1)}, bf16[8,16,128]{2,1,0:T(8,128)(2,1)S(1)}, u32[]{:S(2)}, u32[]{:S(2)}) collective-permute-start(bf16[8,16,128]{2,1,0:T(8,128)(2,1)S(1)} %get-tuple-element.50), channel_id=1, source_target_pairs={{0,1},{1,0},{2,3},{3,2},{4,5},{5,4},{6,7},{7,6},{8,9},{9,8},{10,11... | collective-permute-start | bytes 98312 | tf_op jit(solution)/shard_map/ppermute | solution.py:424
  73.8 16.2 %collective-permute-start.26 = (bf16[8,16,128]{2,1,0:T(8,128)(2,1)S(1)}, bf16[8,16,128]{2,1,0:T(8,128)(2,1)S(1)}, u32[]{:S(2)}, u32[]{:S(2)}) collective-permute-start(bf16[8,16,128]{2,1,0:T(8,128)(2,1)S(1)} %get-tuple-element.50), channel_id=1, source_target_pairs={{0,30},{1,31},{2,28},{3,29},{4,26},{5,27},{6,24},{7,25},{8,6},{9,7... | collective-permute-start | bytes 98312 | tf_op jit(solution)/shard_map/ppermute | solution.py:424
  84.4 5.6 %collective-permute-start.25 = (bf16[24,16,128]{2,1,0:T(8,128)(2,1)S(1)}, bf16[24,16,128]{2,1,0:T(8,128)(2,1)S(1)}, u32[]{:S(2)}, u32[]{:S(2)}) collective-permute-start(bf16[24,16,128]{2,1,0:T(8,128)(2,1)S(1)} %get-tuple-element.49), channel_id=1, source_target_pairs={{0,24},{1,25},{2,26},{3,27},{4,28},{5,29},{6,30},{7,31},{8,0},{9,1... | collective-permute-start | bytes 294920 | tf_op jit(solution)/shard_map/ppermute | solution.py:424
  84.4 6.9 %collective-permute-start.28 = (bf16[2,8,16,128]{3,2,1,0:T(8,128)(2,1)S(1)}, bf16[2,8,16,128]{3,2,1,0:T(8,128)(2,1)S(1)}, u32[]{:S(2)}, u32[]{:S(2)}) collective-permute-start(bf16[2,8,16,128]{3,2,1,0:T(8,128)(2,1)S(1)} %pad_maximum_fusion.11), channel_id=1, source_target_pairs={{0,26},{1,29},{2,24},{3,31},{4,30},{5,25},{6,28},{7,27},{8,2},{9,5... | collective-permute-start | bytes 196616 | tf_op jit(solution)/shard_map/ppermute | solution.py:424
  93.5 9.2 %collective-permute-start.31 = (bf16[8,16,128]{2,1,0:T(8,128)(2,1)S(1)}, bf16[8,16,128]{2,1,0:T(8,128)(2,1)S(1)}, u32[]{:S(2)}, u32[]{:S(2)}) collective-permute-start(bf16[8,16,128]{2,1,0:T(8,128)(2,1)S(1)} %get-tuple-element.54), channel_id=1, source_target_pairs={{0,30},{1,31},{2,28},{3,29},{4,26},{5,27},{6,24},{7,25},{8,6},{9,7... | collective-permute-start | bytes 98312 | tf_op jit(solution)/shard_map/ppermute | solution.py:424
  97.3 5.5 %collective-permute-start.30 = (bf16[24,16,128]{2,1,0:T(8,128)(2,1)S(1)}, bf16[24,16,128]{2,1,0:T(8,128)(2,1)S(1)}, u32[]{:S(2)}, u32[]{:S(2)}) collective-permute-start(bf16[24,16,128]{2,1,0:T(8,128)(2,1)S(1)} %get-tuple-element.53), channel_id=1, source_target_pairs={{0,24},{1,25},{2,26},{3,27},{4,28},{5,29},{6,30},{7,31},{8,0},{9,1... | collective-permute-start | bytes 294920 | tf_op jit(solution)/shard_map/ppermute | solution.py:424
  98.0 5.5 %collective-permute-start.33 = (bf16[2,8,16,128]{3,2,1,0:T(8,128)(2,1)S(1)}, bf16[2,8,16,128]{3,2,1,0:T(8,128)(2,1)S(1)}, u32[]{:S(2)}, u32[]{:S(2)}) collective-permute-start(bf16[2,8,16,128]{3,2,1,0:T(8,128)(2,1)S(1)} %pad_maximum_fusion.12), channel_id=1, source_target_pairs={{0,26},{1,29},{2,24},{3,31},{4,30},{5,25},{6,28},{7,27},{8,2},{9,5... | collective-permute-start | bytes 196616 | tf_op jit(solution)/shard_map/ppermute | solution.py:424
  105.6 9.5 %collective-permute-start.36 = (bf16[8,16,128]{2,1,0:T(8,128)(2,1)S(1)}, bf16[8,16,128]{2,1,0:T(8,128)(2,1)S(1)}, u32[]{:S(2)}, u32[]{:S(2)}) collective-permute-start(bf16[8,16,128]{2,1,0:T(8,128)(2,1)S(1)} %get-tuple-element.58), channel_id=1, source_target_pairs={{0,30},{1,31},{2,28},{3,29},{4,26},{5,27},{6,24},{7,25},{8,6},{9,7... | collective-permute-start | bytes 98312 | tf_op jit(solution)/shard_map/ppermute | solution.py:424
  109.6 5.5 %collective-permute-start.35 = (bf16[24,16,128]{2,1,0:T(8,128)(2,1)S(1)}, bf16[24,16,128]{2,1,0:T(8,128)(2,1)S(1)}, u32[]{:S(2)}, u32[]{:S(2)}) collective-permute-start(bf16[24,16,128]{2,1,0:T(8,128)(2,1)S(1)} %get-tuple-element.57), channel_id=1, source_target_pairs={{0,24},{1,25},{2,26},{3,27},{4,28},{5,29},{6,30},{7,31},{8,0},{9,1... | collective-permute-start | bytes 294920 | tf_op jit(solution)/shard_map/ppermute | solution.py:424
  109.7 6.8 %collective-permute-start.38 = (bf16[2,8,16,128]{3,2,1,0:T(8,128)(2,1)S(1)}, bf16[2,8,16,128]{3,2,1,0:T(8,128)(2,1)S(1)}, u32[]{:S(2)}, u32[]{:S(2)}) collective-permute-start(bf16[2,8,16,128]{3,2,1,0:T(8,128)(2,1)S(1)} %pad_maximum_fusion.13), channel_id=1, source_target_pairs={{0,26},{1,29},{2,24},{3,31},{4,30},{5,25},{6,28},{7,27},{8,2},{9,5... | collective-permute-start | bytes 196616 | tf_op jit(solution)/shard_map/ppermute | solution.py:424
  (16 other events, 34.7 us)

commit v9 on v8

--- a/solution.py
+++ b/solution.py
@@ -206,11 +206,17 @@
         place[layer:layer + 1, :] = places(picked[layer:layer + 1, :], cells)
 
 
-def load_kernel(inverse, loaded, done, sem):
-    load = pltpu.make_async_copy(inverse.at[0], loaded, sem.at[0])
-    load.start()
+def load_kernel(inverse, first, second, done, sems):
+    loads = [
+        pltpu.make_async_copy(inverse.at[layer], half, sems.at[layer])
+        for layer, half in enumerate((first, second))
+    ]
+    later = lax.axis_index("sweep") == 0
+    loads[0].start()
+    pl.when(~later)(loads[1].start)
     done[...] = jnp.zeros(done.shape, F32)
-    load.wait()
+    loads[0].wait()
+    pl.when(~later)(loads[1].wait)
 
 
 def join_kernel(*refs):
@@ -223,9 +229,11 @@
 
 
 def forward_kernel(
-    step, sections, planes, width, per_layer, owners, layers, first_inverse, inverse, packet,
-    place, *rest
+    step, sections, planes, width, per_layer, owners, layers, first_inverse, second_inverse,
+    packet, place, *rest
 ):
+    if not step:
+        inverse, *rest = rest
     blocks, rest = rest[:len(owners)], rest[len(owners):]
     final = step == sections - 1
     if step:
@@ -235,12 +243,10 @@
     kept, front, *rest = rest
     if not final:
         outgoing_packet, *rest = rest
-    if step == 0:
-        stacked, solved, sems, second_inverse = rest
-    elif step == 1:
+    if step:
+        stacked, solved = rest
+    else:
         second_inverse, stacked, solved, sems = rest
-    else:
-        second_inverse, (stacked, solved) = inverse, rest
     own = lax.axis_index("sweep")
     cells = packet.shape[-1]
     count = cells // LANES
@@ -248,11 +254,9 @@
     small = packet.at[2 * rows:]
     mine = own == step
     both = layers[step] == 2
-    loads = [mine, step == 1][step] if step < 2 else False
-    load = pltpu.make_async_copy(inverse.at[1], second_inverse, sems.at[0]) if step < 2 else None
-
-    if step < 2:
-        pl.when(loads)(load.start)
+    if not step:
+        load = pltpu.make_async_copy(inverse.at[1], second_inverse, sems.at[0])
+        pl.when(mine)(load.start)
 
     def whole_solve(layer, matrices):
         stack_fronts(blocks, owners, planes, per_layer, stacked, layer)
@@ -262,8 +266,8 @@
     def _():
         whole_solve(0, first_inverse)
 
-    if step < 2:
-        pl.when(loads)(load.wait)
+    if not step:
+        pl.when(mine)(load.wait)
 
     @pl.when(mine & both)
     def _():
@@ -365,7 +369,7 @@
     return pl.BlockSpec(memory_space=space)
 
 
-def call(kernel, operands, outs, scratch, name, in_place=(), more_vmem=0):
+def call(kernel, operands, outs, scratch, name, in_place=(), aliases={}):
     outs = [jax.ShapeDtypeStruct(*o) if isinstance(o, tuple) else o for o in outs]
     specs = [whole(pltpu.SMEM if o.ndim == 1 else pltpu.VMEM) for o in operands]
     for at in in_place:
@@ -376,7 +380,8 @@
         out_specs=[whole(pltpu.SMEM if len(o.shape) == 1 else pltpu.VMEM) for o in outs],
         out_shape=outs,
         scratch_shapes=scratch,
-        compiler_params=pltpu.CompilerParams(vmem_limit_bytes=8 * 2**20 + more_vmem),
+        input_output_aliases=aliases,
+        compiler_params=pltpu.CompilerParams(vmem_limit_bytes=8 * 2**20),
         name=name,
     )(*operands)
 
@@ -457,10 +462,9 @@
         return spread(front, front, 0, join) if direct else everywhere(front)
 
     def between(front, packet, start, stop):
+        packet = lax.ppermute(packet, "sweep", [(start, stop)])
         if not direct:
-            packet = lax.ppermute(packet, "sweep", [(start, stop)])
             return *everywhere(packet[:2 * per_layer]), packet
-        packet = send(packet, stop - start, 0)
         return *spread(front, packet, stop - start), packet
 
     inverse = in_hbm(front_inverse)
@@ -482,11 +486,11 @@
         range(6),
     )
     after = lax.ppermute(ahead, "sweep", [(i + 1, i) for i in range(sections - 1)])
-    first_inverse, token = call(
+    first_inverse, second_inverse, token = call(
         load_kernel,
         [inverse],
-        [half_inverse, ((8, LANES), F32)],
-        [pltpu.SemaphoreType.DMA((1,))],
+        [half_inverse, half_inverse, ((8, LANES), F32)],
+        [pltpu.SemaphoreType.DMA((2,))],
         "load_first",
         [0],
     )
@@ -503,21 +507,21 @@
         extra = ([held[step]] if step else []) + ([] if final else [after])
         outs = [layers_shape, half_shape if final else front_shape]
         outs += [] if final else [packet_shape]
-        outs += [half_inverse] if step == 1 else []
-        room = [pltpu.SemaphoreType.DMA((1,))] if step < 2 else []
+        outs += [] if step else [half_inverse]
         outs = call(
             functools.partial(
                 forward_kernel, step, sections, planes, width, slots, owners
             ),
-            [layers, first_inverse, inverse, local, place, *gathered, *extra],
+            [layers, first_inverse, second_inverse, local, place]
+            + ([] if step else [inverse]) + [*gathered, *extra],
             outs,
-            scratch + room + ([] if step else [half_inverse]),
+            scratch + ([] if step else [pltpu.SemaphoreType.DMA((1,))]),
             f"forward_section_{step}",
-            [2] if step < 2 else [],
-            0 if step else front_inverse.size,
+            [] if step else [5],
+            {} if step else {2: len(outs) - 1},
         )
-        if step == 1:
-            inverse = outs[-1]
+        if not step:
+            second_inverse = outs[-1]
         kept.append(outs[0])
         if final:
             behind = lax.ppermute(ahead, "sweep", [(i, i + 1) for i in range(sections - 1)])
@@ -533,7 +537,7 @@
             functools.partial(
                 backward_kernel, step, sections, planes, width, slots, owners
             ),
-            [layers, first_inverse, inverse, local, place, *gathered, kept[step], *extra],
+            [layers, first_inverse, second_inverse, local, place, *gathered, kept[step], *extra],
             [layers_shape] + ([front_shape, packet_shape] if step else []),
             scratch,
             f"backward_section_{step}",

time: 123 us -> 122 us (level)
  starting transfers between devices: 45.4 us -> 58.8 us
  Pallas kernels: 27.9 us -> 17.6 us
  waiting for transfers between devices: 50.2 us -> 45.5 us
    ppermute x38 -> x32, waiting for transfers between devices: 49.6 us -> 34.5 us  [send(): return lax.ppermute(block, ('sweep', 'plane'), route)]
    pallas_call x11, Pallas kernels: 27.9 us -> 17.6 us  [call(): pl.pallas_call(kernel, in_specs=specs, out_specs=[whole(pltpu.SMEM if len...]
    ppermute x0 -> x6, waiting for transfers between devices: none -> 8.99 us  [between(): packet = lax.ppermute(packet, 'sweep', [(start, stop)])]
    ppermute x0 -> x6, starting transfers between devices: none -> 7.37 us  [between(): packet = lax.ppermute(packet, 'sweep', [(start, stop)])]
    ppermute x38 -> x32, starting transfers between devices: 42.2 us -> 46.9 us  [send(): return lax.ppermute(block, ('sweep', 'plane'), route)]
    ppermute x1, waiting for transfers between devices: 0.64 us -> 2.07 us  [shards(): lax.ppermute(ahead, 'sweep', [(i, i + 1) for i in range(sections - 1)])]
    ppermute x1, starting transfers between devices: 1.97 us -> 3.22 us  [shards(): lax.ppermute(ahead, 'sweep', [(i, i + 1) for i in range(sections - 1)])]
  transfers between devices with their start and end apart: 40 -> 40, of which waited for: 24 -> 21; matrix products, arithmetic and copies ran while one was open for 0% -> 0% of each run, Pallas kernels for 3% -> 3%
where the time goes in v9:
time: 122 us; the launch traced here: 123 us
  starting transfers between devices  58.8 us (48%)
  waiting for transfers between devices  45.5 us (37%)
  Pallas kernels  17.6 us (14%)
    ppermute x32, starting transfers between devices, send(): return lax.ppermute(block, ('sweep', 'plane'), route)  46.9 us
    ppermute x32, waiting for transfers between devices, send(): return lax.ppermute(block, ('sweep', 'plane'), route)  34.5 us
    pallas_call x11, Pallas kernels, call(): pl.pallas_call(kernel, in_specs=specs, out_specs=[whole(pltpu.SMEM if len...  17.6 us
    ppermute x6, waiting for transfers between devices, between(): packet = lax.ppermute(packet, 'sweep', [(start, stop)])  8.99 us
    ppermute x6, starting transfers between devices, between(): packet = lax.ppermute(packet, 'sweep', [(start, stop)])  7.37 us
    ppermute x1, starting transfers between devices, shards(): lax.ppermute(ahead, 'sweep', [(i, i + 1) for i in range(sections - 1)])  3.22 us
  transfers between devices with their start and end apart: 40, of which 21 were waited for; matrix products, arithmetic and copies ran while one was open for 0% of the time, Pallas kernels for 3%

profile of v9, /device:TPU:0, one launch (start us, length us, event | category | flops | bytes accessed | tf_op | source)
XLA Modules:
  0.0 122.6 jit_solution(3622551775964298949)
XLA Ops:
  0.0 2.4 %first_fronts.1 = (f32[40,1024]{1,0:T(8,128)S(1)}, f32[24,1024]{1,0:T(8,128)S(1)}, s32[2,1024]{1,0:T(2,128)S(1)}, bf16[8,16,128]{2,1,0:T(8,128)(2,1)S(1)}, s32[4]{0:T(128)S(1)}) custom-call(s32[4]{0:T(128)} %layers_in.1, f32[2,16,1024]{2,1,0:T(8,128)} %bitcast.53, f32[2,1024]{1,0:T(2,128)} %isc_in.1, f32[2,1024]{1,0:T(2,128)} %fwd_in.1, f32[2,1024]{1,0:T(2,128)} %bwd_in.1, ...), custom_call_target="tpu_custom_call" | custom-call | tf_op jit(solution)/shard_map/first_fronts/pallas_call | solution.py:377
  4.2 2.6 %collective-permute-start.2 = (bf16[2,8,16,128]{3,2,1,0:T(8,128)(2,1)S(1)}, bf16[2,8,16,128]{3,2,1,0:T(8,128)(2,1)S(1)}, u32[]{:S(2)}, u32[]{:S(2)}) collective-permute-start(bf16[2,8,16,128]{3,2,1,0:T(8,128)(2,1)S(1)} %pad_maximum_fusion.6), channel_id=1, source_target_pairs={{0,2},{1,5},{2,0},{3,7},{4,6},{5,1},{6,4},{7,3},{8,10},{9,13},{10,... | collective-permute-start | bytes 196616 | tf_op jit(solution)/shard_map/ppermute | solution.py:429
  8.3 3.4 %load_first.1 = (bf16[2,512,4096]{2,1,0:T(8,128)(2,1)S(1)}, bf16[2,512,4096]{2,1,0:T(8,128)(2,1)S(1)}, f32[8,128]{1,0:T(8,128)S(1)}) custom-call(bf16[2,2,512,4096]{3,2,1,0:T(8,128)(2,1)} %rest_0_.1), custom_call_target="tpu_custom_call" | custom-call | tf_op jit(solution)/shard_map/load_first/pallas_call | solution.py:377
  13.2 4.5 %forward_section_0.1 = (f32[2,16,1024]{2,1,0:T(8,128)S(1)}, bf16[8,16,128]{2,1,0:T(8,128)(2,1)S(1)}, bf16[24,16,128]{2,1,0:T(8,128)(2,1)S(1)}, bf16[2,512,4096]{2,1,0:T(8,128)(2,1)S(1)}) custom-call(s32[4]{0:T(128)S(1)} %get-tuple-element.34.layers, bf16[2,512,4096]{2,1,0:T(8,128)(2,1)S(1)} %get-tuple-element.35.first_inverse, ...), custom_call_target="tpu_custom_call", output_to_operand_aliasing={{3}: (2, {})} | custom-call | tf_op jit(solution)/shard_map/forward_section_0/pallas_call | solution.py:377
  17.9 2.0 %collective-permute-start.6 = (bf16[8,16,128]{2,1,0:T(8,128)(2,1)S(1)}, bf16[8,16,128]{2,1,0:T(8,128)(2,1)S(1)}, u32[]{:S(2)}, u32[]{:S(2)}) collective-permute-start(bf16[8,16,128]{2,1,0:T(8,128)(2,1)S(1)} %get-tuple-element.44), channel_id=1, source_target_pairs={{0,14},{1,15},{2,12},{3,13},{4,10},{5,11},{6,8},{7,9},{8,22},{9,23... | collective-permute-start | bytes 98312 | tf_op jit(solution)/shard_map/ppermute | solution.py:429
  19.9 3.5 %collective-permute-start.5 = (bf16[24,16,128]{2,1,0:T(8,128)(2,1)S(1)}, bf16[24,16,128]{2,1,0:T(8,128)(2,1)S(1)}, u32[]{:S(2)}, u32[]{:S(2)}) collective-permute-start(bf16[24,16,128]{2,1,0:T(8,128)(2,1)S(1)} %get-tuple-element.43), channel_id=1, source_target_pairs={{0,8},{1,9},{2,10},{3,11},{4,12},{5,13},{6,14},{7,15}} | collective-permute-start | bytes 294920 | tf_op jit(solution)/shard_map/ppermute | solution.py:465
  23.5 2.9 %collective-permute-done.5.rest_0_.rest_4_.rest_8_ = bf16[24,16,128]{2,1,0:T(8,128)(2,1)S(1)} collective-permute-done((bf16[24,16,128]{2,1,0:T(8,128)(2,1)S(1)}, bf16[24,16,128]{2,1,0:T(8,128)(2,1)S(1)}, u32[]{:S(2)}, u32[]{:S(2)}) %collective-permute-start.5) | collective-permute-done | bytes 98336 | tf_op jit(solution)/shard_map/ppermute | solution.py:465
  26.3 4.1 %collective-permute-done.8.rest_2_ = bf16[2,8,16,128]{3,2,1,0:T(8,128)(2,1)S(1)} collective-permute-done((bf16[2,8,16,128]{3,2,1,0:T(8,128)(2,1)S(1)}, bf16[2,8,16,128]{3,2,1,0:T(8,128)(2,1)S(1)}, u32[]{:S(2)}, u32[]{:S(2)}) %collective-permute-start.8) | collective-permute-done | bytes 65568 | tf_op jit(solution)/shard_map/ppermute | solution.py:429
  32.6 6.2 %collective-permute-start.11 = (bf16[8,16,128]{2,1,0:T(8,128)(2,1)S(1)}, bf16[8,16,128]{2,1,0:T(8,128)(2,1)S(1)}, u32[]{:S(2)}, u32[]{:S(2)}) collective-permute-start(bf16[8,16,128]{2,1,0:T(8,128)(2,1)S(1)} %get-tuple-element.46), channel_id=1, source_target_pairs={{0,14},{1,15},{2,12},{3,13},{4,10},{5,11},{6,8},{7,9},{8,22},{9,23... | collective-permute-start | bytes 98312 | tf_op jit(solution)/shard_map/ppermute | solution.py:429
  40.5 6.1 %collective-permute-done.13.rest_2_ = bf16[2,8,16,128]{3,2,1,0:T(8,128)(2,1)S(1)} collective-permute-done((bf16[2,8,16,128]{3,2,1,0:T(8,128)(2,1)S(1)}, bf16[2,8,16,128]{3,2,1,0:T(8,128)(2,1)S(1)}, u32[]{:S(2)}, u32[]{:S(2)}) %collective-permute-start.13) | collective-permute-done | bytes 65568 | tf_op jit(solution)/shard_map/ppermute | solution.py:429
  50.0 3.7 %collective-permute-start.18 = (bf16[2,8,16,128]{3,2,1,0:T(8,128)(2,1)S(1)}, bf16[2,8,16,128]{3,2,1,0:T(8,128)(2,1)S(1)}, u32[]{:S(2)}, u32[]{:S(2)}) collective-permute-start(bf16[2,8,16,128]{3,2,1,0:T(8,128)(2,1)S(1)} %pad_maximum_fusion.9), channel_id=1, source_target_pairs={{0,10},{1,13},{2,8},{3,15},{4,14},{5,9},{6,12},{7,11},{8,18},{9,21... | collective-permute-start | bytes 196616 | tf_op jit(solution)/shard_map/ppermute | solution.py:429
  53.7 3.1 %collective-permute-done.16.rest_1_ = bf16[8,16,128]{2,1,0:T(8,128)(2,1)S(1)} collective-permute-done((bf16[8,16,128]{2,1,0:T(8,128)(2,1)S(1)}, bf16[8,16,128]{2,1,0:T(8,128)(2,1)S(1)}, u32[]{:S(2)}, u32[]{:S(2)}) %collective-permute-start.16) | collective-permute-done | bytes 32800 | tf_op jit(solution)/shard_map/ppermute | solution.py:429
  61.9 1.7 %collective-permute-start.20 = (bf16[4,16,128]{2,1,0:T(8,128)(2,1)S(1)}, bf16[4,16,128]{2,1,0:T(8,128)(2,1)S(1)}, u32[]{:S(2)}, u32[]{:S(2)}) collective-permute-start(bf16[4,16,128]{2,1,0:T(8,128)(2,1)S(1)} %get-tuple-element.49.rest_0_), channel_id=1, source_target_pairs={{0,6},{1,7},{2,4},{3,5},{4,2},{5,3},{6,0},{7,1},{8,14},{9,15},{10,... | collective-permute-start | bytes 49160 | tf_op jit(solution)/shard_map/ppermute | solution.py:429
  63.6 3.2 %collective-permute-start.24 = (f32[24,1024]{1,0:T(8,128)S(1)}, f32[24,1024]{1,0:T(8,128)S(1)}, u32[]{:S(2)}, u32[]{:S(2)}) collective-permute-start(f32[24,1024]{1,0:T(8,128)S(1)} %get-tuple-element.40), channel_id=1, source_target_pairs={{0,8},{8,16},{16,24},{1,9},{9,17},{17,25},{2,10},{10,18},{18,26},{... | collective-permute-start | bytes 294920 | tf_op jit(solution)/shard_map/ppermute | solution.py:527
  66.9 2.1 %collective-permute-done.24.rest_5_.rest_7_ = f32[24,1024]{1,0:T(8,128)S(1)} collective-permute-done((f32[24,1024]{1,0:T(8,128)S(1)}, f32[24,1024]{1,0:T(8,128)S(1)}, u32[]{:S(2)}, u32[]{:S(2)}) %collective-permute-start.24) | collective-permute-done | bytes 98336 | tf_op jit(solution)/shard_map/ppermute | solution.py:527
  69.6 14.1 %collective-permute-start.26 = (bf16[8,16,128]{2,1,0:T(8,128)(2,1)S(1)}, bf16[8,16,128]{2,1,0:T(8,128)(2,1)S(1)}, u32[]{:S(2)}, u32[]{:S(2)}) collective-permute-start(bf16[8,16,128]{2,1,0:T(8,128)(2,1)S(1)} %get-tuple-element.52), channel_id=1, source_target_pairs={{0,30},{1,31},{2,28},{3,29},{4,26},{5,27},{6,24},{7,25},{8,6},{9,7... | collective-permute-start | bytes 98312 | tf_op jit(solution)/shard_map/ppermute | solution.py:429
  85.4 4.4 %collective-permute-done.28.rest_2_ = bf16[2,8,16,128]{3,2,1,0:T(8,128)(2,1)S(1)} collective-permute-done((bf16[2,8,16,128]{3,2,1,0:T(8,128)(2,1)S(1)}, bf16[2,8,16,128]{3,2,1,0:T(8,128)(2,1)S(1)}, u32[]{:S(2)}, u32[]{:S(2)}) %collective-permute-start.28) | collective-permute-done | bytes 65568 | tf_op jit(solution)/shard_map/ppermute | solution.py:429
  92.0 2.7 %collective-permute-start.31 = (bf16[8,16,128]{2,1,0:T(8,128)(2,1)S(1)}, bf16[8,16,128]{2,1,0:T(8,128)(2,1)S(1)}, u32[]{:S(2)}, u32[]{:S(2)}) collective-permute-start(bf16[8,16,128]{2,1,0:T(8,128)(2,1)S(1)} %get-tuple-element.56), channel_id=1, source_target_pairs={{0,30},{1,31},{2,28},{3,29},{4,26},{5,27},{6,24},{7,25},{8,6},{9,7... | collective-permute-start | bytes 98312 | tf_op jit(solution)/shard_map/ppermute | solution.py:429
  95.4 3.3 %collective-permute-start.33 = (bf16[2,8,16,128]{3,2,1,0:T(8,128)(2,1)S(1)}, bf16[2,8,16,128]{3,2,1,0:T(8,128)(2,1)S(1)}, u32[]{:S(2)}, u32[]{:S(2)}) collective-permute-start(bf16[2,8,16,128]{3,2,1,0:T(8,128)(2,1)S(1)} %pad_maximum_fusion.12), channel_id=1, source_target_pairs={{0,26},{1,29},{2,24},{3,31},{4,30},{5,25},{6,28},{7,27},{8,2},{9,5... | collective-permute-start | bytes 196616 | tf_op jit(solution)/shard_map/ppermute | solution.py:429
  98.8 2.1 %collective-permute-done.33.rest_2_ = bf16[2,8,16,128]{3,2,1,0:T(8,128)(2,1)S(1)} collective-permute-done((bf16[2,8,16,128]{3,2,1,0:T(8,128)(2,1)S(1)}, bf16[2,8,16,128]{3,2,1,0:T(8,128)(2,1)S(1)}, u32[]{:S(2)}, u32[]{:S(2)}) %collective-permute-start.33) | collective-permute-done | bytes 65568 | tf_op jit(solution)/shard_map/ppermute | solution.py:429
  103.1 5.1 %collective-permute-start.36 = (bf16[8,16,128]{2,1,0:T(8,128)(2,1)S(1)}, bf16[8,16,128]{2,1,0:T(8,128)(2,1)S(1)}, u32[]{:S(2)}, u32[]{:S(2)}) collective-permute-start(bf16[8,16,128]{2,1,0:T(8,128)(2,1)S(1)} %get-tuple-element.60), channel_id=1, source_target_pairs={{0,30},{1,31},{2,28},{3,29},{4,26},{5,27},{6,24},{7,25},{8,6},{9,7... | collective-permute-start | bytes 98312 | tf_op jit(solution)/shard_map/ppermute | solution.py:429
  109.5 6.1 %collective-permute-done.35.rest_0_.rest_5_ = bf16[24,16,128]{2,1,0:T(8,128)(2,1)S(1)} collective-permute-done((bf16[24,16,128]{2,1,0:T(8,128)(2,1)S(1)}, bf16[24,16,128]{2,1,0:T(8,128)(2,1)S(1)}, u32[]{:S(2)}, u32[]{:S(2)}) %collective-permute-start.35) | collective-permute-done | bytes 98336 | tf_op jit(solution)/shard_map/ppermute | solution.py:465
  115.6 1.7 %collective-permute-done.38.rest_2_ = bf16[2,8,16,128]{3,2,1,0:T(8,128)(2,1)S(1)} collective-permute-done((bf16[2,8,16,128]{3,2,1,0:T(8,128)(2,1)S(1)}, bf16[2,8,16,128]{3,2,1,0:T(8,128)(2,1)S(1)}, u32[]{:S(2)}, u32[]{:S(2)}) %collective-permute-start.38) | collective-permute-done | bytes 65568 | tf_op jit(solution)/shard_map/ppermute | solution.py:429
  118.8 3.8 %backward_section_0.1 = f32[2,16,1024]{2,1,0:T(8,128)} custom-call(s32[4]{0:T(128)S(1)} %get-tuple-element.34.layers, bf16[2,512,4096]{2,1,0:T(8,128)(2,1)S(1)} %get-tuple-element.35.first_inverse, bf16[2,512,4096]{2,1,0:T(8,128)(2,1)S(1)} %get-tuple-element.42.second_inverse, f32[40,1024]{1,0:T(8,128)S(1)} %get-tuple-element.37.packet, ...), custom_call_target="tpu_custom_call" | custom-call | tf_op jit(solution)/shard_map/backward_section_0/pallas_call | solution.py:377
  (88 shorter events, 27.4 us)
Async XLA Ops:
  2.9 8.8 %collective-permute-start.3 = (f32[24,1024]{1,0:T(8,128)S(1)}, f32[24,1024]{1,0:T(8,128)S(1)}, u32[]{:S(2)}, u32[]{:S(2)}) collective-permute-start(f32[24,1024]{1,0:T(8,128)S(1)} %get-tuple-element.40), channel_id=1, source_target_pairs={{8,0},{16,8},{24,16},{9,1},{17,9},{25,17},{10,2},{18,10},{26,18},{... | collective-permute-start | bytes 294920 | tf_op jit(solution)/shard_map/ppermute | solution.py:488
  4.2 7.5 %collective-permute-start.2 = (bf16[2,8,16,128]{3,2,1,0:T(8,128)(2,1)S(1)}, bf16[2,8,16,128]{3,2,1,0:T(8,128)(2,1)S(1)}, u32[]{:S(2)}, u32[]{:S(2)}) collective-permute-start(bf16[2,8,16,128]{3,2,1,0:T(8,128)(2,1)S(1)} %pad_maximum_fusion.6), channel_id=1, source_target_pairs={{0,2},{1,5},{2,0},{3,7},{4,6},{5,1},{6,4},{7,3},{8,10},{9,13},{10,... | collective-permute-start | bytes 196616 | tf_op jit(solution)/shard_map/ppermute | solution.py:429
  6.8 4.9 %collective-permute-start = (bf16[8,16,128]{2,1,0:T(8,128)(2,1)S(1)}, bf16[8,16,128]{2,1,0:T(8,128)(2,1)S(1)}, u32[]{:S(2)}, u32[]{:S(2)}) collective-permute-start(bf16[8,16,128]{2,1,0:T(8,128)(2,1)S(1)} %get-tuple-element.39.refs_0_.rest_1_), channel_id=1, source_target_pairs={{0,6},{1,7},{2,4},{3,5},{4,2},{5,3},{6,0},{7,1},{8,14},{9,15},{10,... | collective-permute-start | bytes 98312 | tf_op jit(solution)/shard_map/ppermute | solution.py:429
  17.6 5.7 %collective-permute-start.7 = (bf16[8,16,128]{2,1,0:T(8,128)(2,1)S(1)}, bf16[8,16,128]{2,1,0:T(8,128)(2,1)S(1)}, u32[]{:S(2)}, u32[]{:S(2)}) collective-permute-start(bf16[8,16,128]{2,1,0:T(8,128)(2,1)S(1)} %get-tuple-element.44), channel_id=1, source_target_pairs={{0,1},{1,0},{2,3},{3,2},{4,5},{5,4},{6,7},{7,6},{8,9},{9,8},{10,11... | collective-permute-start | bytes 98312 | tf_op jit(solution)/shard_map/ppermute | solution.py:429
  17.9 8.5 %collective-permute-start.6 = (bf16[8,16,128]{2,1,0:T(8,128)(2,1)S(1)}, bf16[8,16,128]{2,1,0:T(8,128)(2,1)S(1)}, u32[]{:S(2)}, u32[]{:S(2)}) collective-permute-start(bf16[8,16,128]{2,1,0:T(8,128)(2,1)S(1)} %get-tuple-element.44), channel_id=1, source_target_pairs={{0,14},{1,15},{2,12},{3,13},{4,10},{5,11},{6,8},{7,9},{8,22},{9,23... | collective-permute-start | bytes 98312 | tf_op jit(solution)/shard_map/ppermute | solution.py:429
  19.9 6.4 %collective-permute-start.5 = (bf16[24,16,128]{2,1,0:T(8,128)(2,1)S(1)}, bf16[24,16,128]{2,1,0:T(8,128)(2,1)S(1)}, u32[]{:S(2)}, u32[]{:S(2)}) collective-permute-start(bf16[24,16,128]{2,1,0:T(8,128)(2,1)S(1)} %get-tuple-element.43), channel_id=1, source_target_pairs={{0,8},{1,9},{2,10},{3,11},{4,12},{5,13},{6,14},{7,15}} | collective-permute-start | bytes 294920 | tf_op jit(solution)/shard_map/ppermute | solution.py:465
  23.4 7.0 %collective-permute-start.8 = (bf16[2,8,16,128]{3,2,1,0:T(8,128)(2,1)S(1)}, bf16[2,8,16,128]{3,2,1,0:T(8,128)(2,1)S(1)}, u32[]{:S(2)}, u32[]{:S(2)}) collective-permute-start(bf16[2,8,16,128]{3,2,1,0:T(8,128)(2,1)S(1)} %pad_maximum_fusion.7), channel_id=1, source_target_pairs={{0,10},{1,13},{2,8},{3,15},{4,14},{5,9},{6,12},{7,11},{8,18},{9,21... | collective-permute-start | bytes 196616 | tf_op jit(solution)/shard_map/ppermute | solution.py:429
  32.4 7.1 %collective-permute-start.12 = (bf16[8,16,128]{2,1,0:T(8,128)(2,1)S(1)}, bf16[8,16,128]{2,1,0:T(8,128)(2,1)S(1)}, u32[]{:S(2)}, u32[]{:S(2)}) collective-permute-start(bf16[8,16,128]{2,1,0:T(8,128)(2,1)S(1)} %get-tuple-element.46), channel_id=1, source_target_pairs={{0,1},{1,0},{2,3},{3,2},{4,5},{5,4},{6,7},{7,6},{8,9},{9,8},{10,11... | collective-permute-start | bytes 98312 | tf_op jit(solution)/shard_map/ppermute | solution.py:429
  32.6 7.8 %collective-permute-start.11 = (bf16[8,16,128]{2,1,0:T(8,128)(2,1)S(1)}, bf16[8,16,128]{2,1,0:T(8,128)(2,1)S(1)}, u32[]{:S(2)}, u32[]{:S(2)}) collective-permute-start(bf16[8,16,128]{2,1,0:T(8,128)(2,1)S(1)} %get-tuple-element.46), channel_id=1, source_target_pairs={{0,14},{1,15},{2,12},{3,13},{4,10},{5,11},{6,8},{7,9},{8,22},{9,23... | collective-permute-start | bytes 98312 | tf_op jit(solution)/shard_map/ppermute | solution.py:429
  39.5 7.0 %collective-permute-start.13 = (bf16[2,8,16,128]{3,2,1,0:T(8,128)(2,1)S(1)}, bf16[2,8,16,128]{3,2,1,0:T(8,128)(2,1)S(1)}, u32[]{:S(2)}, u32[]{:S(2)}) collective-permute-start(bf16[2,8,16,128]{3,2,1,0:T(8,128)(2,1)S(1)} %pad_maximum_fusion.8), channel_id=1, source_target_pairs={{0,10},{1,13},{2,8},{3,15},{4,14},{5,9},{6,12},{7,11},{8,18},{9,21... | collective-permute-start | bytes 196616 | tf_op jit(solution)/shard_map/ppermute | solution.py:429
  48.9 7.9 %collective-permute-start.16 = (bf16[8,16,128]{2,1,0:T(8,128)(2,1)S(1)}, bf16[8,16,128]{2,1,0:T(8,128)(2,1)S(1)}, u32[]{:S(2)}, u32[]{:S(2)}) collective-permute-start(bf16[8,16,128]{2,1,0:T(8,128)(2,1)S(1)} %get-tuple-element.48), channel_id=1, source_target_pairs={{0,14},{1,15},{2,12},{3,13},{4,10},{5,11},{6,8},{7,9},{8,22},{9,23... | collective-permute-start | bytes 98312 | tf_op jit(solution)/shard_map/ppermute | solution.py:429
  50.0 7.3 %collective-permute-start.18 = (bf16[2,8,16,128]{3,2,1,0:T(8,128)(2,1)S(1)}, bf16[2,8,16,128]{3,2,1,0:T(8,128)(2,1)S(1)}, u32[]{:S(2)}, u32[]{:S(2)}) collective-permute-start(bf16[2,8,16,128]{3,2,1,0:T(8,128)(2,1)S(1)} %pad_maximum_fusion.9), channel_id=1, source_target_pairs={{0,10},{1,13},{2,8},{3,15},{4,14},{5,9},{6,12},{7,11},{8,18},{9,21... | collective-permute-start | bytes 196616 | tf_op jit(solution)/shard_map/ppermute | solution.py:429
  60.6 6.2 %collective-permute-start.22 = (bf16[2,4,16,128]{3,2,1,0:T(8,128)(2,1)S(1)}, bf16[2,4,16,128]{3,2,1,0:T(8,128)(2,1)S(1)}, u32[]{:S(2)}, u32[]{:S(2)}) collective-permute-start(bf16[2,4,16,128]{3,2,1,0:T(8,128)(2,1)S(1)} %pad_maximum_fusion.14), channel_id=1, source_target_pairs={{0,2},{1,5},{2,0},{3,7},{4,6},{5,1},{6,4},{7,3},{8,10},{9,13},{10,... | collective-permute-start | bytes 98312 | tf_op jit(solution)/shard_map/ppermute | solution.py:429
  61.9 4.9 %collective-permute-start.20 = (bf16[4,16,128]{2,1,0:T(8,128)(2,1)S(1)}, bf16[4,16,128]{2,1,0:T(8,128)(2,1)S(1)}, u32[]{:S(2)}, u32[]{:S(2)}) collective-permute-start(bf16[4,16,128]{2,1,0:T(8,128)(2,1)S(1)} %get-tuple-element.49.rest_0_), channel_id=1, source_target_pairs={{0,6},{1,7},{2,4},{3,5},{4,2},{5,3},{6,0},{7,1},{8,14},{9,15},{10,... | collective-permute-start | bytes 49160 | tf_op jit(solution)/shard_map/ppermute | solution.py:429
  63.6 5.4 %collective-permute-start.24 = (f32[24,1024]{1,0:T(8,128)S(1)}, f32[24,1024]{1,0:T(8,128)S(1)}, u32[]{:S(2)}, u32[]{:S(2)}) collective-permute-start(f32[24,1024]{1,0:T(8,128)S(1)} %get-tuple-element.40), channel_id=1, source_target_pairs={{0,8},{8,16},{16,24},{1,9},{9,17},{17,25},{2,10},{10,18},{18,26},{... | collective-permute-start | bytes 294920 | tf_op jit(solution)/shard_map/ppermute | solution.py:527
  69.5 14.9 %collective-permute-start.27 = (bf16[8,16,128]{2,1,0:T(8,128)(2,1)S(1)}, bf16[8,16,128]{2,1,0:T(8,128)(2,1)S(1)}, u32[]{:S(2)}, u32[]{:S(2)}) collective-permute-start(bf16[8,16,128]{2,1,0:T(8,128)(2,1)S(1)} %get-tuple-element.52), channel_id=1, source_target_pairs={{0,1},{1,0},{2,3},{3,2},{4,5},{5,4},{6,7},{7,6},{8,9},{9,8},{10,11... | collective-permute-start | bytes 98312 | tf_op jit(solution)/shard_map/ppermute | solution.py:429
  69.6 15.7 %collective-permute-start.26 = (bf16[8,16,128]{2,1,0:T(8,128)(2,1)S(1)}, bf16[8,16,128]{2,1,0:T(8,128)(2,1)S(1)}, u32[]{:S(2)}, u32[]{:S(2)}) collective-permute-start(bf16[8,16,128]{2,1,0:T(8,128)(2,1)S(1)} %get-tuple-element.52), channel_id=1, source_target_pairs={{0,30},{1,31},{2,28},{3,29},{4,26},{5,27},{6,24},{7,25},{8,6},{9,7... | collective-permute-start | bytes 98312 | tf_op jit(solution)/shard_map/ppermute | solution.py:429
  84.5 5.3 %collective-permute-start.28 = (bf16[2,8,16,128]{3,2,1,0:T(8,128)(2,1)S(1)}, bf16[2,8,16,128]{3,2,1,0:T(8,128)(2,1)S(1)}, u32[]{:S(2)}, u32[]{:S(2)}) collective-permute-start(bf16[2,8,16,128]{3,2,1,0:T(8,128)(2,1)S(1)} %pad_maximum_fusion.11), channel_id=1, source_target_pairs={{0,26},{1,29},{2,24},{3,31},{4,30},{5,25},{6,28},{7,27},{8,2},{9,5... | collective-permute-start | bytes 196616 | tf_op jit(solution)/shard_map/ppermute | solution.py:429
  92.0 6.8 %collective-permute-start.31 = (bf16[8,16,128]{2,1,0:T(8,128)(2,1)S(1)}, bf16[8,16,128]{2,1,0:T(8,128)(2,1)S(1)}, u32[]{:S(2)}, u32[]{:S(2)}) collective-permute-start(bf16[8,16,128]{2,1,0:T(8,128)(2,1)S(1)} %get-tuple-element.56), channel_id=1, source_target_pairs={{0,30},{1,31},{2,28},{3,29},{4,26},{5,27},{6,24},{7,25},{8,6},{9,7... | collective-permute-start | bytes 98312 | tf_op jit(solution)/shard_map/ppermute | solution.py:429
  95.4 5.4 %collective-permute-start.33 = (bf16[2,8,16,128]{3,2,1,0:T(8,128)(2,1)S(1)}, bf16[2,8,16,128]{3,2,1,0:T(8,128)(2,1)S(1)}, u32[]{:S(2)}, u32[]{:S(2)}) collective-permute-start(bf16[2,8,16,128]{3,2,1,0:T(8,128)(2,1)S(1)} %pad_maximum_fusion.12), channel_id=1, source_target_pairs={{0,26},{1,29},{2,24},{3,31},{4,30},{5,25},{6,28},{7,27},{8,2},{9,5... | collective-permute-start | bytes 196616 | tf_op jit(solution)/shard_map/ppermute | solution.py:429
  102.9 6.6 %collective-permute-start.37 = (bf16[8,16,128]{2,1,0:T(8,128)(2,1)S(1)}, bf16[8,16,128]{2,1,0:T(8,128)(2,1)S(1)}, u32[]{:S(2)}, u32[]{:S(2)}) collective-permute-start(bf16[8,16,128]{2,1,0:T(8,128)(2,1)S(1)} %get-tuple-element.60), channel_id=1, source_target_pairs={{0,1},{1,0},{2,3},{3,2},{4,5},{5,4},{6,7},{7,6},{8,9},{9,8},{10,11... | collective-permute-start | bytes 98312 | tf_op jit(solution)/shard_map/ppermute | solution.py:429
  103.1 12.6 %collective-permute-start.36 = (bf16[8,16,128]{2,1,0:T(8,128)(2,1)S(1)}, bf16[8,16,128]{2,1,0:T(8,128)(2,1)S(1)}, u32[]{:S(2)}, u32[]{:S(2)}) collective-permute-start(bf16[8,16,128]{2,1,0:T(8,128)(2,1)S(1)} %get-tuple-element.60), channel_id=1, source_target_pairs={{0,30},{1,31},{2,28},{3,29},{4,26},{5,27},{6,24},{7,25},{8,6},{9,7... | collective-permute-start | bytes 98312 | tf_op jit(solution)/shard_map/ppermute | solution.py:429
  108.1 7.5 %collective-permute-start.35 = (bf16[24,16,128]{2,1,0:T(8,128)(2,1)S(1)}, bf16[24,16,128]{2,1,0:T(8,128)(2,1)S(1)}, u32[]{:S(2)}, u32[]{:S(2)}) collective-permute-start(bf16[24,16,128]{2,1,0:T(8,128)(2,1)S(1)} %get-tuple-element.59), channel_id=1, source_target_pairs={{8,0},{9,1},{10,2},{11,3},{12,4},{13,5},{14,6},{15,7}} | collective-permute-start | bytes 294920 | tf_op jit(solution)/shard_map/ppermute | solution.py:465
  109.5 7.9 %collective-permute-start.38 = (bf16[2,8,16,128]{3,2,1,0:T(8,128)(2,1)S(1)}, bf16[2,8,16,128]{3,2,1,0:T(8,128)(2,1)S(1)}, u32[]{:S(2)}, u32[]{:S(2)}) collective-permute-start(bf16[2,8,16,128]{3,2,1,0:T(8,128)(2,1)S(1)} %pad_maximum_fusion.13), channel_id=1, source_target_pairs={{0,26},{1,29},{2,24},{3,31},{4,30},{5,25},{6,28},{7,27},{8,2},{9,5... | collective-permute-start | bytes 196616 | tf_op jit(solution)/shard_map/ppermute | solution.py:429
  (16 other events, 30.3 us)

commit v10 on v9

--- a/solution.py
+++ b/solution.py
@@ -421,12 +421,21 @@
         pltpu.VMEM((2, rows, width), F32),
     ]
 
-    def send(block, shift, *flips):
+    def send(block, links, *flips):
         route = [
-            (i * planes + own, (i + shift) % sections * planes + (own ^ flips[own % len(flips)]))
-            for i in range(sections) for own in range(planes)
+            (i * planes + own, j * planes + (own ^ flips[own % len(flips)]))
+            for i, j in links for own in range(planes)
         ]
         return lax.ppermute(block, ("sweep", "plane"), route)
+
+    inside = [(i, i) for i in range(sections)]
+
+    def swapped_pairs(start, stop):
+        order = [start, stop] + [i for i in range(sections) if i not in (start, stop)]
+        links = [(i, i) for i in order[len(order) // 2 * 2:]]
+        for i, j in zip(order[::2], order[1::2]):
+            links += [(i, j), (j, i)]
+        return links
 
     def everywhere(front):
         slots = front.shape[0] // per_layer
@@ -440,32 +449,32 @@
             return [gathered], [[0]], order // LANES
         return [gathered], [list(range(planes))], per_layer
 
-    def spread(front, straight, shift, join=None):
+    def spread(front, straight, some, every, join=None):
         blocks, owners = [straight], [[(0, 0)]]
         for step in [1] if chips == 2 else range(3, chips):
-            blocks.append(send(front, shift, CORES * step))
+            blocks.append(send(front, some, CORES * step))
             owners.append([(CORES * step, CORES * step)])
         if chips == 4:
-            both = jnp.stack([front, send(front, 0, 1)])
-            blocks.append(send(both, shift, CORES, 2 * CORES))
+            both = jnp.stack([front, send(front, inside, 1)])
+            blocks.append(send(both, every, CORES, 2 * CORES))
             owners += [[(CORES + core, 2 * CORES + core) for core in range(CORES)]]
         if join:
             mine = join(blocks)
         else:
             short = [b[:2 * per_layer] if b.ndim == 3 else b for b in blocks]
             mine = jnp.concatenate([b[None] if b.ndim == 3 else b for b in short])
-        blocks.append(send(mine, 0, 1))
+        blocks.append(send(mine, inside, 1))
         owners.append([(one ^ 1, zero ^ 1) for places in owners for zero, one in places])
         return blocks, owners, per_layer
 
     def within(front, join=None):
-        return spread(front, front, 0, join) if direct else everywhere(front)
+        return spread(front, front, inside, inside, join) if direct else everywhere(front)
 
     def between(front, packet, start, stop):
         packet = lax.ppermute(packet, "sweep", [(start, stop)])
         if not direct:
             return *everywhere(packet[:2 * per_layer]), packet
-        return *spread(front, packet, stop - start), packet
+        return *spread(front, packet, [(start, stop)], swapped_pairs(start, stop)), packet
 
     inverse = in_hbm(front_inverse)
     half_inverse = pltpu.VMEM(front_inverse.shape[1:], BF16)

time: 122 us -> 123 us (level)
  waiting for transfers between devices: 45.5 us -> 37.2 us
  Pallas kernels: 17.6 us -> 22.6 us
  starting transfers between devices: 58.8 us -> 62.3 us
    ppermute x32, waiting for transfers between devices: 34.5 us -> 29.5 us  [send(): return lax.ppermute(block, ('sweep', 'plane'), route)]
    pallas_call x11, Pallas kernels: 17.6 us -> 22.6 us  [call(): pl.pallas_call(kernel, in_specs=specs, out_specs=[whole(pltpu.SMEM if len...]
    ppermute x32, starting transfers between devices: 46.9 us -> 51.9 us  [send(): return lax.ppermute(block, ('sweep', 'plane'), route)]
    ppermute x6, waiting for transfers between devices: 8.99 us -> 5.61 us  [between(): packet = lax.ppermute(packet, 'sweep', [(start, stop)])]
    ppermute x6, starting transfers between devices: 7.37 us -> 5.25 us  [between(): packet = lax.ppermute(packet, 'sweep', [(start, stop)])]
  transfers between devices with their start and end apart: 40 -> 40, of which waited for: 21 -> 17; matrix products, arithmetic and copies ran while one was open for 0% -> 0% of each run, Pallas kernels for 3% -> 3%
where the time goes in v10:
time: 123 us
  starting transfers between devices  62.3 us (51%)
  waiting for transfers between devices  37.2 us (30%)
  Pallas kernels  22.6 us (18%)
    ppermute x32, starting transfers between devices, send(): return lax.ppermute(block, ('sweep', 'plane'), route)  51.9 us
    ppermute x32, waiting for transfers between devices, send(): return lax.ppermute(block, ('sweep', 'plane'), route)  29.5 us
    pallas_call x11, Pallas kernels, call(): pl.pallas_call(kernel, in_specs=specs, out_specs=[whole(pltpu.SMEM if len...  22.6 us
    ppermute x6, waiting for transfers between devices, between(): packet = lax.ppermute(packet, 'sweep', [(start, stop)])  5.61 us
    ppermute x6, starting transfers between devices, between(): packet = lax.ppermute(packet, 'sweep', [(start, stop)])  5.25 us
    ppermute x1, starting transfers between devices, shards(): lax.ppermute(ahead, 'sweep', [(i, i + 1) for i in range(sections - 1)])  3.85 us
  transfers between devices with their start and end apart: 40, of which 17 were waited for; matrix products, arithmetic and copies ran while one was open for 0% of the time, Pallas kernels for 3%

profile of v10, /device:TPU:0, one launch (start us, length us, event | category | flops | bytes accessed | tf_op | source)
XLA Modules:
  0.0 122.7 jit_solution(14278896856606183065)
XLA Ops:
  0.0 2.4 %first_fronts.1 = (f32[40,1024]{1,0:T(8,128)S(1)}, f32[24,1024]{1,0:T(8,128)S(1)}, s32[2,1024]{1,0:T(2,128)S(1)}, bf16[8,16,128]{2,1,0:T(8,128)(2,1)S(1)}, s32[4]{0:T(128)S(1)}) custom-call(s32[4]{0:T(128)} %layers_in.1, f32[2,16,1024]{2,1,0:T(8,128)} %bitcast.53, f32[2,1024]{1,0:T(2,128)} %isc_in.1, f32[2,1024]{1,0:T(2,128)} %fwd_in.1, f32[2,1024]{1,0:T(2,128)} %bwd_in.1, ...), custom_call_target="tpu_custom_call" | custom-call | tf_op jit(solution)/shard_map/first_fronts/pallas_call | solution.py:377
  4.2 2.6 %collective-permute-start.2 = (bf16[2,8,16,128]{3,2,1,0:T(8,128)(2,1)S(1)}, bf16[2,8,16,128]{3,2,1,0:T(8,128)(2,1)S(1)}, u32[]{:S(2)}, u32[]{:S(2)}) collective-permute-start(bf16[2,8,16,128]{3,2,1,0:T(8,128)(2,1)S(1)} %pad_maximum_fusion.6), channel_id=1, source_target_pairs={{0,2},{1,5},{2,0},{3,7},{4,6},{5,1},{6,4},{7,3},{8,10},{9,13},{10,... | collective-permute-start | bytes 196616 | tf_op jit(solution)/shard_map/ppermute | solution.py:429
  6.8 1.5 %collective-permute-start = (bf16[8,16,128]{2,1,0:T(8,128)(2,1)S(1)}, bf16[8,16,128]{2,1,0:T(8,128)(2,1)S(1)}, u32[]{:S(2)}, u32[]{:S(2)}) collective-permute-start(bf16[8,16,128]{2,1,0:T(8,128)(2,1)S(1)} %get-tuple-element.39.refs_0_.rest_1_), channel_id=1, source_target_pairs={{0,6},{1,7},{2,4},{3,5},{4,2},{5,3},{6,0},{7,1},{8,14},{9,15},{10,... | collective-permute-start | bytes 98312 | tf_op jit(solution)/shard_map/ppermute | solution.py:429
  8.3 3.4 %load_first.1 = (bf16[2,512,4096]{2,1,0:T(8,128)(2,1)S(1)}, bf16[2,512,4096]{2,1,0:T(8,128)(2,1)S(1)}, f32[8,128]{1,0:T(8,128)S(1)}) custom-call(bf16[2,2,512,4096]{3,2,1,0:T(8,128)(2,1)} %rest_0_.1), custom_call_target="tpu_custom_call" | custom-call | tf_op jit(solution)/shard_map/load_first/pallas_call | solution.py:377
  11.8 1.3 %collective-permute-done.4.rest_4_ = bf16[4,8,16,128]{3,2,1,0:T(8,128)(2,1)S(1)} collective-permute-done((bf16[4,8,16,128]{3,2,1,0:T(8,128)(2,1)S(1)}, bf16[4,8,16,128]{3,2,1,0:T(8,128)(2,1)S(1)}, u32[]{:S(2)}, u32[]{:S(2)}) %collective-permute-start.4) | collective-permute-done | bytes 131104 | tf_op jit(solution)/shard_map/ppermute | solution.py:429
  13.2 6.8 %forward_section_0.1 = (f32[2,16,1024]{2,1,0:T(8,128)S(1)}, bf16[8,16,128]{2,1,0:T(8,128)(2,1)S(1)}, bf16[24,16,128]{2,1,0:T(8,128)(2,1)S(1)}, bf16[2,512,4096]{2,1,0:T(8,128)(2,1)S(1)}) custom-call(s32[4]{0:T(128)S(1)} %get-tuple-element.34.layers, bf16[2,512,4096]{2,1,0:T(8,128)(2,1)S(1)} %get-tuple-element.35.first_inverse, ...), custom_call_target="tpu_custom_call", output_to_operand_aliasing={{3}: (2, {})} | custom-call | tf_op jit(solution)/shard_map/forward_section_0/pallas_call | solution.py:377
  20.2 1.5 %collective-permute-start.6 = (bf16[8,16,128]{2,1,0:T(8,128)(2,1)S(1)}, bf16[8,16,128]{2,1,0:T(8,128)(2,1)S(1)}, u32[]{:S(2)}, u32[]{:S(2)}) collective-permute-start(bf16[8,16,128]{2,1,0:T(8,128)(2,1)S(1)} %get-tuple-element.44), channel_id=1, source_target_pairs={{0,14},{1,15},{2,12},{3,13},{4,10},{5,11},{6,8},{7,9}} | collective-permute-start | bytes 98312 | tf_op jit(solution)/shard_map/ppermute | solution.py:429
  23.2 3.0 %collective-permute-done.5.rest_0_.rest_4_.rest_8_ = bf16[24,16,128]{2,1,0:T(8,128)(2,1)S(1)} collective-permute-done((bf16[24,16,128]{2,1,0:T(8,128)(2,1)S(1)}, bf16[24,16,128]{2,1,0:T(8,128)(2,1)S(1)}, u32[]{:S(2)}, u32[]{:S(2)}) %collective-permute-start.5) | collective-permute-done | bytes 98336 | tf_op jit(solution)/shard_map/ppermute | solution.py:474
  26.2 2.2 %collective-permute-done.8.rest_2_ = bf16[2,8,16,128]{3,2,1,0:T(8,128)(2,1)S(1)} collective-permute-done((bf16[2,8,16,128]{3,2,1,0:T(8,128)(2,1)S(1)}, bf16[2,8,16,128]{3,2,1,0:T(8,128)(2,1)S(1)}, u32[]{:S(2)}, u32[]{:S(2)}) %collective-permute-start.8) | collective-permute-done | bytes 65568 | tf_op jit(solution)/shard_map/ppermute | solution.py:429
  28.5 1.3 %collective-permute-done.9.rest_3_ = bf16[4,8,16,128]{3,2,1,0:T(8,128)(2,1)S(1)} collective-permute-done((bf16[4,8,16,128]{3,2,1,0:T(8,128)(2,1)S(1)}, bf16[4,8,16,128]{3,2,1,0:T(8,128)(2,1)S(1)}, u32[]{:S(2)}, u32[]{:S(2)}) %collective-permute-start.9) | collective-permute-done | bytes 131104 | tf_op jit(solution)/shard_map/ppermute | solution.py:429
  32.2 6.9 %collective-permute-done.13.rest_2_ = bf16[2,8,16,128]{3,2,1,0:T(8,128)(2,1)S(1)} collective-permute-done((bf16[2,8,16,128]{3,2,1,0:T(8,128)(2,1)S(1)}, bf16[2,8,16,128]{3,2,1,0:T(8,128)(2,1)S(1)}, u32[]{:S(2)}, u32[]{:S(2)}) %collective-permute-start.13) | collective-permute-done | bytes 65568 | tf_op jit(solution)/shard_map/ppermute | solution.py:429
  42.8 4.7 %collective-permute-start.18 = (bf16[2,8,16,128]{3,2,1,0:T(8,128)(2,1)S(1)}, bf16[2,8,16,128]{3,2,1,0:T(8,128)(2,1)S(1)}, u32[]{:S(2)}, u32[]{:S(2)}) collective-permute-start(bf16[2,8,16,128]{3,2,1,0:T(8,128)(2,1)S(1)} %pad_maximum_fusion.9), channel_id=1, source_target_pairs={{16,26},{17,29},{18,24},{19,31},{20,30},{21,25},{22,28},{23,27},{2... | collective-permute-start | bytes 196616 | tf_op jit(solution)/shard_map/ppermute | solution.py:429
  47.5 2.6 %collective-permute-done.18.rest_2_ = bf16[2,8,16,128]{3,2,1,0:T(8,128)(2,1)S(1)} collective-permute-done((bf16[2,8,16,128]{3,2,1,0:T(8,128)(2,1)S(1)}, bf16[2,8,16,128]{3,2,1,0:T(8,128)(2,1)S(1)}, u32[]{:S(2)}, u32[]{:S(2)}) %collective-permute-start.18) | collective-permute-done | bytes 65568 | tf_op jit(solution)/shard_map/ppermute | solution.py:429
  54.6 1.5 %collective-permute-start.20 = (bf16[4,16,128]{2,1,0:T(8,128)(2,1)S(1)}, bf16[4,16,128]{2,1,0:T(8,128)(2,1)S(1)}, u32[]{:S(2)}, u32[]{:S(2)}) collective-permute-start(bf16[4,16,128]{2,1,0:T(8,128)(2,1)S(1)} %get-tuple-element.49.rest_0_), channel_id=1, source_target_pairs={{0,6},{1,7},{2,4},{3,5},{4,2},{5,3},{6,0},{7,1},{8,14},{9,15},{10,... | collective-permute-start | bytes 49160 | tf_op jit(solution)/shard_map/ppermute | solution.py:429
  56.1 3.9 %collective-permute-start.24 = (f32[24,1024]{1,0:T(8,128)S(1)}, f32[24,1024]{1,0:T(8,128)S(1)}, u32[]{:S(2)}, u32[]{:S(2)}) collective-permute-start(f32[24,1024]{1,0:T(8,128)S(1)} %get-tuple-element.40), channel_id=1, source_target_pairs={{0,8},{8,16},{16,24},{1,9},{9,17},{17,25},{2,10},{10,18},{18,26},{... | collective-permute-start | bytes 294920 | tf_op jit(solution)/shard_map/ppermute | solution.py:536
  60.1 2.1 %collective-permute-done.24.rest_5_.rest_7_ = f32[24,1024]{1,0:T(8,128)S(1)} collective-permute-done((f32[24,1024]{1,0:T(8,128)S(1)}, f32[24,1024]{1,0:T(8,128)S(1)}, u32[]{:S(2)}, u32[]{:S(2)}) %collective-permute-start.24) | collective-permute-done | bytes 98336 | tf_op jit(solution)/shard_map/ppermute | solution.py:536
  64.2 8.7 %collective-permute-start.28 = (bf16[2,8,16,128]{3,2,1,0:T(8,128)(2,1)S(1)}, bf16[2,8,16,128]{3,2,1,0:T(8,128)(2,1)S(1)}, u32[]{:S(2)}, u32[]{:S(2)}) collective-permute-start(bf16[2,8,16,128]{3,2,1,0:T(8,128)(2,1)S(1)} %pad_maximum_fusion.11), channel_id=1, source_target_pairs={{24,18},{25,21},{26,16},{27,23},{28,22},{29,17},{30,20},{31,19},{1... | collective-permute-start | bytes 196616 | tf_op jit(solution)/shard_map/ppermute | solution.py:429
  72.9 2.7 %collective-permute-done.28.rest_2_ = bf16[2,8,16,128]{3,2,1,0:T(8,128)(2,1)S(1)} collective-permute-done((bf16[2,8,16,128]{3,2,1,0:T(8,128)(2,1)S(1)}, bf16[2,8,16,128]{3,2,1,0:T(8,128)(2,1)S(1)}, u32[]{:S(2)}, u32[]{:S(2)}) %collective-permute-start.28) | collective-permute-done | bytes 65568 | tf_op jit(solution)/shard_map/ppermute | solution.py:429
  79.2 11.0 %collective-permute-start.33 = (bf16[2,8,16,128]{3,2,1,0:T(8,128)(2,1)S(1)}, bf16[2,8,16,128]{3,2,1,0:T(8,128)(2,1)S(1)}, u32[]{:S(2)}, u32[]{:S(2)}) collective-permute-start(bf16[2,8,16,128]{3,2,1,0:T(8,128)(2,1)S(1)} %pad_maximum_fusion.12), channel_id=1, source_target_pairs={{16,10},{17,13},{18,8},{19,15},{20,14},{21,9},{22,12},{23,11},{8,1... | collective-permute-start | bytes 196616 | tf_op jit(solution)/shard_map/ppermute | solution.py:429
  90.3 2.6 %collective-permute-done.33.rest_2_ = bf16[2,8,16,128]{3,2,1,0:T(8,128)(2,1)S(1)} collective-permute-done((bf16[2,8,16,128]{3,2,1,0:T(8,128)(2,1)S(1)}, bf16[2,8,16,128]{3,2,1,0:T(8,128)(2,1)S(1)}, u32[]{:S(2)}, u32[]{:S(2)}) %collective-permute-start.33) | collective-permute-done | bytes 65568 | tf_op jit(solution)/shard_map/ppermute | solution.py:429
  97.9 12.6 %collective-permute-start.38 = (bf16[2,8,16,128]{3,2,1,0:T(8,128)(2,1)S(1)}, bf16[2,8,16,128]{3,2,1,0:T(8,128)(2,1)S(1)}, u32[]{:S(2)}, u32[]{:S(2)}) collective-permute-start(bf16[2,8,16,128]{3,2,1,0:T(8,128)(2,1)S(1)} %pad_maximum_fusion.13), channel_id=1, source_target_pairs={{8,2},{9,5},{10,0},{11,7},{12,6},{13,1},{14,4},{15,3},{0,10},{1,13... | collective-permute-start | bytes 196616 | tf_op jit(solution)/shard_map/ppermute | solution.py:429
  110.5 2.6 %collective-permute-done.35.rest_0_.rest_5_ = bf16[24,16,128]{2,1,0:T(8,128)(2,1)S(1)} collective-permute-done((bf16[24,16,128]{2,1,0:T(8,128)(2,1)S(1)}, bf16[24,16,128]{2,1,0:T(8,128)(2,1)S(1)}, u32[]{:S(2)}, u32[]{:S(2)}) %collective-permute-start.35) | collective-permute-done | bytes 98336 | tf_op jit(solution)/shard_map/ppermute | solution.py:474
  113.1 2.0 %collective-permute-done.38.rest_2_ = bf16[2,8,16,128]{3,2,1,0:T(8,128)(2,1)S(1)} collective-permute-done((bf16[2,8,16,128]{3,2,1,0:T(8,128)(2,1)S(1)}, bf16[2,8,16,128]{3,2,1,0:T(8,128)(2,1)S(1)}, u32[]{:S(2)}, u32[]{:S(2)}) %collective-permute-start.38) | collective-permute-done | bytes 65568 | tf_op jit(solution)/shard_map/ppermute | solution.py:429
  116.5 6.2 %backward_section_0.1 = f32[2,16,1024]{2,1,0:T(8,128)} custom-call(s32[4]{0:T(128)S(1)} %get-tuple-element.34.layers, bf16[2,512,4096]{2,1,0:T(8,128)(2,1)S(1)} %get-tuple-element.35.first_inverse, bf16[2,512,4096]{2,1,0:T(8,128)(2,1)S(1)} %get-tuple-element.42.second_inverse, f32[40,1024]{1,0:T(8,128)S(1)} %get-tuple-element.37.packet, ...), custom_call_target="tpu_custom_call" | custom-call | tf_op jit(solution)/shard_map/backward_section_0/pallas_call | solution.py:377
  (88 shorter events, 26.1 us)
Async XLA Ops:
  2.9 8.8 %collective-permute-start.3 = (f32[24,1024]{1,0:T(8,128)S(1)}, f32[24,1024]{1,0:T(8,128)S(1)}, u32[]{:S(2)}, u32[]{:S(2)}) collective-permute-start(f32[24,1024]{1,0:T(8,128)S(1)} %get-tuple-element.40), channel_id=1, source_target_pairs={{8,0},{16,8},{24,16},{9,1},{17,9},{25,17},{10,2},{18,10},{26,18},{... | collective-permute-start | bytes 294920 | tf_op jit(solution)/shard_map/ppermute | solution.py:497
  4.2 7.5 %collective-permute-start.2 = (bf16[2,8,16,128]{3,2,1,0:T(8,128)(2,1)S(1)}, bf16[2,8,16,128]{3,2,1,0:T(8,128)(2,1)S(1)}, u32[]{:S(2)}, u32[]{:S(2)}) collective-permute-start(bf16[2,8,16,128]{3,2,1,0:T(8,128)(2,1)S(1)} %pad_maximum_fusion.6), channel_id=1, source_target_pairs={{0,2},{1,5},{2,0},{3,7},{4,6},{5,1},{6,4},{7,3},{8,10},{9,13},{10,... | collective-permute-start | bytes 196616 | tf_op jit(solution)/shard_map/ppermute | solution.py:429
  6.8 4.9 %collective-permute-start = (bf16[8,16,128]{2,1,0:T(8,128)(2,1)S(1)}, bf16[8,16,128]{2,1,0:T(8,128)(2,1)S(1)}, u32[]{:S(2)}, u32[]{:S(2)}) collective-permute-start(bf16[8,16,128]{2,1,0:T(8,128)(2,1)S(1)} %get-tuple-element.39.refs_0_.rest_1_), channel_id=1, source_target_pairs={{0,6},{1,7},{2,4},{3,5},{4,2},{5,3},{6,0},{7,1},{8,14},{9,15},{10,... | collective-permute-start | bytes 98312 | tf_op jit(solution)/shard_map/ppermute | solution.py:429
  20.0 3.1 %collective-permute-start.7 = (bf16[8,16,128]{2,1,0:T(8,128)(2,1)S(1)}, bf16[8,16,128]{2,1,0:T(8,128)(2,1)S(1)}, u32[]{:S(2)}, u32[]{:S(2)}) collective-permute-start(bf16[8,16,128]{2,1,0:T(8,128)(2,1)S(1)} %get-tuple-element.44), channel_id=1, source_target_pairs={{0,1},{1,0},{2,3},{3,2},{4,5},{5,4},{6,7},{7,6},{8,9},{9,8},{10,11... | collective-permute-start | bytes 98312 | tf_op jit(solution)/shard_map/ppermute | solution.py:429
  20.2 6.0 %collective-permute-start.6 = (bf16[8,16,128]{2,1,0:T(8,128)(2,1)S(1)}, bf16[8,16,128]{2,1,0:T(8,128)(2,1)S(1)}, u32[]{:S(2)}, u32[]{:S(2)}) collective-permute-start(bf16[8,16,128]{2,1,0:T(8,128)(2,1)S(1)} %get-tuple-element.44), channel_id=1, source_target_pairs={{0,14},{1,15},{2,12},{3,13},{4,10},{5,11},{6,8},{7,9}} | collective-permute-start | bytes 98312 | tf_op jit(solution)/shard_map/ppermute | solution.py:429
  21.8 4.4 %collective-permute-start.5 = (bf16[24,16,128]{2,1,0:T(8,128)(2,1)S(1)}, bf16[24,16,128]{2,1,0:T(8,128)(2,1)S(1)}, u32[]{:S(2)}, u32[]{:S(2)}) collective-permute-start(bf16[24,16,128]{2,1,0:T(8,128)(2,1)S(1)} %get-tuple-element.43), channel_id=1, source_target_pairs={{0,8},{1,9},{2,10},{3,11},{4,12},{5,13},{6,14},{7,15}} | collective-permute-start | bytes 294920 | tf_op jit(solution)/shard_map/ppermute | solution.py:474
  23.1 5.3 %collective-permute-start.8 = (bf16[2,8,16,128]{3,2,1,0:T(8,128)(2,1)S(1)}, bf16[2,8,16,128]{3,2,1,0:T(8,128)(2,1)S(1)}, u32[]{:S(2)}, u32[]{:S(2)}) collective-permute-start(bf16[2,8,16,128]{3,2,1,0:T(8,128)(2,1)S(1)} %pad_maximum_fusion.7), channel_id=1, source_target_pairs={{0,10},{1,13},{2,8},{3,15},{4,14},{5,9},{6,12},{7,11},{8,2},{9,5},... | collective-permute-start | bytes 196616 | tf_op jit(solution)/shard_map/ppermute | solution.py:429
  32.0 7.1 %collective-permute-start.13 = (bf16[2,8,16,128]{3,2,1,0:T(8,128)(2,1)S(1)}, bf16[2,8,16,128]{3,2,1,0:T(8,128)(2,1)S(1)}, u32[]{:S(2)}, u32[]{:S(2)}) collective-permute-start(bf16[2,8,16,128]{3,2,1,0:T(8,128)(2,1)S(1)} %pad_maximum_fusion.8), channel_id=1, source_target_pairs={{8,18},{9,21},{10,16},{11,23},{12,22},{13,17},{14,20},{15,19},{16,... | collective-permute-start | bytes 196616 | tf_op jit(solution)/shard_map/ppermute | solution.py:429
  41.5 6.1 %collective-permute-start.16 = (bf16[8,16,128]{2,1,0:T(8,128)(2,1)S(1)}, bf16[8,16,128]{2,1,0:T(8,128)(2,1)S(1)}, u32[]{:S(2)}, u32[]{:S(2)}) collective-permute-start(bf16[8,16,128]{2,1,0:T(8,128)(2,1)S(1)} %get-tuple-element.48), channel_id=1, source_target_pairs={{16,30},{17,31},{18,28},{19,29},{20,26},{21,27},{22,24},{23,25}} | collective-permute-start | bytes 98312 | tf_op jit(solution)/shard_map/ppermute | solution.py:429
  42.1 5.4 %collective-permute-start.15 = (bf16[24,16,128]{2,1,0:T(8,128)(2,1)S(1)}, bf16[24,16,128]{2,1,0:T(8,128)(2,1)S(1)}, u32[]{:S(2)}, u32[]{:S(2)}) collective-permute-start(bf16[24,16,128]{2,1,0:T(8,128)(2,1)S(1)} %get-tuple-element.47), channel_id=1, source_target_pairs={{16,24},{17,25},{18,26},{19,27},{20,28},{21,29},{22,30},{23,31}} | collective-permute-start | bytes 294920 | tf_op jit(solution)/shard_map/ppermute | solution.py:474
  42.8 7.3 %collective-permute-start.18 = (bf16[2,8,16,128]{3,2,1,0:T(8,128)(2,1)S(1)}, bf16[2,8,16,128]{3,2,1,0:T(8,128)(2,1)S(1)}, u32[]{:S(2)}, u32[]{:S(2)}) collective-permute-start(bf16[2,8,16,128]{3,2,1,0:T(8,128)(2,1)S(1)} %pad_maximum_fusion.9), channel_id=1, source_target_pairs={{16,26},{17,29},{18,24},{19,31},{20,30},{21,25},{22,28},{23,27},{2... | collective-permute-start | bytes 196616 | tf_op jit(solution)/shard_map/ppermute | solution.py:429
  53.4 6.6 %collective-permute-start.22 = (bf16[2,4,16,128]{3,2,1,0:T(8,128)(2,1)S(1)}, bf16[2,4,16,128]{3,2,1,0:T(8,128)(2,1)S(1)}, u32[]{:S(2)}, u32[]{:S(2)}) collective-permute-start(bf16[2,4,16,128]{3,2,1,0:T(8,128)(2,1)S(1)} %pad_maximum_fusion.14), channel_id=1, source_target_pairs={{0,2},{1,5},{2,0},{3,7},{4,6},{5,1},{6,4},{7,3},{8,10},{9,13},{10,... | collective-permute-start | bytes 98312 | tf_op jit(solution)/shard_map/ppermute | solution.py:429
  54.6 5.3 %collective-permute-start.20 = (bf16[4,16,128]{2,1,0:T(8,128)(2,1)S(1)}, bf16[4,16,128]{2,1,0:T(8,128)(2,1)S(1)}, u32[]{:S(2)}, u32[]{:S(2)}) collective-permute-start(bf16[4,16,128]{2,1,0:T(8,128)(2,1)S(1)} %get-tuple-element.49.rest_0_), channel_id=1, source_target_pairs={{0,6},{1,7},{2,4},{3,5},{4,2},{5,3},{6,0},{7,1},{8,14},{9,15},{10,... | collective-permute-start | bytes 49160 | tf_op jit(solution)/shard_map/ppermute | solution.py:429
  56.1 6.1 %collective-permute-start.24 = (f32[24,1024]{1,0:T(8,128)S(1)}, f32[24,1024]{1,0:T(8,128)S(1)}, u32[]{:S(2)}, u32[]{:S(2)}) collective-permute-start(f32[24,1024]{1,0:T(8,128)S(1)} %get-tuple-element.40), channel_id=1, source_target_pairs={{0,8},{8,16},{16,24},{1,9},{9,17},{17,25},{2,10},{10,18},{18,26},{... | collective-permute-start | bytes 294920 | tf_op jit(solution)/shard_map/ppermute | solution.py:536
  62.8 10.1 %collective-permute-start.26 = (bf16[8,16,128]{2,1,0:T(8,128)(2,1)S(1)}, bf16[8,16,128]{2,1,0:T(8,128)(2,1)S(1)}, u32[]{:S(2)}, u32[]{:S(2)}) collective-permute-start(bf16[8,16,128]{2,1,0:T(8,128)(2,1)S(1)} %get-tuple-element.52), channel_id=1, source_target_pairs={{24,22},{25,23},{26,20},{27,21},{28,18},{29,19},{30,16},{31,17}} | collective-permute-start | bytes 98312 | tf_op jit(solution)/shard_map/ppermute | solution.py:429
  63.5 9.4 %collective-permute-start.25 = (bf16[24,16,128]{2,1,0:T(8,128)(2,1)S(1)}, bf16[24,16,128]{2,1,0:T(8,128)(2,1)S(1)}, u32[]{:S(2)}, u32[]{:S(2)}) collective-permute-start(bf16[24,16,128]{2,1,0:T(8,128)(2,1)S(1)} %get-tuple-element.51), channel_id=1, source_target_pairs={{24,16},{25,17},{26,18},{27,19},{28,20},{29,21},{30,22},{31,23}} | collective-permute-start | bytes 294920 | tf_op jit(solution)/shard_map/ppermute | solution.py:474
  64.2 11.4 %collective-permute-start.28 = (bf16[2,8,16,128]{3,2,1,0:T(8,128)(2,1)S(1)}, bf16[2,8,16,128]{3,2,1,0:T(8,128)(2,1)S(1)}, u32[]{:S(2)}, u32[]{:S(2)}) collective-permute-start(bf16[2,8,16,128]{3,2,1,0:T(8,128)(2,1)S(1)} %pad_maximum_fusion.11), channel_id=1, source_target_pairs={{24,18},{25,21},{26,16},{27,23},{28,22},{29,17},{30,20},{31,19},{1... | collective-permute-start | bytes 196616 | tf_op jit(solution)/shard_map/ppermute | solution.py:429
  77.8 12.4 %collective-permute-start.31 = (bf16[8,16,128]{2,1,0:T(8,128)(2,1)S(1)}, bf16[8,16,128]{2,1,0:T(8,128)(2,1)S(1)}, u32[]{:S(2)}, u32[]{:S(2)}) collective-permute-start(bf16[8,16,128]{2,1,0:T(8,128)(2,1)S(1)} %get-tuple-element.56), channel_id=1, source_target_pairs={{16,14},{17,15},{18,12},{19,13},{20,10},{21,11},{22,8},{23,9}} | collective-permute-start | bytes 98312 | tf_op jit(solution)/shard_map/ppermute | solution.py:429
  78.5 11.7 %collective-permute-start.30 = (bf16[24,16,128]{2,1,0:T(8,128)(2,1)S(1)}, bf16[24,16,128]{2,1,0:T(8,128)(2,1)S(1)}, u32[]{:S(2)}, u32[]{:S(2)}) collective-permute-start(bf16[24,16,128]{2,1,0:T(8,128)(2,1)S(1)} %get-tuple-element.55), channel_id=1, source_target_pairs={{16,8},{17,9},{18,10},{19,11},{20,12},{21,13},{22,14},{23,15}} | collective-permute-start | bytes 294920 | tf_op jit(solution)/shard_map/ppermute | solution.py:474
  79.2 13.7 %collective-permute-start.33 = (bf16[2,8,16,128]{3,2,1,0:T(8,128)(2,1)S(1)}, bf16[2,8,16,128]{3,2,1,0:T(8,128)(2,1)S(1)}, u32[]{:S(2)}, u32[]{:S(2)}) collective-permute-start(bf16[2,8,16,128]{3,2,1,0:T(8,128)(2,1)S(1)} %pad_maximum_fusion.12), channel_id=1, source_target_pairs={{16,10},{17,13},{18,8},{19,15},{20,14},{21,9},{22,12},{23,11},{8,1... | collective-permute-start | bytes 196616 | tf_op jit(solution)/shard_map/ppermute | solution.py:429
  95.1 2.8 %collective-permute-start.37 = (bf16[8,16,128]{2,1,0:T(8,128)(2,1)S(1)}, bf16[8,16,128]{2,1,0:T(8,128)(2,1)S(1)}, u32[]{:S(2)}, u32[]{:S(2)}) collective-permute-start(bf16[8,16,128]{2,1,0:T(8,128)(2,1)S(1)} %get-tuple-element.60), channel_id=1, source_target_pairs={{0,1},{1,0},{2,3},{3,2},{4,5},{5,4},{6,7},{7,6},{8,9},{9,8},{10,11... | collective-permute-start | bytes 98312 | tf_op jit(solution)/shard_map/ppermute | solution.py:429
  95.3 17.8 %collective-permute-start.36 = (bf16[8,16,128]{2,1,0:T(8,128)(2,1)S(1)}, bf16[8,16,128]{2,1,0:T(8,128)(2,1)S(1)}, u32[]{:S(2)}, u32[]{:S(2)}) collective-permute-start(bf16[8,16,128]{2,1,0:T(8,128)(2,1)S(1)} %get-tuple-element.60), channel_id=1, source_target_pairs={{8,6},{9,7},{10,4},{11,5},{12,2},{13,3},{14,0},{15,1}} | collective-permute-start | bytes 98312 | tf_op jit(solution)/shard_map/ppermute | solution.py:429
  96.6 16.5 %collective-permute-start.35 = (bf16[24,16,128]{2,1,0:T(8,128)(2,1)S(1)}, bf16[24,16,128]{2,1,0:T(8,128)(2,1)S(1)}, u32[]{:S(2)}, u32[]{:S(2)}) collective-permute-start(bf16[24,16,128]{2,1,0:T(8,128)(2,1)S(1)} %get-tuple-element.59), channel_id=1, source_target_pairs={{8,0},{9,1},{10,2},{11,3},{12,4},{13,5},{14,6},{15,7}} | collective-permute-start | bytes 294920 | tf_op jit(solution)/shard_map/ppermute | solution.py:474
  97.9 17.2 %collective-permute-start.38 = (bf16[2,8,16,128]{3,2,1,0:T(8,128)(2,1)S(1)}, bf16[2,8,16,128]{3,2,1,0:T(8,128)(2,1)S(1)}, u32[]{:S(2)}, u32[]{:S(2)}) collective-permute-start(bf16[2,8,16,128]{3,2,1,0:T(8,128)(2,1)S(1)} %pad_maximum_fusion.13), channel_id=1, source_target_pairs={{8,2},{9,5},{10,0},{11,7},{12,6},{13,1},{14,4},{15,3},{0,10},{1,13... | collective-permute-start | bytes 196616 | tf_op jit(solution)/shard_map/ppermute | solution.py:429
  (16 other events, 23.6 us)

commit v11 on v10

--- a/solution.py
+++ b/solution.py
@@ -89,18 +89,13 @@
 
 
 def write_front(ref, chunks, field=()):
-    high = [c.astype(BF16) for c in field]
-    low = [(c - h.astype(F32)).astype(BF16) for c, h in zip(field, high)]
-    for at, chunk in enumerate(chunks + high + low):
+    for at, chunk in enumerate([*chunks, *field]):
         ref[at] = chunk.astype(BF16)
 
 
 def read_field(packet, count):
-    start = packet.shape[0] - 2 * count
-    return [
-        packet[start + i].astype(F32) + packet[start + count + i].astype(F32)
-        for i in range(count)
-    ]
+    start = packet.shape[0] - count
+    return [packet[start + i].astype(F32) for i in range(count)]
 
 
 def write_field(ref, chunks):
@@ -157,7 +152,7 @@
 
 
 def first_kernel(
-    width, layers_in, rhs_in, isc_in, fwd_in, bwd_in, picked_in, local, ahead, place, front,
+    width, layers_in, rhs_in, isc_in, fwd_in, bwd_in, picked_in, local, ahead, longer, place, front,
     layers, rhs, isc, fwd, bwd, picked, sems,
 ):
     pairs = (
@@ -202,6 +197,8 @@
         for i, chunk in enumerate(chunks):
             ahead[count + at:count + at + 1, i * LANES:(i + 1) * LANES] = chunk[0:1]
     write_field(ahead.at[0:count], base_a + base_b)
+    longer[0:ahead.shape[0], :] = ahead[...]
+    longer[ahead.shape[0]:, :] = jnp.zeros((longer.shape[0] - ahead.shape[0], longer.shape[1]), F32)
     for layer in range(2):
         place[layer:layer + 1, :] = places(picked[layer:layer + 1, :], cells)
 
@@ -291,7 +288,7 @@
             write_front(front, gather_lanes(rounded(z), picks(small, PICK, width)))
         else:
             outgoing = choose(both, second, first)
-            chunks = forward_front(after.at[0:rows], after.at[rows:], outgoing)
+            chunks = forward_front(after.at[0:rows], after.at[rows:rows + NEEDS], outgoing)
             write_front(front, chunks)
             write_front(outgoing_packet, chunks, outgoing)
         write_field(kept.at[0], first)
@@ -357,7 +354,7 @@
         first = minus(first_fwd, change)
         if step:
             chunks = backward_front(
-                behind.at[kept.shape[1]:], first, read_field(held, count), layers[step - 1] == 2
+                behind.at[kept.shape[1]:kept.shape[1] + NEEDS], first, read_field(held, count), layers[step - 1] == 2
             )
             write_front(front, chunks)
             write_front(outgoing_packet, chunks, first)
@@ -414,7 +411,7 @@
 
     half_shape = ((per_layer, rows, LANES), BF16)
     front_shape = ((2 * per_layer, rows, LANES), BF16)
-    packet_shape = ((2 * per_layer + 2 * (cells // LANES), rows, LANES), BF16)
+    packet_shape = ((2 * per_layer + cells // LANES, rows, LANES), BF16)
     layers_shape = ((layer_slots, rows, cells), F32)
     scratch = [
         pltpu.VMEM((2, rows, order), BF16),
@@ -422,20 +419,18 @@
     ]
 
     def send(block, links, *flips):
-        route = [
-            (i * planes + own, j * planes + (own ^ flips[own % len(flips)]))
-            for i, j in links for own in range(planes)
-        ]
+        route = []
+        for i, j in links:
+            for own in range(planes):
+                flip = flips[own % len(flips)] or (i == j and planes % CORES == 0)
+                route.append((i * planes + own, j * planes + (own ^ int(flip))))
         return lax.ppermute(block, ("sweep", "plane"), route)
 
     inside = [(i, i) for i in range(sections)]
 
-    def swapped_pairs(start, stop):
-        order = [start, stop] + [i for i in range(sections) if i not in (start, stop)]
-        links = [(i, i) for i in order[len(order) // 2 * 2:]]
-        for i, j in zip(order[::2], order[1::2]):
-            links += [(i, j), (j, i)]
-        return links
+    def cycle(*members):
+        links = list(zip(members, members[1:] + members[:1]))
+        return links + [(i, i) for i in range(sections) if i not in members]
 
     def everywhere(front):
         slots = front.shape[0] // per_layer
@@ -474,18 +469,21 @@
         packet = lax.ppermute(packet, "sweep", [(start, stop)])
         if not direct:
             return *everywhere(packet[:2 * per_layer]), packet
-        return *spread(front, packet, [(start, stop)], swapped_pairs(start, stop)), packet
+        third = [i for i in (2 * start - stop, 2 * stop - start) if 0 <= i < sections]
+        some, every = cycle(start, stop, *third[:1]), cycle(start, stop)
+        return *spread(front, packet, some, every), packet
 
     inverse = in_hbm(front_inverse)
     half_inverse = pltpu.VMEM(front_inverse.shape[1:], BF16)
     coefficients = (interior_scale, forward_coupling, backward_coupling)
     operands = [section_layers, rhs, *coefficients, picked]
-    local, ahead, place, front, layers = call(
+    local, ahead, longer, place, front, layers = call(
         functools.partial(first_kernel, width),
         [in_hbm(a) for a in operands],
         [
             ((2 * rows + 8, cells), F32),
             ((rows + NEEDS, 2 * width), F32),
+            ((2 * rows + NEEDS, 2 * width), F32),
             ((2, cells), jnp.int32),
             front_shape,
             (section_layers.shape, jnp.int32),
@@ -494,7 +492,12 @@
         "first_fronts",
         range(6),
     )
-    after = lax.ppermute(ahead, "sweep", [(i + 1, i) for i in range(sections - 1)])
+    def neighbours(first):
+        pairs = [(i, i + 1) for i in range(first, sections - 1, 2)]
+        alone = [i for i in range(sections) if not any(i in pair for pair in pairs)]
+        return pairs + [(j, i) for i, j in pairs] + [(i, i) for i in alone]
+
+    near = [send(ahead, neighbours(0), 0, 0), None]
     first_inverse, second_inverse, token = call(
         load_kernel,
         [inverse],
@@ -506,14 +509,15 @@
 
     def join(blocks):
         shape = (sum(b.shape[0] if b.ndim == 4 else 1 for b in blocks), *front_shape[0])
-        return call(join_kernel, [*blocks, after, token], [(shape, BF16)], [], "join")[0]
+        return call(join_kernel, [*blocks, near[0], token], [(shape, BF16)], [], "join")[0]
 
     gathered, owners, slots = within(front, join)
 
+    near[1] = send(longer, neighbours(1), 0)
     kept, held = [], [None]
     for step in range(sections):
         final = step == sections - 1
-        extra = ([held[step]] if step else []) + ([] if final else [after])
+        extra = ([held[step]] if step else []) + ([] if final else [near[step % 2]])
         outs = [layers_shape, half_shape if final else front_shape]
         outs += [] if final else [packet_shape]
         outs += [] if step else [half_inverse]
@@ -533,7 +537,6 @@
             second_inverse = outs[-1]
         kept.append(outs[0])
         if final:
-            behind = lax.ppermute(ahead, "sweep", [(i, i + 1) for i in range(sections - 1)])
             gathered, owners, slots = within(outs[1])
         else:
             gathered, owners, slots, incoming = between(outs[1], outs[2], step, step + 1)
@@ -541,7 +544,7 @@
 
     result = incoming = None
     for step in reversed(range(sections)):
-        extra = ([] if result is None else [incoming, result]) + ([behind, held[step]] if step else [])
+        extra = ([] if result is None else [incoming, result]) + ([near[(step - 1) % 2], held[step]] if step else [])
         outs = call(
             functools.partial(
                 backward_kernel, step, sections, planes, width, slots, owners

time: 123 us -> 113 us (0.919)
  starting transfers between devices: 62.3 us -> 53.1 us
    ppermute x2 -> x0, starting transfers between devices: 5.13 us -> none  [the longest x1 3.85 us: shards(): lax.ppermute(ahead, 'sweep', [(i, i + 1) for i in range(sections - 1)])]
    ppermute x32 -> x34, starting transfers between devices: 51.9 us -> 47.6 us  [send(): return lax.ppermute(block, ('sweep', 'plane'), route)]
    ppermute x32 -> x34, waiting for transfers between devices: 29.5 us -> 32.2 us  [send(): return lax.ppermute(block, ('sweep', 'plane'), route)]
    ppermute x2 -> x0, waiting for transfers between devices: 2.07 us -> none  [the longest x1 2.07 us: shards(): lax.ppermute(ahead, 'sweep', [(i, i + 1) for i in range(sections - 1)])]
  transfers between devices with their start and end apart: 40 -> 40, of which waited for: 17 -> 23; matrix products, arithmetic and copies ran while one was open for 0% -> 0% of each run, Pallas kernels for 3% -> 3%
where the time goes in v11:
time: 113 us
  starting transfers between devices  53.1 us (47%)
  waiting for transfers between devices  36.6 us (32%)
  Pallas kernels  22.6 us (20%)
    ppermute x34, starting transfers between devices, send(): return lax.ppermute(block, ('sweep', 'plane'), route)  47.6 us
    ppermute x34, waiting for transfers between devices, send(): return lax.ppermute(block, ('sweep', 'plane'), route)  32.2 us
    pallas_call x11, Pallas kernels, call(): pl.pallas_call(kernel, in_specs=specs, out_specs=[whole(pltpu.SMEM if len...  22.6 us
    ppermute x6, starting transfers between devices, between(): packet = lax.ppermute(packet, 'sweep', [(start, stop)])  5.57 us
    ppermute x6, waiting for transfers between devices, between(): packet = lax.ppermute(packet, 'sweep', [(start, stop)])  4.39 us
  transfers between devices with their start and end apart: 40, of which 23 were waited for; matrix products, arithmetic and copies ran while one was open for 0% of the time, Pallas kernels for 3%

profile of v11, /device:TPU:0, one launch (start us, length us, event | category | flops | bytes accessed | tf_op | source)
XLA Modules:
  0.0 112.9 jit_solution(13094900326406869318)
XLA Ops:
  0.0 2.4 %first_fronts.1 = (f32[40,1024]{1,0:T(8,128)S(1)}, f32[24,1024]{1,0:T(8,128)S(1)}, f32[40,1024]{1,0:T(8,128)S(1)}, s32[2,1024]{1,0:T(2,128)S(1)}, bf16[8,16,128]{2,1,0:T(8,128)(2,1)S(1)}, /*index=5*/s32[4]{0:T(128)S(1)}) custom-call(s32[4]{0:T(128)} %layers_in.1, f32[2,16,1024]{2,1,0:T(8,128)} %bitcast.53, f32[2,1024]{1,0:T(2,128)} %isc_in.1, ...), custom_call_target="tpu_custom_call" | custom-call | tf_op jit(solution)/shard_map/first_fronts/pallas_call | solution.py:374
  2.9 2.6 %collective-permute-start.3 = (f32[24,1024]{1,0:T(8,128)S(1)}, f32[24,1024]{1,0:T(8,128)S(1)}, u32[]{:S(2)}, u32[]{:S(2)}) collective-permute-start(f32[24,1024]{1,0:T(8,128)S(1)} %get-tuple-element.41), channel_id=1, source_target_pairs={{0,8},{1,9},{2,10},{3,11},{4,12},{5,13},{6,14},{7,15},{16,24},{17,... | collective-permute-start | bytes 294920 | tf_op jit(solution)/shard_map/ppermute | solution.py:427
  5.6 1.6 %collective-permute-start.2 = (bf16[2,8,16,128]{3,2,1,0:T(8,128)(2,1)S(1)}, bf16[2,8,16,128]{3,2,1,0:T(8,128)(2,1)S(1)}, u32[]{:S(2)}, u32[]{:S(2)}) collective-permute-start(bf16[2,8,16,128]{3,2,1,0:T(8,128)(2,1)S(1)} %pad_maximum_fusion.6), channel_id=1, source_target_pairs={{0,2},{1,5},{2,0},{3,7},{4,6},{5,1},{6,4},{7,3},{8,10},{9,13},{10,... | collective-permute-start | bytes 196616 | tf_op jit(solution)/shard_map/ppermute | solution.py:427
  7.2 1.5 %collective-permute-start = (bf16[8,16,128]{2,1,0:T(8,128)(2,1)S(1)}, bf16[8,16,128]{2,1,0:T(8,128)(2,1)S(1)}, u32[]{:S(2)}, u32[]{:S(2)}) collective-permute-start(bf16[8,16,128]{2,1,0:T(8,128)(2,1)S(1)} %get-tuple-element.40.refs_0_.rest_1_), channel_id=1, source_target_pairs={{0,6},{1,7},{2,4},{3,5},{4,2},{5,3},{6,0},{7,1},{8,14},{9,15},{10,... | collective-permute-start | bytes 98312 | tf_op jit(solution)/shard_map/ppermute | solution.py:427
  8.6 3.4 %load_first.1 = (bf16[2,512,4096]{2,1,0:T(8,128)(2,1)S(1)}, bf16[2,512,4096]{2,1,0:T(8,128)(2,1)S(1)}, f32[8,128]{1,0:T(8,128)S(1)}) custom-call(bf16[2,2,512,4096]{3,2,1,0:T(8,128)(2,1)} %rest_0_.1), custom_call_target="tpu_custom_call" | custom-call | tf_op jit(solution)/shard_map/load_first/pallas_call | solution.py:374
  13.5 6.8 %forward_section_0.1 = (f32[2,16,1024]{2,1,0:T(8,128)S(1)}, bf16[8,16,128]{2,1,0:T(8,128)(2,1)S(1)}, bf16[16,16,128]{2,1,0:T(8,128)(2,1)S(1)}, bf16[2,512,4096]{2,1,0:T(8,128)(2,1)S(1)}) custom-call(s32[4]{0:T(128)S(1)} %get-tuple-element.35.layers, bf16[2,512,4096]{2,1,0:T(8,128)(2,1)S(1)} %get-tuple-element.36.first_inverse, ...), custom_call_target="tpu_custom_call", output_to_operand_aliasing={{3}: (2, {})} | custom-call | tf_op jit(solution)/shard_map/forward_section_0/pallas_call | solution.py:374
  20.9 1.7 %collective-permute-start.5 = (bf16[16,16,128]{2,1,0:T(8,128)(2,1)S(1)}, bf16[16,16,128]{2,1,0:T(8,128)(2,1)S(1)}, u32[]{:S(2)}, u32[]{:S(2)}) collective-permute-start(bf16[16,16,128]{2,1,0:T(8,128)(2,1)S(1)} %get-tuple-element.44), channel_id=1, source_target_pairs={{0,8},{1,9},{2,10},{3,11},{4,12},{5,13},{6,14},{7,15}} | collective-permute-start | bytes 196616 | tf_op jit(solution)/shard_map/ppermute | solution.py:469
  22.7 2.2 %collective-permute-done.5.rest_0_.rest_4_.rest_8_ = bf16[16,16,128]{2,1,0:T(8,128)(2,1)S(1)} collective-permute-done((bf16[16,16,128]{2,1,0:T(8,128)(2,1)S(1)}, bf16[16,16,128]{2,1,0:T(8,128)(2,1)S(1)}, u32[]{:S(2)}, u32[]{:S(2)}) %collective-permute-start.5) | collective-permute-done | bytes 65568 | tf_op jit(solution)/shard_map/ppermute | solution.py:469
  24.9 2.7 %collective-permute-done.6.rest_1_ = bf16[8,16,128]{2,1,0:T(8,128)(2,1)S(1)} collective-permute-done((bf16[8,16,128]{2,1,0:T(8,128)(2,1)S(1)}, bf16[8,16,128]{2,1,0:T(8,128)(2,1)S(1)}, u32[]{:S(2)}, u32[]{:S(2)}) %collective-permute-start.6) | collective-permute-done | bytes 32800 | tf_op jit(solution)/shard_map/ppermute | solution.py:427
  30.4 4.6 %collective-permute-start.12 = (bf16[8,16,128]{2,1,0:T(8,128)(2,1)S(1)}, bf16[8,16,128]{2,1,0:T(8,128)(2,1)S(1)}, u32[]{:S(2)}, u32[]{:S(2)}) collective-permute-start(bf16[8,16,128]{2,1,0:T(8,128)(2,1)S(1)} %get-tuple-element.48), channel_id=1, source_target_pairs={{8,22},{9,23},{10,20},{11,21},{12,18},{13,19},{14,16},{15,17},{16,... | collective-permute-start | bytes 98312 | tf_op jit(solution)/shard_map/ppermute | solution.py:427
  37.1 3.0 %collective-permute-done.14.rest_2_ = bf16[2,8,16,128]{3,2,1,0:T(8,128)(2,1)S(1)} collective-permute-done((bf16[2,8,16,128]{3,2,1,0:T(8,128)(2,1)S(1)}, bf16[2,8,16,128]{3,2,1,0:T(8,128)(2,1)S(1)}, u32[]{:S(2)}, u32[]{:S(2)}) %collective-permute-start.14) | collective-permute-done | bytes 65568 | tf_op jit(solution)/shard_map/ppermute | solution.py:427
  45.2 2.1 %collective-permute-done.17.rest_1_ = bf16[8,16,128]{2,1,0:T(8,128)(2,1)S(1)} collective-permute-done((bf16[8,16,128]{2,1,0:T(8,128)(2,1)S(1)}, bf16[8,16,128]{2,1,0:T(8,128)(2,1)S(1)}, u32[]{:S(2)}, u32[]{:S(2)}) %collective-permute-start.17) | collective-permute-done | bytes 32800 | tf_op jit(solution)/shard_map/ppermute | solution.py:427
  47.3 1.6 %collective-permute-done.19.rest_2_ = bf16[2,8,16,128]{3,2,1,0:T(8,128)(2,1)S(1)} collective-permute-done((bf16[2,8,16,128]{3,2,1,0:T(8,128)(2,1)S(1)}, bf16[2,8,16,128]{3,2,1,0:T(8,128)(2,1)S(1)}, u32[]{:S(2)}, u32[]{:S(2)}) %collective-permute-start.19) | collective-permute-done | bytes 65568 | tf_op jit(solution)/shard_map/ppermute | solution.py:427
  52.7 1.5 %collective-permute-start.21 = (bf16[4,16,128]{2,1,0:T(8,128)(2,1)S(1)}, bf16[4,16,128]{2,1,0:T(8,128)(2,1)S(1)}, u32[]{:S(2)}, u32[]{:S(2)}) collective-permute-start(bf16[4,16,128]{2,1,0:T(8,128)(2,1)S(1)} %get-tuple-element.51.rest_0_), channel_id=1, source_target_pairs={{0,6},{1,7},{2,4},{3,5},{4,2},{5,3},{6,0},{7,1},{8,14},{9,15},{10,... | collective-permute-start | bytes 49160 | tf_op jit(solution)/shard_map/ppermute | solution.py:427
  54.2 3.1 %collective-permute-done.21.rest_1_ = bf16[4,16,128]{2,1,0:T(8,128)(2,1)S(1)} collective-permute-done((bf16[4,16,128]{2,1,0:T(8,128)(2,1)S(1)}, bf16[4,16,128]{2,1,0:T(8,128)(2,1)S(1)}, u32[]{:S(2)}, u32[]{:S(2)}) %collective-permute-start.21) | collective-permute-done | bytes 16416 | tf_op jit(solution)/shard_map/ppermute | solution.py:427
  59.5 1.5 %collective-permute-start.26 = (bf16[8,16,128]{2,1,0:T(8,128)(2,1)S(1)}, bf16[8,16,128]{2,1,0:T(8,128)(2,1)S(1)}, u32[]{:S(2)}, u32[]{:S(2)}) collective-permute-start(bf16[8,16,128]{2,1,0:T(8,128)(2,1)S(1)} %get-tuple-element.54), channel_id=1, source_target_pairs={{24,22},{25,23},{26,20},{27,21},{28,18},{29,19},{30,16},{31,17},{1... | collective-permute-start | bytes 98312 | tf_op jit(solution)/shard_map/ppermute | solution.py:427
  61.6 1.6 %collective-permute-start.28 = (bf16[2,8,16,128]{3,2,1,0:T(8,128)(2,1)S(1)}, bf16[2,8,16,128]{3,2,1,0:T(8,128)(2,1)S(1)}, u32[]{:S(2)}, u32[]{:S(2)}) collective-permute-start(bf16[2,8,16,128]{3,2,1,0:T(8,128)(2,1)S(1)} %pad_maximum_fusion.11), channel_id=1, source_target_pairs={{24,18},{25,21},{26,16},{27,23},{28,22},{29,17},{30,20},{31,19},{1... | collective-permute-start | bytes 196616 | tf_op jit(solution)/shard_map/ppermute | solution.py:427
  64.3 1.7 %collective-permute-done.28.rest_2_ = bf16[2,8,16,128]{3,2,1,0:T(8,128)(2,1)S(1)} collective-permute-done((bf16[2,8,16,128]{3,2,1,0:T(8,128)(2,1)S(1)}, bf16[2,8,16,128]{3,2,1,0:T(8,128)(2,1)S(1)}, u32[]{:S(2)}, u32[]{:S(2)}) %collective-permute-start.28) | collective-permute-done | bytes 65568 | tf_op jit(solution)/shard_map/ppermute | solution.py:427
  70.3 1.5 %collective-permute-start.33 = (bf16[2,8,16,128]{3,2,1,0:T(8,128)(2,1)S(1)}, bf16[2,8,16,128]{3,2,1,0:T(8,128)(2,1)S(1)}, u32[]{:S(2)}, u32[]{:S(2)}) collective-permute-start(bf16[2,8,16,128]{3,2,1,0:T(8,128)(2,1)S(1)} %pad_maximum_fusion.12), channel_id=1, source_target_pairs={{16,10},{17,13},{18,8},{19,15},{20,14},{21,9},{22,12},{23,11},{8,1... | collective-permute-start | bytes 196616 | tf_op jit(solution)/shard_map/ppermute | solution.py:427
  73.0 1.6 %collective-permute-done.33.rest_2_ = bf16[2,8,16,128]{3,2,1,0:T(8,128)(2,1)S(1)} collective-permute-done((bf16[2,8,16,128]{3,2,1,0:T(8,128)(2,1)S(1)}, bf16[2,8,16,128]{3,2,1,0:T(8,128)(2,1)S(1)}, u32[]{:S(2)}, u32[]{:S(2)}) %collective-permute-start.33) | collective-permute-done | bytes 65568 | tf_op jit(solution)/shard_map/ppermute | solution.py:427
  77.1 20.4 %collective-permute-start.36 = (bf16[8,16,128]{2,1,0:T(8,128)(2,1)S(1)}, bf16[8,16,128]{2,1,0:T(8,128)(2,1)S(1)}, u32[]{:S(2)}, u32[]{:S(2)}) collective-permute-start(bf16[8,16,128]{2,1,0:T(8,128)(2,1)S(1)} %get-tuple-element.62), channel_id=1, source_target_pairs={{8,6},{9,7},{10,4},{11,5},{12,2},{13,3},{14,0},{15,1},{0,22},{1,23... | collective-permute-start | bytes 98312 | tf_op jit(solution)/shard_map/ppermute | solution.py:427
  98.8 3.1 %collective-permute-start.38 = (bf16[2,8,16,128]{3,2,1,0:T(8,128)(2,1)S(1)}, bf16[2,8,16,128]{3,2,1,0:T(8,128)(2,1)S(1)}, u32[]{:S(2)}, u32[]{:S(2)}) collective-permute-start(bf16[2,8,16,128]{3,2,1,0:T(8,128)(2,1)S(1)} %pad_maximum_fusion.13), channel_id=1, source_target_pairs={{8,2},{9,5},{10,0},{11,7},{12,6},{13,1},{14,4},{15,3},{0,10},{1,13... | collective-permute-start | bytes 196616 | tf_op jit(solution)/shard_map/ppermute | solution.py:427
  101.9 2.2 %collective-permute-done.35.rest_0_.rest_5_ = bf16[16,16,128]{2,1,0:T(8,128)(2,1)S(1)} collective-permute-done((bf16[16,16,128]{2,1,0:T(8,128)(2,1)S(1)}, bf16[16,16,128]{2,1,0:T(8,128)(2,1)S(1)}, u32[]{:S(2)}, u32[]{:S(2)}) %collective-permute-start.35) | collective-permute-done | bytes 65568 | tf_op jit(solution)/shard_map/ppermute | solution.py:469
  106.7 6.2 %backward_section_0.1 = f32[2,16,1024]{2,1,0:T(8,128)} custom-call(s32[4]{0:T(128)S(1)} %get-tuple-element.35.layers, bf16[2,512,4096]{2,1,0:T(8,128)(2,1)S(1)} %get-tuple-element.36.first_inverse, bf16[2,512,4096]{2,1,0:T(8,128)(2,1)S(1)} %get-tuple-element.43.second_inverse, f32[40,1024]{1,0:T(8,128)S(1)} %get-tuple-element.38.packet, ...), custom_call_target="tpu_custom_call" | custom-call | tf_op jit(solution)/shard_map/backward_section_0/pallas_call | solution.py:374
  (88 shorter events, 31.9 us)
Async XLA Ops:
  2.4 3.2 %collective-permute-start.1 = (bf16[8,16,128]{2,1,0:T(8,128)(2,1)S(1)}, bf16[8,16,128]{2,1,0:T(8,128)(2,1)S(1)}, u32[]{:S(2)}, u32[]{:S(2)}) collective-permute-start(bf16[8,16,128]{2,1,0:T(8,128)(2,1)S(1)} %get-tuple-element.40.refs_0_.rest_1_), channel_id=1, source_target_pairs={{0,1},{1,0},{2,3},{3,2},{4,5},{5,4},{6,7},{7,6},{8,9},{9,8},{10,11... | collective-permute-start | bytes 98312 | tf_op jit(solution)/shard_map/ppermute | solution.py:427
  2.9 9.1 %collective-permute-start.3 = (f32[24,1024]{1,0:T(8,128)S(1)}, f32[24,1024]{1,0:T(8,128)S(1)}, u32[]{:S(2)}, u32[]{:S(2)}) collective-permute-start(f32[24,1024]{1,0:T(8,128)S(1)} %get-tuple-element.41), channel_id=1, source_target_pairs={{0,8},{1,9},{2,10},{3,11},{4,12},{5,13},{6,14},{7,15},{16,24},{17,... | collective-permute-start | bytes 294920 | tf_op jit(solution)/shard_map/ppermute | solution.py:427
  5.6 6.5 %collective-permute-start.2 = (bf16[2,8,16,128]{3,2,1,0:T(8,128)(2,1)S(1)}, bf16[2,8,16,128]{3,2,1,0:T(8,128)(2,1)S(1)}, u32[]{:S(2)}, u32[]{:S(2)}) collective-permute-start(bf16[2,8,16,128]{3,2,1,0:T(8,128)(2,1)S(1)} %pad_maximum_fusion.6), channel_id=1, source_target_pairs={{0,2},{1,5},{2,0},{3,7},{4,6},{5,1},{6,4},{7,3},{8,10},{9,13},{10,... | collective-permute-start | bytes 196616 | tf_op jit(solution)/shard_map/ppermute | solution.py:427
  7.2 4.9 %collective-permute-start = (bf16[8,16,128]{2,1,0:T(8,128)(2,1)S(1)}, bf16[8,16,128]{2,1,0:T(8,128)(2,1)S(1)}, u32[]{:S(2)}, u32[]{:S(2)}) collective-permute-start(bf16[8,16,128]{2,1,0:T(8,128)(2,1)S(1)} %get-tuple-element.40.refs_0_.rest_1_), channel_id=1, source_target_pairs={{0,6},{1,7},{2,4},{3,5},{4,2},{5,3},{6,0},{7,1},{8,14},{9,15},{10,... | collective-permute-start | bytes 98312 | tf_op jit(solution)/shard_map/ppermute | solution.py:427
  20.6 7.7 %collective-permute-start.10 = (f32[40,1024]{1,0:T(8,128)S(1)}, f32[40,1024]{1,0:T(8,128)S(1)}, u32[]{:S(2)}, u32[]{:S(2)}) collective-permute-start(f32[40,1024]{1,0:T(8,128)S(1)} %get-tuple-element.46), channel_id=1, source_target_pairs={{8,16},{9,17},{10,18},{11,19},{12,20},{13,21},{14,22},{15,23},{16,... | collective-permute-start | bytes 491528 | tf_op jit(solution)/shard_map/ppermute | solution.py:427
  20.9 6.7 %collective-permute-start.6 = (bf16[8,16,128]{2,1,0:T(8,128)(2,1)S(1)}, bf16[8,16,128]{2,1,0:T(8,128)(2,1)S(1)}, u32[]{:S(2)}, u32[]{:S(2)}) collective-permute-start(bf16[8,16,128]{2,1,0:T(8,128)(2,1)S(1)} %get-tuple-element.45), channel_id=1, source_target_pairs={{0,14},{1,15},{2,12},{3,13},{4,10},{5,11},{6,8},{7,9},{8,22},{9,23... | collective-permute-start | bytes 98312 | tf_op jit(solution)/shard_map/ppermute | solution.py:427
  20.9 4.0 %collective-permute-start.5 = (bf16[16,16,128]{2,1,0:T(8,128)(2,1)S(1)}, bf16[16,16,128]{2,1,0:T(8,128)(2,1)S(1)}, u32[]{:S(2)}, u32[]{:S(2)}) collective-permute-start(bf16[16,16,128]{2,1,0:T(8,128)(2,1)S(1)} %get-tuple-element.44), channel_id=1, source_target_pairs={{0,8},{1,9},{2,10},{3,11},{4,12},{5,13},{6,14},{7,15}} | collective-permute-start | bytes 196616 | tf_op jit(solution)/shard_map/ppermute | solution.py:469
  22.7 5.5 %collective-permute-start.8 = (bf16[2,8,16,128]{3,2,1,0:T(8,128)(2,1)S(1)}, bf16[2,8,16,128]{3,2,1,0:T(8,128)(2,1)S(1)}, u32[]{:S(2)}, u32[]{:S(2)}) collective-permute-start(bf16[2,8,16,128]{3,2,1,0:T(8,128)(2,1)S(1)} %pad_maximum_fusion.7), channel_id=1, source_target_pairs={{0,10},{1,13},{2,8},{3,15},{4,14},{5,9},{6,12},{7,11},{8,2},{9,5},... | collective-permute-start | bytes 196616 | tf_op jit(solution)/shard_map/ppermute | solution.py:427
  30.2 5.5 %collective-permute-start.13 = (bf16[8,16,128]{2,1,0:T(8,128)(2,1)S(1)}, bf16[8,16,128]{2,1,0:T(8,128)(2,1)S(1)}, u32[]{:S(2)}, u32[]{:S(2)}) collective-permute-start(bf16[8,16,128]{2,1,0:T(8,128)(2,1)S(1)} %get-tuple-element.48), channel_id=1, source_target_pairs={{0,1},{1,0},{2,3},{3,2},{4,5},{5,4},{6,7},{7,6},{8,9},{9,8},{10,11... | collective-permute-start | bytes 98312 | tf_op jit(solution)/shard_map/ppermute | solution.py:427
  30.4 6.6 %collective-permute-start.12 = (bf16[8,16,128]{2,1,0:T(8,128)(2,1)S(1)}, bf16[8,16,128]{2,1,0:T(8,128)(2,1)S(1)}, u32[]{:S(2)}, u32[]{:S(2)}) collective-permute-start(bf16[8,16,128]{2,1,0:T(8,128)(2,1)S(1)} %get-tuple-element.48), channel_id=1, source_target_pairs={{8,22},{9,23},{10,20},{11,21},{12,18},{13,19},{14,16},{15,17},{16,... | collective-permute-start | bytes 98312 | tf_op jit(solution)/shard_map/ppermute | solution.py:427
  35.7 4.3 %collective-permute-start.14 = (bf16[2,8,16,128]{3,2,1,0:T(8,128)(2,1)S(1)}, bf16[2,8,16,128]{3,2,1,0:T(8,128)(2,1)S(1)}, u32[]{:S(2)}, u32[]{:S(2)}) collective-permute-start(bf16[2,8,16,128]{3,2,1,0:T(8,128)(2,1)S(1)} %pad_maximum_fusion.8), channel_id=1, source_target_pairs={{8,18},{9,21},{10,16},{11,23},{12,22},{13,17},{14,20},{15,19},{16,... | collective-permute-start | bytes 196616 | tf_op jit(solution)/shard_map/ppermute | solution.py:427
  42.4 4.8 %collective-permute-start.17 = (bf16[8,16,128]{2,1,0:T(8,128)(2,1)S(1)}, bf16[8,16,128]{2,1,0:T(8,128)(2,1)S(1)}, u32[]{:S(2)}, u32[]{:S(2)}) collective-permute-start(bf16[8,16,128]{2,1,0:T(8,128)(2,1)S(1)} %get-tuple-element.50), channel_id=1, source_target_pairs={{16,30},{17,31},{18,28},{19,29},{20,26},{21,27},{22,24},{23,25},{2... | collective-permute-start | bytes 98312 | tf_op jit(solution)/shard_map/ppermute | solution.py:427
  44.5 4.3 %collective-permute-start.19 = (bf16[2,8,16,128]{3,2,1,0:T(8,128)(2,1)S(1)}, bf16[2,8,16,128]{3,2,1,0:T(8,128)(2,1)S(1)}, u32[]{:S(2)}, u32[]{:S(2)}) collective-permute-start(bf16[2,8,16,128]{3,2,1,0:T(8,128)(2,1)S(1)} %pad_maximum_fusion.9), channel_id=1, source_target_pairs={{16,26},{17,29},{18,24},{19,31},{20,30},{21,25},{22,28},{23,27},{2... | collective-permute-start | bytes 196616 | tf_op jit(solution)/shard_map/ppermute | solution.py:427
  52.1 5.2 %collective-permute-start.23 = (bf16[2,4,16,128]{3,2,1,0:T(8,128)(2,1)S(1)}, bf16[2,4,16,128]{3,2,1,0:T(8,128)(2,1)S(1)}, u32[]{:S(2)}, u32[]{:S(2)}) collective-permute-start(bf16[2,4,16,128]{3,2,1,0:T(8,128)(2,1)S(1)} %pad_maximum_fusion.14), channel_id=1, source_target_pairs={{0,2},{1,5},{2,0},{3,7},{4,6},{5,1},{6,4},{7,3},{8,10},{9,13},{10,... | collective-permute-start | bytes 98312 | tf_op jit(solution)/shard_map/ppermute | solution.py:427
  52.7 4.6 %collective-permute-start.21 = (bf16[4,16,128]{2,1,0:T(8,128)(2,1)S(1)}, bf16[4,16,128]{2,1,0:T(8,128)(2,1)S(1)}, u32[]{:S(2)}, u32[]{:S(2)}) collective-permute-start(bf16[4,16,128]{2,1,0:T(8,128)(2,1)S(1)} %get-tuple-element.51.rest_0_), channel_id=1, source_target_pairs={{0,6},{1,7},{2,4},{3,5},{4,2},{5,3},{6,0},{7,1},{8,14},{9,15},{10,... | collective-permute-start | bytes 49160 | tf_op jit(solution)/shard_map/ppermute | solution.py:427
  59.2 2.4 %collective-permute-start.27 = (bf16[8,16,128]{2,1,0:T(8,128)(2,1)S(1)}, bf16[8,16,128]{2,1,0:T(8,128)(2,1)S(1)}, u32[]{:S(2)}, u32[]{:S(2)}) collective-permute-start(bf16[8,16,128]{2,1,0:T(8,128)(2,1)S(1)} %get-tuple-element.54), channel_id=1, source_target_pairs={{0,1},{1,0},{2,3},{3,2},{4,5},{5,4},{6,7},{7,6},{8,9},{9,8},{10,11... | collective-permute-start | bytes 98312 | tf_op jit(solution)/shard_map/ppermute | solution.py:427
  59.5 4.8 %collective-permute-start.26 = (bf16[8,16,128]{2,1,0:T(8,128)(2,1)S(1)}, bf16[8,16,128]{2,1,0:T(8,128)(2,1)S(1)}, u32[]{:S(2)}, u32[]{:S(2)}) collective-permute-start(bf16[8,16,128]{2,1,0:T(8,128)(2,1)S(1)} %get-tuple-element.54), channel_id=1, source_target_pairs={{24,22},{25,23},{26,20},{27,21},{28,18},{29,19},{30,16},{31,17},{1... | collective-permute-start | bytes 98312 | tf_op jit(solution)/shard_map/ppermute | solution.py:427
  61.6 4.3 %collective-permute-start.28 = (bf16[2,8,16,128]{3,2,1,0:T(8,128)(2,1)S(1)}, bf16[2,8,16,128]{3,2,1,0:T(8,128)(2,1)S(1)}, u32[]{:S(2)}, u32[]{:S(2)}) collective-permute-start(bf16[2,8,16,128]{3,2,1,0:T(8,128)(2,1)S(1)} %pad_maximum_fusion.11), channel_id=1, source_target_pairs={{24,18},{25,21},{26,16},{27,23},{28,22},{29,17},{30,20},{31,19},{1... | collective-permute-start | bytes 196616 | tf_op jit(solution)/shard_map/ppermute | solution.py:427
  68.2 4.8 %collective-permute-start.31 = (bf16[8,16,128]{2,1,0:T(8,128)(2,1)S(1)}, bf16[8,16,128]{2,1,0:T(8,128)(2,1)S(1)}, u32[]{:S(2)}, u32[]{:S(2)}) collective-permute-start(bf16[8,16,128]{2,1,0:T(8,128)(2,1)S(1)} %get-tuple-element.58), channel_id=1, source_target_pairs={{16,14},{17,15},{18,12},{19,13},{20,10},{21,11},{22,8},{23,9},{8,3... | collective-permute-start | bytes 98312 | tf_op jit(solution)/shard_map/ppermute | solution.py:427
  70.3 4.3 %collective-permute-start.33 = (bf16[2,8,16,128]{3,2,1,0:T(8,128)(2,1)S(1)}, bf16[2,8,16,128]{3,2,1,0:T(8,128)(2,1)S(1)}, u32[]{:S(2)}, u32[]{:S(2)}) collective-permute-start(bf16[2,8,16,128]{3,2,1,0:T(8,128)(2,1)S(1)} %pad_maximum_fusion.12), channel_id=1, source_target_pairs={{16,10},{17,13},{18,8},{19,15},{20,14},{21,9},{22,12},{23,11},{8,1... | collective-permute-start | bytes 196616 | tf_op jit(solution)/shard_map/ppermute | solution.py:427
  76.9 21.9 %collective-permute-start.37 = (bf16[8,16,128]{2,1,0:T(8,128)(2,1)S(1)}, bf16[8,16,128]{2,1,0:T(8,128)(2,1)S(1)}, u32[]{:S(2)}, u32[]{:S(2)}) collective-permute-start(bf16[8,16,128]{2,1,0:T(8,128)(2,1)S(1)} %get-tuple-element.62), channel_id=1, source_target_pairs={{0,1},{1,0},{2,3},{3,2},{4,5},{5,4},{6,7},{7,6},{8,9},{9,8},{10,11... | collective-permute-start | bytes 98312 | tf_op jit(solution)/shard_map/ppermute | solution.py:427
  77.1 27.1 %collective-permute-start.36 = (bf16[8,16,128]{2,1,0:T(8,128)(2,1)S(1)}, bf16[8,16,128]{2,1,0:T(8,128)(2,1)S(1)}, u32[]{:S(2)}, u32[]{:S(2)}) collective-permute-start(bf16[8,16,128]{2,1,0:T(8,128)(2,1)S(1)} %get-tuple-element.62), channel_id=1, source_target_pairs={{8,6},{9,7},{10,4},{11,5},{12,2},{13,3},{14,0},{15,1},{0,22},{1,23... | collective-permute-start | bytes 98312 | tf_op jit(solution)/shard_map/ppermute | solution.py:427
  97.5 6.6 %collective-permute-start.35 = (bf16[16,16,128]{2,1,0:T(8,128)(2,1)S(1)}, bf16[16,16,128]{2,1,0:T(8,128)(2,1)S(1)}, u32[]{:S(2)}, u32[]{:S(2)}) collective-permute-start(bf16[16,16,128]{2,1,0:T(8,128)(2,1)S(1)} %get-tuple-element.61), channel_id=1, source_target_pairs={{8,0},{9,1},{10,2},{11,3},{12,4},{13,5},{14,6},{15,7}} | collective-permute-start | bytes 196616 | tf_op jit(solution)/shard_map/ppermute | solution.py:469
  98.8 6.4 %collective-permute-start.38 = (bf16[2,8,16,128]{3,2,1,0:T(8,128)(2,1)S(1)}, bf16[2,8,16,128]{3,2,1,0:T(8,128)(2,1)S(1)}, u32[]{:S(2)}, u32[]{:S(2)}) collective-permute-start(bf16[2,8,16,128]{3,2,1,0:T(8,128)(2,1)S(1)} %pad_maximum_fusion.13), channel_id=1, source_target_pairs={{8,2},{9,5},{10,0},{11,7},{12,6},{13,1},{14,4},{15,3},{0,10},{1,13... | collective-permute-start | bytes 196616 | tf_op jit(solution)/shard_map/ppermute | solution.py:427
  (16 other events, 26.4 us)

commit v12 on v11

--- a/solution.py
+++ b/solution.py
@@ -153,11 +153,11 @@
 
 def first_kernel(
     width, layers_in, rhs_in, isc_in, fwd_in, bwd_in, picked_in, local, ahead, longer, place, front,
-    layers, rhs, isc, fwd, bwd, picked, sems,
+    layers, rhs, isc, fwd, bwd, picked, counts, sems,
 ):
     pairs = (
         (rhs_in, rhs), (isc_in, isc), (fwd_in, fwd), (bwd_in, bwd), (picked_in, picked),
-        (layers_in, layers),
+        (layers_in, counts),
     )
     copies = [pltpu.make_async_copy(a, b, sems.at[i]) for i, (a, b) in enumerate(pairs)]
     for copy in copies:
@@ -166,6 +166,9 @@
         copy.wait()
     cells = rhs.shape[-1]
     count = rhs.shape[1]
+    layers[...] = jnp.zeros(layers.shape, jnp.int32)
+    for section in range(counts.shape[0]):
+        layers[section:section + 1, :] = jnp.full((1, LANES), counts[section], jnp.int32)
     small = local.at[2 * count:]
     small[ISC:ISC + 2, :] = isc[...]
     small[FWD:FWD + 2, :] = fwd[...]
@@ -203,17 +206,12 @@
         place[layer:layer + 1, :] = places(picked[layer:layer + 1, :], cells)
 
 
-def load_kernel(inverse, first, second, done, sems):
-    loads = [
-        pltpu.make_async_copy(inverse.at[layer], half, sems.at[layer])
-        for layer, half in enumerate((first, second))
-    ]
-    later = lax.axis_index("sweep") == 0
-    loads[0].start()
-    pl.when(~later)(loads[1].start)
+def load_kernel(inverse, first, second, done, sem):
+    load = pltpu.make_async_copy(inverse.at[0], first, sem.at[0])
+    load.start()
     done[...] = jnp.zeros(done.shape, F32)
-    loads[0].wait()
-    pl.when(~later)(loads[1].wait)
+    second[:, 0:16, 0:LANES] = jnp.zeros((2, 16, LANES), BF16)
+    load.wait()
 
 
 def join_kernel(*refs):
@@ -225,12 +223,14 @@
             at += 1
 
 
+def two_layers(layers, section):
+    return jnp.max(layers[section:section + 1, :]) == 2
+
+
 def forward_kernel(
-    step, sections, planes, width, per_layer, owners, layers, first_inverse, second_inverse,
-    packet, place, *rest
+    step, sections, planes, width, per_layer, owners, layers, first_inverse, _, inverse, packet,
+    place, *rest
 ):
-    if not step:
-        inverse, *rest = rest
     blocks, rest = rest[:len(owners)], rest[len(owners):]
     final = step == sections - 1
     if step:
@@ -240,35 +240,42 @@
     kept, front, *rest = rest
     if not final:
         outgoing_packet, *rest = rest
-    if step:
-        stacked, solved = rest
-    else:
-        second_inverse, stacked, solved, sems = rest
+    second_inverse, stacked, solved, sems = rest
     own = lax.axis_index("sweep")
     cells = packet.shape[-1]
     count = cells // LANES
     rows = kept.shape[1]
     small = packet.at[2 * rows:]
     mine = own == step
-    both = layers[step] == 2
-    if not step:
-        load = pltpu.make_async_copy(inverse.at[1], second_inverse, sems.at[0])
-        pl.when(mine)(load.start)
-
-    def whole_solve(layer, matrices):
-        stack_fronts(blocks, owners, planes, per_layer, stacked, layer)
-        solve(matrices, stacked, solved, layer)
+    both = two_layers(layers, step)
+
+    cuts = 2
+    depth = inverse.shape[-1] // cuts
+    spans = [(slice(None), slice(None), pl.ds(cut * depth, depth)) for cut in range(cuts)]
+    loads = [
+        pltpu.make_async_copy(inverse.at[(1, *span)], second_inverse.at[span], sems.at[cut])
+        for cut, span in enumerate(spans)
+    ]
+
+    @pl.when(mine & both)
+    def _():
+        for load in loads:
+            load.start()
 
     @pl.when(mine)
     def _():
-        whole_solve(0, first_inverse)
-
-    if not step:
-        pl.when(mine)(load.wait)
+        stack_fronts(blocks, owners, planes, per_layer, stacked, 0)
+        solve(first_inverse, stacked, solved, 0)
 
     @pl.when(mine & both)
     def _():
-        whole_solve(1, second_inverse)
+        stack_fronts(blocks, owners, planes, per_layer, stacked, 1)
+        out = 0
+        for load, (_, _, columns) in zip(loads, spans):
+            load.wait()
+            out = out + product(second_inverse[0, :, columns], stacked[0, :, columns])
+            out = out + product(second_inverse[1, :, columns], stacked[1, :, columns])
+        store_solved(solved, 1, out)
 
     @pl.when(mine)
     def _():
@@ -315,7 +322,7 @@
     count = kept.shape[-1] // LANES
     small = packet.at[2 * kept.shape[1]:]
     mine = own == step
-    both = layers[step] == 2
+    both = two_layers(layers, step)
 
     def whole_solve(layer):
         stack_fronts(blocks, owners, planes, per_layer, stacked, layer)
@@ -354,7 +361,7 @@
         first = minus(first_fwd, change)
         if step:
             chunks = backward_front(
-                behind.at[kept.shape[1]:kept.shape[1] + NEEDS], first, read_field(held, count), layers[step - 1] == 2
+                behind.at[kept.shape[1]:kept.shape[1] + NEEDS], first, read_field(held, count), two_layers(layers, step - 1)
             )
             write_front(front, chunks)
             write_front(outgoing_packet, chunks, first)
@@ -469,7 +476,7 @@
         packet = lax.ppermute(packet, "sweep", [(start, stop)])
         if not direct:
             return *everywhere(packet[:2 * per_layer]), packet
-        third = [i for i in (2 * start - stop, 2 * stop - start) if 0 <= i < sections]
+        third = [i for i in (2 * stop - start, 2 * start - stop) if 0 <= i < sections]
         some, every = cycle(start, stop, *third[:1]), cycle(start, stop)
         return *spread(front, packet, some, every), packet
 
@@ -486,9 +493,10 @@
             ((2 * rows + NEEDS, 2 * width), F32),
             ((2, cells), jnp.int32),
             front_shape,
-            (section_layers.shape, jnp.int32),
+            ((-(-sections // 8) * 8, LANES), jnp.int32),
         ],
-        [pltpu.VMEM(a.shape, a.dtype) for a in operands[1:]] + [pltpu.SemaphoreType.DMA((6,))],
+        [pltpu.VMEM(a.shape, a.dtype) for a in operands[1:]]
+        + [pltpu.SMEM(section_layers.shape, jnp.int32), pltpu.SemaphoreType.DMA((6,))],
         "first_fronts",
         range(6),
     )
@@ -502,7 +510,7 @@
         load_kernel,
         [inverse],
         [half_inverse, half_inverse, ((8, LANES), F32)],
-        [pltpu.SemaphoreType.DMA((2,))],
+        [pltpu.SemaphoreType.DMA((1,))],
         "load_first",
         [0],
     )
@@ -520,21 +528,19 @@
         extra = ([held[step]] if step else []) + ([] if final else [near[step % 2]])
         outs = [layers_shape, half_shape if final else front_shape]
         outs += [] if final else [packet_shape]
-        outs += [] if step else [half_inverse]
+        outs += [half_inverse]
         outs = call(
             functools.partial(
                 forward_kernel, step, sections, planes, width, slots, owners
             ),
-            [layers, first_inverse, second_inverse, local, place]
-            + ([] if step else [inverse]) + [*gathered, *extra],
+            [layers, first_inverse, second_inverse, inverse, local, place, *gathered, *extra],
             outs,
-            scratch + ([] if step else [pltpu.SemaphoreType.DMA((1,))]),
+            scratch + [pltpu.SemaphoreType.DMA((2,))],
             f"forward_section_{step}",
-            [] if step else [5],
-            {} if step else {2: len(outs) - 1},
+            [3],
+            {2: len(outs) - 1},
         )
-        if not step:
-            second_inverse = outs[-1]
+        second_inverse = outs[-1]
         kept.append(outs[0])
         if final:
             gathered, owners, slots = within(outs[1])

time: 113 us -> 112 us (level)
  Pallas kernels: 22.6 us -> 14 us
  starting transfers between devices: 53.1 us -> 60.8 us
    pallas_call x11, Pallas kernels: 22.6 us -> 14 us  [call(): pl.pallas_call(kernel, in_specs=specs, out_specs=[whole(pltpu.SMEM if len...]
    ppermute x34, starting transfers between devices: 47.6 us -> 55 us  [send(): return lax.ppermute(block, ('sweep', 'plane'), route)]
  transfers between devices with their start and end apart: 40 -> 40, of which waited for: 23 -> 22; matrix products, arithmetic and copies ran while one was open for 0% -> 0% of each run, Pallas kernels for 3% -> 3%
where the time goes in v12:
time: 112 us; the launch traced here: 111 us
  starting transfers between devices  60.8 us (54%)
  waiting for transfers between devices  36 us (32%)
  Pallas kernels  14 us (12%)
    ppermute x34, starting transfers between devices, send(): return lax.ppermute(block, ('sweep', 'plane'), route)  55 us
    ppermute x34, waiting for transfers between devices, send(): return lax.ppermute(block, ('sweep', 'plane'), route)  31.6 us
    pallas_call x11, Pallas kernels, call(): pl.pallas_call(kernel, in_specs=specs, out_specs=[whole(pltpu.SMEM if len...  14 us
    ppermute x6, starting transfers between devices, between(): packet = lax.ppermute(packet, 'sweep', [(start, stop)])  5.78 us
    ppermute x6, waiting for transfers between devices, between(): packet = lax.ppermute(packet, 'sweep', [(start, stop)])  4.38 us
  transfers between devices with their start and end apart: 40, of which 22 were waited for; matrix products, arithmetic and copies ran while one was open for 0% of the time, Pallas kernels for 3%

profile of v12, /device:TPU:0, one launch (start us, length us, event | category | flops | bytes accessed | tf_op | source)
XLA Modules:
  0.0 111.4 jit_solution(9781904274672302035)
XLA Ops:
  0.0 2.4 %first_fronts.1 = (f32[40,1024]{1,0:T(8,128)S(1)}, f32[24,1024]{1,0:T(8,128)S(1)}, f32[40,1024]{1,0:T(8,128)S(1)}, s32[2,1024]{1,0:T(2,128)S(1)}, bf16[8,16,128]{2,1,0:T(8,128)(2,1)S(1)}, /*index=5*/s32[8,128]{1,0:T(8,128)S(1)}) custom-call(s32[4]{0:T(128)} %layers_in.1, f32[2,16,1024]{2,1,0:T(8,128)} %bitcast.53, f32[2,1024]{1,0:T(2,128)} %isc_in.1, ...), custom_call_target="tpu_custom_call" | custom-call | tf_op jit(solution)/shard_map/first_fronts/pallas_call | solution.py:381
  2.9 2.6 %collective-permute-start.3 = (f32[24,1024]{1,0:T(8,128)S(1)}, f32[24,1024]{1,0:T(8,128)S(1)}, u32[]{:S(2)}, u32[]{:S(2)}) collective-permute-start(f32[24,1024]{1,0:T(8,128)S(1)} %get-tuple-element.44), channel_id=1, source_target_pairs={{0,8},{1,9},{2,10},{3,11},{4,12},{5,13},{6,14},{7,15},{16,24},{17,... | collective-permute-start | bytes 294920 | tf_op jit(solution)/shard_map/ppermute | solution.py:434
  5.6 1.6 %collective-permute-start.2 = (bf16[2,8,16,128]{3,2,1,0:T(8,128)(2,1)S(1)}, bf16[2,8,16,128]{3,2,1,0:T(8,128)(2,1)S(1)}, u32[]{:S(2)}, u32[]{:S(2)}) collective-permute-start(bf16[2,8,16,128]{3,2,1,0:T(8,128)(2,1)S(1)} %pad_maximum_fusion.6), channel_id=1, source_target_pairs={{0,2},{1,5},{2,0},{3,7},{4,6},{5,1},{6,4},{7,3},{8,10},{9,13},{10,... | collective-permute-start | bytes 196616 | tf_op jit(solution)/shard_map/ppermute | solution.py:434
  8.6 3.4 %load_first.1 = (bf16[2,512,4096]{2,1,0:T(8,128)(2,1)S(1)}, bf16[2,512,4096]{2,1,0:T(8,128)(2,1)S(1)}, f32[8,128]{1,0:T(8,128)S(1)}) custom-call(bf16[2,2,512,4096]{3,2,1,0:T(8,128)(2,1)} %inverse.9), custom_call_target="tpu_custom_call" | custom-call | tf_op jit(solution)/shard_map/load_first/pallas_call | solution.py:381
  13.5 3.1 %forward_section_0.1 = (f32[2,16,1024]{2,1,0:T(8,128)S(1)}, bf16[8,16,128]{2,1,0:T(8,128)(2,1)S(1)}, bf16[16,16,128]{2,1,0:T(8,128)(2,1)S(1)}, bf16[2,512,4096]{2,1,0:T(8,128)(2,1)S(1)}) custom-call(s32[8,128]{1,0:T(8,128)S(1)} %get-tuple-element.38.layers, ...), custom_call_target="tpu_custom_call", output_to_operand_aliasing={{3}: (2, {})} | custom-call | tf_op jit(solution)/shard_map/forward_section_0/pallas_call | solution.py:381
  18.0 1.9 %collective-permute-start.5 = (bf16[16,16,128]{2,1,0:T(8,128)(2,1)S(1)}, bf16[16,16,128]{2,1,0:T(8,128)(2,1)S(1)}, u32[]{:S(2)}, u32[]{:S(2)}) collective-permute-start(bf16[16,16,128]{2,1,0:T(8,128)(2,1)S(1)} %get-tuple-element.47), channel_id=1, source_target_pairs={{0,8},{1,9},{2,10},{3,11},{4,12},{5,13},{6,14},{7,15}} | collective-permute-start | bytes 196616 | tf_op jit(solution)/shard_map/ppermute | solution.py:476
  20.2 1.9 %collective-permute-done.5.rest_0_.rest_4_.rest_8_ = bf16[16,16,128]{2,1,0:T(8,128)(2,1)S(1)} collective-permute-done((bf16[16,16,128]{2,1,0:T(8,128)(2,1)S(1)}, bf16[16,16,128]{2,1,0:T(8,128)(2,1)S(1)}, u32[]{:S(2)}, u32[]{:S(2)}) %collective-permute-start.5) | collective-permute-done | bytes 65568 | tf_op jit(solution)/shard_map/ppermute | solution.py:476
  22.2 1.7 %collective-permute-done.6.rest_1_ = bf16[8,16,128]{2,1,0:T(8,128)(2,1)S(1)} collective-permute-done((bf16[8,16,128]{2,1,0:T(8,128)(2,1)S(1)}, bf16[8,16,128]{2,1,0:T(8,128)(2,1)S(1)}, u32[]{:S(2)}, u32[]{:S(2)}) %collective-permute-start.6) | collective-permute-done | bytes 32800 | tf_op jit(solution)/shard_map/ppermute | solution.py:434
  27.0 1.5 %collective-permute-start.12 = (bf16[8,16,128]{2,1,0:T(8,128)(2,1)S(1)}, bf16[8,16,128]{2,1,0:T(8,128)(2,1)S(1)}, u32[]{:S(2)}, u32[]{:S(2)}) collective-permute-start(bf16[8,16,128]{2,1,0:T(8,128)(2,1)S(1)} %get-tuple-element.52), channel_id=1, source_target_pairs={{8,22},{9,23},{10,20},{11,21},{12,18},{13,19},{14,16},{15,17},{16,... | collective-permute-start | bytes 98312 | tf_op jit(solution)/shard_map/ppermute | solution.py:434
  29.2 1.6 %collective-permute-start.14 = (bf16[2,8,16,128]{3,2,1,0:T(8,128)(2,1)S(1)}, bf16[2,8,16,128]{3,2,1,0:T(8,128)(2,1)S(1)}, u32[]{:S(2)}, u32[]{:S(2)}) collective-permute-start(bf16[2,8,16,128]{3,2,1,0:T(8,128)(2,1)S(1)} %pad_maximum_fusion.8), channel_id=1, source_target_pairs={{8,18},{9,21},{10,16},{11,23},{12,22},{13,17},{14,20},{15,19},{16,... | collective-permute-start | bytes 196616 | tf_op jit(solution)/shard_map/ppermute | solution.py:434
  31.9 1.7 %collective-permute-done.14.rest_2_ = bf16[2,8,16,128]{3,2,1,0:T(8,128)(2,1)S(1)} collective-permute-done((bf16[2,8,16,128]{3,2,1,0:T(8,128)(2,1)S(1)}, bf16[2,8,16,128]{3,2,1,0:T(8,128)(2,1)S(1)}, u32[]{:S(2)}, u32[]{:S(2)}) %collective-permute-start.14) | collective-permute-done | bytes 65568 | tf_op jit(solution)/shard_map/ppermute | solution.py:434
  37.7 1.5 %collective-permute-start.19 = (bf16[2,8,16,128]{3,2,1,0:T(8,128)(2,1)S(1)}, bf16[2,8,16,128]{3,2,1,0:T(8,128)(2,1)S(1)}, u32[]{:S(2)}, u32[]{:S(2)}) collective-permute-start(bf16[2,8,16,128]{3,2,1,0:T(8,128)(2,1)S(1)} %pad_maximum_fusion.9), channel_id=1, source_target_pairs={{16,26},{17,29},{18,24},{19,31},{20,30},{21,25},{22,28},{23,27},{2... | collective-permute-start | bytes 196616 | tf_op jit(solution)/shard_map/ppermute | solution.py:434
  40.4 1.6 %collective-permute-done.19.rest_2_ = bf16[2,8,16,128]{3,2,1,0:T(8,128)(2,1)S(1)} collective-permute-done((bf16[2,8,16,128]{3,2,1,0:T(8,128)(2,1)S(1)}, bf16[2,8,16,128]{3,2,1,0:T(8,128)(2,1)S(1)}, u32[]{:S(2)}, u32[]{:S(2)}) %collective-permute-start.19) | collective-permute-done | bytes 65568 | tf_op jit(solution)/shard_map/ppermute | solution.py:434
  46.4 1.5 %collective-permute-start.21 = (bf16[4,16,128]{2,1,0:T(8,128)(2,1)S(1)}, bf16[4,16,128]{2,1,0:T(8,128)(2,1)S(1)}, u32[]{:S(2)}, u32[]{:S(2)}) collective-permute-start(bf16[4,16,128]{2,1,0:T(8,128)(2,1)S(1)} %get-tuple-element.57.rest_0_), channel_id=1, source_target_pairs={{0,6},{1,7},{2,4},{3,5},{4,2},{5,3},{6,0},{7,1},{8,14},{9,15},{10,... | collective-permute-start | bytes 49160 | tf_op jit(solution)/shard_map/ppermute | solution.py:434
  48.0 3.1 %collective-permute-done.21.rest_1_ = bf16[4,16,128]{2,1,0:T(8,128)(2,1)S(1)} collective-permute-done((bf16[4,16,128]{2,1,0:T(8,128)(2,1)S(1)}, bf16[4,16,128]{2,1,0:T(8,128)(2,1)S(1)}, u32[]{:S(2)}, u32[]{:S(2)}) %collective-permute-start.21) | collective-permute-done | bytes 16416 | tf_op jit(solution)/shard_map/ppermute | solution.py:434
  52.9 1.5 %collective-permute-start.26 = (bf16[8,16,128]{2,1,0:T(8,128)(2,1)S(1)}, bf16[8,16,128]{2,1,0:T(8,128)(2,1)S(1)}, u32[]{:S(2)}, u32[]{:S(2)}) collective-permute-start(bf16[8,16,128]{2,1,0:T(8,128)(2,1)S(1)} %get-tuple-element.60), channel_id=1, source_target_pairs={{24,22},{25,23},{26,20},{27,21},{28,18},{29,19},{30,16},{31,17},{1... | collective-permute-start | bytes 98312 | tf_op jit(solution)/shard_map/ppermute | solution.py:434
  55.7 2.0 %collective-permute-done.26.rest_1_ = bf16[8,16,128]{2,1,0:T(8,128)(2,1)S(1)} collective-permute-done((bf16[8,16,128]{2,1,0:T(8,128)(2,1)S(1)}, bf16[8,16,128]{2,1,0:T(8,128)(2,1)S(1)}, u32[]{:S(2)}, u32[]{:S(2)}) %collective-permute-start.26) | collective-permute-done | bytes 32800 | tf_op jit(solution)/shard_map/ppermute | solution.py:434
  57.7 1.7 %collective-permute-done.28.rest_2_ = bf16[2,8,16,128]{3,2,1,0:T(8,128)(2,1)S(1)} collective-permute-done((bf16[2,8,16,128]{3,2,1,0:T(8,128)(2,1)S(1)}, bf16[2,8,16,128]{3,2,1,0:T(8,128)(2,1)S(1)}, u32[]{:S(2)}, u32[]{:S(2)}) %collective-permute-start.28) | collective-permute-done | bytes 65568 | tf_op jit(solution)/shard_map/ppermute | solution.py:434
  61.5 26.8 %collective-permute-start.31 = (bf16[8,16,128]{2,1,0:T(8,128)(2,1)S(1)}, bf16[8,16,128]{2,1,0:T(8,128)(2,1)S(1)}, u32[]{:S(2)}, u32[]{:S(2)}) collective-permute-start(bf16[8,16,128]{2,1,0:T(8,128)(2,1)S(1)} %get-tuple-element.64), channel_id=1, source_target_pairs={{16,14},{17,15},{18,12},{19,13},{20,10},{21,11},{22,8},{23,9},{8,6... | collective-permute-start | bytes 98312 | tf_op jit(solution)/shard_map/ppermute | solution.py:434
  90.2 3.1 %collective-permute-done.33.rest_2_ = bf16[2,8,16,128]{3,2,1,0:T(8,128)(2,1)S(1)} collective-permute-done((bf16[2,8,16,128]{3,2,1,0:T(8,128)(2,1)S(1)}, bf16[2,8,16,128]{3,2,1,0:T(8,128)(2,1)S(1)}, u32[]{:S(2)}, u32[]{:S(2)}) %collective-permute-start.33) | collective-permute-done | bytes 65568 | tf_op jit(solution)/shard_map/ppermute | solution.py:434
  95.2 2.3 %collective-permute-start.36 = (bf16[8,16,128]{2,1,0:T(8,128)(2,1)S(1)}, bf16[8,16,128]{2,1,0:T(8,128)(2,1)S(1)}, u32[]{:S(2)}, u32[]{:S(2)}) collective-permute-start(bf16[8,16,128]{2,1,0:T(8,128)(2,1)S(1)} %get-tuple-element.68), channel_id=1, source_target_pairs={{8,6},{9,7},{10,4},{11,5},{12,2},{13,3},{14,0},{15,1},{0,22},{1,23... | collective-permute-start | bytes 98312 | tf_op jit(solution)/shard_map/ppermute | solution.py:434
  98.8 3.8 %collective-permute-start.38 = (bf16[2,8,16,128]{3,2,1,0:T(8,128)(2,1)S(1)}, bf16[2,8,16,128]{3,2,1,0:T(8,128)(2,1)S(1)}, u32[]{:S(2)}, u32[]{:S(2)}) collective-permute-start(bf16[2,8,16,128]{3,2,1,0:T(8,128)(2,1)S(1)} %pad_maximum_fusion.13), channel_id=1, source_target_pairs={{8,2},{9,5},{10,0},{11,7},{12,6},{13,1},{14,4},{15,3},{0,10},{1,13... | collective-permute-start | bytes 196616 | tf_op jit(solution)/shard_map/ppermute | solution.py:434
  102.6 2.5 %collective-permute-done.35.rest_0_.rest_5_ = bf16[16,16,128]{2,1,0:T(8,128)(2,1)S(1)} collective-permute-done((bf16[16,16,128]{2,1,0:T(8,128)(2,1)S(1)}, bf16[16,16,128]{2,1,0:T(8,128)(2,1)S(1)}, u32[]{:S(2)}, u32[]{:S(2)}) %collective-permute-start.35) | collective-permute-done | bytes 65568 | tf_op jit(solution)/shard_map/ppermute | solution.py:476
  107.9 3.4 %backward_section_0.1 = f32[2,16,1024]{2,1,0:T(8,128)} custom-call(s32[8,128]{1,0:T(8,128)S(1)} %get-tuple-element.38.layers, bf16[2,512,4096]{2,1,0:T(8,128)(2,1)S(1)} %get-tuple-element.39.first_inverse, bf16[2,512,4096]{2,1,0:T(8,128)(2,1)S(1)} %get-tuple-element.56.second_inverse, f32[40,1024]{1,0:T(8,128)S(1)} %get-tuple-element.41.packet, ...), custom_call_target="tpu_custom_call" | custom-call | tf_op jit(solution)/shard_map/backward_section_0/pallas_call | solution.py:381
  (88 shorter events, 32.7 us)
Async XLA Ops:
  2.4 3.2 %collective-permute-start.1 = (bf16[8,16,128]{2,1,0:T(8,128)(2,1)S(1)}, bf16[8,16,128]{2,1,0:T(8,128)(2,1)S(1)}, u32[]{:S(2)}, u32[]{:S(2)}) collective-permute-start(bf16[8,16,128]{2,1,0:T(8,128)(2,1)S(1)} %get-tuple-element.43.refs_0_.rest_0_), channel_id=1, source_target_pairs={{0,1},{1,0},{2,3},{3,2},{4,5},{5,4},{6,7},{7,6},{8,9},{9,8},{10,11... | collective-permute-start | bytes 98312 | tf_op jit(solution)/shard_map/ppermute | solution.py:434
  2.9 9.1 %collective-permute-start.3 = (f32[24,1024]{1,0:T(8,128)S(1)}, f32[24,1024]{1,0:T(8,128)S(1)}, u32[]{:S(2)}, u32[]{:S(2)}) collective-permute-start(f32[24,1024]{1,0:T(8,128)S(1)} %get-tuple-element.44), channel_id=1, source_target_pairs={{0,8},{1,9},{2,10},{3,11},{4,12},{5,13},{6,14},{7,15},{16,24},{17,... | collective-permute-start | bytes 294920 | tf_op jit(solution)/shard_map/ppermute | solution.py:434
  5.6 6.5 %collective-permute-start.2 = (bf16[2,8,16,128]{3,2,1,0:T(8,128)(2,1)S(1)}, bf16[2,8,16,128]{3,2,1,0:T(8,128)(2,1)S(1)}, u32[]{:S(2)}, u32[]{:S(2)}) collective-permute-start(bf16[2,8,16,128]{3,2,1,0:T(8,128)(2,1)S(1)} %pad_maximum_fusion.6), channel_id=1, source_target_pairs={{0,2},{1,5},{2,0},{3,7},{4,6},{5,1},{6,4},{7,3},{8,10},{9,13},{10,... | collective-permute-start | bytes 196616 | tf_op jit(solution)/shard_map/ppermute | solution.py:434
  7.1 4.9 %collective-permute-start = (bf16[8,16,128]{2,1,0:T(8,128)(2,1)S(1)}, bf16[8,16,128]{2,1,0:T(8,128)(2,1)S(1)}, u32[]{:S(2)}, u32[]{:S(2)}) collective-permute-start(bf16[8,16,128]{2,1,0:T(8,128)(2,1)S(1)} %get-tuple-element.43.refs_0_.rest_0_), channel_id=1, source_target_pairs={{0,6},{1,7},{2,4},{3,5},{4,2},{5,3},{6,0},{7,1},{8,14},{9,15},{10,... | collective-permute-start | bytes 98312 | tf_op jit(solution)/shard_map/ppermute | solution.py:434
  16.6 3.3 %collective-permute-start.7 = (bf16[8,16,128]{2,1,0:T(8,128)(2,1)S(1)}, bf16[8,16,128]{2,1,0:T(8,128)(2,1)S(1)}, u32[]{:S(2)}, u32[]{:S(2)}) collective-permute-start(bf16[8,16,128]{2,1,0:T(8,128)(2,1)S(1)} %get-tuple-element.48), channel_id=1, source_target_pairs={{0,1},{1,0},{2,3},{3,2},{4,5},{5,4},{6,7},{7,6},{8,9},{9,8},{10,11... | collective-permute-start | bytes 98312 | tf_op jit(solution)/shard_map/ppermute | solution.py:434
  16.8 8.5 %collective-permute-start.10 = (f32[40,1024]{1,0:T(8,128)S(1)}, f32[40,1024]{1,0:T(8,128)S(1)}, u32[]{:S(2)}, u32[]{:S(2)}) collective-permute-start(f32[40,1024]{1,0:T(8,128)S(1)} %get-tuple-element.49), channel_id=1, source_target_pairs={{8,16},{9,17},{10,18},{11,19},{12,20},{13,21},{14,22},{15,23},{16,... | collective-permute-start | bytes 491528 | tf_op jit(solution)/shard_map/ppermute | solution.py:434
  17.2 6.7 %collective-permute-start.6 = (bf16[8,16,128]{2,1,0:T(8,128)(2,1)S(1)}, bf16[8,16,128]{2,1,0:T(8,128)(2,1)S(1)}, u32[]{:S(2)}, u32[]{:S(2)}) collective-permute-start(bf16[8,16,128]{2,1,0:T(8,128)(2,1)S(1)} %get-tuple-element.48), channel_id=1, source_target_pairs={{0,14},{1,15},{2,12},{3,13},{4,10},{5,11},{6,8},{7,9},{8,22},{9,23... | collective-permute-start | bytes 98312 | tf_op jit(solution)/shard_map/ppermute | solution.py:434
  18.0 4.2 %collective-permute-start.5 = (bf16[16,16,128]{2,1,0:T(8,128)(2,1)S(1)}, bf16[16,16,128]{2,1,0:T(8,128)(2,1)S(1)}, u32[]{:S(2)}, u32[]{:S(2)}) collective-permute-start(bf16[16,16,128]{2,1,0:T(8,128)(2,1)S(1)} %get-tuple-element.47), channel_id=1, source_target_pairs={{0,8},{1,9},{2,10},{3,11},{4,12},{5,13},{6,14},{7,15}} | collective-permute-start | bytes 196616 | tf_op jit(solution)/shard_map/ppermute | solution.py:476
  19.9 5.2 %collective-permute-start.8 = (bf16[2,8,16,128]{3,2,1,0:T(8,128)(2,1)S(1)}, bf16[2,8,16,128]{3,2,1,0:T(8,128)(2,1)S(1)}, u32[]{:S(2)}, u32[]{:S(2)}) collective-permute-start(bf16[2,8,16,128]{3,2,1,0:T(8,128)(2,1)S(1)} %pad_maximum_fusion.7), channel_id=1, source_target_pairs={{0,10},{1,13},{2,8},{3,15},{4,14},{5,9},{6,12},{7,11},{8,2},{9,5},... | collective-permute-start | bytes 196616 | tf_op jit(solution)/shard_map/ppermute | solution.py:434
  27.0 4.8 %collective-permute-start.12 = (bf16[8,16,128]{2,1,0:T(8,128)(2,1)S(1)}, bf16[8,16,128]{2,1,0:T(8,128)(2,1)S(1)}, u32[]{:S(2)}, u32[]{:S(2)}) collective-permute-start(bf16[8,16,128]{2,1,0:T(8,128)(2,1)S(1)} %get-tuple-element.52), channel_id=1, source_target_pairs={{8,22},{9,23},{10,20},{11,21},{12,18},{13,19},{14,16},{15,17},{16,... | collective-permute-start | bytes 98312 | tf_op jit(solution)/shard_map/ppermute | solution.py:434
  29.2 4.3 %collective-permute-start.14 = (bf16[2,8,16,128]{3,2,1,0:T(8,128)(2,1)S(1)}, bf16[2,8,16,128]{3,2,1,0:T(8,128)(2,1)S(1)}, u32[]{:S(2)}, u32[]{:S(2)}) collective-permute-start(bf16[2,8,16,128]{3,2,1,0:T(8,128)(2,1)S(1)} %pad_maximum_fusion.8), channel_id=1, source_target_pairs={{8,18},{9,21},{10,16},{11,23},{12,22},{13,17},{14,20},{15,19},{16,... | collective-permute-start | bytes 196616 | tf_op jit(solution)/shard_map/ppermute | solution.py:434
  35.6 4.8 %collective-permute-start.17 = (bf16[8,16,128]{2,1,0:T(8,128)(2,1)S(1)}, bf16[8,16,128]{2,1,0:T(8,128)(2,1)S(1)}, u32[]{:S(2)}, u32[]{:S(2)}) collective-permute-start(bf16[8,16,128]{2,1,0:T(8,128)(2,1)S(1)} %get-tuple-element.55), channel_id=1, source_target_pairs={{16,30},{17,31},{18,28},{19,29},{20,26},{21,27},{22,24},{23,25},{2... | collective-permute-start | bytes 98312 | tf_op jit(solution)/shard_map/ppermute | solution.py:434
  37.7 4.3 %collective-permute-start.19 = (bf16[2,8,16,128]{3,2,1,0:T(8,128)(2,1)S(1)}, bf16[2,8,16,128]{3,2,1,0:T(8,128)(2,1)S(1)}, u32[]{:S(2)}, u32[]{:S(2)}) collective-permute-start(bf16[2,8,16,128]{3,2,1,0:T(8,128)(2,1)S(1)} %pad_maximum_fusion.9), channel_id=1, source_target_pairs={{16,26},{17,29},{18,24},{19,31},{20,30},{21,25},{22,28},{23,27},{2... | collective-permute-start | bytes 196616 | tf_op jit(solution)/shard_map/ppermute | solution.py:434
  45.0 6.1 %collective-permute-start.23 = (bf16[2,4,16,128]{3,2,1,0:T(8,128)(2,1)S(1)}, bf16[2,4,16,128]{3,2,1,0:T(8,128)(2,1)S(1)}, u32[]{:S(2)}, u32[]{:S(2)}) collective-permute-start(bf16[2,4,16,128]{3,2,1,0:T(8,128)(2,1)S(1)} %pad_maximum_fusion.14), channel_id=1, source_target_pairs={{0,2},{1,5},{2,0},{3,7},{4,6},{5,1},{6,4},{7,3},{8,10},{9,13},{10,... | collective-permute-start | bytes 98312 | tf_op jit(solution)/shard_map/ppermute | solution.py:434
  46.4 4.6 %collective-permute-start.21 = (bf16[4,16,128]{2,1,0:T(8,128)(2,1)S(1)}, bf16[4,16,128]{2,1,0:T(8,128)(2,1)S(1)}, u32[]{:S(2)}, u32[]{:S(2)}) collective-permute-start(bf16[4,16,128]{2,1,0:T(8,128)(2,1)S(1)} %get-tuple-element.57.rest_0_), channel_id=1, source_target_pairs={{0,6},{1,7},{2,4},{3,5},{4,2},{5,3},{6,0},{7,1},{8,14},{9,15},{10,... | collective-permute-start | bytes 49160 | tf_op jit(solution)/shard_map/ppermute | solution.py:434
  52.9 4.8 %collective-permute-start.26 = (bf16[8,16,128]{2,1,0:T(8,128)(2,1)S(1)}, bf16[8,16,128]{2,1,0:T(8,128)(2,1)S(1)}, u32[]{:S(2)}, u32[]{:S(2)}) collective-permute-start(bf16[8,16,128]{2,1,0:T(8,128)(2,1)S(1)} %get-tuple-element.60), channel_id=1, source_target_pairs={{24,22},{25,23},{26,20},{27,21},{28,18},{29,19},{30,16},{31,17},{1... | collective-permute-start | bytes 98312 | tf_op jit(solution)/shard_map/ppermute | solution.py:434
  55.1 4.3 %collective-permute-start.28 = (bf16[2,8,16,128]{3,2,1,0:T(8,128)(2,1)S(1)}, bf16[2,8,16,128]{3,2,1,0:T(8,128)(2,1)S(1)}, u32[]{:S(2)}, u32[]{:S(2)}) collective-permute-start(bf16[2,8,16,128]{3,2,1,0:T(8,128)(2,1)S(1)} %pad_maximum_fusion.11), channel_id=1, source_target_pairs={{24,18},{25,21},{26,16},{27,23},{28,22},{29,17},{30,20},{31,19},{1... | collective-permute-start | bytes 196616 | tf_op jit(solution)/shard_map/ppermute | solution.py:434
  61.3 27.7 %collective-permute-start.32 = (bf16[8,16,128]{2,1,0:T(8,128)(2,1)S(1)}, bf16[8,16,128]{2,1,0:T(8,128)(2,1)S(1)}, u32[]{:S(2)}, u32[]{:S(2)}) collective-permute-start(bf16[8,16,128]{2,1,0:T(8,128)(2,1)S(1)} %get-tuple-element.64), channel_id=1, source_target_pairs={{0,1},{1,0},{2,3},{3,2},{4,5},{5,4},{6,7},{7,6},{8,9},{9,8},{10,11... | collective-permute-start | bytes 98312 | tf_op jit(solution)/shard_map/ppermute | solution.py:434
  61.5 28.7 %collective-permute-start.31 = (bf16[8,16,128]{2,1,0:T(8,128)(2,1)S(1)}, bf16[8,16,128]{2,1,0:T(8,128)(2,1)S(1)}, u32[]{:S(2)}, u32[]{:S(2)}) collective-permute-start(bf16[8,16,128]{2,1,0:T(8,128)(2,1)S(1)} %get-tuple-element.64), channel_id=1, source_target_pairs={{16,14},{17,15},{18,12},{19,13},{20,10},{21,11},{22,8},{23,9},{8,6... | collective-permute-start | bytes 98312 | tf_op jit(solution)/shard_map/ppermute | solution.py:434
  89.0 4.3 %collective-permute-start.33 = (bf16[2,8,16,128]{3,2,1,0:T(8,128)(2,1)S(1)}, bf16[2,8,16,128]{3,2,1,0:T(8,128)(2,1)S(1)}, u32[]{:S(2)}, u32[]{:S(2)}) collective-permute-start(bf16[2,8,16,128]{3,2,1,0:T(8,128)(2,1)S(1)} %pad_maximum_fusion.12), channel_id=1, source_target_pairs={{16,10},{17,13},{18,8},{19,15},{20,14},{21,9},{22,12},{23,11},{8,1... | collective-permute-start | bytes 196616 | tf_op jit(solution)/shard_map/ppermute | solution.py:434
  95.0 3.8 %collective-permute-start.37 = (bf16[8,16,128]{2,1,0:T(8,128)(2,1)S(1)}, bf16[8,16,128]{2,1,0:T(8,128)(2,1)S(1)}, u32[]{:S(2)}, u32[]{:S(2)}) collective-permute-start(bf16[8,16,128]{2,1,0:T(8,128)(2,1)S(1)} %get-tuple-element.68), channel_id=1, source_target_pairs={{0,1},{1,0},{2,3},{3,2},{4,5},{5,4},{6,7},{7,6},{8,9},{9,8},{10,11... | collective-permute-start | bytes 98312 | tf_op jit(solution)/shard_map/ppermute | solution.py:434
  95.2 9.8 %collective-permute-start.36 = (bf16[8,16,128]{2,1,0:T(8,128)(2,1)S(1)}, bf16[8,16,128]{2,1,0:T(8,128)(2,1)S(1)}, u32[]{:S(2)}, u32[]{:S(2)}) collective-permute-start(bf16[8,16,128]{2,1,0:T(8,128)(2,1)S(1)} %get-tuple-element.68), channel_id=1, source_target_pairs={{8,6},{9,7},{10,4},{11,5},{12,2},{13,3},{14,0},{15,1},{0,22},{1,23... | collective-permute-start | bytes 98312 | tf_op jit(solution)/shard_map/ppermute | solution.py:434
  97.5 7.5 %collective-permute-start.35 = (bf16[16,16,128]{2,1,0:T(8,128)(2,1)S(1)}, bf16[16,16,128]{2,1,0:T(8,128)(2,1)S(1)}, u32[]{:S(2)}, u32[]{:S(2)}) collective-permute-start(bf16[16,16,128]{2,1,0:T(8,128)(2,1)S(1)} %get-tuple-element.67), channel_id=1, source_target_pairs={{8,0},{9,1},{10,2},{11,3},{12,4},{13,5},{14,6},{15,7}} | collective-permute-start | bytes 196616 | tf_op jit(solution)/shard_map/ppermute | solution.py:476
  98.8 7.7 %collective-permute-start.38 = (bf16[2,8,16,128]{3,2,1,0:T(8,128)(2,1)S(1)}, bf16[2,8,16,128]{3,2,1,0:T(8,128)(2,1)S(1)}, u32[]{:S(2)}, u32[]{:S(2)}) collective-permute-start(bf16[2,8,16,128]{3,2,1,0:T(8,128)(2,1)S(1)} %pad_maximum_fusion.13), channel_id=1, source_target_pairs={{8,2},{9,5},{10,0},{11,7},{12,6},{13,1},{14,4},{15,3},{0,10},{1,13... | collective-permute-start | bytes 196616 | tf_op jit(solution)/shard_map/ppermute | solution.py:434
  (16 other events, 27.2 us)

commit v13 on v12

--- a/solution.py
+++ b/solution.py
@@ -249,18 +249,22 @@
     mine = own == step
     both = two_layers(layers, step)
 
-    cuts = 2
-    depth = inverse.shape[-1] // cuts
-    spans = [(slice(None), slice(None), pl.ds(cut * depth, depth)) for cut in range(cuts)]
     loads = [
-        pltpu.make_async_copy(inverse.at[(1, *span)], second_inverse.at[span], sems.at[cut])
-        for cut, span in enumerate(spans)
+        pltpu.make_async_copy(inverse.at[1, part], second_inverse.at[part], sems.at[part])
+        for part in range(2)
     ]
-
-    @pl.when(mine & both)
-    def _():
-        for load in loads:
-            load.start()
+    early = own >= 3
+
+    def when(condition, *actions):
+        @pl.when(condition)
+        def _():
+            for action in actions:
+                action()
+
+    starts, waits = [load.start for load in loads], [load.wait for load in loads]
+    if step == 1:
+        when(early, *starts, *waits)
+    when(mine & both & ~early, *starts)
 
     @pl.when(mine)
     def _():
@@ -270,12 +274,10 @@
     @pl.when(mine & both)
     def _():
         stack_fronts(blocks, owners, planes, per_layer, stacked, 1)
-        out = 0
-        for load, (_, _, columns) in zip(loads, spans):
-            load.wait()
-            out = out + product(second_inverse[0, :, columns], stacked[0, :, columns])
-            out = out + product(second_inverse[1, :, columns], stacked[1, :, columns])
-        store_solved(solved, 1, out)
+        when(~early, waits[0])
+        out = product(second_inverse[0], stacked[0])
+        when(~early, waits[1])
+        store_solved(solved, 1, out + product(second_inverse[1], stacked[1]))
 
     @pl.when(mine)
     def _():
@@ -476,7 +478,8 @@
         packet = lax.ppermute(packet, "sweep", [(start, stop)])
         if not direct:
             return *everywhere(packet[:2 * per_layer]), packet
-        third = [i for i in (2 * stop - start, 2 * start - stop) if 0 <= i < sections]
+        ahead_of = 2 * stop - start, 3 * start - 2 * stop, 2 * start - stop
+        third = [i for i in ahead_of if 0 <= i < sections]
         some, every = cycle(start, stop, *third[:1]), cycle(start, stop)
         return *spread(front, packet, some, every), packet
 

time: 112 us -> 107 us (0.955)
  starting transfers between devices: 60.8 us -> 56.1 us
    ppermute x34, starting transfers between devices: 55 us -> 50.4 us  [send(): return lax.ppermute(block, ('sweep', 'plane'), route)]
    ppermute x34, waiting for transfers between devices: 31.6 us -> 32.8 us  [send(): return lax.ppermute(block, ('sweep', 'plane'), route)]
where the time goes in v13:
time: 107 us
  starting transfers between devices  56.1 us (52%)
  waiting for transfers between devices  36.6 us (34%)
  Pallas kernels  13.8 us (13%)
    ppermute x34, starting transfers between devices, send(): return lax.ppermute(block, ('sweep', 'plane'), route)  50.4 us
    ppermute x34, waiting for transfers between devices, send(): return lax.ppermute(block, ('sweep', 'plane'), route)  32.8 us
    pallas_call x11, Pallas kernels, call(): pl.pallas_call(kernel, in_specs=specs, out_specs=[whole(pltpu.SMEM if len...  13.8 us
    ppermute x6, starting transfers between devices, between(): packet = lax.ppermute(packet, 'sweep', [(start, stop)])  5.78 us
    ppermute x6, waiting for transfers between devices, between(): packet = lax.ppermute(packet, 'sweep', [(start, stop)])  3.86 us
  transfers between devices with their start and end apart: 40, of which 22 were waited for; matrix products, arithmetic and copies ran while one was open for 0% of the time, Pallas kernels for 3%

profile of v13, /device:TPU:0, one launch (start us, length us, event | category | flops | bytes accessed | tf_op | source)
XLA Modules:
  0.0 107.2 jit_solution(8767608288927796225)
XLA Ops:
  0.0 2.4 %first_fronts.1 = (f32[40,1024]{1,0:T(8,128)S(1)}, f32[24,1024]{1,0:T(8,128)S(1)}, f32[40,1024]{1,0:T(8,128)S(1)}, s32[2,1024]{1,0:T(2,128)S(1)}, bf16[8,16,128]{2,1,0:T(8,128)(2,1)S(1)}, /*index=5*/s32[8,128]{1,0:T(8,128)S(1)}) custom-call(s32[4]{0:T(128)} %layers_in.1, f32[2,16,1024]{2,1,0:T(8,128)} %bitcast.53, f32[2,1024]{1,0:T(2,128)} %isc_in.1, ...), custom_call_target="tpu_custom_call" | custom-call | tf_op jit(solution)/shard_map/first_fronts/pallas_call | solution.py:383
  2.9 2.6 %collective-permute-start.3 = (f32[24,1024]{1,0:T(8,128)S(1)}, f32[24,1024]{1,0:T(8,128)S(1)}, u32[]{:S(2)}, u32[]{:S(2)}) collective-permute-start(f32[24,1024]{1,0:T(8,128)S(1)} %get-tuple-element.44), channel_id=1, source_target_pairs={{0,8},{1,9},{2,10},{3,11},{4,12},{5,13},{6,14},{7,15},{16,24},{17,... | collective-permute-start | bytes 294920 | tf_op jit(solution)/shard_map/ppermute | solution.py:436
  5.6 1.6 %collective-permute-start.2 = (bf16[2,8,16,128]{3,2,1,0:T(8,128)(2,1)S(1)}, bf16[2,8,16,128]{3,2,1,0:T(8,128)(2,1)S(1)}, u32[]{:S(2)}, u32[]{:S(2)}) collective-permute-start(bf16[2,8,16,128]{3,2,1,0:T(8,128)(2,1)S(1)} %pad_maximum_fusion.6), channel_id=1, source_target_pairs={{0,2},{1,5},{2,0},{3,7},{4,6},{5,1},{6,4},{7,3},{8,10},{9,13},{10,... | collective-permute-start | bytes 196616 | tf_op jit(solution)/shard_map/ppermute | solution.py:436
  7.1 1.5 %collective-permute-start = (bf16[8,16,128]{2,1,0:T(8,128)(2,1)S(1)}, bf16[8,16,128]{2,1,0:T(8,128)(2,1)S(1)}, u32[]{:S(2)}, u32[]{:S(2)}) collective-permute-start(bf16[8,16,128]{2,1,0:T(8,128)(2,1)S(1)} %get-tuple-element.43.refs_0_.rest_0_), channel_id=1, source_target_pairs={{0,6},{1,7},{2,4},{3,5},{4,2},{5,3},{6,0},{7,1},{8,14},{9,15},{10,... | collective-permute-start | bytes 98312 | tf_op jit(solution)/shard_map/ppermute | solution.py:436
  8.6 3.4 %load_first.1 = (bf16[2,512,4096]{2,1,0:T(8,128)(2,1)S(1)}, bf16[2,512,4096]{2,1,0:T(8,128)(2,1)S(1)}, f32[8,128]{1,0:T(8,128)S(1)}) custom-call(bf16[2,2,512,4096]{3,2,1,0:T(8,128)(2,1)} %inverse.9), custom_call_target="tpu_custom_call" | custom-call | tf_op jit(solution)/shard_map/load_first/pallas_call | solution.py:383
  13.5 3.1 %forward_section_0.1 = (f32[2,16,1024]{2,1,0:T(8,128)S(1)}, bf16[8,16,128]{2,1,0:T(8,128)(2,1)S(1)}, bf16[16,16,128]{2,1,0:T(8,128)(2,1)S(1)}, bf16[2,512,4096]{2,1,0:T(8,128)(2,1)S(1)}) custom-call(s32[8,128]{1,0:T(8,128)S(1)} %get-tuple-element.38.layers, ...), custom_call_target="tpu_custom_call", output_to_operand_aliasing={{3}: (2, {})} | custom-call | tf_op jit(solution)/shard_map/forward_section_0/pallas_call | solution.py:383
  18.0 1.9 %collective-permute-start.5 = (bf16[16,16,128]{2,1,0:T(8,128)(2,1)S(1)}, bf16[16,16,128]{2,1,0:T(8,128)(2,1)S(1)}, u32[]{:S(2)}, u32[]{:S(2)}) collective-permute-start(bf16[16,16,128]{2,1,0:T(8,128)(2,1)S(1)} %get-tuple-element.47), channel_id=1, source_target_pairs={{0,8},{1,9},{2,10},{3,11},{4,12},{5,13},{6,14},{7,15}} | collective-permute-start | bytes 196616 | tf_op jit(solution)/shard_map/ppermute | solution.py:478
  20.2 1.9 %collective-permute-done.5.rest_0_.rest_4_.rest_8_ = bf16[16,16,128]{2,1,0:T(8,128)(2,1)S(1)} collective-permute-done((bf16[16,16,128]{2,1,0:T(8,128)(2,1)S(1)}, bf16[16,16,128]{2,1,0:T(8,128)(2,1)S(1)}, u32[]{:S(2)}, u32[]{:S(2)}) %collective-permute-start.5) | collective-permute-done | bytes 65568 | tf_op jit(solution)/shard_map/ppermute | solution.py:478
  22.2 1.7 %collective-permute-done.6.rest_1_ = bf16[8,16,128]{2,1,0:T(8,128)(2,1)S(1)} collective-permute-done((bf16[8,16,128]{2,1,0:T(8,128)(2,1)S(1)}, bf16[8,16,128]{2,1,0:T(8,128)(2,1)S(1)}, u32[]{:S(2)}, u32[]{:S(2)}) %collective-permute-start.6) | collective-permute-done | bytes 32800 | tf_op jit(solution)/shard_map/ppermute | solution.py:436
  27.0 1.5 %collective-permute-start.12 = (bf16[8,16,128]{2,1,0:T(8,128)(2,1)S(1)}, bf16[8,16,128]{2,1,0:T(8,128)(2,1)S(1)}, u32[]{:S(2)}, u32[]{:S(2)}) collective-permute-start(bf16[8,16,128]{2,1,0:T(8,128)(2,1)S(1)} %get-tuple-element.52), channel_id=1, source_target_pairs={{8,22},{9,23},{10,20},{11,21},{12,18},{13,19},{14,16},{15,17},{16,... | collective-permute-start | bytes 98312 | tf_op jit(solution)/shard_map/ppermute | solution.py:436
  29.2 1.6 %collective-permute-start.14 = (bf16[2,8,16,128]{3,2,1,0:T(8,128)(2,1)S(1)}, bf16[2,8,16,128]{3,2,1,0:T(8,128)(2,1)S(1)}, u32[]{:S(2)}, u32[]{:S(2)}) collective-permute-start(bf16[2,8,16,128]{3,2,1,0:T(8,128)(2,1)S(1)} %pad_maximum_fusion.8), channel_id=1, source_target_pairs={{8,18},{9,21},{10,16},{11,23},{12,22},{13,17},{14,20},{15,19},{16,... | collective-permute-start | bytes 196616 | tf_op jit(solution)/shard_map/ppermute | solution.py:436
  31.9 1.7 %collective-permute-done.14.rest_2_ = bf16[2,8,16,128]{3,2,1,0:T(8,128)(2,1)S(1)} collective-permute-done((bf16[2,8,16,128]{3,2,1,0:T(8,128)(2,1)S(1)}, bf16[2,8,16,128]{3,2,1,0:T(8,128)(2,1)S(1)}, u32[]{:S(2)}, u32[]{:S(2)}) %collective-permute-start.14) | collective-permute-done | bytes 65568 | tf_op jit(solution)/shard_map/ppermute | solution.py:436
  35.6 11.3 %collective-permute-start.17 = (bf16[8,16,128]{2,1,0:T(8,128)(2,1)S(1)}, bf16[8,16,128]{2,1,0:T(8,128)(2,1)S(1)}, u32[]{:S(2)}, u32[]{:S(2)}) collective-permute-start(bf16[8,16,128]{2,1,0:T(8,128)(2,1)S(1)} %get-tuple-element.55), channel_id=1, source_target_pairs={{16,30},{17,31},{18,28},{19,29},{20,26},{21,27},{22,24},{23,25},{2... | collective-permute-start | bytes 98312 | tf_op jit(solution)/shard_map/ppermute | solution.py:436
  47.6 1.6 %collective-permute-start.19 = (bf16[2,8,16,128]{3,2,1,0:T(8,128)(2,1)S(1)}, bf16[2,8,16,128]{3,2,1,0:T(8,128)(2,1)S(1)}, u32[]{:S(2)}, u32[]{:S(2)}) collective-permute-start(bf16[2,8,16,128]{3,2,1,0:T(8,128)(2,1)S(1)} %pad_maximum_fusion.9), channel_id=1, source_target_pairs={{16,26},{17,29},{18,24},{19,31},{20,30},{21,25},{22,28},{23,27},{2... | collective-permute-start | bytes 196616 | tf_op jit(solution)/shard_map/ppermute | solution.py:436
  49.2 2.8 %collective-permute-done.19.rest_2_ = bf16[2,8,16,128]{3,2,1,0:T(8,128)(2,1)S(1)} collective-permute-done((bf16[2,8,16,128]{3,2,1,0:T(8,128)(2,1)S(1)}, bf16[2,8,16,128]{3,2,1,0:T(8,128)(2,1)S(1)}, u32[]{:S(2)}, u32[]{:S(2)}) %collective-permute-start.19) | collective-permute-done | bytes 65568 | tf_op jit(solution)/shard_map/ppermute | solution.py:436
  57.8 3.2 %collective-permute-done.21.rest_1_ = bf16[4,16,128]{2,1,0:T(8,128)(2,1)S(1)} collective-permute-done((bf16[4,16,128]{2,1,0:T(8,128)(2,1)S(1)}, bf16[4,16,128]{2,1,0:T(8,128)(2,1)S(1)}, u32[]{:S(2)}, u32[]{:S(2)}) %collective-permute-start.21) | collective-permute-done | bytes 16416 | tf_op jit(solution)/shard_map/ppermute | solution.py:436
  65.5 2.1 %collective-permute-done.26.rest_1_ = bf16[8,16,128]{2,1,0:T(8,128)(2,1)S(1)} collective-permute-done((bf16[8,16,128]{2,1,0:T(8,128)(2,1)S(1)}, bf16[8,16,128]{2,1,0:T(8,128)(2,1)S(1)}, u32[]{:S(2)}, u32[]{:S(2)}) %collective-permute-start.26) | collective-permute-done | bytes 32800 | tf_op jit(solution)/shard_map/ppermute | solution.py:436
  67.6 1.6 %collective-permute-done.28.rest_2_ = bf16[2,8,16,128]{3,2,1,0:T(8,128)(2,1)S(1)} collective-permute-done((bf16[2,8,16,128]{3,2,1,0:T(8,128)(2,1)S(1)}, bf16[2,8,16,128]{3,2,1,0:T(8,128)(2,1)S(1)}, u32[]{:S(2)}, u32[]{:S(2)}) %collective-permute-start.28) | collective-permute-done | bytes 65568 | tf_op jit(solution)/shard_map/ppermute | solution.py:436
  71.1 13.2 %collective-permute-start.31 = (bf16[8,16,128]{2,1,0:T(8,128)(2,1)S(1)}, bf16[8,16,128]{2,1,0:T(8,128)(2,1)S(1)}, u32[]{:S(2)}, u32[]{:S(2)}) collective-permute-start(bf16[8,16,128]{2,1,0:T(8,128)(2,1)S(1)} %get-tuple-element.64), channel_id=1, source_target_pairs={{16,14},{17,15},{18,12},{19,13},{20,10},{21,11},{22,8},{23,9},{8,6... | collective-permute-start | bytes 98312 | tf_op jit(solution)/shard_map/ppermute | solution.py:436
  85.9 3.4 %collective-permute-done.33.rest_2_ = bf16[2,8,16,128]{3,2,1,0:T(8,128)(2,1)S(1)} collective-permute-done((bf16[2,8,16,128]{3,2,1,0:T(8,128)(2,1)S(1)}, bf16[2,8,16,128]{3,2,1,0:T(8,128)(2,1)S(1)}, u32[]{:S(2)}, u32[]{:S(2)}) %collective-permute-start.33) | collective-permute-done | bytes 65568 | tf_op jit(solution)/shard_map/ppermute | solution.py:436
  92.5 5.9 %collective-permute-start.38 = (bf16[2,8,16,128]{3,2,1,0:T(8,128)(2,1)S(1)}, bf16[2,8,16,128]{3,2,1,0:T(8,128)(2,1)S(1)}, u32[]{:S(2)}, u32[]{:S(2)}) collective-permute-start(bf16[2,8,16,128]{3,2,1,0:T(8,128)(2,1)S(1)} %pad_maximum_fusion.13), channel_id=1, source_target_pairs={{8,2},{9,5},{10,0},{11,7},{12,6},{13,1},{14,4},{15,3},{0,10},{1,13... | collective-permute-start | bytes 196616 | tf_op jit(solution)/shard_map/ppermute | solution.py:436
  98.4 1.9 %collective-permute-done.35.rest_0_.rest_5_ = bf16[16,16,128]{2,1,0:T(8,128)(2,1)S(1)} collective-permute-done((bf16[16,16,128]{2,1,0:T(8,128)(2,1)S(1)}, bf16[16,16,128]{2,1,0:T(8,128)(2,1)S(1)}, u32[]{:S(2)}, u32[]{:S(2)}) %collective-permute-start.35) | collective-permute-done | bytes 65568 | tf_op jit(solution)/shard_map/ppermute | solution.py:478
  100.3 2.0 %collective-permute-done.38.rest_2_ = bf16[2,8,16,128]{3,2,1,0:T(8,128)(2,1)S(1)} collective-permute-done((bf16[2,8,16,128]{3,2,1,0:T(8,128)(2,1)S(1)}, bf16[2,8,16,128]{3,2,1,0:T(8,128)(2,1)S(1)}, u32[]{:S(2)}, u32[]{:S(2)}) %collective-permute-start.38) | collective-permute-done | bytes 65568 | tf_op jit(solution)/shard_map/ppermute | solution.py:436
  103.7 3.5 %backward_section_0.1 = f32[2,16,1024]{2,1,0:T(8,128)} custom-call(s32[8,128]{1,0:T(8,128)S(1)} %get-tuple-element.38.layers, bf16[2,512,4096]{2,1,0:T(8,128)(2,1)S(1)} %get-tuple-element.39.first_inverse, bf16[2,512,4096]{2,1,0:T(8,128)(2,1)S(1)} %get-tuple-element.56.second_inverse, f32[40,1024]{1,0:T(8,128)S(1)} %get-tuple-element.41.packet, ...), custom_call_target="tpu_custom_call" | custom-call | tf_op jit(solution)/shard_map/backward_section_0/pallas_call | solution.py:383
  (88 shorter events, 29.5 us)
Async XLA Ops:
  2.4 3.2 %collective-permute-start.1 = (bf16[8,16,128]{2,1,0:T(8,128)(2,1)S(1)}, bf16[8,16,128]{2,1,0:T(8,128)(2,1)S(1)}, u32[]{:S(2)}, u32[]{:S(2)}) collective-permute-start(bf16[8,16,128]{2,1,0:T(8,128)(2,1)S(1)} %get-tuple-element.43.refs_0_.rest_0_), channel_id=1, source_target_pairs={{0,1},{1,0},{2,3},{3,2},{4,5},{5,4},{6,7},{7,6},{8,9},{9,8},{10,11... | collective-permute-start | bytes 98312 | tf_op jit(solution)/shard_map/ppermute | solution.py:436
  2.9 9.1 %collective-permute-start.3 = (f32[24,1024]{1,0:T(8,128)S(1)}, f32[24,1024]{1,0:T(8,128)S(1)}, u32[]{:S(2)}, u32[]{:S(2)}) collective-permute-start(f32[24,1024]{1,0:T(8,128)S(1)} %get-tuple-element.44), channel_id=1, source_target_pairs={{0,8},{1,9},{2,10},{3,11},{4,12},{5,13},{6,14},{7,15},{16,24},{17,... | collective-permute-start | bytes 294920 | tf_op jit(solution)/shard_map/ppermute | solution.py:436
  5.6 6.5 %collective-permute-start.2 = (bf16[2,8,16,128]{3,2,1,0:T(8,128)(2,1)S(1)}, bf16[2,8,16,128]{3,2,1,0:T(8,128)(2,1)S(1)}, u32[]{:S(2)}, u32[]{:S(2)}) collective-permute-start(bf16[2,8,16,128]{3,2,1,0:T(8,128)(2,1)S(1)} %pad_maximum_fusion.6), channel_id=1, source_target_pairs={{0,2},{1,5},{2,0},{3,7},{4,6},{5,1},{6,4},{7,3},{8,10},{9,13},{10,... | collective-permute-start | bytes 196616 | tf_op jit(solution)/shard_map/ppermute | solution.py:436
  7.1 4.9 %collective-permute-start = (bf16[8,16,128]{2,1,0:T(8,128)(2,1)S(1)}, bf16[8,16,128]{2,1,0:T(8,128)(2,1)S(1)}, u32[]{:S(2)}, u32[]{:S(2)}) collective-permute-start(bf16[8,16,128]{2,1,0:T(8,128)(2,1)S(1)} %get-tuple-element.43.refs_0_.rest_0_), channel_id=1, source_target_pairs={{0,6},{1,7},{2,4},{3,5},{4,2},{5,3},{6,0},{7,1},{8,14},{9,15},{10,... | collective-permute-start | bytes 98312 | tf_op jit(solution)/shard_map/ppermute | solution.py:436
  16.6 3.3 %collective-permute-start.7 = (bf16[8,16,128]{2,1,0:T(8,128)(2,1)S(1)}, bf16[8,16,128]{2,1,0:T(8,128)(2,1)S(1)}, u32[]{:S(2)}, u32[]{:S(2)}) collective-permute-start(bf16[8,16,128]{2,1,0:T(8,128)(2,1)S(1)} %get-tuple-element.48), channel_id=1, source_target_pairs={{0,1},{1,0},{2,3},{3,2},{4,5},{5,4},{6,7},{7,6},{8,9},{9,8},{10,11... | collective-permute-start | bytes 98312 | tf_op jit(solution)/shard_map/ppermute | solution.py:436
  16.8 8.4 %collective-permute-start.10 = (f32[40,1024]{1,0:T(8,128)S(1)}, f32[40,1024]{1,0:T(8,128)S(1)}, u32[]{:S(2)}, u32[]{:S(2)}) collective-permute-start(f32[40,1024]{1,0:T(8,128)S(1)} %get-tuple-element.49), channel_id=1, source_target_pairs={{8,16},{9,17},{10,18},{11,19},{12,20},{13,21},{14,22},{15,23},{16,... | collective-permute-start | bytes 491528 | tf_op jit(solution)/shard_map/ppermute | solution.py:436
  17.2 6.7 %collective-permute-start.6 = (bf16[8,16,128]{2,1,0:T(8,128)(2,1)S(1)}, bf16[8,16,128]{2,1,0:T(8,128)(2,1)S(1)}, u32[]{:S(2)}, u32[]{:S(2)}) collective-permute-start(bf16[8,16,128]{2,1,0:T(8,128)(2,1)S(1)} %get-tuple-element.48), channel_id=1, source_target_pairs={{0,14},{1,15},{2,12},{3,13},{4,10},{5,11},{6,8},{7,9},{8,22},{9,23... | collective-permute-start | bytes 98312 | tf_op jit(solution)/shard_map/ppermute | solution.py:436
  18.0 4.2 %collective-permute-start.5 = (bf16[16,16,128]{2,1,0:T(8,128)(2,1)S(1)}, bf16[16,16,128]{2,1,0:T(8,128)(2,1)S(1)}, u32[]{:S(2)}, u32[]{:S(2)}) collective-permute-start(bf16[16,16,128]{2,1,0:T(8,128)(2,1)S(1)} %get-tuple-element.47), channel_id=1, source_target_pairs={{0,8},{1,9},{2,10},{3,11},{4,12},{5,13},{6,14},{7,15}} | collective-permute-start | bytes 196616 | tf_op jit(solution)/shard_map/ppermute | solution.py:478
  19.9 5.2 %collective-permute-start.8 = (bf16[2,8,16,128]{3,2,1,0:T(8,128)(2,1)S(1)}, bf16[2,8,16,128]{3,2,1,0:T(8,128)(2,1)S(1)}, u32[]{:S(2)}, u32[]{:S(2)}) collective-permute-start(bf16[2,8,16,128]{3,2,1,0:T(8,128)(2,1)S(1)} %pad_maximum_fusion.7), channel_id=1, source_target_pairs={{0,10},{1,13},{2,8},{3,15},{4,14},{5,9},{6,12},{7,11},{8,2},{9,5},... | collective-permute-start | bytes 196616 | tf_op jit(solution)/shard_map/ppermute | solution.py:436
  27.0 4.8 %collective-permute-start.12 = (bf16[8,16,128]{2,1,0:T(8,128)(2,1)S(1)}, bf16[8,16,128]{2,1,0:T(8,128)(2,1)S(1)}, u32[]{:S(2)}, u32[]{:S(2)}) collective-permute-start(bf16[8,16,128]{2,1,0:T(8,128)(2,1)S(1)} %get-tuple-element.52), channel_id=1, source_target_pairs={{8,22},{9,23},{10,20},{11,21},{12,18},{13,19},{14,16},{15,17},{16,... | collective-permute-start | bytes 98312 | tf_op jit(solution)/shard_map/ppermute | solution.py:436
  29.2 4.3 %collective-permute-start.14 = (bf16[2,8,16,128]{3,2,1,0:T(8,128)(2,1)S(1)}, bf16[2,8,16,128]{3,2,1,0:T(8,128)(2,1)S(1)}, u32[]{:S(2)}, u32[]{:S(2)}) collective-permute-start(bf16[2,8,16,128]{3,2,1,0:T(8,128)(2,1)S(1)} %pad_maximum_fusion.8), channel_id=1, source_target_pairs={{8,18},{9,21},{10,16},{11,23},{12,22},{13,17},{14,20},{15,19},{16,... | collective-permute-start | bytes 196616 | tf_op jit(solution)/shard_map/ppermute | solution.py:436
  35.4 12.2 %collective-permute-start.18 = (bf16[8,16,128]{2,1,0:T(8,128)(2,1)S(1)}, bf16[8,16,128]{2,1,0:T(8,128)(2,1)S(1)}, u32[]{:S(2)}, u32[]{:S(2)}) collective-permute-start(bf16[8,16,128]{2,1,0:T(8,128)(2,1)S(1)} %get-tuple-element.55), channel_id=1, source_target_pairs={{0,1},{1,0},{2,3},{3,2},{4,5},{5,4},{6,7},{7,6},{8,9},{9,8},{10,11... | collective-permute-start | bytes 98312 | tf_op jit(solution)/shard_map/ppermute | solution.py:436
  35.6 13.6 %collective-permute-start.17 = (bf16[8,16,128]{2,1,0:T(8,128)(2,1)S(1)}, bf16[8,16,128]{2,1,0:T(8,128)(2,1)S(1)}, u32[]{:S(2)}, u32[]{:S(2)}) collective-permute-start(bf16[8,16,128]{2,1,0:T(8,128)(2,1)S(1)} %get-tuple-element.55), channel_id=1, source_target_pairs={{16,30},{17,31},{18,28},{19,29},{20,26},{21,27},{22,24},{23,25},{2... | collective-permute-start | bytes 98312 | tf_op jit(solution)/shard_map/ppermute | solution.py:436
  47.6 4.3 %collective-permute-start.19 = (bf16[2,8,16,128]{3,2,1,0:T(8,128)(2,1)S(1)}, bf16[2,8,16,128]{3,2,1,0:T(8,128)(2,1)S(1)}, u32[]{:S(2)}, u32[]{:S(2)}) collective-permute-start(bf16[2,8,16,128]{3,2,1,0:T(8,128)(2,1)S(1)} %pad_maximum_fusion.9), channel_id=1, source_target_pairs={{16,26},{17,29},{18,24},{19,31},{20,30},{21,25},{22,28},{23,27},{2... | collective-permute-start | bytes 196616 | tf_op jit(solution)/shard_map/ppermute | solution.py:436
  54.9 6.1 %collective-permute-start.23 = (bf16[2,4,16,128]{3,2,1,0:T(8,128)(2,1)S(1)}, bf16[2,4,16,128]{3,2,1,0:T(8,128)(2,1)S(1)}, u32[]{:S(2)}, u32[]{:S(2)}) collective-permute-start(bf16[2,4,16,128]{3,2,1,0:T(8,128)(2,1)S(1)} %pad_maximum_fusion.14), channel_id=1, source_target_pairs={{0,2},{1,5},{2,0},{3,7},{4,6},{5,1},{6,4},{7,3},{8,10},{9,13},{10,... | collective-permute-start | bytes 98312 | tf_op jit(solution)/shard_map/ppermute | solution.py:436
  56.4 4.6 %collective-permute-start.21 = (bf16[4,16,128]{2,1,0:T(8,128)(2,1)S(1)}, bf16[4,16,128]{2,1,0:T(8,128)(2,1)S(1)}, u32[]{:S(2)}, u32[]{:S(2)}) collective-permute-start(bf16[4,16,128]{2,1,0:T(8,128)(2,1)S(1)} %get-tuple-element.57.rest_0_), channel_id=1, source_target_pairs={{0,6},{1,7},{2,4},{3,5},{4,2},{5,3},{6,0},{7,1},{8,14},{9,15},{10,... | collective-permute-start | bytes 49160 | tf_op jit(solution)/shard_map/ppermute | solution.py:436
  62.8 4.8 %collective-permute-start.26 = (bf16[8,16,128]{2,1,0:T(8,128)(2,1)S(1)}, bf16[8,16,128]{2,1,0:T(8,128)(2,1)S(1)}, u32[]{:S(2)}, u32[]{:S(2)}) collective-permute-start(bf16[8,16,128]{2,1,0:T(8,128)(2,1)S(1)} %get-tuple-element.60), channel_id=1, source_target_pairs={{24,22},{25,23},{26,20},{27,21},{28,18},{29,19},{30,16},{31,17},{1... | collective-permute-start | bytes 98312 | tf_op jit(solution)/shard_map/ppermute | solution.py:436
  64.9 4.3 %collective-permute-start.28 = (bf16[2,8,16,128]{3,2,1,0:T(8,128)(2,1)S(1)}, bf16[2,8,16,128]{3,2,1,0:T(8,128)(2,1)S(1)}, u32[]{:S(2)}, u32[]{:S(2)}) collective-permute-start(bf16[2,8,16,128]{3,2,1,0:T(8,128)(2,1)S(1)} %pad_maximum_fusion.11), channel_id=1, source_target_pairs={{24,18},{25,21},{26,16},{27,23},{28,22},{29,17},{30,20},{31,19},{1... | collective-permute-start | bytes 196616 | tf_op jit(solution)/shard_map/ppermute | solution.py:436
  70.8 14.1 %collective-permute-start.32 = (bf16[8,16,128]{2,1,0:T(8,128)(2,1)S(1)}, bf16[8,16,128]{2,1,0:T(8,128)(2,1)S(1)}, u32[]{:S(2)}, u32[]{:S(2)}) collective-permute-start(bf16[8,16,128]{2,1,0:T(8,128)(2,1)S(1)} %get-tuple-element.64), channel_id=1, source_target_pairs={{0,1},{1,0},{2,3},{3,2},{4,5},{5,4},{6,7},{7,6},{8,9},{9,8},{10,11... | collective-permute-start | bytes 98312 | tf_op jit(solution)/shard_map/ppermute | solution.py:436
  71.1 14.8 %collective-permute-start.31 = (bf16[8,16,128]{2,1,0:T(8,128)(2,1)S(1)}, bf16[8,16,128]{2,1,0:T(8,128)(2,1)S(1)}, u32[]{:S(2)}, u32[]{:S(2)}) collective-permute-start(bf16[8,16,128]{2,1,0:T(8,128)(2,1)S(1)} %get-tuple-element.64), channel_id=1, source_target_pairs={{16,14},{17,15},{18,12},{19,13},{20,10},{21,11},{22,8},{23,9},{8,6... | collective-permute-start | bytes 98312 | tf_op jit(solution)/shard_map/ppermute | solution.py:436
  85.0 4.3 %collective-permute-start.33 = (bf16[2,8,16,128]{3,2,1,0:T(8,128)(2,1)S(1)}, bf16[2,8,16,128]{3,2,1,0:T(8,128)(2,1)S(1)}, u32[]{:S(2)}, u32[]{:S(2)}) collective-permute-start(bf16[2,8,16,128]{3,2,1,0:T(8,128)(2,1)S(1)} %pad_maximum_fusion.12), channel_id=1, source_target_pairs={{16,10},{17,13},{18,8},{19,15},{20,14},{21,9},{22,12},{23,11},{8,1... | collective-permute-start | bytes 196616 | tf_op jit(solution)/shard_map/ppermute | solution.py:436
  91.2 9.1 %collective-permute-start.36 = (bf16[8,16,128]{2,1,0:T(8,128)(2,1)S(1)}, bf16[8,16,128]{2,1,0:T(8,128)(2,1)S(1)}, u32[]{:S(2)}, u32[]{:S(2)}) collective-permute-start(bf16[8,16,128]{2,1,0:T(8,128)(2,1)S(1)} %get-tuple-element.68), channel_id=1, source_target_pairs={{8,6},{9,7},{10,4},{11,5},{12,2},{13,3},{14,0},{15,1},{0,30},{1,31... | collective-permute-start | bytes 98312 | tf_op jit(solution)/shard_map/ppermute | solution.py:436
  91.2 9.1 %collective-permute-start.35 = (bf16[16,16,128]{2,1,0:T(8,128)(2,1)S(1)}, bf16[16,16,128]{2,1,0:T(8,128)(2,1)S(1)}, u32[]{:S(2)}, u32[]{:S(2)}) collective-permute-start(bf16[16,16,128]{2,1,0:T(8,128)(2,1)S(1)} %get-tuple-element.67), channel_id=1, source_target_pairs={{8,0},{9,1},{10,2},{11,3},{12,4},{13,5},{14,6},{15,7}} | collective-permute-start | bytes 196616 | tf_op jit(solution)/shard_map/ppermute | solution.py:478
  92.5 9.8 %collective-permute-start.38 = (bf16[2,8,16,128]{3,2,1,0:T(8,128)(2,1)S(1)}, bf16[2,8,16,128]{3,2,1,0:T(8,128)(2,1)S(1)}, u32[]{:S(2)}, u32[]{:S(2)}) collective-permute-start(bf16[2,8,16,128]{3,2,1,0:T(8,128)(2,1)S(1)} %pad_maximum_fusion.13), channel_id=1, source_target_pairs={{8,2},{9,5},{10,0},{11,7},{12,6},{13,1},{14,4},{15,3},{0,10},{1,13... | collective-permute-start | bytes 196616 | tf_op jit(solution)/shard_map/ppermute | solution.py:436
  (16 other events, 25.8 us)

commit v14 on v13

--- a/solution.py
+++ b/solution.py
@@ -475,12 +475,14 @@
         return spread(front, front, inside, inside, join) if direct else everywhere(front)
 
     def between(front, packet, start, stop):
-        packet = lax.ppermute(packet, "sweep", [(start, stop)])
         if not direct:
+            packet = lax.ppermute(packet, "sweep", [(start, stop)])
             return *everywhere(packet[:2 * per_layer]), packet
         ahead_of = 2 * stop - start, 3 * start - 2 * stop, 2 * start - stop
         third = [i for i in ahead_of if 0 <= i < sections]
         some, every = cycle(start, stop, *third[:1]), cycle(start, stop)
+        fourth = [i for i in range(sections) if i not in (start, stop, *third[:1])]
+        packet = send(packet, cycle(start, stop, *fourth[:1]), 0)
         return *spread(front, packet, some, every), packet
 
     inverse = in_hbm(front_inverse)

time: 107 us -> 105 us (0.981)
  starting transfers between devices: 56.1 us -> 53.4 us
    ppermute x6 -> x0, starting transfers between devices: 5.78 us -> none  [between(): packet = lax.ppermute(packet, 'sweep', [(start, stop)])]
    ppermute x6 -> x0, waiting for transfers between devices: 3.86 us -> none  [between(): packet = lax.ppermute(packet, 'sweep', [(start, stop)])]
    ppermute x34 -> x40, waiting for transfers between devices: 32.8 us -> 36.4 us  [send(): return lax.ppermute(block, ('sweep', 'plane'), route)]
    ppermute x34 -> x40, starting transfers between devices: 50.4 us -> 53.4 us  [send(): return lax.ppermute(block, ('sweep', 'plane'), route)]
  transfers between devices with their start and end apart: 40 -> 40, of which waited for: 22 -> 24; matrix products, arithmetic and copies ran while one was open for 0% -> 0% of each run, Pallas kernels for 3% -> 3%
where the time goes in v14:
time: 105 us; the launch traced here: 104 us
  starting transfers between devices  53.4 us (51%)
  waiting for transfers between devices  36.4 us (35%)
  Pallas kernels  14 us (13%)
    ppermute x40, starting transfers between devices, send(): return lax.ppermute(block, ('sweep', 'plane'), route)  53.4 us
    ppermute x40, waiting for transfers between devices, send(): return lax.ppermute(block, ('sweep', 'plane'), route)  36.4 us
    pallas_call x11, Pallas kernels, call(): pl.pallas_call(kernel, in_specs=specs, out_specs=[whole(pltpu.SMEM if len...  14 us
  transfers between devices with their start and end apart: 40, of which 24 were waited for; matrix products, arithmetic and copies ran while one was open for 0% of the time, Pallas kernels for 3%

profile of v14, /device:TPU:0, one launch (start us, length us, event | category | flops | bytes accessed | tf_op | source)
XLA Modules:
  0.0 104.2 jit_solution(14803852355901677673)
XLA Ops:
  0.0 2.4 %first_fronts.1 = (f32[40,1024]{1,0:T(8,128)S(1)}, f32[24,1024]{1,0:T(8,128)S(1)}, f32[40,1024]{1,0:T(8,128)S(1)}, s32[2,1024]{1,0:T(2,128)S(1)}, bf16[8,16,128]{2,1,0:T(8,128)(2,1)S(1)}, /*index=5*/s32[8,128]{1,0:T(8,128)S(1)}) custom-call(s32[4]{0:T(128)} %layers_in.1, f32[2,16,1024]{2,1,0:T(8,128)} %bitcast.53, f32[2,1024]{1,0:T(2,128)} %isc_in.1, ...), custom_call_target="tpu_custom_call" | custom-call | tf_op jit(solution)/shard_map/first_fronts/pallas_call | solution.py:383
  2.9 2.6 %collective-permute-start.3 = (f32[24,1024]{1,0:T(8,128)S(1)}, f32[24,1024]{1,0:T(8,128)S(1)}, u32[]{:S(2)}, u32[]{:S(2)}) collective-permute-start(f32[24,1024]{1,0:T(8,128)S(1)} %get-tuple-element.44), channel_id=1, source_target_pairs={{0,8},{1,9},{2,10},{3,11},{4,12},{5,13},{6,14},{7,15},{16,24},{17,... | collective-permute-start | bytes 294920 | tf_op jit(solution)/shard_map/ppermute | solution.py:436
  5.6 1.6 %collective-permute-start.2 = (bf16[2,8,16,128]{3,2,1,0:T(8,128)(2,1)S(1)}, bf16[2,8,16,128]{3,2,1,0:T(8,128)(2,1)S(1)}, u32[]{:S(2)}, u32[]{:S(2)}) collective-permute-start(bf16[2,8,16,128]{3,2,1,0:T(8,128)(2,1)S(1)} %pad_maximum_fusion.6), channel_id=1, source_target_pairs={{0,2},{1,5},{2,0},{3,7},{4,6},{5,1},{6,4},{7,3},{8,10},{9,13},{10,... | collective-permute-start | bytes 196616 | tf_op jit(solution)/shard_map/ppermute | solution.py:436
  7.1 1.5 %collective-permute-start = (bf16[8,16,128]{2,1,0:T(8,128)(2,1)S(1)}, bf16[8,16,128]{2,1,0:T(8,128)(2,1)S(1)}, u32[]{:S(2)}, u32[]{:S(2)}) collective-permute-start(bf16[8,16,128]{2,1,0:T(8,128)(2,1)S(1)} %get-tuple-element.43.refs_0_.rest_0_), channel_id=1, source_target_pairs={{0,6},{1,7},{2,4},{3,5},{4,2},{5,3},{6,0},{7,1},{8,14},{9,15},{10,... | collective-permute-start | bytes 98312 | tf_op jit(solution)/shard_map/ppermute | solution.py:436
  8.6 3.4 %load_first.1 = (bf16[2,512,4096]{2,1,0:T(8,128)(2,1)S(1)}, bf16[2,512,4096]{2,1,0:T(8,128)(2,1)S(1)}, f32[8,128]{1,0:T(8,128)S(1)}) custom-call(bf16[2,2,512,4096]{3,2,1,0:T(8,128)(2,1)} %inverse.9), custom_call_target="tpu_custom_call" | custom-call | tf_op jit(solution)/shard_map/load_first/pallas_call | solution.py:383
  13.5 3.1 %forward_section_0.1 = (f32[2,16,1024]{2,1,0:T(8,128)S(1)}, bf16[8,16,128]{2,1,0:T(8,128)(2,1)S(1)}, bf16[16,16,128]{2,1,0:T(8,128)(2,1)S(1)}, bf16[2,512,4096]{2,1,0:T(8,128)(2,1)S(1)}) custom-call(s32[8,128]{1,0:T(8,128)S(1)} %get-tuple-element.38.layers, ...), custom_call_target="tpu_custom_call", output_to_operand_aliasing={{3}: (2, {})} | custom-call | tf_op jit(solution)/shard_map/forward_section_0/pallas_call | solution.py:383
  18.0 2.4 %collective-permute-start.8 = (bf16[2,8,16,128]{3,2,1,0:T(8,128)(2,1)S(1)}, bf16[2,8,16,128]{3,2,1,0:T(8,128)(2,1)S(1)}, u32[]{:S(2)}, u32[]{:S(2)}) collective-permute-start(bf16[2,8,16,128]{3,2,1,0:T(8,128)(2,1)S(1)} %pad_maximum_fusion.7), channel_id=1, source_target_pairs={{0,10},{1,13},{2,8},{3,15},{4,14},{5,9},{6,12},{7,11},{8,2},{9,5},... | collective-permute-start | bytes 196616 | tf_op jit(solution)/shard_map/ppermute | solution.py:436
  20.4 3.6 %collective-permute-done.5.rest_0_.rest_4_.rest_8_ = bf16[16,16,128]{2,1,0:T(8,128)(2,1)S(1)} collective-permute-done((bf16[16,16,128]{2,1,0:T(8,128)(2,1)S(1)}, bf16[16,16,128]{2,1,0:T(8,128)(2,1)S(1)}, u32[]{:S(2)}, u32[]{:S(2)}) %collective-permute-start.5) | collective-permute-done | bytes 65568 | tf_op jit(solution)/shard_map/ppermute | solution.py:436
  27.2 1.5 %collective-permute-start.12 = (bf16[8,16,128]{2,1,0:T(8,128)(2,1)S(1)}, bf16[8,16,128]{2,1,0:T(8,128)(2,1)S(1)}, u32[]{:S(2)}, u32[]{:S(2)}) collective-permute-start(bf16[8,16,128]{2,1,0:T(8,128)(2,1)S(1)} %get-tuple-element.52), channel_id=1, source_target_pairs={{8,22},{9,23},{10,20},{11,21},{12,18},{13,19},{14,16},{15,17},{16,... | collective-permute-start | bytes 98312 | tf_op jit(solution)/shard_map/ppermute | solution.py:436
  28.7 4.5 %collective-permute-start.11 = (bf16[16,16,128]{2,1,0:T(8,128)(2,1)S(1)}, bf16[16,16,128]{2,1,0:T(8,128)(2,1)S(1)}, u32[]{:S(2)}, u32[]{:S(2)}) collective-permute-start(bf16[16,16,128]{2,1,0:T(8,128)(2,1)S(1)} %get-tuple-element.51), channel_id=1, source_target_pairs={{8,16},{9,17},{10,18},{11,19},{12,20},{13,21},{14,22},{15,23},{16,... | collective-permute-start | bytes 196616 | tf_op jit(solution)/shard_map/ppermute | solution.py:436
  35.1 2.4 %collective-permute-done.14.rest_2_ = bf16[2,8,16,128]{3,2,1,0:T(8,128)(2,1)S(1)} collective-permute-done((bf16[2,8,16,128]{3,2,1,0:T(8,128)(2,1)S(1)}, bf16[2,8,16,128]{3,2,1,0:T(8,128)(2,1)S(1)}, u32[]{:S(2)}, u32[]{:S(2)}) %collective-permute-start.14) | collective-permute-done | bytes 65568 | tf_op jit(solution)/shard_map/ppermute | solution.py:436
  39.6 9.4 %collective-permute-start.17 = (bf16[8,16,128]{2,1,0:T(8,128)(2,1)S(1)}, bf16[8,16,128]{2,1,0:T(8,128)(2,1)S(1)}, u32[]{:S(2)}, u32[]{:S(2)}) collective-permute-start(bf16[8,16,128]{2,1,0:T(8,128)(2,1)S(1)} %get-tuple-element.55), channel_id=1, source_target_pairs={{16,30},{17,31},{18,28},{19,29},{20,26},{21,27},{22,24},{23,25},{2... | collective-permute-start | bytes 98312 | tf_op jit(solution)/shard_map/ppermute | solution.py:436
  50.6 2.8 %collective-permute-done.19.rest_2_ = bf16[2,8,16,128]{3,2,1,0:T(8,128)(2,1)S(1)} collective-permute-done((bf16[2,8,16,128]{3,2,1,0:T(8,128)(2,1)S(1)}, bf16[2,8,16,128]{3,2,1,0:T(8,128)(2,1)S(1)}, u32[]{:S(2)}, u32[]{:S(2)}) %collective-permute-start.19) | collective-permute-done | bytes 65568 | tf_op jit(solution)/shard_map/ppermute | solution.py:436
  58.7 3.3 %collective-permute-done.21.rest_1_ = bf16[4,16,128]{2,1,0:T(8,128)(2,1)S(1)} collective-permute-done((bf16[4,16,128]{2,1,0:T(8,128)(2,1)S(1)}, bf16[4,16,128]{2,1,0:T(8,128)(2,1)S(1)}, u32[]{:S(2)}, u32[]{:S(2)}) %collective-permute-start.21) | collective-permute-done | bytes 16416 | tf_op jit(solution)/shard_map/ppermute | solution.py:436
  65.1 3.1 %collective-permute-start.25 = (bf16[16,16,128]{2,1,0:T(8,128)(2,1)S(1)}, bf16[16,16,128]{2,1,0:T(8,128)(2,1)S(1)}, u32[]{:S(2)}, u32[]{:S(2)}) collective-permute-start(bf16[16,16,128]{2,1,0:T(8,128)(2,1)S(1)} %get-tuple-element.59), channel_id=1, source_target_pairs={{24,16},{25,17},{26,18},{27,19},{28,20},{29,21},{30,22},{31,23},{1... | collective-permute-start | bytes 196616 | tf_op jit(solution)/shard_map/ppermute | solution.py:436
  70.3 2.3 %collective-permute-done.28.rest_2_ = bf16[2,8,16,128]{3,2,1,0:T(8,128)(2,1)S(1)} collective-permute-done((bf16[2,8,16,128]{3,2,1,0:T(8,128)(2,1)S(1)}, bf16[2,8,16,128]{3,2,1,0:T(8,128)(2,1)S(1)}, u32[]{:S(2)}, u32[]{:S(2)}) %collective-permute-start.28) | collective-permute-done | bytes 65568 | tf_op jit(solution)/shard_map/ppermute | solution.py:436
  74.6 7.6 %collective-permute-start.31 = (bf16[8,16,128]{2,1,0:T(8,128)(2,1)S(1)}, bf16[8,16,128]{2,1,0:T(8,128)(2,1)S(1)}, u32[]{:S(2)}, u32[]{:S(2)}) collective-permute-start(bf16[8,16,128]{2,1,0:T(8,128)(2,1)S(1)} %get-tuple-element.64), channel_id=1, source_target_pairs={{16,14},{17,15},{18,12},{19,13},{20,10},{21,11},{22,8},{23,9},{8,6... | collective-permute-start | bytes 98312 | tf_op jit(solution)/shard_map/ppermute | solution.py:436
  83.8 2.8 %collective-permute-done.33.rest_2_ = bf16[2,8,16,128]{3,2,1,0:T(8,128)(2,1)S(1)} collective-permute-done((bf16[2,8,16,128]{3,2,1,0:T(8,128)(2,1)S(1)}, bf16[2,8,16,128]{3,2,1,0:T(8,128)(2,1)S(1)}, u32[]{:S(2)}, u32[]{:S(2)}) %collective-permute-start.33) | collective-permute-done | bytes 65568 | tf_op jit(solution)/shard_map/ppermute | solution.py:436
  88.5 1.4 %collective-permute-start.36 = (bf16[8,16,128]{2,1,0:T(8,128)(2,1)S(1)}, bf16[8,16,128]{2,1,0:T(8,128)(2,1)S(1)}, u32[]{:S(2)}, u32[]{:S(2)}) collective-permute-start(bf16[8,16,128]{2,1,0:T(8,128)(2,1)S(1)} %get-tuple-element.68), channel_id=1, source_target_pairs={{8,6},{9,7},{10,4},{11,5},{12,2},{13,3},{14,0},{15,1},{0,30},{1,31... | collective-permute-start | bytes 98312 | tf_op jit(solution)/shard_map/ppermute | solution.py:436
  89.9 1.7 %collective-permute-start.35 = (bf16[16,16,128]{2,1,0:T(8,128)(2,1)S(1)}, bf16[16,16,128]{2,1,0:T(8,128)(2,1)S(1)}, u32[]{:S(2)}, u32[]{:S(2)}) collective-permute-start(bf16[16,16,128]{2,1,0:T(8,128)(2,1)S(1)} %get-tuple-element.67), channel_id=1, source_target_pairs={{8,0},{9,1},{10,2},{11,3},{12,4},{13,5},{14,6},{15,7},{0,16},{1,17... | collective-permute-start | bytes 196616 | tf_op jit(solution)/shard_map/ppermute | solution.py:436
  91.6 4.1 %collective-permute-start.38 = (bf16[2,8,16,128]{3,2,1,0:T(8,128)(2,1)S(1)}, bf16[2,8,16,128]{3,2,1,0:T(8,128)(2,1)S(1)}, u32[]{:S(2)}, u32[]{:S(2)}) collective-permute-start(bf16[2,8,16,128]{3,2,1,0:T(8,128)(2,1)S(1)} %pad_maximum_fusion.13), channel_id=1, source_target_pairs={{8,2},{9,5},{10,0},{11,7},{12,6},{13,1},{14,4},{15,3},{0,10},{1,13... | collective-permute-start | bytes 196616 | tf_op jit(solution)/shard_map/ppermute | solution.py:436
  95.8 2.2 %collective-permute-done.35.rest_0_.rest_5_ = bf16[16,16,128]{2,1,0:T(8,128)(2,1)S(1)} collective-permute-done((bf16[16,16,128]{2,1,0:T(8,128)(2,1)S(1)}, bf16[16,16,128]{2,1,0:T(8,128)(2,1)S(1)}, u32[]{:S(2)}, u32[]{:S(2)}) %collective-permute-start.35) | collective-permute-done | bytes 65568 | tf_op jit(solution)/shard_map/ppermute | solution.py:436
  97.9 1.4 %collective-permute-done.38.rest_2_ = bf16[2,8,16,128]{3,2,1,0:T(8,128)(2,1)S(1)} collective-permute-done((bf16[2,8,16,128]{3,2,1,0:T(8,128)(2,1)S(1)}, bf16[2,8,16,128]{3,2,1,0:T(8,128)(2,1)S(1)}, u32[]{:S(2)}, u32[]{:S(2)}) %collective-permute-start.38) | collective-permute-done | bytes 65568 | tf_op jit(solution)/shard_map/ppermute | solution.py:436
  100.8 3.5 %backward_section_0.1 = f32[2,16,1024]{2,1,0:T(8,128)} custom-call(s32[8,128]{1,0:T(8,128)S(1)} %get-tuple-element.38.layers, bf16[2,512,4096]{2,1,0:T(8,128)(2,1)S(1)} %get-tuple-element.39.first_inverse, bf16[2,512,4096]{2,1,0:T(8,128)(2,1)S(1)} %get-tuple-element.56.second_inverse, f32[40,1024]{1,0:T(8,128)S(1)} %get-tuple-element.41.packet, ...), custom_call_target="tpu_custom_call" | custom-call | tf_op jit(solution)/shard_map/backward_section_0/pallas_call | solution.py:383
  (88 shorter events, 29.4 us)
Async XLA Ops:
  2.9 9.1 %collective-permute-start.3 = (f32[24,1024]{1,0:T(8,128)S(1)}, f32[24,1024]{1,0:T(8,128)S(1)}, u32[]{:S(2)}, u32[]{:S(2)}) collective-permute-start(f32[24,1024]{1,0:T(8,128)S(1)} %get-tuple-element.44), channel_id=1, source_target_pairs={{0,8},{1,9},{2,10},{3,11},{4,12},{5,13},{6,14},{7,15},{16,24},{17,... | collective-permute-start | bytes 294920 | tf_op jit(solution)/shard_map/ppermute | solution.py:436
  5.6 6.5 %collective-permute-start.2 = (bf16[2,8,16,128]{3,2,1,0:T(8,128)(2,1)S(1)}, bf16[2,8,16,128]{3,2,1,0:T(8,128)(2,1)S(1)}, u32[]{:S(2)}, u32[]{:S(2)}) collective-permute-start(bf16[2,8,16,128]{3,2,1,0:T(8,128)(2,1)S(1)} %pad_maximum_fusion.6), channel_id=1, source_target_pairs={{0,2},{1,5},{2,0},{3,7},{4,6},{5,1},{6,4},{7,3},{8,10},{9,13},{10,... | collective-permute-start | bytes 196616 | tf_op jit(solution)/shard_map/ppermute | solution.py:436
  7.1 4.9 %collective-permute-start = (bf16[8,16,128]{2,1,0:T(8,128)(2,1)S(1)}, bf16[8,16,128]{2,1,0:T(8,128)(2,1)S(1)}, u32[]{:S(2)}, u32[]{:S(2)}) collective-permute-start(bf16[8,16,128]{2,1,0:T(8,128)(2,1)S(1)} %get-tuple-element.43.refs_0_.rest_0_), channel_id=1, source_target_pairs={{0,6},{1,7},{2,4},{3,5},{4,2},{5,3},{6,0},{7,1},{8,14},{9,15},{10,... | collective-permute-start | bytes 98312 | tf_op jit(solution)/shard_map/ppermute | solution.py:436
  16.8 8.6 %collective-permute-start.10 = (f32[40,1024]{1,0:T(8,128)S(1)}, f32[40,1024]{1,0:T(8,128)S(1)}, u32[]{:S(2)}, u32[]{:S(2)}) collective-permute-start(f32[40,1024]{1,0:T(8,128)S(1)} %get-tuple-element.49), channel_id=1, source_target_pairs={{8,16},{9,17},{10,18},{11,19},{12,20},{13,21},{14,22},{15,23},{16,... | collective-permute-start | bytes 491528 | tf_op jit(solution)/shard_map/ppermute | solution.py:436
  17.2 7.0 %collective-permute-start.6 = (bf16[8,16,128]{2,1,0:T(8,128)(2,1)S(1)}, bf16[8,16,128]{2,1,0:T(8,128)(2,1)S(1)}, u32[]{:S(2)}, u32[]{:S(2)}) collective-permute-start(bf16[8,16,128]{2,1,0:T(8,128)(2,1)S(1)} %get-tuple-element.48), channel_id=1, source_target_pairs={{0,14},{1,15},{2,12},{3,13},{4,10},{5,11},{6,8},{7,9},{8,22},{9,23... | collective-permute-start | bytes 98312 | tf_op jit(solution)/shard_map/ppermute | solution.py:436
  18.0 6.1 %collective-permute-start.5 = (bf16[16,16,128]{2,1,0:T(8,128)(2,1)S(1)}, bf16[16,16,128]{2,1,0:T(8,128)(2,1)S(1)}, u32[]{:S(2)}, u32[]{:S(2)}) collective-permute-start(bf16[16,16,128]{2,1,0:T(8,128)(2,1)S(1)} %get-tuple-element.47), channel_id=1, source_target_pairs={{0,8},{1,9},{2,10},{3,11},{4,12},{5,13},{6,14},{7,15},{8,24},{9,25... | collective-permute-start | bytes 196616 | tf_op jit(solution)/shard_map/ppermute | solution.py:436
  18.0 7.3 %collective-permute-start.8 = (bf16[2,8,16,128]{3,2,1,0:T(8,128)(2,1)S(1)}, bf16[2,8,16,128]{3,2,1,0:T(8,128)(2,1)S(1)}, u32[]{:S(2)}, u32[]{:S(2)}) collective-permute-start(bf16[2,8,16,128]{3,2,1,0:T(8,128)(2,1)S(1)} %pad_maximum_fusion.7), channel_id=1, source_target_pairs={{0,10},{1,13},{2,8},{3,15},{4,14},{5,9},{6,12},{7,11},{8,2},{9,5},... | collective-permute-start | bytes 196616 | tf_op jit(solution)/shard_map/ppermute | solution.py:436
  27.0 6.2 %collective-permute-start.13 = (bf16[8,16,128]{2,1,0:T(8,128)(2,1)S(1)}, bf16[8,16,128]{2,1,0:T(8,128)(2,1)S(1)}, u32[]{:S(2)}, u32[]{:S(2)}) collective-permute-start(bf16[8,16,128]{2,1,0:T(8,128)(2,1)S(1)} %get-tuple-element.52), channel_id=1, source_target_pairs={{0,1},{1,0},{2,3},{3,2},{4,5},{5,4},{6,7},{7,6},{8,9},{9,8},{10,11... | collective-permute-start | bytes 98312 | tf_op jit(solution)/shard_map/ppermute | solution.py:436
  27.2 7.9 %collective-permute-start.12 = (bf16[8,16,128]{2,1,0:T(8,128)(2,1)S(1)}, bf16[8,16,128]{2,1,0:T(8,128)(2,1)S(1)}, u32[]{:S(2)}, u32[]{:S(2)}) collective-permute-start(bf16[8,16,128]{2,1,0:T(8,128)(2,1)S(1)} %get-tuple-element.52), channel_id=1, source_target_pairs={{8,22},{9,23},{10,20},{11,21},{12,18},{13,19},{14,16},{15,17},{16,... | collective-permute-start | bytes 98312 | tf_op jit(solution)/shard_map/ppermute | solution.py:436
  28.7 6.4 %collective-permute-start.11 = (bf16[16,16,128]{2,1,0:T(8,128)(2,1)S(1)}, bf16[16,16,128]{2,1,0:T(8,128)(2,1)S(1)}, u32[]{:S(2)}, u32[]{:S(2)}) collective-permute-start(bf16[16,16,128]{2,1,0:T(8,128)(2,1)S(1)} %get-tuple-element.51), channel_id=1, source_target_pairs={{8,16},{9,17},{10,18},{11,19},{12,20},{13,21},{14,22},{15,23},{16,... | collective-permute-start | bytes 196616 | tf_op jit(solution)/shard_map/ppermute | solution.py:436
  33.2 4.3 %collective-permute-start.14 = (bf16[2,8,16,128]{3,2,1,0:T(8,128)(2,1)S(1)}, bf16[2,8,16,128]{3,2,1,0:T(8,128)(2,1)S(1)}, u32[]{:S(2)}, u32[]{:S(2)}) collective-permute-start(bf16[2,8,16,128]{3,2,1,0:T(8,128)(2,1)S(1)} %pad_maximum_fusion.8), channel_id=1, source_target_pairs={{8,18},{9,21},{10,16},{11,23},{12,22},{13,17},{14,20},{15,19},{16,... | collective-permute-start | bytes 196616 | tf_op jit(solution)/shard_map/ppermute | solution.py:436
  39.4 9.7 %collective-permute-start.18 = (bf16[8,16,128]{2,1,0:T(8,128)(2,1)S(1)}, bf16[8,16,128]{2,1,0:T(8,128)(2,1)S(1)}, u32[]{:S(2)}, u32[]{:S(2)}) collective-permute-start(bf16[8,16,128]{2,1,0:T(8,128)(2,1)S(1)} %get-tuple-element.55), channel_id=1, source_target_pairs={{0,1},{1,0},{2,3},{3,2},{4,5},{5,4},{6,7},{7,6},{8,9},{9,8},{10,11... | collective-permute-start | bytes 98312 | tf_op jit(solution)/shard_map/ppermute | solution.py:436
  39.6 11.0 %collective-permute-start.17 = (bf16[8,16,128]{2,1,0:T(8,128)(2,1)S(1)}, bf16[8,16,128]{2,1,0:T(8,128)(2,1)S(1)}, u32[]{:S(2)}, u32[]{:S(2)}) collective-permute-start(bf16[8,16,128]{2,1,0:T(8,128)(2,1)S(1)} %get-tuple-element.55), channel_id=1, source_target_pairs={{16,30},{17,31},{18,28},{19,29},{20,26},{21,27},{22,24},{23,25},{2... | collective-permute-start | bytes 98312 | tf_op jit(solution)/shard_map/ppermute | solution.py:436
  56.4 5.6 %collective-permute-start.23 = (bf16[2,4,16,128]{3,2,1,0:T(8,128)(2,1)S(1)}, bf16[2,4,16,128]{3,2,1,0:T(8,128)(2,1)S(1)}, u32[]{:S(2)}, u32[]{:S(2)}) collective-permute-start(bf16[2,4,16,128]{3,2,1,0:T(8,128)(2,1)S(1)} %pad_maximum_fusion.14), channel_id=1, source_target_pairs={{0,2},{1,5},{2,0},{3,7},{4,6},{5,1},{6,4},{7,3},{8,10},{9,13},{10,... | collective-permute-start | bytes 98312 | tf_op jit(solution)/shard_map/ppermute | solution.py:436
  57.3 4.6 %collective-permute-start.21 = (bf16[4,16,128]{2,1,0:T(8,128)(2,1)S(1)}, bf16[4,16,128]{2,1,0:T(8,128)(2,1)S(1)}, u32[]{:S(2)}, u32[]{:S(2)}) collective-permute-start(bf16[4,16,128]{2,1,0:T(8,128)(2,1)S(1)} %get-tuple-element.57.rest_0_), channel_id=1, source_target_pairs={{0,6},{1,7},{2,4},{3,5},{4,2},{5,3},{6,0},{7,1},{8,14},{9,15},{10,... | collective-permute-start | bytes 49160 | tf_op jit(solution)/shard_map/ppermute | solution.py:436
  63.5 4.7 %collective-permute-start.27 = (bf16[8,16,128]{2,1,0:T(8,128)(2,1)S(1)}, bf16[8,16,128]{2,1,0:T(8,128)(2,1)S(1)}, u32[]{:S(2)}, u32[]{:S(2)}) collective-permute-start(bf16[8,16,128]{2,1,0:T(8,128)(2,1)S(1)} %get-tuple-element.60), channel_id=1, source_target_pairs={{0,1},{1,0},{2,3},{3,2},{4,5},{5,4},{6,7},{7,6},{8,9},{9,8},{10,11... | collective-permute-start | bytes 98312 | tf_op jit(solution)/shard_map/ppermute | solution.py:436
  63.7 6.6 %collective-permute-start.26 = (bf16[8,16,128]{2,1,0:T(8,128)(2,1)S(1)}, bf16[8,16,128]{2,1,0:T(8,128)(2,1)S(1)}, u32[]{:S(2)}, u32[]{:S(2)}) collective-permute-start(bf16[8,16,128]{2,1,0:T(8,128)(2,1)S(1)} %get-tuple-element.60), channel_id=1, source_target_pairs={{24,22},{25,23},{26,20},{27,21},{28,18},{29,19},{30,16},{31,17},{1... | collective-permute-start | bytes 98312 | tf_op jit(solution)/shard_map/ppermute | solution.py:436
  65.1 5.2 %collective-permute-start.25 = (bf16[16,16,128]{2,1,0:T(8,128)(2,1)S(1)}, bf16[16,16,128]{2,1,0:T(8,128)(2,1)S(1)}, u32[]{:S(2)}, u32[]{:S(2)}) collective-permute-start(bf16[16,16,128]{2,1,0:T(8,128)(2,1)S(1)} %get-tuple-element.59), channel_id=1, source_target_pairs={{24,16},{25,17},{26,18},{27,19},{28,20},{29,21},{30,22},{31,23},{1... | collective-permute-start | bytes 196616 | tf_op jit(solution)/shard_map/ppermute | solution.py:436
  68.2 4.3 %collective-permute-start.28 = (bf16[2,8,16,128]{3,2,1,0:T(8,128)(2,1)S(1)}, bf16[2,8,16,128]{3,2,1,0:T(8,128)(2,1)S(1)}, u32[]{:S(2)}, u32[]{:S(2)}) collective-permute-start(bf16[2,8,16,128]{3,2,1,0:T(8,128)(2,1)S(1)} %pad_maximum_fusion.11), channel_id=1, source_target_pairs={{24,18},{25,21},{26,16},{27,23},{28,22},{29,17},{30,20},{31,19},{1... | collective-permute-start | bytes 196616 | tf_op jit(solution)/shard_map/ppermute | solution.py:436
  74.4 7.9 %collective-permute-start.32 = (bf16[8,16,128]{2,1,0:T(8,128)(2,1)S(1)}, bf16[8,16,128]{2,1,0:T(8,128)(2,1)S(1)}, u32[]{:S(2)}, u32[]{:S(2)}) collective-permute-start(bf16[8,16,128]{2,1,0:T(8,128)(2,1)S(1)} %get-tuple-element.64), channel_id=1, source_target_pairs={{0,1},{1,0},{2,3},{3,2},{4,5},{5,4},{6,7},{7,6},{8,9},{9,8},{10,11... | collective-permute-start | bytes 98312 | tf_op jit(solution)/shard_map/ppermute | solution.py:436
  74.6 9.2 %collective-permute-start.31 = (bf16[8,16,128]{2,1,0:T(8,128)(2,1)S(1)}, bf16[8,16,128]{2,1,0:T(8,128)(2,1)S(1)}, u32[]{:S(2)}, u32[]{:S(2)}) collective-permute-start(bf16[8,16,128]{2,1,0:T(8,128)(2,1)S(1)} %get-tuple-element.64), channel_id=1, source_target_pairs={{16,14},{17,15},{18,12},{19,13},{20,10},{21,11},{22,8},{23,9},{8,6... | collective-permute-start | bytes 98312 | tf_op jit(solution)/shard_map/ppermute | solution.py:436
  88.5 9.4 %collective-permute-start.36 = (bf16[8,16,128]{2,1,0:T(8,128)(2,1)S(1)}, bf16[8,16,128]{2,1,0:T(8,128)(2,1)S(1)}, u32[]{:S(2)}, u32[]{:S(2)}) collective-permute-start(bf16[8,16,128]{2,1,0:T(8,128)(2,1)S(1)} %get-tuple-element.68), channel_id=1, source_target_pairs={{8,6},{9,7},{10,4},{11,5},{12,2},{13,3},{14,0},{15,1},{0,30},{1,31... | collective-permute-start | bytes 98312 | tf_op jit(solution)/shard_map/ppermute | solution.py:436
  89.9 8.0 %collective-permute-start.35 = (bf16[16,16,128]{2,1,0:T(8,128)(2,1)S(1)}, bf16[16,16,128]{2,1,0:T(8,128)(2,1)S(1)}, u32[]{:S(2)}, u32[]{:S(2)}) collective-permute-start(bf16[16,16,128]{2,1,0:T(8,128)(2,1)S(1)} %get-tuple-element.67), channel_id=1, source_target_pairs={{8,0},{9,1},{10,2},{11,3},{12,4},{13,5},{14,6},{15,7},{0,16},{1,17... | collective-permute-start | bytes 196616 | tf_op jit(solution)/shard_map/ppermute | solution.py:436
  91.6 7.7 %collective-permute-start.38 = (bf16[2,8,16,128]{3,2,1,0:T(8,128)(2,1)S(1)}, bf16[2,8,16,128]{3,2,1,0:T(8,128)(2,1)S(1)}, u32[]{:S(2)}, u32[]{:S(2)}) collective-permute-start(bf16[2,8,16,128]{3,2,1,0:T(8,128)(2,1)S(1)} %pad_maximum_fusion.13), channel_id=1, source_target_pairs={{8,2},{9,5},{10,0},{11,7},{12,6},{13,1},{14,4},{15,3},{0,10},{1,13... | collective-permute-start | bytes 196616 | tf_op jit(solution)/shard_map/ppermute | solution.py:436
  (16 other events, 31.6 us)

commit v15 on v14

--- a/solution.py
+++ b/solution.py
@@ -526,6 +526,20 @@
 
     gathered, owners, slots = within(front, join)
 
+    def only_if(condition, exchange, front):
+        known = []
+
+        def needed(front):
+            gathered, *fixed = exchange(front)
+            known.append(fixed)
+            return gathered
+
+        shapes = jax.eval_shape(needed, front)
+        gathered = lax.cond(
+            condition, needed, lambda _: [jnp.zeros(o.shape, o.dtype) for o in shapes], front
+        )
+        return gathered, *known[-1]
+
     near[1] = send(longer, neighbours(1), 0)
     kept, held = [], [None]
     for step in range(sections):
@@ -548,7 +562,7 @@
         second_inverse = outs[-1]
         kept.append(outs[0])
         if final:
-            gathered, owners, slots = within(outs[1])
+            gathered, owners, slots = only_if(section_layers[step] == 2, within, outs[1])
         else:
             gathered, owners, slots, incoming = between(outs[1], outs[2], step, step + 1)
             held.append(incoming)

time: 105 us -> 119 us (1.13)
  local copies, waits for them, and re-layouts: 0.02 us -> 10.6 us
    unnamed x0 -> x12, local copies, waits for them, and re-layouts: none -> 10 us
  transfers between devices with their start and end apart: 40 -> 40, of which waited for: 24 -> 23; matrix products, arithmetic and copies ran while one was open for 0% -> 1% of each run, Pallas kernels for 3% -> 3%
where the time goes in v15:
time: 119 us; the launch traced here: 118 us
  starting transfers between devices  53.5 us (45%)
  waiting for transfers between devices  36.9 us (31%)
  Pallas kernels  15 us (13%)
  local copies, waits for them, and re-layouts  10.6 us (9%)
    ppermute x40, starting transfers between devices, send(): return lax.ppermute(block, ('sweep', 'plane'), route)  53.5 us
    ppermute x40, waiting for transfers between devices, send(): return lax.ppermute(block, ('sweep', 'plane'), route)  36.9 us
    pallas_call x11, Pallas kernels, call(): pl.pallas_call(kernel, in_specs=specs, out_specs=[whole(pltpu.SMEM if len...  15 us
    unnamed x12, local copies, waits for them, and re-layouts  10 us
  transfers between devices with their start and end apart: 40, of which 23 were waited for; matrix products, arithmetic and copies ran while one was open for 1% of the time, Pallas kernels for 3%

profile of v15, /device:TPU:0, one launch (start us, length us, event | category | flops | bytes accessed | tf_op | source)
XLA Modules:
  0.0 117.9 jit_solution(10003090684547629539)
XLA Ops:
  0.0 2.4 %first_fronts.1 = (f32[40,1024]{1,0:T(8,128)S(1)}, f32[24,1024]{1,0:T(8,128)S(1)}, f32[40,1024]{1,0:T(8,128)S(1)}, s32[2,1024]{1,0:T(2,128)S(1)}, bf16[8,16,128]{2,1,0:T(8,128)(2,1)S(1)}, /*index=5*/s32[8,128]{1,0:T(8,128)S(1)}) custom-call(s32[4]{0:T(128)} %layers_in.1, f32[2,16,1024]{2,1,0:T(8,128)} %bitcast.53, f32[2,1024]{1,0:T(2,128)} %isc_in.1, ...), custom_call_target="tpu_custom_call" | custom-call | tf_op jit(solution)/shard_map/first_fronts/pallas_call | solution.py:383
  2.9 2.6 %collective-permute-start.7 = (f32[24,1024]{1,0:T(8,128)S(1)}, f32[24,1024]{1,0:T(8,128)S(1)}, u32[]{:S(2)}, u32[]{:S(2)}) collective-permute-start(f32[24,1024]{1,0:T(8,128)S(1)} %get-tuple-element.49), channel_id=1, source_target_pairs={{0,8},{1,9},{2,10},{3,11},{4,12},{5,13},{6,14},{7,15},{16,24},{17,... | collective-permute-start | bytes 294920 | tf_op jit(solution)/shard_map/ppermute | solution.py:436
  5.6 1.6 %collective-permute-start.6 = (bf16[2,8,16,128]{3,2,1,0:T(8,128)(2,1)S(1)}, bf16[2,8,16,128]{3,2,1,0:T(8,128)(2,1)S(1)}, u32[]{:S(2)}, u32[]{:S(2)}) collective-permute-start(bf16[2,8,16,128]{3,2,1,0:T(8,128)(2,1)S(1)} %pad_maximum_fusion.8), channel_id=1, source_target_pairs={{0,2},{1,5},{2,0},{3,7},{4,6},{5,1},{6,4},{7,3},{8,10},{9,13},{10,... | collective-permute-start | bytes 196616 | tf_op jit(solution)/shard_map/ppermute | solution.py:436
  8.6 3.4 %load_first.1 = (bf16[2,512,4096]{2,1,0:T(8,128)(2,1)S(1)}, bf16[2,512,4096]{2,1,0:T(8,128)(2,1)S(1)}, f32[8,128]{1,0:T(8,128)S(1)}) custom-call(bf16[2,2,512,4096]{3,2,1,0:T(8,128)(2,1)} %inverse.9), custom_call_target="tpu_custom_call" | custom-call | tf_op jit(solution)/shard_map/load_first/pallas_call | solution.py:383
  13.5 3.1 %forward_section_0.1 = (f32[2,16,1024]{2,1,0:T(8,128)S(1)}, bf16[8,16,128]{2,1,0:T(8,128)(2,1)S(1)}, bf16[16,16,128]{2,1,0:T(8,128)(2,1)S(1)}, bf16[2,512,4096]{2,1,0:T(8,128)(2,1)S(1)}) custom-call(s32[8,128]{1,0:T(8,128)S(1)} %get-tuple-element.43.layers, ...), custom_call_target="tpu_custom_call", output_to_operand_aliasing={{3}: (2, {})} | custom-call | tf_op jit(solution)/shard_map/forward_section_0/pallas_call | solution.py:383
  18.0 2.4 %collective-permute-start.12 = (bf16[2,8,16,128]{3,2,1,0:T(8,128)(2,1)S(1)}, bf16[2,8,16,128]{3,2,1,0:T(8,128)(2,1)S(1)}, u32[]{:S(2)}, u32[]{:S(2)}) collective-permute-start(bf16[2,8,16,128]{3,2,1,0:T(8,128)(2,1)S(1)} %pad_maximum_fusion.9), channel_id=1, source_target_pairs={{0,10},{1,13},{2,8},{3,15},{4,14},{5,9},{6,12},{7,11},{8,2},{9,5},... | collective-permute-start | bytes 196616 | tf_op jit(solution)/shard_map/ppermute | solution.py:436
  20.4 3.6 %collective-permute-done.9.rest_0_.rest_4_.rest_8_ = bf16[16,16,128]{2,1,0:T(8,128)(2,1)S(1)} collective-permute-done((bf16[16,16,128]{2,1,0:T(8,128)(2,1)S(1)}, bf16[16,16,128]{2,1,0:T(8,128)(2,1)S(1)}, u32[]{:S(2)}, u32[]{:S(2)}) %collective-permute-start.9) | collective-permute-done | bytes 65568 | tf_op jit(solution)/shard_map/ppermute | solution.py:436
  27.2 1.5 %collective-permute-start.16 = (bf16[8,16,128]{2,1,0:T(8,128)(2,1)S(1)}, bf16[8,16,128]{2,1,0:T(8,128)(2,1)S(1)}, u32[]{:S(2)}, u32[]{:S(2)}) collective-permute-start(bf16[8,16,128]{2,1,0:T(8,128)(2,1)S(1)} %get-tuple-element.57), channel_id=1, source_target_pairs={{8,22},{9,23},{10,20},{11,21},{12,18},{13,19},{14,16},{15,17},{16,... | collective-permute-start | bytes 98312 | tf_op jit(solution)/shard_map/ppermute | solution.py:436
  31.0 4.9 %collective-permute-done.15.rest_0_.rest_4_.rest_8_ = bf16[16,16,128]{2,1,0:T(8,128)(2,1)S(1)} collective-permute-done((bf16[16,16,128]{2,1,0:T(8,128)(2,1)S(1)}, bf16[16,16,128]{2,1,0:T(8,128)(2,1)S(1)}, u32[]{:S(2)}, u32[]{:S(2)}) %collective-permute-start.15) | collective-permute-done | bytes 65568 | tf_op jit(solution)/shard_map/ppermute | solution.py:436
  37.9 10.3 %collective-permute-start.21 = (bf16[8,16,128]{2,1,0:T(8,128)(2,1)S(1)}, bf16[8,16,128]{2,1,0:T(8,128)(2,1)S(1)}, u32[]{:S(2)}, u32[]{:S(2)}) collective-permute-start(bf16[8,16,128]{2,1,0:T(8,128)(2,1)S(1)} %get-tuple-element.60), channel_id=1, source_target_pairs={{16,30},{17,31},{18,28},{19,29},{20,26},{21,27},{22,24},{23,25},{2... | collective-permute-start | bytes 98312 | tf_op jit(solution)/shard_map/ppermute | solution.py:436
  49.8 2.8 %collective-permute-done.23.rest_2_ = bf16[2,8,16,128]{3,2,1,0:T(8,128)(2,1)S(1)} collective-permute-done((bf16[2,8,16,128]{3,2,1,0:T(8,128)(2,1)S(1)}, bf16[2,8,16,128]{3,2,1,0:T(8,128)(2,1)S(1)}, u32[]{:S(2)}, u32[]{:S(2)}) %collective-permute-start.23) | collective-permute-done | bytes 65568 | tf_op jit(solution)/shard_map/ppermute | solution.py:436
  54.3 3.3 %copy-done.3 = bf16[2,512,4096]{2,1,0:T(8,128)(2,1)} copy-done((bf16[2,512,4096]{2,1,0:T(8,128)(2,1)}, bf16[2,512,4096]{2,1,0:T(8,128)(2,1)S(1)}, u32[]{:S(2)}) %copy-start.3) | copy-done | bytes 8388632
  57.5 9.0 %conditional.1 = (bf16[4,16,128]{2,1,0:T(8,128)(2,1)S(1)}, bf16[4,16,128]{2,1,0:T(8,128)(2,1)}, bf16[2,4,16,128]{3,2,1,0:T(8,128)(2,1)}, bf16[4,4,16,128]{3,2,1,0:T(8,128)(2,1)}) conditional(s32[]{:T(128)} %bitcast.18, () %tuple.13, bf16[4,16,128]{2,1,0:T(8,128)(2,1)S(1)} %get-tuple-element.62), branch_computations={%region_0.1_spmd, %region_1.2_spmd} | conditional | flops 81920 | bytes 753856 | solution.py:538
  61.1 3.3 %collective-permute-done = bf16[4,16,128]{2,1,0:T(8,128)(2,1)} collective-permute-done((bf16[4,16,128]{2,1,0:T(8,128)(2,1)S(1)}, bf16[4,16,128]{2,1,0:T(8,128)(2,1)}, u32[]{:S(2)}, u32[]{:S(2)}) %collective-permute-start) | collective-permute-done | bytes 16416 | tf_op jit(solution)/shard_map/cond/branch_1_fun/ppermute | solution.py:436
  66.6 3.4 %copy-done.1 = bf16[2,512,4096]{2,1,0:T(8,128)(2,1)S(1)} copy-done((bf16[2,512,4096]{2,1,0:T(8,128)(2,1)S(1)}, bf16[2,512,4096]{2,1,0:T(8,128)(2,1)}, u32[]{:S(2)}) %copy-start.1) | copy-done | bytes 8388632
  70.0 3.4 %copy-done.4 = bf16[2,512,4096]{2,1,0:T(8,128)(2,1)S(1)} copy-done((bf16[2,512,4096]{2,1,0:T(8,128)(2,1)S(1)}, bf16[2,512,4096]{2,1,0:T(8,128)(2,1)}, u32[]{:S(2)}) %copy-start.4) | copy-done | bytes 8388632
  76.3 8.3 %collective-permute-start.25 = (bf16[16,16,128]{2,1,0:T(8,128)(2,1)S(1)}, bf16[16,16,128]{2,1,0:T(8,128)(2,1)S(1)}, u32[]{:S(2)}, u32[]{:S(2)}) collective-permute-start(bf16[16,16,128]{2,1,0:T(8,128)(2,1)S(1)} %get-tuple-element.68), channel_id=1, source_target_pairs={{24,16},{25,17},{26,18},{27,19},{28,20},{29,21},{30,22},{31,23},{1... | collective-permute-start | bytes 196616 | tf_op jit(solution)/shard_map/ppermute | solution.py:436
  86.5 2.4 %collective-permute-done.28.rest_2_ = bf16[2,8,16,128]{3,2,1,0:T(8,128)(2,1)S(1)} collective-permute-done((bf16[2,8,16,128]{3,2,1,0:T(8,128)(2,1)S(1)}, bf16[2,8,16,128]{3,2,1,0:T(8,128)(2,1)S(1)}, u32[]{:S(2)}, u32[]{:S(2)}) %collective-permute-start.28) | collective-permute-done | bytes 65568 | tf_op jit(solution)/shard_map/ppermute | solution.py:436
  91.1 7.4 %collective-permute-start.31 = (bf16[8,16,128]{2,1,0:T(8,128)(2,1)S(1)}, bf16[8,16,128]{2,1,0:T(8,128)(2,1)S(1)}, u32[]{:S(2)}, u32[]{:S(2)}) collective-permute-start(bf16[8,16,128]{2,1,0:T(8,128)(2,1)S(1)} %get-tuple-element.73), channel_id=1, source_target_pairs={{16,14},{17,15},{18,12},{19,13},{20,10},{21,11},{22,8},{23,9},{8,6... | collective-permute-start | bytes 98312 | tf_op jit(solution)/shard_map/ppermute | solution.py:436
  100.0 2.8 %collective-permute-done.33.rest_2_ = bf16[2,8,16,128]{3,2,1,0:T(8,128)(2,1)S(1)} collective-permute-done((bf16[2,8,16,128]{3,2,1,0:T(8,128)(2,1)S(1)}, bf16[2,8,16,128]{3,2,1,0:T(8,128)(2,1)S(1)}, u32[]{:S(2)}, u32[]{:S(2)}) %collective-permute-start.33) | collective-permute-done | bytes 65568 | tf_op jit(solution)/shard_map/ppermute | solution.py:436
  106.1 1.6 %collective-permute-start.35 = (bf16[16,16,128]{2,1,0:T(8,128)(2,1)S(1)}, bf16[16,16,128]{2,1,0:T(8,128)(2,1)S(1)}, u32[]{:S(2)}, u32[]{:S(2)}) collective-permute-start(bf16[16,16,128]{2,1,0:T(8,128)(2,1)S(1)} %get-tuple-element.76), channel_id=1, source_target_pairs={{8,0},{9,1},{10,2},{11,3},{12,4},{13,5},{14,6},{15,7},{0,16},{1,17... | collective-permute-start | bytes 196616 | tf_op jit(solution)/shard_map/ppermute | solution.py:436
  107.7 1.8 %collective-permute-start.38 = (bf16[2,8,16,128]{3,2,1,0:T(8,128)(2,1)S(1)}, bf16[2,8,16,128]{3,2,1,0:T(8,128)(2,1)S(1)}, u32[]{:S(2)}, u32[]{:S(2)}) collective-permute-start(bf16[2,8,16,128]{3,2,1,0:T(8,128)(2,1)S(1)} %pad_maximum_fusion.14), channel_id=1, source_target_pairs={{8,2},{9,5},{10,0},{11,7},{12,6},{13,1},{14,4},{15,3},{0,10},{1,13... | collective-permute-start | bytes 196616 | tf_op jit(solution)/shard_map/ppermute | solution.py:436
  109.5 2.3 %collective-permute-done.35.rest_0_.rest_5_ = bf16[16,16,128]{2,1,0:T(8,128)(2,1)S(1)} collective-permute-done((bf16[16,16,128]{2,1,0:T(8,128)(2,1)S(1)}, bf16[16,16,128]{2,1,0:T(8,128)(2,1)S(1)}, u32[]{:S(2)}, u32[]{:S(2)}) %collective-permute-start.35) | collective-permute-done | bytes 65568 | tf_op jit(solution)/shard_map/ppermute | solution.py:436
  114.5 3.4 %backward_section_0.1 = f32[2,16,1024]{2,1,0:T(8,128)} custom-call(s32[8,128]{1,0:T(8,128)S(1)} %get-tuple-element.43.layers, bf16[2,512,4096]{2,1,0:T(8,128)(2,1)S(1)} %copy-done.2, bf16[2,512,4096]{2,1,0:T(8,128)(2,1)S(1)} %copy-done.4, f32[40,1024]{1,0:T(8,128)S(1)} %get-tuple-element.46.packet, s32[2,1024]{1,0:T(2,128)S(1)} %get-tuple-element.47.place, ...), custom_call_target="tpu_custom_call" | custom-call | tf_op jit(solution)/shard_map/backward_section_0/pallas_call | solution.py:383
  (103 shorter events, 35.1 us)
Async XLA Ops:
  2.9 9.1 %collective-permute-start.7 = (f32[24,1024]{1,0:T(8,128)S(1)}, f32[24,1024]{1,0:T(8,128)S(1)}, u32[]{:S(2)}, u32[]{:S(2)}) collective-permute-start(f32[24,1024]{1,0:T(8,128)S(1)} %get-tuple-element.49), channel_id=1, source_target_pairs={{0,8},{1,9},{2,10},{3,11},{4,12},{5,13},{6,14},{7,15},{16,24},{17,... | collective-permute-start | bytes 294920 | tf_op jit(solution)/shard_map/ppermute | solution.py:436
  5.6 6.5 %collective-permute-start.6 = (bf16[2,8,16,128]{3,2,1,0:T(8,128)(2,1)S(1)}, bf16[2,8,16,128]{3,2,1,0:T(8,128)(2,1)S(1)}, u32[]{:S(2)}, u32[]{:S(2)}) collective-permute-start(bf16[2,8,16,128]{3,2,1,0:T(8,128)(2,1)S(1)} %pad_maximum_fusion.8), channel_id=1, source_target_pairs={{0,2},{1,5},{2,0},{3,7},{4,6},{5,1},{6,4},{7,3},{8,10},{9,13},{10,... | collective-permute-start | bytes 196616 | tf_op jit(solution)/shard_map/ppermute | solution.py:436
  7.1 4.9 %collective-permute-start.4 = (bf16[8,16,128]{2,1,0:T(8,128)(2,1)S(1)}, bf16[8,16,128]{2,1,0:T(8,128)(2,1)S(1)}, u32[]{:S(2)}, u32[]{:S(2)}) collective-permute-start(bf16[8,16,128]{2,1,0:T(8,128)(2,1)S(1)} %get-tuple-element.48.refs_0_.rest_0_), channel_id=1, source_target_pairs={{0,6},{1,7},{2,4},{3,5},{4,2},{5,3},{6,0},{7,1},{8,14},{9,15},{10,... | collective-permute-start | bytes 98312 | tf_op jit(solution)/shard_map/ppermute | solution.py:436
  16.8 8.6 %collective-permute-start.14 = (f32[40,1024]{1,0:T(8,128)S(1)}, f32[40,1024]{1,0:T(8,128)S(1)}, u32[]{:S(2)}, u32[]{:S(2)}) collective-permute-start(f32[40,1024]{1,0:T(8,128)S(1)} %get-tuple-element.54), channel_id=1, source_target_pairs={{8,16},{9,17},{10,18},{11,19},{12,20},{13,21},{14,22},{15,23},{16,... | collective-permute-start | bytes 491528 | tf_op jit(solution)/shard_map/ppermute | solution.py:436
  17.2 7.0 %collective-permute-start.10 = (bf16[8,16,128]{2,1,0:T(8,128)(2,1)S(1)}, bf16[8,16,128]{2,1,0:T(8,128)(2,1)S(1)}, u32[]{:S(2)}, u32[]{:S(2)}) collective-permute-start(bf16[8,16,128]{2,1,0:T(8,128)(2,1)S(1)} %get-tuple-element.53), channel_id=1, source_target_pairs={{0,14},{1,15},{2,12},{3,13},{4,10},{5,11},{6,8},{7,9},{8,22},{9,23... | collective-permute-start | bytes 98312 | tf_op jit(solution)/shard_map/ppermute | solution.py:436
  18.0 6.1 %collective-permute-start.9 = (bf16[16,16,128]{2,1,0:T(8,128)(2,1)S(1)}, bf16[16,16,128]{2,1,0:T(8,128)(2,1)S(1)}, u32[]{:S(2)}, u32[]{:S(2)}) collective-permute-start(bf16[16,16,128]{2,1,0:T(8,128)(2,1)S(1)} %get-tuple-element.52), channel_id=1, source_target_pairs={{0,8},{1,9},{2,10},{3,11},{4,12},{5,13},{6,14},{7,15},{8,24},{9,25... | collective-permute-start | bytes 196616 | tf_op jit(solution)/shard_map/ppermute | solution.py:436
  18.0 7.3 %collective-permute-start.12 = (bf16[2,8,16,128]{3,2,1,0:T(8,128)(2,1)S(1)}, bf16[2,8,16,128]{3,2,1,0:T(8,128)(2,1)S(1)}, u32[]{:S(2)}, u32[]{:S(2)}) collective-permute-start(bf16[2,8,16,128]{3,2,1,0:T(8,128)(2,1)S(1)} %pad_maximum_fusion.9), channel_id=1, source_target_pairs={{0,10},{1,13},{2,8},{3,15},{4,14},{5,9},{6,12},{7,11},{8,2},{9,5},... | collective-permute-start | bytes 196616 | tf_op jit(solution)/shard_map/ppermute | solution.py:436
  27.2 8.6 %collective-permute-start.16 = (bf16[8,16,128]{2,1,0:T(8,128)(2,1)S(1)}, bf16[8,16,128]{2,1,0:T(8,128)(2,1)S(1)}, u32[]{:S(2)}, u32[]{:S(2)}) collective-permute-start(bf16[8,16,128]{2,1,0:T(8,128)(2,1)S(1)} %get-tuple-element.57), channel_id=1, source_target_pairs={{8,22},{9,23},{10,20},{11,21},{12,18},{13,19},{14,16},{15,17},{16,... | collective-permute-start | bytes 98312 | tf_op jit(solution)/shard_map/ppermute | solution.py:436
  28.7 7.1 %collective-permute-start.15 = (bf16[16,16,128]{2,1,0:T(8,128)(2,1)S(1)}, bf16[16,16,128]{2,1,0:T(8,128)(2,1)S(1)}, u32[]{:S(2)}, u32[]{:S(2)}) collective-permute-start(bf16[16,16,128]{2,1,0:T(8,128)(2,1)S(1)} %get-tuple-element.56), channel_id=1, source_target_pairs={{8,16},{9,17},{10,18},{11,19},{12,20},{13,21},{14,22},{15,23},{16,... | collective-permute-start | bytes 196616 | tf_op jit(solution)/shard_map/ppermute | solution.py:436
  29.8 6.0 %collective-permute-start.18 = (bf16[2,8,16,128]{3,2,1,0:T(8,128)(2,1)S(1)}, bf16[2,8,16,128]{3,2,1,0:T(8,128)(2,1)S(1)}, u32[]{:S(2)}, u32[]{:S(2)}) collective-permute-start(bf16[2,8,16,128]{3,2,1,0:T(8,128)(2,1)S(1)} %pad_maximum_fusion.10), channel_id=1, source_target_pairs={{8,18},{9,21},{10,16},{11,23},{12,22},{13,17},{14,20},{15,19},{16,... | collective-permute-start | bytes 196616 | tf_op jit(solution)/shard_map/ppermute | solution.py:436
  37.7 10.5 %collective-permute-start.22 = (bf16[8,16,128]{2,1,0:T(8,128)(2,1)S(1)}, bf16[8,16,128]{2,1,0:T(8,128)(2,1)S(1)}, u32[]{:S(2)}, u32[]{:S(2)}) collective-permute-start(bf16[8,16,128]{2,1,0:T(8,128)(2,1)S(1)} %get-tuple-element.60), channel_id=1, source_target_pairs={{0,1},{1,0},{2,3},{3,2},{4,5},{5,4},{6,7},{7,6},{8,9},{9,8},{10,11... | collective-permute-start | bytes 98312 | tf_op jit(solution)/shard_map/ppermute | solution.py:436
  37.9 11.9 %collective-permute-start.21 = (bf16[8,16,128]{2,1,0:T(8,128)(2,1)S(1)}, bf16[8,16,128]{2,1,0:T(8,128)(2,1)S(1)}, u32[]{:S(2)}, u32[]{:S(2)}) collective-permute-start(bf16[8,16,128]{2,1,0:T(8,128)(2,1)S(1)} %get-tuple-element.60), channel_id=1, source_target_pairs={{16,30},{17,31},{18,28},{19,29},{20,26},{21,27},{22,24},{23,25},{2... | collective-permute-start | bytes 98312 | tf_op jit(solution)/shard_map/ppermute | solution.py:436
  58.8 5.5 %collective-permute-start.2 = (bf16[2,4,16,128]{3,2,1,0:T(8,128)(2,1)S(1)}, bf16[2,4,16,128]{3,2,1,0:T(8,128)(2,1)}, u32[]{:S(2)}, u32[]{:S(2)}) collective-permute-start(bf16[2,4,16,128]{3,2,1,0:T(8,128)(2,1)S(1)} %pad_maximum_fusion.1), channel_id=1, source_target_pairs={{0,2},{1,5},{2,0},{3,7},{4,6},{5,1},{6,4},{7,3},{8,10},{9,13},{10,... | collective-permute-start | bytes 98312 | tf_op jit(solution)/shard_map/cond/branch_1_fun/ppermute | solution.py:436
  59.6 4.7 %collective-permute-start = (bf16[4,16,128]{2,1,0:T(8,128)(2,1)S(1)}, bf16[4,16,128]{2,1,0:T(8,128)(2,1)}, u32[]{:S(2)}, u32[]{:S(2)}) collective-permute-start(bf16[4,16,128]{2,1,0:T(8,128)(2,1)S(1)} %param.1), channel_id=1, source_target_pairs={{0,6},{1,7},{2,4},{3,5},{4,2},{5,3},{6,0},{7,1},{8,14},{9,15},{10,... | collective-permute-start | bytes 49160 | tf_op jit(solution)/shard_map/cond/branch_1_fun/ppermute | solution.py:436
  74.6 10.1 %collective-permute-start.27 = (bf16[8,16,128]{2,1,0:T(8,128)(2,1)S(1)}, bf16[8,16,128]{2,1,0:T(8,128)(2,1)S(1)}, u32[]{:S(2)}, u32[]{:S(2)}) collective-permute-start(bf16[8,16,128]{2,1,0:T(8,128)(2,1)S(1)} %get-tuple-element.69), channel_id=1, source_target_pairs={{0,1},{1,0},{2,3},{3,2},{4,5},{5,4},{6,7},{7,6},{8,9},{9,8},{10,11... | collective-permute-start | bytes 98312 | tf_op jit(solution)/shard_map/ppermute | solution.py:436
  74.8 11.8 %collective-permute-start.26 = (bf16[8,16,128]{2,1,0:T(8,128)(2,1)S(1)}, bf16[8,16,128]{2,1,0:T(8,128)(2,1)S(1)}, u32[]{:S(2)}, u32[]{:S(2)}) collective-permute-start(bf16[8,16,128]{2,1,0:T(8,128)(2,1)S(1)} %get-tuple-element.69), channel_id=1, source_target_pairs={{24,22},{25,23},{26,20},{27,21},{28,18},{29,19},{30,16},{31,17},{1... | collective-permute-start | bytes 98312 | tf_op jit(solution)/shard_map/ppermute | solution.py:436
  76.3 10.3 %collective-permute-start.25 = (bf16[16,16,128]{2,1,0:T(8,128)(2,1)S(1)}, bf16[16,16,128]{2,1,0:T(8,128)(2,1)S(1)}, u32[]{:S(2)}, u32[]{:S(2)}) collective-permute-start(bf16[16,16,128]{2,1,0:T(8,128)(2,1)S(1)} %get-tuple-element.68), channel_id=1, source_target_pairs={{24,16},{25,17},{26,18},{27,19},{28,20},{29,21},{30,22},{31,23},{1... | collective-permute-start | bytes 196616 | tf_op jit(solution)/shard_map/ppermute | solution.py:436
  84.6 4.3 %collective-permute-start.28 = (bf16[2,8,16,128]{3,2,1,0:T(8,128)(2,1)S(1)}, bf16[2,8,16,128]{3,2,1,0:T(8,128)(2,1)S(1)}, u32[]{:S(2)}, u32[]{:S(2)}) collective-permute-start(bf16[2,8,16,128]{3,2,1,0:T(8,128)(2,1)S(1)} %pad_maximum_fusion.12), channel_id=1, source_target_pairs={{24,18},{25,21},{26,16},{27,23},{28,22},{29,17},{30,20},{31,19},{1... | collective-permute-start | bytes 196616 | tf_op jit(solution)/shard_map/ppermute | solution.py:436
  90.8 7.7 %collective-permute-start.32 = (bf16[8,16,128]{2,1,0:T(8,128)(2,1)S(1)}, bf16[8,16,128]{2,1,0:T(8,128)(2,1)S(1)}, u32[]{:S(2)}, u32[]{:S(2)}) collective-permute-start(bf16[8,16,128]{2,1,0:T(8,128)(2,1)S(1)} %get-tuple-element.73), channel_id=1, source_target_pairs={{0,1},{1,0},{2,3},{3,2},{4,5},{5,4},{6,7},{7,6},{8,9},{9,8},{10,11... | collective-permute-start | bytes 98312 | tf_op jit(solution)/shard_map/ppermute | solution.py:436
  91.1 9.0 %collective-permute-start.31 = (bf16[8,16,128]{2,1,0:T(8,128)(2,1)S(1)}, bf16[8,16,128]{2,1,0:T(8,128)(2,1)S(1)}, u32[]{:S(2)}, u32[]{:S(2)}) collective-permute-start(bf16[8,16,128]{2,1,0:T(8,128)(2,1)S(1)} %get-tuple-element.73), channel_id=1, source_target_pairs={{16,14},{17,15},{18,12},{19,13},{20,10},{21,11},{22,8},{23,9},{8,6... | collective-permute-start | bytes 98312 | tf_op jit(solution)/shard_map/ppermute | solution.py:436
  98.5 4.3 %collective-permute-start.33 = (bf16[2,8,16,128]{3,2,1,0:T(8,128)(2,1)S(1)}, bf16[2,8,16,128]{3,2,1,0:T(8,128)(2,1)S(1)}, u32[]{:S(2)}, u32[]{:S(2)}) collective-permute-start(bf16[2,8,16,128]{3,2,1,0:T(8,128)(2,1)S(1)} %pad_maximum_fusion.13), channel_id=1, source_target_pairs={{16,10},{17,13},{18,8},{19,15},{20,14},{21,9},{22,12},{23,11},{8,1... | collective-permute-start | bytes 196616 | tf_op jit(solution)/shard_map/ppermute | solution.py:436
  104.7 7.1 %collective-permute-start.36 = (bf16[8,16,128]{2,1,0:T(8,128)(2,1)S(1)}, bf16[8,16,128]{2,1,0:T(8,128)(2,1)S(1)}, u32[]{:S(2)}, u32[]{:S(2)}) collective-permute-start(bf16[8,16,128]{2,1,0:T(8,128)(2,1)S(1)} %get-tuple-element.77), channel_id=1, source_target_pairs={{8,6},{9,7},{10,4},{11,5},{12,2},{13,3},{14,0},{15,1},{0,30},{1,31... | collective-permute-start | bytes 98312 | tf_op jit(solution)/shard_map/ppermute | solution.py:436
  106.1 5.7 %collective-permute-start.35 = (bf16[16,16,128]{2,1,0:T(8,128)(2,1)S(1)}, bf16[16,16,128]{2,1,0:T(8,128)(2,1)S(1)}, u32[]{:S(2)}, u32[]{:S(2)}) collective-permute-start(bf16[16,16,128]{2,1,0:T(8,128)(2,1)S(1)} %get-tuple-element.76), channel_id=1, source_target_pairs={{8,0},{9,1},{10,2},{11,3},{12,4},{13,5},{14,6},{15,7},{0,16},{1,17... | collective-permute-start | bytes 196616 | tf_op jit(solution)/shard_map/ppermute | solution.py:436
  107.7 5.3 %collective-permute-start.38 = (bf16[2,8,16,128]{3,2,1,0:T(8,128)(2,1)S(1)}, bf16[2,8,16,128]{3,2,1,0:T(8,128)(2,1)S(1)}, u32[]{:S(2)}, u32[]{:S(2)}) collective-permute-start(bf16[2,8,16,128]{3,2,1,0:T(8,128)(2,1)S(1)} %pad_maximum_fusion.14), channel_id=1, source_target_pairs={{8,2},{9,5},{10,0},{11,7},{12,6},{13,1},{14,4},{15,3},{0,10},{1,13... | collective-permute-start | bytes 196616 | tf_op jit(solution)/shard_map/ppermute | solution.py:436
  (22 other events, 114.7 us)

commit v16 on v14

--- a/solution.py
+++ b/solution.py
@@ -127,15 +127,15 @@
 
 def product(matrix, columns):
     return lax.dot_general(
-        matrix, columns, (((1,), (1,)), ((), ())), preferred_element_type=F32
+        columns, matrix, (((1,), (1,)), ((), ())), preferred_element_type=F32
     )
 
 
 def store_solved(solved, layer, out):
-    rows = out.shape[0]
+    rows = out.shape[1]
     if rows % LANES:
-        out = jnp.concatenate([out, jnp.zeros((-rows % LANES, out.shape[1]), F32)], axis=0)
-    solved[layer] = out.T
+        out = jnp.concatenate([out, jnp.zeros((out.shape[0], -rows % LANES), F32)], axis=1)
+    solved[layer] = out
 
 
 def solve(inverse, stacked, solved, layer):

time: 105 us -> 105 us (level); the launches traced: 104 us -> 105 us
  starting transfers between devices: 53.4 us -> 44.3 us
  Pallas kernels: 14 us -> 19.5 us
  waiting for transfers between devices: 36.4 us -> 41.1 us
    ppermute x40, starting transfers between devices: 53.4 us -> 44.3 us  [send(): return lax.ppermute(block, ('sweep', 'plane'), route)]
    pallas_call x11, Pallas kernels: 14 us -> 19.5 us  [call(): pl.pallas_call(kernel, in_specs=specs, out_specs=[whole(pltpu.SMEM if len...]
    ppermute x40, waiting for transfers between devices: 36.4 us -> 41.1 us  [send(): return lax.ppermute(block, ('sweep', 'plane'), route)]
where the time goes in v16:
time: 105 us
  starting transfers between devices  44.3 us (42%)
  waiting for transfers between devices  41.1 us (39%)
  Pallas kernels  19.5 us (19%)
    ppermute x40, starting transfers between devices, send(): return lax.ppermute(block, ('sweep', 'plane'), route)  44.3 us
    ppermute x40, waiting for transfers between devices, send(): return lax.ppermute(block, ('sweep', 'plane'), route)  41.1 us
    pallas_call x11, Pallas kernels, call(): pl.pallas_call(kernel, in_specs=specs, out_specs=[whole(pltpu.SMEM if len...  19.5 us
  transfers between devices with their start and end apart: 40, of which 24 were waited for; matrix products, arithmetic and copies ran while one was open for 0% of the time, Pallas kernels for 3%

profile of v16, /device:TPU:0, one launch (start us, length us, event | category | flops | bytes accessed | tf_op | source)
XLA Modules:
  0.0 105.4 jit_solution(17232702564373186336)
XLA Ops:
  0.0 2.4 %first_fronts.1 = (f32[40,1024]{1,0:T(8,128)S(1)}, f32[24,1024]{1,0:T(8,128)S(1)}, f32[40,1024]{1,0:T(8,128)S(1)}, s32[2,1024]{1,0:T(2,128)S(1)}, bf16[8,16,128]{2,1,0:T(8,128)(2,1)S(1)}, /*index=5*/s32[8,128]{1,0:T(8,128)S(1)}) custom-call(s32[4]{0:T(128)} %layers_in.1, f32[2,16,1024]{2,1,0:T(8,128)} %bitcast.53, f32[2,1024]{1,0:T(2,128)} %isc_in.1, ...), custom_call_target="tpu_custom_call" | custom-call | tf_op jit(solution)/shard_map/first_fronts/pallas_call | solution.py:383
  2.9 2.6 %collective-permute-start.3 = (f32[24,1024]{1,0:T(8,128)S(1)}, f32[24,1024]{1,0:T(8,128)S(1)}, u32[]{:S(2)}, u32[]{:S(2)}) collective-permute-start(f32[24,1024]{1,0:T(8,128)S(1)} %get-tuple-element.44), channel_id=1, source_target_pairs={{0,8},{1,9},{2,10},{3,11},{4,12},{5,13},{6,14},{7,15},{16,24},{17,... | collective-permute-start | bytes 294920 | tf_op jit(solution)/shard_map/ppermute | solution.py:436
  5.6 1.6 %collective-permute-start.2 = (bf16[2,8,16,128]{3,2,1,0:T(8,128)(2,1)S(1)}, bf16[2,8,16,128]{3,2,1,0:T(8,128)(2,1)S(1)}, u32[]{:S(2)}, u32[]{:S(2)}) collective-permute-start(bf16[2,8,16,128]{3,2,1,0:T(8,128)(2,1)S(1)} %pad_maximum_fusion.6), channel_id=1, source_target_pairs={{0,2},{1,5},{2,0},{3,7},{4,6},{5,1},{6,4},{7,3},{8,10},{9,13},{10,... | collective-permute-start | bytes 196616 | tf_op jit(solution)/shard_map/ppermute | solution.py:436
  7.1 1.5 %collective-permute-start = (bf16[8,16,128]{2,1,0:T(8,128)(2,1)S(1)}, bf16[8,16,128]{2,1,0:T(8,128)(2,1)S(1)}, u32[]{:S(2)}, u32[]{:S(2)}) collective-permute-start(bf16[8,16,128]{2,1,0:T(8,128)(2,1)S(1)} %get-tuple-element.43.refs_0_.rest_0_), channel_id=1, source_target_pairs={{0,6},{1,7},{2,4},{3,5},{4,2},{5,3},{6,0},{7,1},{8,14},{9,15},{10,... | collective-permute-start | bytes 98312 | tf_op jit(solution)/shard_map/ppermute | solution.py:436
  8.6 3.4 %load_first.1 = (bf16[2,512,4096]{2,1,0:T(8,128)(2,1)S(1)}, bf16[2,512,4096]{2,1,0:T(8,128)(2,1)S(1)}, f32[8,128]{1,0:T(8,128)S(1)}) custom-call(bf16[2,2,512,4096]{3,2,1,0:T(8,128)(2,1)} %inverse.9), custom_call_target="tpu_custom_call" | custom-call | tf_op jit(solution)/shard_map/load_first/pallas_call | solution.py:383
  12.2 1.3 %collective-permute-done.4.rest_3_ = bf16[4,8,16,128]{3,2,1,0:T(8,128)(2,1)S(1)} collective-permute-done((bf16[4,8,16,128]{3,2,1,0:T(8,128)(2,1)S(1)}, bf16[4,8,16,128]{3,2,1,0:T(8,128)(2,1)S(1)}, u32[]{:S(2)}, u32[]{:S(2)}) %collective-permute-start.4) | collective-permute-done | bytes 131104 | tf_op jit(solution)/shard_map/ppermute | solution.py:436
  13.5 6.4 %forward_section_0.1 = (f32[2,16,1024]{2,1,0:T(8,128)S(1)}, bf16[8,16,128]{2,1,0:T(8,128)(2,1)S(1)}, bf16[16,16,128]{2,1,0:T(8,128)(2,1)S(1)}, bf16[2,512,4096]{2,1,0:T(8,128)(2,1)S(1)}) custom-call(s32[8,128]{1,0:T(8,128)S(1)} %get-tuple-element.38.layers, ...), custom_call_target="tpu_custom_call", output_to_operand_aliasing={{3}: (2, {})} | custom-call | tf_op jit(solution)/shard_map/forward_section_0/pallas_call | solution.py:383
  21.3 5.4 %collective-permute-done.5.rest_0_.rest_4_.rest_8_ = bf16[16,16,128]{2,1,0:T(8,128)(2,1)S(1)} collective-permute-done((bf16[16,16,128]{2,1,0:T(8,128)(2,1)S(1)}, bf16[16,16,128]{2,1,0:T(8,128)(2,1)S(1)}, u32[]{:S(2)}, u32[]{:S(2)}) %collective-permute-start.5) | collective-permute-done | bytes 65568 | tf_op jit(solution)/shard_map/ppermute | solution.py:436
  26.7 1.4 %collective-permute-done.6.rest_1_ = bf16[8,16,128]{2,1,0:T(8,128)(2,1)S(1)} collective-permute-done((bf16[8,16,128]{2,1,0:T(8,128)(2,1)S(1)}, bf16[8,16,128]{2,1,0:T(8,128)(2,1)S(1)}, u32[]{:S(2)}, u32[]{:S(2)}) %collective-permute-start.6) | collective-permute-done | bytes 32800 | tf_op jit(solution)/shard_map/ppermute | solution.py:436
  30.4 1.4 %collective-permute-start.12 = (bf16[8,16,128]{2,1,0:T(8,128)(2,1)S(1)}, bf16[8,16,128]{2,1,0:T(8,128)(2,1)S(1)}, u32[]{:S(2)}, u32[]{:S(2)}) collective-permute-start(bf16[8,16,128]{2,1,0:T(8,128)(2,1)S(1)} %get-tuple-element.52), channel_id=1, source_target_pairs={{8,22},{9,23},{10,20},{11,21},{12,18},{13,19},{14,16},{15,17},{16,... | collective-permute-start | bytes 98312 | tf_op jit(solution)/shard_map/ppermute | solution.py:436
  33.6 4.7 %collective-permute-done.11.rest_0_.rest_4_.rest_8_ = bf16[16,16,128]{2,1,0:T(8,128)(2,1)S(1)} collective-permute-done((bf16[16,16,128]{2,1,0:T(8,128)(2,1)S(1)}, bf16[16,16,128]{2,1,0:T(8,128)(2,1)S(1)}, u32[]{:S(2)}, u32[]{:S(2)}) %collective-permute-start.11) | collective-permute-done | bytes 65568 | tf_op jit(solution)/shard_map/ppermute | solution.py:436
  40.4 6.9 %collective-permute-start.17 = (bf16[8,16,128]{2,1,0:T(8,128)(2,1)S(1)}, bf16[8,16,128]{2,1,0:T(8,128)(2,1)S(1)}, u32[]{:S(2)}, u32[]{:S(2)}) collective-permute-start(bf16[8,16,128]{2,1,0:T(8,128)(2,1)S(1)} %get-tuple-element.55), channel_id=1, source_target_pairs={{16,30},{17,31},{18,28},{19,29},{20,26},{21,27},{22,24},{23,25},{2... | collective-permute-start | bytes 98312 | tf_op jit(solution)/shard_map/ppermute | solution.py:436
  48.9 2.8 %collective-permute-done.19.rest_2_ = bf16[2,8,16,128]{3,2,1,0:T(8,128)(2,1)S(1)} collective-permute-done((bf16[2,8,16,128]{3,2,1,0:T(8,128)(2,1)S(1)}, bf16[2,8,16,128]{3,2,1,0:T(8,128)(2,1)S(1)}, u32[]{:S(2)}, u32[]{:S(2)}) %collective-permute-start.19) | collective-permute-done | bytes 65568 | tf_op jit(solution)/shard_map/ppermute | solution.py:436
  55.3 1.4 %collective-permute-start.21 = (bf16[4,16,128]{2,1,0:T(8,128)(2,1)S(1)}, bf16[4,16,128]{2,1,0:T(8,128)(2,1)S(1)}, u32[]{:S(2)}, u32[]{:S(2)}) collective-permute-start(bf16[4,16,128]{2,1,0:T(8,128)(2,1)S(1)} %get-tuple-element.57.rest_0_), channel_id=1, source_target_pairs={{0,6},{1,7},{2,4},{3,5},{4,2},{5,3},{6,0},{7,1},{8,14},{9,15},{10,... | collective-permute-start | bytes 49160 | tf_op jit(solution)/shard_map/ppermute | solution.py:436
  56.8 3.2 %collective-permute-done.21.rest_1_ = bf16[4,16,128]{2,1,0:T(8,128)(2,1)S(1)} collective-permute-done((bf16[4,16,128]{2,1,0:T(8,128)(2,1)S(1)}, bf16[4,16,128]{2,1,0:T(8,128)(2,1)S(1)}, u32[]{:S(2)}, u32[]{:S(2)}) %collective-permute-start.21) | collective-permute-done | bytes 16416 | tf_op jit(solution)/shard_map/ppermute | solution.py:436
  61.8 1.4 %collective-permute-start.26 = (bf16[8,16,128]{2,1,0:T(8,128)(2,1)S(1)}, bf16[8,16,128]{2,1,0:T(8,128)(2,1)S(1)}, u32[]{:S(2)}, u32[]{:S(2)}) collective-permute-start(bf16[8,16,128]{2,1,0:T(8,128)(2,1)S(1)} %get-tuple-element.60), channel_id=1, source_target_pairs={{24,22},{25,23},{26,20},{27,21},{28,18},{29,19},{30,16},{31,17},{1... | collective-permute-start | bytes 98312 | tf_op jit(solution)/shard_map/ppermute | solution.py:436
  63.2 8.0 %collective-permute-start.25 = (bf16[16,16,128]{2,1,0:T(8,128)(2,1)S(1)}, bf16[16,16,128]{2,1,0:T(8,128)(2,1)S(1)}, u32[]{:S(2)}, u32[]{:S(2)}) collective-permute-start(bf16[16,16,128]{2,1,0:T(8,128)(2,1)S(1)} %get-tuple-element.59), channel_id=1, source_target_pairs={{24,16},{25,17},{26,18},{27,19},{28,20},{29,21},{30,22},{31,23},{1... | collective-permute-start | bytes 196616 | tf_op jit(solution)/shard_map/ppermute | solution.py:436
  73.1 2.4 %collective-permute-done.28.rest_2_ = bf16[2,8,16,128]{3,2,1,0:T(8,128)(2,1)S(1)} collective-permute-done((bf16[2,8,16,128]{3,2,1,0:T(8,128)(2,1)S(1)}, bf16[2,8,16,128]{3,2,1,0:T(8,128)(2,1)S(1)}, u32[]{:S(2)}, u32[]{:S(2)}) %collective-permute-start.28) | collective-permute-done | bytes 65568 | tf_op jit(solution)/shard_map/ppermute | solution.py:436
  77.4 4.9 %collective-permute-start.31 = (bf16[8,16,128]{2,1,0:T(8,128)(2,1)S(1)}, bf16[8,16,128]{2,1,0:T(8,128)(2,1)S(1)}, u32[]{:S(2)}, u32[]{:S(2)}) collective-permute-start(bf16[8,16,128]{2,1,0:T(8,128)(2,1)S(1)} %get-tuple-element.64), channel_id=1, source_target_pairs={{16,14},{17,15},{18,12},{19,13},{20,10},{21,11},{22,8},{23,9},{8,6... | collective-permute-start | bytes 98312 | tf_op jit(solution)/shard_map/ppermute | solution.py:436
  83.9 2.8 %collective-permute-done.33.rest_2_ = bf16[2,8,16,128]{3,2,1,0:T(8,128)(2,1)S(1)} collective-permute-done((bf16[2,8,16,128]{3,2,1,0:T(8,128)(2,1)S(1)}, bf16[2,8,16,128]{3,2,1,0:T(8,128)(2,1)S(1)}, u32[]{:S(2)}, u32[]{:S(2)}) %collective-permute-start.33) | collective-permute-done | bytes 65568 | tf_op jit(solution)/shard_map/ppermute | solution.py:436
  88.8 3.5 %collective-permute-start.36 = (bf16[8,16,128]{2,1,0:T(8,128)(2,1)S(1)}, bf16[8,16,128]{2,1,0:T(8,128)(2,1)S(1)}, u32[]{:S(2)}, u32[]{:S(2)}) collective-permute-start(bf16[8,16,128]{2,1,0:T(8,128)(2,1)S(1)} %get-tuple-element.68), channel_id=1, source_target_pairs={{8,6},{9,7},{10,4},{11,5},{12,2},{13,3},{14,0},{15,1},{0,30},{1,31... | collective-permute-start | bytes 98312 | tf_op jit(solution)/shard_map/ppermute | solution.py:436
  92.8 1.9 %collective-permute-start.38 = (bf16[2,8,16,128]{3,2,1,0:T(8,128)(2,1)S(1)}, bf16[2,8,16,128]{3,2,1,0:T(8,128)(2,1)S(1)}, u32[]{:S(2)}, u32[]{:S(2)}) collective-permute-start(bf16[2,8,16,128]{3,2,1,0:T(8,128)(2,1)S(1)} %pad_maximum_fusion.13), channel_id=1, source_target_pairs={{8,2},{9,5},{10,0},{11,7},{12,6},{13,1},{14,4},{15,3},{0,10},{1,13... | collective-permute-start | bytes 196616 | tf_op jit(solution)/shard_map/ppermute | solution.py:436
  94.7 2.5 %collective-permute-done.35.rest_0_.rest_5_ = bf16[16,16,128]{2,1,0:T(8,128)(2,1)S(1)} collective-permute-done((bf16[16,16,128]{2,1,0:T(8,128)(2,1)S(1)}, bf16[16,16,128]{2,1,0:T(8,128)(2,1)S(1)}, u32[]{:S(2)}, u32[]{:S(2)}) %collective-permute-start.35) | collective-permute-done | bytes 65568 | tf_op jit(solution)/shard_map/ppermute | solution.py:436
  99.8 5.6 %backward_section_0.1 = f32[2,16,1024]{2,1,0:T(8,128)} custom-call(s32[8,128]{1,0:T(8,128)S(1)} %get-tuple-element.38.layers, bf16[2,512,4096]{2,1,0:T(8,128)(2,1)S(1)} %get-tuple-element.39.first_inverse, bf16[2,512,4096]{2,1,0:T(8,128)(2,1)S(1)} %get-tuple-element.56.second_inverse, f32[40,1024]{1,0:T(8,128)S(1)} %get-tuple-element.41.packet, ...), custom_call_target="tpu_custom_call" | custom-call | tf_op jit(solution)/shard_map/backward_section_0/pallas_call | solution.py:383
  (88 shorter events, 25.4 us)
Async XLA Ops:
  2.9 9.1 %collective-permute-start.3 = (f32[24,1024]{1,0:T(8,128)S(1)}, f32[24,1024]{1,0:T(8,128)S(1)}, u32[]{:S(2)}, u32[]{:S(2)}) collective-permute-start(f32[24,1024]{1,0:T(8,128)S(1)} %get-tuple-element.44), channel_id=1, source_target_pairs={{0,8},{1,9},{2,10},{3,11},{4,12},{5,13},{6,14},{7,15},{16,24},{17,... | collective-permute-start | bytes 294920 | tf_op jit(solution)/shard_map/ppermute | solution.py:436
  5.6 6.5 %collective-permute-start.2 = (bf16[2,8,16,128]{3,2,1,0:T(8,128)(2,1)S(1)}, bf16[2,8,16,128]{3,2,1,0:T(8,128)(2,1)S(1)}, u32[]{:S(2)}, u32[]{:S(2)}) collective-permute-start(bf16[2,8,16,128]{3,2,1,0:T(8,128)(2,1)S(1)} %pad_maximum_fusion.6), channel_id=1, source_target_pairs={{0,2},{1,5},{2,0},{3,7},{4,6},{5,1},{6,4},{7,3},{8,10},{9,13},{10,... | collective-permute-start | bytes 196616 | tf_op jit(solution)/shard_map/ppermute | solution.py:436
  7.1 4.9 %collective-permute-start = (bf16[8,16,128]{2,1,0:T(8,128)(2,1)S(1)}, bf16[8,16,128]{2,1,0:T(8,128)(2,1)S(1)}, u32[]{:S(2)}, u32[]{:S(2)}) collective-permute-start(bf16[8,16,128]{2,1,0:T(8,128)(2,1)S(1)} %get-tuple-element.43.refs_0_.rest_0_), channel_id=1, source_target_pairs={{0,6},{1,7},{2,4},{3,5},{4,2},{5,3},{6,0},{7,1},{8,14},{9,15},{10,... | collective-permute-start | bytes 98312 | tf_op jit(solution)/shard_map/ppermute | solution.py:436
  20.1 8.5 %collective-permute-start.10 = (f32[40,1024]{1,0:T(8,128)S(1)}, f32[40,1024]{1,0:T(8,128)S(1)}, u32[]{:S(2)}, u32[]{:S(2)}) collective-permute-start(f32[40,1024]{1,0:T(8,128)S(1)} %get-tuple-element.49), channel_id=1, source_target_pairs={{8,16},{9,17},{10,18},{11,19},{12,20},{13,21},{14,22},{15,23},{16,... | collective-permute-start | bytes 491528 | tf_op jit(solution)/shard_map/ppermute | solution.py:436
  20.5 7.6 %collective-permute-start.6 = (bf16[8,16,128]{2,1,0:T(8,128)(2,1)S(1)}, bf16[8,16,128]{2,1,0:T(8,128)(2,1)S(1)}, u32[]{:S(2)}, u32[]{:S(2)}) collective-permute-start(bf16[8,16,128]{2,1,0:T(8,128)(2,1)S(1)} %get-tuple-element.48), channel_id=1, source_target_pairs={{0,14},{1,15},{2,12},{3,13},{4,10},{5,11},{6,8},{7,9},{8,22},{9,23... | collective-permute-start | bytes 98312 | tf_op jit(solution)/shard_map/ppermute | solution.py:436
  20.5 6.2 %collective-permute-start.5 = (bf16[16,16,128]{2,1,0:T(8,128)(2,1)S(1)}, bf16[16,16,128]{2,1,0:T(8,128)(2,1)S(1)}, u32[]{:S(2)}, u32[]{:S(2)}) collective-permute-start(bf16[16,16,128]{2,1,0:T(8,128)(2,1)S(1)} %get-tuple-element.47), channel_id=1, source_target_pairs={{0,8},{1,9},{2,10},{3,11},{4,12},{5,13},{6,14},{7,15},{8,24},{9,25... | collective-permute-start | bytes 196616 | tf_op jit(solution)/shard_map/ppermute | solution.py:436
  21.2 7.3 %collective-permute-start.8 = (bf16[2,8,16,128]{3,2,1,0:T(8,128)(2,1)S(1)}, bf16[2,8,16,128]{3,2,1,0:T(8,128)(2,1)S(1)}, u32[]{:S(2)}, u32[]{:S(2)}) collective-permute-start(bf16[2,8,16,128]{3,2,1,0:T(8,128)(2,1)S(1)} %pad_maximum_fusion.7), channel_id=1, source_target_pairs={{0,10},{1,13},{2,8},{3,15},{4,14},{5,9},{6,12},{7,11},{8,2},{9,5},... | collective-permute-start | bytes 196616 | tf_op jit(solution)/shard_map/ppermute | solution.py:436
  30.4 7.9 %collective-permute-start.12 = (bf16[8,16,128]{2,1,0:T(8,128)(2,1)S(1)}, bf16[8,16,128]{2,1,0:T(8,128)(2,1)S(1)}, u32[]{:S(2)}, u32[]{:S(2)}) collective-permute-start(bf16[8,16,128]{2,1,0:T(8,128)(2,1)S(1)} %get-tuple-element.52), channel_id=1, source_target_pairs={{8,22},{9,23},{10,20},{11,21},{12,18},{13,19},{14,16},{15,17},{16,... | collective-permute-start | bytes 98312 | tf_op jit(solution)/shard_map/ppermute | solution.py:436
  31.9 6.4 %collective-permute-start.11 = (bf16[16,16,128]{2,1,0:T(8,128)(2,1)S(1)}, bf16[16,16,128]{2,1,0:T(8,128)(2,1)S(1)}, u32[]{:S(2)}, u32[]{:S(2)}) collective-permute-start(bf16[16,16,128]{2,1,0:T(8,128)(2,1)S(1)} %get-tuple-element.51), channel_id=1, source_target_pairs={{8,16},{9,17},{10,18},{11,19},{12,20},{13,21},{14,22},{15,23},{16,... | collective-permute-start | bytes 196616 | tf_op jit(solution)/shard_map/ppermute | solution.py:436
  32.6 5.7 %collective-permute-start.14 = (bf16[2,8,16,128]{3,2,1,0:T(8,128)(2,1)S(1)}, bf16[2,8,16,128]{3,2,1,0:T(8,128)(2,1)S(1)}, u32[]{:S(2)}, u32[]{:S(2)}) collective-permute-start(bf16[2,8,16,128]{3,2,1,0:T(8,128)(2,1)S(1)} %pad_maximum_fusion.8), channel_id=1, source_target_pairs={{8,18},{9,21},{10,16},{11,23},{12,22},{13,17},{14,20},{15,19},{16,... | collective-permute-start | bytes 196616 | tf_op jit(solution)/shard_map/ppermute | solution.py:436
  40.2 7.2 %collective-permute-start.18 = (bf16[8,16,128]{2,1,0:T(8,128)(2,1)S(1)}, bf16[8,16,128]{2,1,0:T(8,128)(2,1)S(1)}, u32[]{:S(2)}, u32[]{:S(2)}) collective-permute-start(bf16[8,16,128]{2,1,0:T(8,128)(2,1)S(1)} %get-tuple-element.55), channel_id=1, source_target_pairs={{0,1},{1,0},{2,3},{3,2},{4,5},{5,4},{6,7},{7,6},{8,9},{9,8},{10,11... | collective-permute-start | bytes 98312 | tf_op jit(solution)/shard_map/ppermute | solution.py:436
  40.4 8.5 %collective-permute-start.17 = (bf16[8,16,128]{2,1,0:T(8,128)(2,1)S(1)}, bf16[8,16,128]{2,1,0:T(8,128)(2,1)S(1)}, u32[]{:S(2)}, u32[]{:S(2)}) collective-permute-start(bf16[8,16,128]{2,1,0:T(8,128)(2,1)S(1)} %get-tuple-element.55), channel_id=1, source_target_pairs={{16,30},{17,31},{18,28},{19,29},{20,26},{21,27},{22,24},{23,25},{2... | collective-permute-start | bytes 98312 | tf_op jit(solution)/shard_map/ppermute | solution.py:436
  54.6 5.4 %collective-permute-start.23 = (bf16[2,4,16,128]{3,2,1,0:T(8,128)(2,1)S(1)}, bf16[2,4,16,128]{3,2,1,0:T(8,128)(2,1)S(1)}, u32[]{:S(2)}, u32[]{:S(2)}) collective-permute-start(bf16[2,4,16,128]{3,2,1,0:T(8,128)(2,1)S(1)} %pad_maximum_fusion.14), channel_id=1, source_target_pairs={{0,2},{1,5},{2,0},{3,7},{4,6},{5,1},{6,4},{7,3},{8,10},{9,13},{10,... | collective-permute-start | bytes 98312 | tf_op jit(solution)/shard_map/ppermute | solution.py:436
  55.3 4.6 %collective-permute-start.21 = (bf16[4,16,128]{2,1,0:T(8,128)(2,1)S(1)}, bf16[4,16,128]{2,1,0:T(8,128)(2,1)S(1)}, u32[]{:S(2)}, u32[]{:S(2)}) collective-permute-start(bf16[4,16,128]{2,1,0:T(8,128)(2,1)S(1)} %get-tuple-element.57.rest_0_), channel_id=1, source_target_pairs={{0,6},{1,7},{2,4},{3,5},{4,2},{5,3},{6,0},{7,1},{8,14},{9,15},{10,... | collective-permute-start | bytes 49160 | tf_op jit(solution)/shard_map/ppermute | solution.py:436
  61.5 9.7 %collective-permute-start.27 = (bf16[8,16,128]{2,1,0:T(8,128)(2,1)S(1)}, bf16[8,16,128]{2,1,0:T(8,128)(2,1)S(1)}, u32[]{:S(2)}, u32[]{:S(2)}) collective-permute-start(bf16[8,16,128]{2,1,0:T(8,128)(2,1)S(1)} %get-tuple-element.60), channel_id=1, source_target_pairs={{0,1},{1,0},{2,3},{3,2},{4,5},{5,4},{6,7},{7,6},{8,9},{9,8},{10,11... | collective-permute-start | bytes 98312 | tf_op jit(solution)/shard_map/ppermute | solution.py:436
  61.8 11.4 %collective-permute-start.26 = (bf16[8,16,128]{2,1,0:T(8,128)(2,1)S(1)}, bf16[8,16,128]{2,1,0:T(8,128)(2,1)S(1)}, u32[]{:S(2)}, u32[]{:S(2)}) collective-permute-start(bf16[8,16,128]{2,1,0:T(8,128)(2,1)S(1)} %get-tuple-element.60), channel_id=1, source_target_pairs={{24,22},{25,23},{26,20},{27,21},{28,18},{29,19},{30,16},{31,17},{1... | collective-permute-start | bytes 98312 | tf_op jit(solution)/shard_map/ppermute | solution.py:436
  63.2 9.9 %collective-permute-start.25 = (bf16[16,16,128]{2,1,0:T(8,128)(2,1)S(1)}, bf16[16,16,128]{2,1,0:T(8,128)(2,1)S(1)}, u32[]{:S(2)}, u32[]{:S(2)}) collective-permute-start(bf16[16,16,128]{2,1,0:T(8,128)(2,1)S(1)} %get-tuple-element.59), channel_id=1, source_target_pairs={{24,16},{25,17},{26,18},{27,19},{28,20},{29,21},{30,22},{31,23},{1... | collective-permute-start | bytes 196616 | tf_op jit(solution)/shard_map/ppermute | solution.py:436
  71.2 4.3 %collective-permute-start.28 = (bf16[2,8,16,128]{3,2,1,0:T(8,128)(2,1)S(1)}, bf16[2,8,16,128]{3,2,1,0:T(8,128)(2,1)S(1)}, u32[]{:S(2)}, u32[]{:S(2)}) collective-permute-start(bf16[2,8,16,128]{3,2,1,0:T(8,128)(2,1)S(1)} %pad_maximum_fusion.11), channel_id=1, source_target_pairs={{24,18},{25,21},{26,16},{27,23},{28,22},{29,17},{30,20},{31,19},{1... | collective-permute-start | bytes 196616 | tf_op jit(solution)/shard_map/ppermute | solution.py:436
  77.2 5.2 %collective-permute-start.32 = (bf16[8,16,128]{2,1,0:T(8,128)(2,1)S(1)}, bf16[8,16,128]{2,1,0:T(8,128)(2,1)S(1)}, u32[]{:S(2)}, u32[]{:S(2)}) collective-permute-start(bf16[8,16,128]{2,1,0:T(8,128)(2,1)S(1)} %get-tuple-element.64), channel_id=1, source_target_pairs={{0,1},{1,0},{2,3},{3,2},{4,5},{5,4},{6,7},{7,6},{8,9},{9,8},{10,11... | collective-permute-start | bytes 98312 | tf_op jit(solution)/shard_map/ppermute | solution.py:436
  77.4 6.5 %collective-permute-start.31 = (bf16[8,16,128]{2,1,0:T(8,128)(2,1)S(1)}, bf16[8,16,128]{2,1,0:T(8,128)(2,1)S(1)}, u32[]{:S(2)}, u32[]{:S(2)}) collective-permute-start(bf16[8,16,128]{2,1,0:T(8,128)(2,1)S(1)} %get-tuple-element.64), channel_id=1, source_target_pairs={{16,14},{17,15},{18,12},{19,13},{20,10},{21,11},{22,8},{23,9},{8,6... | collective-permute-start | bytes 98312 | tf_op jit(solution)/shard_map/ppermute | solution.py:436
  82.4 4.3 %collective-permute-start.33 = (bf16[2,8,16,128]{3,2,1,0:T(8,128)(2,1)S(1)}, bf16[2,8,16,128]{3,2,1,0:T(8,128)(2,1)S(1)}, u32[]{:S(2)}, u32[]{:S(2)}) collective-permute-start(bf16[2,8,16,128]{3,2,1,0:T(8,128)(2,1)S(1)} %pad_maximum_fusion.12), channel_id=1, source_target_pairs={{16,10},{17,13},{18,8},{19,15},{20,14},{21,9},{22,12},{23,11},{8,1... | collective-permute-start | bytes 196616 | tf_op jit(solution)/shard_map/ppermute | solution.py:436
  88.8 8.5 %collective-permute-start.36 = (bf16[8,16,128]{2,1,0:T(8,128)(2,1)S(1)}, bf16[8,16,128]{2,1,0:T(8,128)(2,1)S(1)}, u32[]{:S(2)}, u32[]{:S(2)}) collective-permute-start(bf16[8,16,128]{2,1,0:T(8,128)(2,1)S(1)} %get-tuple-element.68), channel_id=1, source_target_pairs={{8,6},{9,7},{10,4},{11,5},{12,2},{13,3},{14,0},{15,1},{0,30},{1,31... | collective-permute-start | bytes 98312 | tf_op jit(solution)/shard_map/ppermute | solution.py:436
  92.3 5.0 %collective-permute-start.35 = (bf16[16,16,128]{2,1,0:T(8,128)(2,1)S(1)}, bf16[16,16,128]{2,1,0:T(8,128)(2,1)S(1)}, u32[]{:S(2)}, u32[]{:S(2)}) collective-permute-start(bf16[16,16,128]{2,1,0:T(8,128)(2,1)S(1)} %get-tuple-element.67), channel_id=1, source_target_pairs={{8,0},{9,1},{10,2},{11,3},{12,4},{13,5},{14,6},{15,7},{0,16},{1,17... | collective-permute-start | bytes 196616 | tf_op jit(solution)/shard_map/ppermute | solution.py:436
  92.8 5.5 %collective-permute-start.38 = (bf16[2,8,16,128]{3,2,1,0:T(8,128)(2,1)S(1)}, bf16[2,8,16,128]{3,2,1,0:T(8,128)(2,1)S(1)}, u32[]{:S(2)}, u32[]{:S(2)}) collective-permute-start(bf16[2,8,16,128]{3,2,1,0:T(8,128)(2,1)S(1)} %pad_maximum_fusion.13), channel_id=1, source_target_pairs={{8,2},{9,5},{10,0},{11,7},{12,6},{13,1},{14,4},{15,3},{0,10},{1,13... | collective-permute-start | bytes 196616 | tf_op jit(solution)/shard_map/ppermute | solution.py:436
  (16 other events, 30.5 us)

commit v17 on v16

--- a/solution.py
+++ b/solution.py
@@ -294,7 +294,8 @@
         )
         if final:
             z = scaled(row_of(small, BWD), choose(both, second, [jnp.zeros_like(c) for c in first]))
-            write_front(front, gather_lanes(rounded(z), picks(small, PICK, width)))
+            chunks = gather_lanes(rounded(z), picks(small, PICK, width))
+            write_front(front, chunks, [jnp.zeros_like(c) for c in chunks])
         else:
             outgoing = choose(both, second, first)
             chunks = forward_front(after.at[0:rows], after.at[rows:rows + NEEDS], outgoing)
@@ -418,7 +419,6 @@
     picked = jnp.pad(front_cells, ((0, 0), (0, width - owned)), constant_values=-1)
     layers = section_layers
 
-    half_shape = ((per_layer, rows, LANES), BF16)
     front_shape = ((2 * per_layer, rows, LANES), BF16)
     packet_shape = ((2 * per_layer + cells // LANES, rows, LANES), BF16)
     layers_shape = ((layer_slots, rows, cells), F32)
@@ -453,10 +453,10 @@
             return [gathered], [[0]], order // LANES
         return [gathered], [list(range(planes))], per_layer
 
-    def spread(front, straight, some, every, join=None):
+    def spread(front, straight, some, every, join=None, diagonal=None):
         blocks, owners = [straight], [[(0, 0)]]
         for step in [1] if chips == 2 else range(3, chips):
-            blocks.append(send(front, some, CORES * step))
+            blocks.append(send(front if diagonal is None else diagonal, some, CORES * step))
             owners.append([(CORES * step, CORES * step)])
         if chips == 4:
             both = jnp.stack([front, send(front, inside, 1)])
@@ -465,14 +465,16 @@
         if join:
             mine = join(blocks)
         else:
-            short = [b[:2 * per_layer] if b.ndim == 3 else b for b in blocks]
+            short = [b[:front.shape[0]] if b.ndim == 3 else b for b in blocks]
             mine = jnp.concatenate([b[None] if b.ndim == 3 else b for b in short])
         blocks.append(send(mine, inside, 1))
         owners.append([(one ^ 1, zero ^ 1) for places in owners for zero, one in places])
         return blocks, owners, per_layer
 
-    def within(front, join=None):
-        return spread(front, front, inside, inside, join) if direct else everywhere(front)
+    def within(front, join=None, used=None):
+        if not direct:
+            return everywhere(front[:used])
+        return spread(front[:used], front, inside, inside, join, front)
 
     def between(front, packet, start, stop):
         if not direct:
@@ -531,7 +533,7 @@
     for step in range(sections):
         final = step == sections - 1
         extra = ([held[step]] if step else []) + ([] if final else [near[step % 2]])
-        outs = [layers_shape, half_shape if final else front_shape]
+        outs = [layers_shape, front_shape]
         outs += [] if final else [packet_shape]
         outs += [half_inverse]
         outs = call(
@@ -548,7 +550,7 @@
         second_inverse = outs[-1]
         kept.append(outs[0])
         if final:
-            gathered, owners, slots = within(outs[1])
+            gathered, owners, slots = within(outs[1], used=per_layer)
         else:
             gathered, owners, slots, incoming = between(outs[1], outs[2], step, step + 1)
             held.append(incoming)

time: 105 us -> 103 us (0.981); the launches traced: 105 us -> 104 us
  waiting for transfers between devices: 41.1 us -> 40 us
    ppermute x40, waiting for transfers between devices: 41.1 us -> 40 us  [send(): return lax.ppermute(block, ('sweep', 'plane'), route)]
  transfers between devices with their start and end apart: 40 -> 40, of which waited for: 24 -> 25; matrix products, arithmetic and copies ran while one was open for 0% -> 0% of each run, Pallas kernels for 3% -> 3%
where the time goes in v17:
time: 103 us; the launch traced here: 104 us
  starting transfers between devices  44.5 us (43%)
  waiting for transfers between devices  40 us (39%)
  Pallas kernels  19.5 us (19%)
    ppermute x40, starting transfers between devices, send(): return lax.ppermute(block, ('sweep', 'plane'), route)  44.5 us
    ppermute x40, waiting for transfers between devices, send(): return lax.ppermute(block, ('sweep', 'plane'), route)  40 us
    pallas_call x11, Pallas kernels, call(): pl.pallas_call(kernel, in_specs=specs, out_specs=[whole(pltpu.SMEM if len...  19.5 us
  transfers between devices with their start and end apart: 40, of which 25 were waited for; matrix products, arithmetic and copies ran while one was open for 0% of the time, Pallas kernels for 3%

profile of v17, /device:TPU:0, one launch (start us, length us, event | category | flops | bytes accessed | tf_op | source)
XLA Modules:
  0.0 104.5 jit_solution(2481163932036398656)
XLA Ops:
  0.0 2.4 %first_fronts.1 = (f32[40,1024]{1,0:T(8,128)S(1)}, f32[24,1024]{1,0:T(8,128)S(1)}, f32[40,1024]{1,0:T(8,128)S(1)}, s32[2,1024]{1,0:T(2,128)S(1)}, bf16[8,16,128]{2,1,0:T(8,128)(2,1)S(1)}, /*index=5*/s32[8,128]{1,0:T(8,128)S(1)}) custom-call(s32[4]{0:T(128)} %layers_in.1, f32[2,16,1024]{2,1,0:T(8,128)} %bitcast.52, f32[2,1024]{1,0:T(2,128)} %isc_in.1, ...), custom_call_target="tpu_custom_call" | custom-call | tf_op jit(solution)/shard_map/first_fronts/pallas_call | solution.py:384
  2.9 2.6 %collective-permute-start.3 = (f32[24,1024]{1,0:T(8,128)S(1)}, f32[24,1024]{1,0:T(8,128)S(1)}, u32[]{:S(2)}, u32[]{:S(2)}) collective-permute-start(f32[24,1024]{1,0:T(8,128)S(1)} %get-tuple-element.44), channel_id=1, source_target_pairs={{0,8},{1,9},{2,10},{3,11},{4,12},{5,13},{6,14},{7,15},{16,24},{17,... | collective-permute-start | bytes 294920 | tf_op jit(solution)/shard_map/ppermute | solution.py:436
  5.6 1.6 %collective-permute-start.2 = (bf16[2,8,16,128]{3,2,1,0:T(8,128)(2,1)S(1)}, bf16[2,8,16,128]{3,2,1,0:T(8,128)(2,1)S(1)}, u32[]{:S(2)}, u32[]{:S(2)}) collective-permute-start(bf16[2,8,16,128]{3,2,1,0:T(8,128)(2,1)S(1)} %pad_maximum_fusion.6), channel_id=1, source_target_pairs={{0,2},{1,5},{2,0},{3,7},{4,6},{5,1},{6,4},{7,3},{8,10},{9,13},{10,... | collective-permute-start | bytes 196616 | tf_op jit(solution)/shard_map/ppermute | solution.py:436
  7.1 1.5 %collective-permute-start = (bf16[8,16,128]{2,1,0:T(8,128)(2,1)S(1)}, bf16[8,16,128]{2,1,0:T(8,128)(2,1)S(1)}, u32[]{:S(2)}, u32[]{:S(2)}) collective-permute-start(bf16[8,16,128]{2,1,0:T(8,128)(2,1)S(1)} %get-tuple-element.43.refs_0_.rest_0_), channel_id=1, source_target_pairs={{0,6},{1,7},{2,4},{3,5},{4,2},{5,3},{6,0},{7,1},{8,14},{9,15},{10,... | collective-permute-start | bytes 98312 | tf_op jit(solution)/shard_map/ppermute | solution.py:436
  8.6 3.4 %load_first.1 = (bf16[2,512,4096]{2,1,0:T(8,128)(2,1)S(1)}, bf16[2,512,4096]{2,1,0:T(8,128)(2,1)S(1)}, f32[8,128]{1,0:T(8,128)S(1)}) custom-call(bf16[2,2,512,4096]{3,2,1,0:T(8,128)(2,1)} %inverse.9), custom_call_target="tpu_custom_call" | custom-call | tf_op jit(solution)/shard_map/load_first/pallas_call | solution.py:384
  13.5 6.4 %forward_section_0.1 = (f32[2,16,1024]{2,1,0:T(8,128)S(1)}, bf16[8,16,128]{2,1,0:T(8,128)(2,1)S(1)}, bf16[16,16,128]{2,1,0:T(8,128)(2,1)S(1)}, bf16[2,512,4096]{2,1,0:T(8,128)(2,1)S(1)}) custom-call(s32[8,128]{1,0:T(8,128)S(1)} %get-tuple-element.38.layers, ...), custom_call_target="tpu_custom_call", output_to_operand_aliasing={{3}: (2, {})} | custom-call | tf_op jit(solution)/shard_map/forward_section_0/pallas_call | solution.py:384
  21.3 5.4 %collective-permute-done.5.rest_0_.rest_4_.rest_8_ = bf16[16,16,128]{2,1,0:T(8,128)(2,1)S(1)} collective-permute-done((bf16[16,16,128]{2,1,0:T(8,128)(2,1)S(1)}, bf16[16,16,128]{2,1,0:T(8,128)(2,1)S(1)}, u32[]{:S(2)}, u32[]{:S(2)}) %collective-permute-start.5) | collective-permute-done | bytes 65568 | tf_op jit(solution)/shard_map/ppermute | solution.py:436
  26.7 1.4 %collective-permute-done.6.rest_1_ = bf16[8,16,128]{2,1,0:T(8,128)(2,1)S(1)} collective-permute-done((bf16[8,16,128]{2,1,0:T(8,128)(2,1)S(1)}, bf16[8,16,128]{2,1,0:T(8,128)(2,1)S(1)}, u32[]{:S(2)}, u32[]{:S(2)}) %collective-permute-start.6) | collective-permute-done | bytes 32800 | tf_op jit(solution)/shard_map/ppermute | solution.py:436
  30.4 1.4 %collective-permute-start.12 = (bf16[8,16,128]{2,1,0:T(8,128)(2,1)S(1)}, bf16[8,16,128]{2,1,0:T(8,128)(2,1)S(1)}, u32[]{:S(2)}, u32[]{:S(2)}) collective-permute-start(bf16[8,16,128]{2,1,0:T(8,128)(2,1)S(1)} %get-tuple-element.52), channel_id=1, source_target_pairs={{8,22},{9,23},{10,20},{11,21},{12,18},{13,19},{14,16},{15,17},{16,... | collective-permute-start | bytes 98312 | tf_op jit(solution)/shard_map/ppermute | solution.py:436
  33.6 4.7 %collective-permute-done.11.rest_0_.rest_4_.rest_8_ = bf16[16,16,128]{2,1,0:T(8,128)(2,1)S(1)} collective-permute-done((bf16[16,16,128]{2,1,0:T(8,128)(2,1)S(1)}, bf16[16,16,128]{2,1,0:T(8,128)(2,1)S(1)}, u32[]{:S(2)}, u32[]{:S(2)}) %collective-permute-start.11) | collective-permute-done | bytes 65568 | tf_op jit(solution)/shard_map/ppermute | solution.py:436
  40.4 6.9 %collective-permute-start.17 = (bf16[8,16,128]{2,1,0:T(8,128)(2,1)S(1)}, bf16[8,16,128]{2,1,0:T(8,128)(2,1)S(1)}, u32[]{:S(2)}, u32[]{:S(2)}) collective-permute-start(bf16[8,16,128]{2,1,0:T(8,128)(2,1)S(1)} %get-tuple-element.55), channel_id=1, source_target_pairs={{16,30},{17,31},{18,28},{19,29},{20,26},{21,27},{22,24},{23,25},{2... | collective-permute-start | bytes 98312 | tf_op jit(solution)/shard_map/ppermute | solution.py:436
  48.9 2.8 %collective-permute-done.19.rest_2_ = bf16[2,8,16,128]{3,2,1,0:T(8,128)(2,1)S(1)} collective-permute-done((bf16[2,8,16,128]{3,2,1,0:T(8,128)(2,1)S(1)}, bf16[2,8,16,128]{3,2,1,0:T(8,128)(2,1)S(1)}, u32[]{:S(2)}, u32[]{:S(2)}) %collective-permute-start.19) | collective-permute-done | bytes 65568 | tf_op jit(solution)/shard_map/ppermute | solution.py:436
  53.6 1.4 %collective-permute-start.21 = (bf16[8,16,128]{2,1,0:T(8,128)(2,1)S(1)}, bf16[8,16,128]{2,1,0:T(8,128)(2,1)S(1)}, u32[]{:S(2)}, u32[]{:S(2)}) collective-permute-start(bf16[8,16,128]{2,1,0:T(8,128)(2,1)S(1)} %get-tuple-element.57.rest_0_), channel_id=1, source_target_pairs={{0,6},{1,7},{2,4},{3,5},{4,2},{5,3},{6,0},{7,1},{8,14},{9,15},{10,... | collective-permute-start | bytes 98312 | tf_op jit(solution)/shard_map/ppermute | solution.py:436
  55.8 2.6 %collective-permute-done.21.rest_1_ = bf16[8,16,128]{2,1,0:T(8,128)(2,1)S(1)} collective-permute-done((bf16[8,16,128]{2,1,0:T(8,128)(2,1)S(1)}, bf16[8,16,128]{2,1,0:T(8,128)(2,1)S(1)}, u32[]{:S(2)}, u32[]{:S(2)}) %collective-permute-start.21) | collective-permute-done | bytes 32800 | tf_op jit(solution)/shard_map/ppermute | solution.py:436
  60.7 1.5 %collective-permute-start.26 = (bf16[8,16,128]{2,1,0:T(8,128)(2,1)S(1)}, bf16[8,16,128]{2,1,0:T(8,128)(2,1)S(1)}, u32[]{:S(2)}, u32[]{:S(2)}) collective-permute-start(bf16[8,16,128]{2,1,0:T(8,128)(2,1)S(1)} %get-tuple-element.60), channel_id=1, source_target_pairs={{24,22},{25,23},{26,20},{27,21},{28,18},{29,19},{30,16},{31,17},{1... | collective-permute-start | bytes 98312 | tf_op jit(solution)/shard_map/ppermute | solution.py:436
  62.3 7.5 %collective-permute-start.25 = (bf16[16,16,128]{2,1,0:T(8,128)(2,1)S(1)}, bf16[16,16,128]{2,1,0:T(8,128)(2,1)S(1)}, u32[]{:S(2)}, u32[]{:S(2)}) collective-permute-start(bf16[16,16,128]{2,1,0:T(8,128)(2,1)S(1)} %get-tuple-element.59), channel_id=1, source_target_pairs={{24,16},{25,17},{26,18},{27,19},{28,20},{29,21},{30,22},{31,23},{1... | collective-permute-start | bytes 196616 | tf_op jit(solution)/shard_map/ppermute | solution.py:436
  71.7 2.4 %collective-permute-done.28.rest_2_ = bf16[2,8,16,128]{3,2,1,0:T(8,128)(2,1)S(1)} collective-permute-done((bf16[2,8,16,128]{3,2,1,0:T(8,128)(2,1)S(1)}, bf16[2,8,16,128]{3,2,1,0:T(8,128)(2,1)S(1)}, u32[]{:S(2)}, u32[]{:S(2)}) %collective-permute-start.28) | collective-permute-done | bytes 65568 | tf_op jit(solution)/shard_map/ppermute | solution.py:436
  76.0 5.4 %collective-permute-start.31 = (bf16[8,16,128]{2,1,0:T(8,128)(2,1)S(1)}, bf16[8,16,128]{2,1,0:T(8,128)(2,1)S(1)}, u32[]{:S(2)}, u32[]{:S(2)}) collective-permute-start(bf16[8,16,128]{2,1,0:T(8,128)(2,1)S(1)} %get-tuple-element.64), channel_id=1, source_target_pairs={{16,14},{17,15},{18,12},{19,13},{20,10},{21,11},{22,8},{23,9},{8,6... | collective-permute-start | bytes 98312 | tf_op jit(solution)/shard_map/ppermute | solution.py:436
  83.0 2.8 %collective-permute-done.33.rest_2_ = bf16[2,8,16,128]{3,2,1,0:T(8,128)(2,1)S(1)} collective-permute-done((bf16[2,8,16,128]{3,2,1,0:T(8,128)(2,1)S(1)}, bf16[2,8,16,128]{3,2,1,0:T(8,128)(2,1)S(1)}, u32[]{:S(2)}, u32[]{:S(2)}) %collective-permute-start.33) | collective-permute-done | bytes 65568 | tf_op jit(solution)/shard_map/ppermute | solution.py:436
  87.9 2.8 %collective-permute-start.36 = (bf16[8,16,128]{2,1,0:T(8,128)(2,1)S(1)}, bf16[8,16,128]{2,1,0:T(8,128)(2,1)S(1)}, u32[]{:S(2)}, u32[]{:S(2)}) collective-permute-start(bf16[8,16,128]{2,1,0:T(8,128)(2,1)S(1)} %get-tuple-element.68), channel_id=1, source_target_pairs={{8,6},{9,7},{10,4},{11,5},{12,2},{13,3},{14,0},{15,1},{0,30},{1,31... | collective-permute-start | bytes 98312 | tf_op jit(solution)/shard_map/ppermute | solution.py:436
  91.8 2.0 %collective-permute-start.38 = (bf16[2,8,16,128]{3,2,1,0:T(8,128)(2,1)S(1)}, bf16[2,8,16,128]{3,2,1,0:T(8,128)(2,1)S(1)}, u32[]{:S(2)}, u32[]{:S(2)}) collective-permute-start(bf16[2,8,16,128]{3,2,1,0:T(8,128)(2,1)S(1)} %pad_maximum_fusion.13), channel_id=1, source_target_pairs={{8,2},{9,5},{10,0},{11,7},{12,6},{13,1},{14,4},{15,3},{0,10},{1,13... | collective-permute-start | bytes 196616 | tf_op jit(solution)/shard_map/ppermute | solution.py:436
  93.8 1.9 %collective-permute-done.35.rest_0_.rest_5_ = bf16[16,16,128]{2,1,0:T(8,128)(2,1)S(1)} collective-permute-done((bf16[16,16,128]{2,1,0:T(8,128)(2,1)S(1)}, bf16[16,16,128]{2,1,0:T(8,128)(2,1)S(1)}, u32[]{:S(2)}, u32[]{:S(2)}) %collective-permute-start.35) | collective-permute-done | bytes 65568 | tf_op jit(solution)/shard_map/ppermute | solution.py:436
  95.7 1.7 %collective-permute-done.38.rest_2_ = bf16[2,8,16,128]{3,2,1,0:T(8,128)(2,1)S(1)} collective-permute-done((bf16[2,8,16,128]{3,2,1,0:T(8,128)(2,1)S(1)}, bf16[2,8,16,128]{3,2,1,0:T(8,128)(2,1)S(1)}, u32[]{:S(2)}, u32[]{:S(2)}) %collective-permute-start.38) | collective-permute-done | bytes 65568 | tf_op jit(solution)/shard_map/ppermute | solution.py:436
  98.9 5.6 %backward_section_0.1 = f32[2,16,1024]{2,1,0:T(8,128)} custom-call(s32[8,128]{1,0:T(8,128)S(1)} %get-tuple-element.38.layers, bf16[2,512,4096]{2,1,0:T(8,128)(2,1)S(1)} %get-tuple-element.39.first_inverse, bf16[2,512,4096]{2,1,0:T(8,128)(2,1)S(1)} %get-tuple-element.56.second_inverse, f32[40,1024]{1,0:T(8,128)S(1)} %get-tuple-element.41.packet, ...), custom_call_target="tpu_custom_call" | custom-call | tf_op jit(solution)/shard_map/backward_section_0/pallas_call | solution.py:384
  (90 shorter events, 25.8 us)
Async XLA Ops:
  2.9 9.1 %collective-permute-start.3 = (f32[24,1024]{1,0:T(8,128)S(1)}, f32[24,1024]{1,0:T(8,128)S(1)}, u32[]{:S(2)}, u32[]{:S(2)}) collective-permute-start(f32[24,1024]{1,0:T(8,128)S(1)} %get-tuple-element.44), channel_id=1, source_target_pairs={{0,8},{1,9},{2,10},{3,11},{4,12},{5,13},{6,14},{7,15},{16,24},{17,... | collective-permute-start | bytes 294920 | tf_op jit(solution)/shard_map/ppermute | solution.py:436
  5.6 6.5 %collective-permute-start.2 = (bf16[2,8,16,128]{3,2,1,0:T(8,128)(2,1)S(1)}, bf16[2,8,16,128]{3,2,1,0:T(8,128)(2,1)S(1)}, u32[]{:S(2)}, u32[]{:S(2)}) collective-permute-start(bf16[2,8,16,128]{3,2,1,0:T(8,128)(2,1)S(1)} %pad_maximum_fusion.6), channel_id=1, source_target_pairs={{0,2},{1,5},{2,0},{3,7},{4,6},{5,1},{6,4},{7,3},{8,10},{9,13},{10,... | collective-permute-start | bytes 196616 | tf_op jit(solution)/shard_map/ppermute | solution.py:436
  7.1 4.9 %collective-permute-start = (bf16[8,16,128]{2,1,0:T(8,128)(2,1)S(1)}, bf16[8,16,128]{2,1,0:T(8,128)(2,1)S(1)}, u32[]{:S(2)}, u32[]{:S(2)}) collective-permute-start(bf16[8,16,128]{2,1,0:T(8,128)(2,1)S(1)} %get-tuple-element.43.refs_0_.rest_0_), channel_id=1, source_target_pairs={{0,6},{1,7},{2,4},{3,5},{4,2},{5,3},{6,0},{7,1},{8,14},{9,15},{10,... | collective-permute-start | bytes 98312 | tf_op jit(solution)/shard_map/ppermute | solution.py:436
  20.1 8.5 %collective-permute-start.10 = (f32[40,1024]{1,0:T(8,128)S(1)}, f32[40,1024]{1,0:T(8,128)S(1)}, u32[]{:S(2)}, u32[]{:S(2)}) collective-permute-start(f32[40,1024]{1,0:T(8,128)S(1)} %get-tuple-element.49), channel_id=1, source_target_pairs={{8,16},{9,17},{10,18},{11,19},{12,20},{13,21},{14,22},{15,23},{16,... | collective-permute-start | bytes 491528 | tf_op jit(solution)/shard_map/ppermute | solution.py:436
  20.5 7.6 %collective-permute-start.6 = (bf16[8,16,128]{2,1,0:T(8,128)(2,1)S(1)}, bf16[8,16,128]{2,1,0:T(8,128)(2,1)S(1)}, u32[]{:S(2)}, u32[]{:S(2)}) collective-permute-start(bf16[8,16,128]{2,1,0:T(8,128)(2,1)S(1)} %get-tuple-element.48), channel_id=1, source_target_pairs={{0,14},{1,15},{2,12},{3,13},{4,10},{5,11},{6,8},{7,9},{8,22},{9,23... | collective-permute-start | bytes 98312 | tf_op jit(solution)/shard_map/ppermute | solution.py:436
  20.5 6.2 %collective-permute-start.5 = (bf16[16,16,128]{2,1,0:T(8,128)(2,1)S(1)}, bf16[16,16,128]{2,1,0:T(8,128)(2,1)S(1)}, u32[]{:S(2)}, u32[]{:S(2)}) collective-permute-start(bf16[16,16,128]{2,1,0:T(8,128)(2,1)S(1)} %get-tuple-element.47), channel_id=1, source_target_pairs={{0,8},{1,9},{2,10},{3,11},{4,12},{5,13},{6,14},{7,15},{8,24},{9,25... | collective-permute-start | bytes 196616 | tf_op jit(solution)/shard_map/ppermute | solution.py:436
  21.2 7.3 %collective-permute-start.8 = (bf16[2,8,16,128]{3,2,1,0:T(8,128)(2,1)S(1)}, bf16[2,8,16,128]{3,2,1,0:T(8,128)(2,1)S(1)}, u32[]{:S(2)}, u32[]{:S(2)}) collective-permute-start(bf16[2,8,16,128]{3,2,1,0:T(8,128)(2,1)S(1)} %pad_maximum_fusion.7), channel_id=1, source_target_pairs={{0,10},{1,13},{2,8},{3,15},{4,14},{5,9},{6,12},{7,11},{8,2},{9,5},... | collective-permute-start | bytes 196616 | tf_op jit(solution)/shard_map/ppermute | solution.py:436
  30.4 7.9 %collective-permute-start.12 = (bf16[8,16,128]{2,1,0:T(8,128)(2,1)S(1)}, bf16[8,16,128]{2,1,0:T(8,128)(2,1)S(1)}, u32[]{:S(2)}, u32[]{:S(2)}) collective-permute-start(bf16[8,16,128]{2,1,0:T(8,128)(2,1)S(1)} %get-tuple-element.52), channel_id=1, source_target_pairs={{8,22},{9,23},{10,20},{11,21},{12,18},{13,19},{14,16},{15,17},{16,... | collective-permute-start | bytes 98312 | tf_op jit(solution)/shard_map/ppermute | solution.py:436
  31.9 6.4 %collective-permute-start.11 = (bf16[16,16,128]{2,1,0:T(8,128)(2,1)S(1)}, bf16[16,16,128]{2,1,0:T(8,128)(2,1)S(1)}, u32[]{:S(2)}, u32[]{:S(2)}) collective-permute-start(bf16[16,16,128]{2,1,0:T(8,128)(2,1)S(1)} %get-tuple-element.51), channel_id=1, source_target_pairs={{8,16},{9,17},{10,18},{11,19},{12,20},{13,21},{14,22},{15,23},{16,... | collective-permute-start | bytes 196616 | tf_op jit(solution)/shard_map/ppermute | solution.py:436
  32.6 5.7 %collective-permute-start.14 = (bf16[2,8,16,128]{3,2,1,0:T(8,128)(2,1)S(1)}, bf16[2,8,16,128]{3,2,1,0:T(8,128)(2,1)S(1)}, u32[]{:S(2)}, u32[]{:S(2)}) collective-permute-start(bf16[2,8,16,128]{3,2,1,0:T(8,128)(2,1)S(1)} %pad_maximum_fusion.8), channel_id=1, source_target_pairs={{8,18},{9,21},{10,16},{11,23},{12,22},{13,17},{14,20},{15,19},{16,... | collective-permute-start | bytes 196616 | tf_op jit(solution)/shard_map/ppermute | solution.py:436
  40.2 7.2 %collective-permute-start.18 = (bf16[8,16,128]{2,1,0:T(8,128)(2,1)S(1)}, bf16[8,16,128]{2,1,0:T(8,128)(2,1)S(1)}, u32[]{:S(2)}, u32[]{:S(2)}) collective-permute-start(bf16[8,16,128]{2,1,0:T(8,128)(2,1)S(1)} %get-tuple-element.55), channel_id=1, source_target_pairs={{0,1},{1,0},{2,3},{3,2},{4,5},{5,4},{6,7},{7,6},{8,9},{9,8},{10,11... | collective-permute-start | bytes 98312 | tf_op jit(solution)/shard_map/ppermute | solution.py:436
  40.4 8.5 %collective-permute-start.17 = (bf16[8,16,128]{2,1,0:T(8,128)(2,1)S(1)}, bf16[8,16,128]{2,1,0:T(8,128)(2,1)S(1)}, u32[]{:S(2)}, u32[]{:S(2)}) collective-permute-start(bf16[8,16,128]{2,1,0:T(8,128)(2,1)S(1)} %get-tuple-element.55), channel_id=1, source_target_pairs={{16,30},{17,31},{18,28},{19,29},{20,26},{21,27},{22,24},{23,25},{2... | collective-permute-start | bytes 98312 | tf_op jit(solution)/shard_map/ppermute | solution.py:436
  47.4 4.3 %collective-permute-start.19 = (bf16[2,8,16,128]{3,2,1,0:T(8,128)(2,1)S(1)}, bf16[2,8,16,128]{3,2,1,0:T(8,128)(2,1)S(1)}, u32[]{:S(2)}, u32[]{:S(2)}) collective-permute-start(bf16[2,8,16,128]{3,2,1,0:T(8,128)(2,1)S(1)} %pad_maximum_fusion.9), channel_id=1, source_target_pairs={{16,26},{17,29},{18,24},{19,31},{20,30},{21,25},{22,28},{23,27},{2... | collective-permute-start | bytes 196616 | tf_op jit(solution)/shard_map/ppermute | solution.py:436
  53.6 4.9 %collective-permute-start.21 = (bf16[8,16,128]{2,1,0:T(8,128)(2,1)S(1)}, bf16[8,16,128]{2,1,0:T(8,128)(2,1)S(1)}, u32[]{:S(2)}, u32[]{:S(2)}) collective-permute-start(bf16[8,16,128]{2,1,0:T(8,128)(2,1)S(1)} %get-tuple-element.57.rest_0_), channel_id=1, source_target_pairs={{0,6},{1,7},{2,4},{3,5},{4,2},{5,3},{6,0},{7,1},{8,14},{9,15},{10,... | collective-permute-start | bytes 98312 | tf_op jit(solution)/shard_map/ppermute | solution.py:436
  60.5 9.3 %collective-permute-start.27 = (bf16[8,16,128]{2,1,0:T(8,128)(2,1)S(1)}, bf16[8,16,128]{2,1,0:T(8,128)(2,1)S(1)}, u32[]{:S(2)}, u32[]{:S(2)}) collective-permute-start(bf16[8,16,128]{2,1,0:T(8,128)(2,1)S(1)} %get-tuple-element.60), channel_id=1, source_target_pairs={{0,1},{1,0},{2,3},{3,2},{4,5},{5,4},{6,7},{7,6},{8,9},{9,8},{10,11... | collective-permute-start | bytes 98312 | tf_op jit(solution)/shard_map/ppermute | solution.py:436
  60.7 11.0 %collective-permute-start.26 = (bf16[8,16,128]{2,1,0:T(8,128)(2,1)S(1)}, bf16[8,16,128]{2,1,0:T(8,128)(2,1)S(1)}, u32[]{:S(2)}, u32[]{:S(2)}) collective-permute-start(bf16[8,16,128]{2,1,0:T(8,128)(2,1)S(1)} %get-tuple-element.60), channel_id=1, source_target_pairs={{24,22},{25,23},{26,20},{27,21},{28,18},{29,19},{30,16},{31,17},{1... | collective-permute-start | bytes 98312 | tf_op jit(solution)/shard_map/ppermute | solution.py:436
  62.3 9.4 %collective-permute-start.25 = (bf16[16,16,128]{2,1,0:T(8,128)(2,1)S(1)}, bf16[16,16,128]{2,1,0:T(8,128)(2,1)S(1)}, u32[]{:S(2)}, u32[]{:S(2)}) collective-permute-start(bf16[16,16,128]{2,1,0:T(8,128)(2,1)S(1)} %get-tuple-element.59), channel_id=1, source_target_pairs={{24,16},{25,17},{26,18},{27,19},{28,20},{29,21},{30,22},{31,23},{1... | collective-permute-start | bytes 196616 | tf_op jit(solution)/shard_map/ppermute | solution.py:436
  69.8 4.3 %collective-permute-start.28 = (bf16[2,8,16,128]{3,2,1,0:T(8,128)(2,1)S(1)}, bf16[2,8,16,128]{3,2,1,0:T(8,128)(2,1)S(1)}, u32[]{:S(2)}, u32[]{:S(2)}) collective-permute-start(bf16[2,8,16,128]{3,2,1,0:T(8,128)(2,1)S(1)} %pad_maximum_fusion.11), channel_id=1, source_target_pairs={{24,18},{25,21},{26,16},{27,23},{28,22},{29,17},{30,20},{31,19},{1... | collective-permute-start | bytes 196616 | tf_op jit(solution)/shard_map/ppermute | solution.py:436
  75.8 5.7 %collective-permute-start.32 = (bf16[8,16,128]{2,1,0:T(8,128)(2,1)S(1)}, bf16[8,16,128]{2,1,0:T(8,128)(2,1)S(1)}, u32[]{:S(2)}, u32[]{:S(2)}) collective-permute-start(bf16[8,16,128]{2,1,0:T(8,128)(2,1)S(1)} %get-tuple-element.64), channel_id=1, source_target_pairs={{0,1},{1,0},{2,3},{3,2},{4,5},{5,4},{6,7},{7,6},{8,9},{9,8},{10,11... | collective-permute-start | bytes 98312 | tf_op jit(solution)/shard_map/ppermute | solution.py:436
  76.0 7.0 %collective-permute-start.31 = (bf16[8,16,128]{2,1,0:T(8,128)(2,1)S(1)}, bf16[8,16,128]{2,1,0:T(8,128)(2,1)S(1)}, u32[]{:S(2)}, u32[]{:S(2)}) collective-permute-start(bf16[8,16,128]{2,1,0:T(8,128)(2,1)S(1)} %get-tuple-element.64), channel_id=1, source_target_pairs={{16,14},{17,15},{18,12},{19,13},{20,10},{21,11},{22,8},{23,9},{8,6... | collective-permute-start | bytes 98312 | tf_op jit(solution)/shard_map/ppermute | solution.py:436
  81.5 4.3 %collective-permute-start.33 = (bf16[2,8,16,128]{3,2,1,0:T(8,128)(2,1)S(1)}, bf16[2,8,16,128]{3,2,1,0:T(8,128)(2,1)S(1)}, u32[]{:S(2)}, u32[]{:S(2)}) collective-permute-start(bf16[2,8,16,128]{3,2,1,0:T(8,128)(2,1)S(1)} %pad_maximum_fusion.12), channel_id=1, source_target_pairs={{16,10},{17,13},{18,8},{19,15},{20,14},{21,9},{22,12},{23,11},{8,1... | collective-permute-start | bytes 196616 | tf_op jit(solution)/shard_map/ppermute | solution.py:436
  87.9 7.8 %collective-permute-start.36 = (bf16[8,16,128]{2,1,0:T(8,128)(2,1)S(1)}, bf16[8,16,128]{2,1,0:T(8,128)(2,1)S(1)}, u32[]{:S(2)}, u32[]{:S(2)}) collective-permute-start(bf16[8,16,128]{2,1,0:T(8,128)(2,1)S(1)} %get-tuple-element.68), channel_id=1, source_target_pairs={{8,6},{9,7},{10,4},{11,5},{12,2},{13,3},{14,0},{15,1},{0,30},{1,31... | collective-permute-start | bytes 98312 | tf_op jit(solution)/shard_map/ppermute | solution.py:436
  90.8 5.0 %collective-permute-start.35 = (bf16[16,16,128]{2,1,0:T(8,128)(2,1)S(1)}, bf16[16,16,128]{2,1,0:T(8,128)(2,1)S(1)}, u32[]{:S(2)}, u32[]{:S(2)}) collective-permute-start(bf16[16,16,128]{2,1,0:T(8,128)(2,1)S(1)} %get-tuple-element.67), channel_id=1, source_target_pairs={{8,0},{9,1},{10,2},{11,3},{12,4},{13,5},{14,6},{15,7},{0,16},{1,17... | collective-permute-start | bytes 196616 | tf_op jit(solution)/shard_map/ppermute | solution.py:436
  91.8 5.6 %collective-permute-start.38 = (bf16[2,8,16,128]{3,2,1,0:T(8,128)(2,1)S(1)}, bf16[2,8,16,128]{3,2,1,0:T(8,128)(2,1)S(1)}, u32[]{:S(2)}, u32[]{:S(2)}) collective-permute-start(bf16[2,8,16,128]{3,2,1,0:T(8,128)(2,1)S(1)} %pad_maximum_fusion.13), channel_id=1, source_target_pairs={{8,2},{9,5},{10,0},{11,7},{12,6},{13,1},{14,4},{15,3},{0,10},{1,13... | collective-permute-start | bytes 196616 | tf_op jit(solution)/shard_map/ppermute | solution.py:436
  (16 other events, 30.2 us)

commit v18 on v17

--- a/solution.py
+++ b/solution.py
@@ -483,8 +483,7 @@
         ahead_of = 2 * stop - start, 3 * start - 2 * stop, 2 * start - stop
         third = [i for i in ahead_of if 0 <= i < sections]
         some, every = cycle(start, stop, *third[:1]), cycle(start, stop)
-        fourth = [i for i in range(sections) if i not in (start, stop, *third[:1])]
-        packet = send(packet, cycle(start, stop, *fourth[:1]), 0)
+        packet = send(packet, every, 0)
         return *spread(front, packet, some, every), packet
 
     inverse = in_hbm(front_inverse)

time: 103 us -> 102 us (level); the launches traced: 104 us -> 101 us
  waiting for transfers between devices: 40 us -> 34.8 us
  starting transfers between devices: 44.5 us -> 46.3 us
    ppermute x40, waiting for transfers between devices: 40 us -> 34.8 us  [send(): return lax.ppermute(block, ('sweep', 'plane'), route)]
    ppermute x40, starting transfers between devices: 44.5 us -> 46.3 us  [send(): return lax.ppermute(block, ('sweep', 'plane'), route)]
where the time goes in v18:
time: 102 us; the launch traced here: 101 us
  starting transfers between devices  46.3 us (45%)
  waiting for transfers between devices  34.8 us (34%)
  Pallas kernels  19.5 us (19%)
    ppermute x40, starting transfers between devices, send(): return lax.ppermute(block, ('sweep', 'plane'), route)  46.3 us
    ppermute x40, waiting for transfers between devices, send(): return lax.ppermute(block, ('sweep', 'plane'), route)  34.8 us
    pallas_call x11, Pallas kernels, call(): pl.pallas_call(kernel, in_specs=specs, out_specs=[whole(pltpu.SMEM if len...  19.5 us
  transfers between devices with their start and end apart: 40, of which 25 were waited for; matrix products, arithmetic and copies ran while one was open for 0% of the time, Pallas kernels for 3%

profile of v18, /device:TPU:0, one launch (start us, length us, event | category | flops | bytes accessed | tf_op | source)
XLA Modules:
  0.0 101.1 jit_solution(18050114568311352077)
XLA Ops:
  0.0 2.4 %first_fronts.1 = (f32[40,1024]{1,0:T(8,128)S(1)}, f32[24,1024]{1,0:T(8,128)S(1)}, f32[40,1024]{1,0:T(8,128)S(1)}, s32[2,1024]{1,0:T(2,128)S(1)}, bf16[8,16,128]{2,1,0:T(8,128)(2,1)S(1)}, /*index=5*/s32[8,128]{1,0:T(8,128)S(1)}) custom-call(s32[4]{0:T(128)} %layers_in.1, f32[2,16,1024]{2,1,0:T(8,128)} %bitcast.52, f32[2,1024]{1,0:T(2,128)} %isc_in.1, ...), custom_call_target="tpu_custom_call" | custom-call | tf_op jit(solution)/shard_map/first_fronts/pallas_call | solution.py:384
  2.9 2.6 %collective-permute-start.3 = (f32[24,1024]{1,0:T(8,128)S(1)}, f32[24,1024]{1,0:T(8,128)S(1)}, u32[]{:S(2)}, u32[]{:S(2)}) collective-permute-start(f32[24,1024]{1,0:T(8,128)S(1)} %get-tuple-element.44), channel_id=1, source_target_pairs={{0,8},{1,9},{2,10},{3,11},{4,12},{5,13},{6,14},{7,15},{16,24},{17,... | collective-permute-start | bytes 294920 | tf_op jit(solution)/shard_map/ppermute | solution.py:436
  5.6 1.6 %collective-permute-start.2 = (bf16[2,8,16,128]{3,2,1,0:T(8,128)(2,1)S(1)}, bf16[2,8,16,128]{3,2,1,0:T(8,128)(2,1)S(1)}, u32[]{:S(2)}, u32[]{:S(2)}) collective-permute-start(bf16[2,8,16,128]{3,2,1,0:T(8,128)(2,1)S(1)} %pad_maximum_fusion.6), channel_id=1, source_target_pairs={{0,2},{1,5},{2,0},{3,7},{4,6},{5,1},{6,4},{7,3},{8,10},{9,13},{10,... | collective-permute-start | bytes 196616 | tf_op jit(solution)/shard_map/ppermute | solution.py:436
  7.1 1.5 %collective-permute-start = (bf16[8,16,128]{2,1,0:T(8,128)(2,1)S(1)}, bf16[8,16,128]{2,1,0:T(8,128)(2,1)S(1)}, u32[]{:S(2)}, u32[]{:S(2)}) collective-permute-start(bf16[8,16,128]{2,1,0:T(8,128)(2,1)S(1)} %get-tuple-element.43.refs_0_.rest_0_), channel_id=1, source_target_pairs={{0,6},{1,7},{2,4},{3,5},{4,2},{5,3},{6,0},{7,1},{8,14},{9,15},{10,... | collective-permute-start | bytes 98312 | tf_op jit(solution)/shard_map/ppermute | solution.py:436
  8.6 3.4 %load_first.1 = (bf16[2,512,4096]{2,1,0:T(8,128)(2,1)S(1)}, bf16[2,512,4096]{2,1,0:T(8,128)(2,1)S(1)}, f32[8,128]{1,0:T(8,128)S(1)}) custom-call(bf16[2,2,512,4096]{3,2,1,0:T(8,128)(2,1)} %inverse.9), custom_call_target="tpu_custom_call" | custom-call | tf_op jit(solution)/shard_map/load_first/pallas_call | solution.py:384
  12.2 1.3 %collective-permute-done.4.rest_3_ = bf16[4,8,16,128]{3,2,1,0:T(8,128)(2,1)S(1)} collective-permute-done((bf16[4,8,16,128]{3,2,1,0:T(8,128)(2,1)S(1)}, bf16[4,8,16,128]{3,2,1,0:T(8,128)(2,1)S(1)}, u32[]{:S(2)}, u32[]{:S(2)}) %collective-permute-start.4) | collective-permute-done | bytes 131104 | tf_op jit(solution)/shard_map/ppermute | solution.py:436
  13.5 6.4 %forward_section_0.1 = (f32[2,16,1024]{2,1,0:T(8,128)S(1)}, bf16[8,16,128]{2,1,0:T(8,128)(2,1)S(1)}, bf16[16,16,128]{2,1,0:T(8,128)(2,1)S(1)}, bf16[2,512,4096]{2,1,0:T(8,128)(2,1)S(1)}) custom-call(s32[8,128]{1,0:T(8,128)S(1)} %get-tuple-element.38.layers, ...), custom_call_target="tpu_custom_call", output_to_operand_aliasing={{3}: (2, {})} | custom-call | tf_op jit(solution)/shard_map/forward_section_0/pallas_call | solution.py:384
  21.2 2.3 %collective-permute-start.8 = (bf16[2,8,16,128]{3,2,1,0:T(8,128)(2,1)S(1)}, bf16[2,8,16,128]{3,2,1,0:T(8,128)(2,1)S(1)}, u32[]{:S(2)}, u32[]{:S(2)}) collective-permute-start(bf16[2,8,16,128]{3,2,1,0:T(8,128)(2,1)S(1)} %pad_maximum_fusion.7), channel_id=1, source_target_pairs={{0,10},{1,13},{2,8},{3,15},{4,14},{5,9},{6,12},{7,11},{8,2},{9,5},... | collective-permute-start | bytes 196616 | tf_op jit(solution)/shard_map/ppermute | solution.py:436
  24.8 2.3 %collective-permute-done.6.rest_1_ = bf16[8,16,128]{2,1,0:T(8,128)(2,1)S(1)} collective-permute-done((bf16[8,16,128]{2,1,0:T(8,128)(2,1)S(1)}, bf16[8,16,128]{2,1,0:T(8,128)(2,1)S(1)}, u32[]{:S(2)}, u32[]{:S(2)}) %collective-permute-start.6) | collective-permute-done | bytes 32800 | tf_op jit(solution)/shard_map/ppermute | solution.py:436
  29.6 1.5 %collective-permute-start.12 = (bf16[8,16,128]{2,1,0:T(8,128)(2,1)S(1)}, bf16[8,16,128]{2,1,0:T(8,128)(2,1)S(1)}, u32[]{:S(2)}, u32[]{:S(2)}) collective-permute-start(bf16[8,16,128]{2,1,0:T(8,128)(2,1)S(1)} %get-tuple-element.52), channel_id=1, source_target_pairs={{8,22},{9,23},{10,20},{11,21},{12,18},{13,19},{14,16},{15,17},{16,... | collective-permute-start | bytes 98312 | tf_op jit(solution)/shard_map/ppermute | solution.py:436
  32.4 2.1 %collective-permute-done.12.rest_1_ = bf16[8,16,128]{2,1,0:T(8,128)(2,1)S(1)} collective-permute-done((bf16[8,16,128]{2,1,0:T(8,128)(2,1)S(1)}, bf16[8,16,128]{2,1,0:T(8,128)(2,1)S(1)}, u32[]{:S(2)}, u32[]{:S(2)}) %collective-permute-start.12) | collective-permute-done | bytes 32800 | tf_op jit(solution)/shard_map/ppermute | solution.py:436
  37.6 7.4 %collective-permute-start.17 = (bf16[8,16,128]{2,1,0:T(8,128)(2,1)S(1)}, bf16[8,16,128]{2,1,0:T(8,128)(2,1)S(1)}, u32[]{:S(2)}, u32[]{:S(2)}) collective-permute-start(bf16[8,16,128]{2,1,0:T(8,128)(2,1)S(1)} %get-tuple-element.55), channel_id=1, source_target_pairs={{16,30},{17,31},{18,28},{19,29},{20,26},{21,27},{22,24},{23,25},{2... | collective-permute-start | bytes 98312 | tf_op jit(solution)/shard_map/ppermute | solution.py:436
  46.6 2.8 %collective-permute-done.19.rest_2_ = bf16[2,8,16,128]{3,2,1,0:T(8,128)(2,1)S(1)} collective-permute-done((bf16[2,8,16,128]{3,2,1,0:T(8,128)(2,1)S(1)}, bf16[2,8,16,128]{3,2,1,0:T(8,128)(2,1)S(1)}, u32[]{:S(2)}, u32[]{:S(2)}) %collective-permute-start.19) | collective-permute-done | bytes 65568 | tf_op jit(solution)/shard_map/ppermute | solution.py:436
  51.3 1.6 %collective-permute-start.21 = (bf16[8,16,128]{2,1,0:T(8,128)(2,1)S(1)}, bf16[8,16,128]{2,1,0:T(8,128)(2,1)S(1)}, u32[]{:S(2)}, u32[]{:S(2)}) collective-permute-start(bf16[8,16,128]{2,1,0:T(8,128)(2,1)S(1)} %get-tuple-element.57.rest_0_), channel_id=1, source_target_pairs={{0,6},{1,7},{2,4},{3,5},{4,2},{5,3},{6,0},{7,1},{8,14},{9,15},{10,... | collective-permute-start | bytes 98312 | tf_op jit(solution)/shard_map/ppermute | solution.py:436
  54.1 2.2 %collective-permute-done.21.rest_1_ = bf16[8,16,128]{2,1,0:T(8,128)(2,1)S(1)} collective-permute-done((bf16[8,16,128]{2,1,0:T(8,128)(2,1)S(1)}, bf16[8,16,128]{2,1,0:T(8,128)(2,1)S(1)}, u32[]{:S(2)}, u32[]{:S(2)}) %collective-permute-start.21) | collective-permute-done | bytes 32800 | tf_op jit(solution)/shard_map/ppermute | solution.py:436
  58.6 1.4 %collective-permute-start.26 = (bf16[8,16,128]{2,1,0:T(8,128)(2,1)S(1)}, bf16[8,16,128]{2,1,0:T(8,128)(2,1)S(1)}, u32[]{:S(2)}, u32[]{:S(2)}) collective-permute-start(bf16[8,16,128]{2,1,0:T(8,128)(2,1)S(1)} %get-tuple-element.60), channel_id=1, source_target_pairs={{24,22},{25,23},{26,20},{27,21},{28,18},{29,19},{30,16},{31,17},{1... | collective-permute-start | bytes 98312 | tf_op jit(solution)/shard_map/ppermute | solution.py:436
  61.3 2.2 %collective-permute-done.26.rest_1_ = bf16[8,16,128]{2,1,0:T(8,128)(2,1)S(1)} collective-permute-done((bf16[8,16,128]{2,1,0:T(8,128)(2,1)S(1)}, bf16[8,16,128]{2,1,0:T(8,128)(2,1)S(1)}, u32[]{:S(2)}, u32[]{:S(2)}) %collective-permute-start.26) | collective-permute-done | bytes 32800 | tf_op jit(solution)/shard_map/ppermute | solution.py:436
  66.3 12.9 %collective-permute-start.31 = (bf16[8,16,128]{2,1,0:T(8,128)(2,1)S(1)}, bf16[8,16,128]{2,1,0:T(8,128)(2,1)S(1)}, u32[]{:S(2)}, u32[]{:S(2)}) collective-permute-start(bf16[8,16,128]{2,1,0:T(8,128)(2,1)S(1)} %get-tuple-element.64), channel_id=1, source_target_pairs={{16,14},{17,15},{18,12},{19,13},{20,10},{21,11},{22,8},{23,9},{8,6... | collective-permute-start | bytes 98312 | tf_op jit(solution)/shard_map/ppermute | solution.py:436
  80.8 2.8 %collective-permute-done.33.rest_2_ = bf16[2,8,16,128]{3,2,1,0:T(8,128)(2,1)S(1)} collective-permute-done((bf16[2,8,16,128]{3,2,1,0:T(8,128)(2,1)S(1)}, bf16[2,8,16,128]{3,2,1,0:T(8,128)(2,1)S(1)}, u32[]{:S(2)}, u32[]{:S(2)}) %collective-permute-start.33) | collective-permute-done | bytes 65568 | tf_op jit(solution)/shard_map/ppermute | solution.py:436
  85.7 3.1 %collective-permute-start.35 = (bf16[16,16,128]{2,1,0:T(8,128)(2,1)S(1)}, bf16[16,16,128]{2,1,0:T(8,128)(2,1)S(1)}, u32[]{:S(2)}, u32[]{:S(2)}) collective-permute-start(bf16[16,16,128]{2,1,0:T(8,128)(2,1)S(1)} %get-tuple-element.67), channel_id=1, source_target_pairs={{8,0},{9,1},{10,2},{11,3},{12,4},{13,5},{14,6},{15,7},{0,8},{1,9},... | collective-permute-start | bytes 196616 | tf_op jit(solution)/shard_map/ppermute | solution.py:436
  88.9 1.6 %collective-permute-start.38 = (bf16[2,8,16,128]{3,2,1,0:T(8,128)(2,1)S(1)}, bf16[2,8,16,128]{3,2,1,0:T(8,128)(2,1)S(1)}, u32[]{:S(2)}, u32[]{:S(2)}) collective-permute-start(bf16[2,8,16,128]{3,2,1,0:T(8,128)(2,1)S(1)} %pad_maximum_fusion.13), channel_id=1, source_target_pairs={{8,2},{9,5},{10,0},{11,7},{12,6},{13,1},{14,4},{15,3},{0,10},{1,13... | collective-permute-start | bytes 196616 | tf_op jit(solution)/shard_map/ppermute | solution.py:436
  90.5 1.6 %collective-permute-done.35.rest_0_.rest_5_ = bf16[16,16,128]{2,1,0:T(8,128)(2,1)S(1)} collective-permute-done((bf16[16,16,128]{2,1,0:T(8,128)(2,1)S(1)}, bf16[16,16,128]{2,1,0:T(8,128)(2,1)S(1)}, u32[]{:S(2)}, u32[]{:S(2)}) %collective-permute-start.35) | collective-permute-done | bytes 65568 | tf_op jit(solution)/shard_map/ppermute | solution.py:436
  92.1 1.9 %collective-permute-done.38.rest_2_ = bf16[2,8,16,128]{3,2,1,0:T(8,128)(2,1)S(1)} collective-permute-done((bf16[2,8,16,128]{3,2,1,0:T(8,128)(2,1)S(1)}, bf16[2,8,16,128]{3,2,1,0:T(8,128)(2,1)S(1)}, u32[]{:S(2)}, u32[]{:S(2)}) %collective-permute-start.38) | collective-permute-done | bytes 65568 | tf_op jit(solution)/shard_map/ppermute | solution.py:436
  95.5 5.6 %backward_section_0.1 = f32[2,16,1024]{2,1,0:T(8,128)} custom-call(s32[8,128]{1,0:T(8,128)S(1)} %get-tuple-element.38.layers, bf16[2,512,4096]{2,1,0:T(8,128)(2,1)S(1)} %get-tuple-element.39.first_inverse, bf16[2,512,4096]{2,1,0:T(8,128)(2,1)S(1)} %get-tuple-element.56.second_inverse, f32[40,1024]{1,0:T(8,128)S(1)} %get-tuple-element.41.packet, ...), custom_call_target="tpu_custom_call" | custom-call | tf_op jit(solution)/shard_map/backward_section_0/pallas_call | solution.py:384
  (90 shorter events, 26.1 us)
Async XLA Ops:
  2.4 3.2 %collective-permute-start.1 = (bf16[8,16,128]{2,1,0:T(8,128)(2,1)S(1)}, bf16[8,16,128]{2,1,0:T(8,128)(2,1)S(1)}, u32[]{:S(2)}, u32[]{:S(2)}) collective-permute-start(bf16[8,16,128]{2,1,0:T(8,128)(2,1)S(1)} %get-tuple-element.43.refs_0_.rest_0_), channel_id=1, source_target_pairs={{0,1},{1,0},{2,3},{3,2},{4,5},{5,4},{6,7},{7,6},{8,9},{9,8},{10,11... | collective-permute-start | bytes 98312 | tf_op jit(solution)/shard_map/ppermute | solution.py:436
  2.9 9.1 %collective-permute-start.3 = (f32[24,1024]{1,0:T(8,128)S(1)}, f32[24,1024]{1,0:T(8,128)S(1)}, u32[]{:S(2)}, u32[]{:S(2)}) collective-permute-start(f32[24,1024]{1,0:T(8,128)S(1)} %get-tuple-element.44), channel_id=1, source_target_pairs={{0,8},{1,9},{2,10},{3,11},{4,12},{5,13},{6,14},{7,15},{16,24},{17,... | collective-permute-start | bytes 294920 | tf_op jit(solution)/shard_map/ppermute | solution.py:436
  5.6 6.5 %collective-permute-start.2 = (bf16[2,8,16,128]{3,2,1,0:T(8,128)(2,1)S(1)}, bf16[2,8,16,128]{3,2,1,0:T(8,128)(2,1)S(1)}, u32[]{:S(2)}, u32[]{:S(2)}) collective-permute-start(bf16[2,8,16,128]{3,2,1,0:T(8,128)(2,1)S(1)} %pad_maximum_fusion.6), channel_id=1, source_target_pairs={{0,2},{1,5},{2,0},{3,7},{4,6},{5,1},{6,4},{7,3},{8,10},{9,13},{10,... | collective-permute-start | bytes 196616 | tf_op jit(solution)/shard_map/ppermute | solution.py:436
  7.1 4.9 %collective-permute-start = (bf16[8,16,128]{2,1,0:T(8,128)(2,1)S(1)}, bf16[8,16,128]{2,1,0:T(8,128)(2,1)S(1)}, u32[]{:S(2)}, u32[]{:S(2)}) collective-permute-start(bf16[8,16,128]{2,1,0:T(8,128)(2,1)S(1)} %get-tuple-element.43.refs_0_.rest_0_), channel_id=1, source_target_pairs={{0,6},{1,7},{2,4},{3,5},{4,2},{5,3},{6,0},{7,1},{8,14},{9,15},{10,... | collective-permute-start | bytes 98312 | tf_op jit(solution)/shard_map/ppermute | solution.py:436
  20.1 7.7 %collective-permute-start.10 = (f32[40,1024]{1,0:T(8,128)S(1)}, f32[40,1024]{1,0:T(8,128)S(1)}, u32[]{:S(2)}, u32[]{:S(2)}) collective-permute-start(f32[40,1024]{1,0:T(8,128)S(1)} %get-tuple-element.49), channel_id=1, source_target_pairs={{8,16},{9,17},{10,18},{11,19},{12,20},{13,21},{14,22},{15,23},{16,... | collective-permute-start | bytes 491528 | tf_op jit(solution)/shard_map/ppermute | solution.py:436
  20.5 6.6 %collective-permute-start.6 = (bf16[8,16,128]{2,1,0:T(8,128)(2,1)S(1)}, bf16[8,16,128]{2,1,0:T(8,128)(2,1)S(1)}, u32[]{:S(2)}, u32[]{:S(2)}) collective-permute-start(bf16[8,16,128]{2,1,0:T(8,128)(2,1)S(1)} %get-tuple-element.48), channel_id=1, source_target_pairs={{0,14},{1,15},{2,12},{3,13},{4,10},{5,11},{6,8},{7,9},{8,22},{9,23... | collective-permute-start | bytes 98312 | tf_op jit(solution)/shard_map/ppermute | solution.py:436
  20.5 4.3 %collective-permute-start.5 = (bf16[16,16,128]{2,1,0:T(8,128)(2,1)S(1)}, bf16[16,16,128]{2,1,0:T(8,128)(2,1)S(1)}, u32[]{:S(2)}, u32[]{:S(2)}) collective-permute-start(bf16[16,16,128]{2,1,0:T(8,128)(2,1)S(1)} %get-tuple-element.47), channel_id=1, source_target_pairs={{0,8},{1,9},{2,10},{3,11},{4,12},{5,13},{6,14},{7,15},{8,0},{9,1},... | collective-permute-start | bytes 196616 | tf_op jit(solution)/shard_map/ppermute | solution.py:436
  21.2 6.5 %collective-permute-start.8 = (bf16[2,8,16,128]{3,2,1,0:T(8,128)(2,1)S(1)}, bf16[2,8,16,128]{3,2,1,0:T(8,128)(2,1)S(1)}, u32[]{:S(2)}, u32[]{:S(2)}) collective-permute-start(bf16[2,8,16,128]{3,2,1,0:T(8,128)(2,1)S(1)} %pad_maximum_fusion.7), channel_id=1, source_target_pairs={{0,10},{1,13},{2,8},{3,15},{4,14},{5,9},{6,12},{7,11},{8,2},{9,5},... | collective-permute-start | bytes 196616 | tf_op jit(solution)/shard_map/ppermute | solution.py:436
  29.6 4.8 %collective-permute-start.12 = (bf16[8,16,128]{2,1,0:T(8,128)(2,1)S(1)}, bf16[8,16,128]{2,1,0:T(8,128)(2,1)S(1)}, u32[]{:S(2)}, u32[]{:S(2)}) collective-permute-start(bf16[8,16,128]{2,1,0:T(8,128)(2,1)S(1)} %get-tuple-element.52), channel_id=1, source_target_pairs={{8,22},{9,23},{10,20},{11,21},{12,18},{13,19},{14,16},{15,17},{16,... | collective-permute-start | bytes 98312 | tf_op jit(solution)/shard_map/ppermute | solution.py:436
  31.2 4.3 %collective-permute-start.14 = (bf16[2,8,16,128]{3,2,1,0:T(8,128)(2,1)S(1)}, bf16[2,8,16,128]{3,2,1,0:T(8,128)(2,1)S(1)}, u32[]{:S(2)}, u32[]{:S(2)}) collective-permute-start(bf16[2,8,16,128]{3,2,1,0:T(8,128)(2,1)S(1)} %pad_maximum_fusion.8), channel_id=1, source_target_pairs={{8,18},{9,21},{10,16},{11,23},{12,22},{13,17},{14,20},{15,19},{16,... | collective-permute-start | bytes 196616 | tf_op jit(solution)/shard_map/ppermute | solution.py:436
  37.4 7.7 %collective-permute-start.18 = (bf16[8,16,128]{2,1,0:T(8,128)(2,1)S(1)}, bf16[8,16,128]{2,1,0:T(8,128)(2,1)S(1)}, u32[]{:S(2)}, u32[]{:S(2)}) collective-permute-start(bf16[8,16,128]{2,1,0:T(8,128)(2,1)S(1)} %get-tuple-element.55), channel_id=1, source_target_pairs={{0,1},{1,0},{2,3},{3,2},{4,5},{5,4},{6,7},{7,6},{8,9},{9,8},{10,11... | collective-permute-start | bytes 98312 | tf_op jit(solution)/shard_map/ppermute | solution.py:436
  37.6 9.0 %collective-permute-start.17 = (bf16[8,16,128]{2,1,0:T(8,128)(2,1)S(1)}, bf16[8,16,128]{2,1,0:T(8,128)(2,1)S(1)}, u32[]{:S(2)}, u32[]{:S(2)}) collective-permute-start(bf16[8,16,128]{2,1,0:T(8,128)(2,1)S(1)} %get-tuple-element.55), channel_id=1, source_target_pairs={{16,30},{17,31},{18,28},{19,29},{20,26},{21,27},{22,24},{23,25},{2... | collective-permute-start | bytes 98312 | tf_op jit(solution)/shard_map/ppermute | solution.py:436
  45.1 4.3 %collective-permute-start.19 = (bf16[2,8,16,128]{3,2,1,0:T(8,128)(2,1)S(1)}, bf16[2,8,16,128]{3,2,1,0:T(8,128)(2,1)S(1)}, u32[]{:S(2)}, u32[]{:S(2)}) collective-permute-start(bf16[2,8,16,128]{3,2,1,0:T(8,128)(2,1)S(1)} %pad_maximum_fusion.9), channel_id=1, source_target_pairs={{16,26},{17,29},{18,24},{19,31},{20,30},{21,25},{22,28},{23,27},{2... | collective-permute-start | bytes 196616 | tf_op jit(solution)/shard_map/ppermute | solution.py:436
  51.3 4.9 %collective-permute-start.21 = (bf16[8,16,128]{2,1,0:T(8,128)(2,1)S(1)}, bf16[8,16,128]{2,1,0:T(8,128)(2,1)S(1)}, u32[]{:S(2)}, u32[]{:S(2)}) collective-permute-start(bf16[8,16,128]{2,1,0:T(8,128)(2,1)S(1)} %get-tuple-element.57.rest_0_), channel_id=1, source_target_pairs={{0,6},{1,7},{2,4},{3,5},{4,2},{5,3},{6,0},{7,1},{8,14},{9,15},{10,... | collective-permute-start | bytes 98312 | tf_op jit(solution)/shard_map/ppermute | solution.py:436
  52.9 4.0 %collective-permute-start.23 = (bf16[2,4,16,128]{3,2,1,0:T(8,128)(2,1)S(1)}, bf16[2,4,16,128]{3,2,1,0:T(8,128)(2,1)S(1)}, u32[]{:S(2)}, u32[]{:S(2)}) collective-permute-start(bf16[2,4,16,128]{3,2,1,0:T(8,128)(2,1)S(1)} %pad_maximum_fusion.14), channel_id=1, source_target_pairs={{0,2},{1,5},{2,0},{3,7},{4,6},{5,1},{6,4},{7,3},{8,10},{9,13},{10,... | collective-permute-start | bytes 98312 | tf_op jit(solution)/shard_map/ppermute | solution.py:436
  58.6 4.8 %collective-permute-start.26 = (bf16[8,16,128]{2,1,0:T(8,128)(2,1)S(1)}, bf16[8,16,128]{2,1,0:T(8,128)(2,1)S(1)}, u32[]{:S(2)}, u32[]{:S(2)}) collective-permute-start(bf16[8,16,128]{2,1,0:T(8,128)(2,1)S(1)} %get-tuple-element.60), channel_id=1, source_target_pairs={{24,22},{25,23},{26,20},{27,21},{28,18},{29,19},{30,16},{31,17},{1... | collective-permute-start | bytes 98312 | tf_op jit(solution)/shard_map/ppermute | solution.py:436
  60.1 4.3 %collective-permute-start.28 = (bf16[2,8,16,128]{3,2,1,0:T(8,128)(2,1)S(1)}, bf16[2,8,16,128]{3,2,1,0:T(8,128)(2,1)S(1)}, u32[]{:S(2)}, u32[]{:S(2)}) collective-permute-start(bf16[2,8,16,128]{3,2,1,0:T(8,128)(2,1)S(1)} %pad_maximum_fusion.11), channel_id=1, source_target_pairs={{24,18},{25,21},{26,16},{27,23},{28,22},{29,17},{30,20},{31,19},{1... | collective-permute-start | bytes 196616 | tf_op jit(solution)/shard_map/ppermute | solution.py:436
  66.1 13.2 %collective-permute-start.32 = (bf16[8,16,128]{2,1,0:T(8,128)(2,1)S(1)}, bf16[8,16,128]{2,1,0:T(8,128)(2,1)S(1)}, u32[]{:S(2)}, u32[]{:S(2)}) collective-permute-start(bf16[8,16,128]{2,1,0:T(8,128)(2,1)S(1)} %get-tuple-element.64), channel_id=1, source_target_pairs={{0,1},{1,0},{2,3},{3,2},{4,5},{5,4},{6,7},{7,6},{8,9},{9,8},{10,11... | collective-permute-start | bytes 98312 | tf_op jit(solution)/shard_map/ppermute | solution.py:436
  66.3 14.5 %collective-permute-start.31 = (bf16[8,16,128]{2,1,0:T(8,128)(2,1)S(1)}, bf16[8,16,128]{2,1,0:T(8,128)(2,1)S(1)}, u32[]{:S(2)}, u32[]{:S(2)}) collective-permute-start(bf16[8,16,128]{2,1,0:T(8,128)(2,1)S(1)} %get-tuple-element.64), channel_id=1, source_target_pairs={{16,14},{17,15},{18,12},{19,13},{20,10},{21,11},{22,8},{23,9},{8,6... | collective-permute-start | bytes 98312 | tf_op jit(solution)/shard_map/ppermute | solution.py:436
  79.3 4.3 %collective-permute-start.33 = (bf16[2,8,16,128]{3,2,1,0:T(8,128)(2,1)S(1)}, bf16[2,8,16,128]{3,2,1,0:T(8,128)(2,1)S(1)}, u32[]{:S(2)}, u32[]{:S(2)}) collective-permute-start(bf16[2,8,16,128]{3,2,1,0:T(8,128)(2,1)S(1)} %pad_maximum_fusion.12), channel_id=1, source_target_pairs={{16,10},{17,13},{18,8},{19,15},{20,14},{21,9},{22,12},{23,11},{8,1... | collective-permute-start | bytes 196616 | tf_op jit(solution)/shard_map/ppermute | solution.py:436
  85.5 3.3 %collective-permute-start.37 = (bf16[8,16,128]{2,1,0:T(8,128)(2,1)S(1)}, bf16[8,16,128]{2,1,0:T(8,128)(2,1)S(1)}, u32[]{:S(2)}, u32[]{:S(2)}) collective-permute-start(bf16[8,16,128]{2,1,0:T(8,128)(2,1)S(1)} %get-tuple-element.68), channel_id=1, source_target_pairs={{0,1},{1,0},{2,3},{3,2},{4,5},{5,4},{6,7},{7,6},{8,9},{9,8},{10,11... | collective-permute-start | bytes 98312 | tf_op jit(solution)/shard_map/ppermute | solution.py:436
  85.7 6.4 %collective-permute-start.36 = (bf16[8,16,128]{2,1,0:T(8,128)(2,1)S(1)}, bf16[8,16,128]{2,1,0:T(8,128)(2,1)S(1)}, u32[]{:S(2)}, u32[]{:S(2)}) collective-permute-start(bf16[8,16,128]{2,1,0:T(8,128)(2,1)S(1)} %get-tuple-element.68), channel_id=1, source_target_pairs={{8,6},{9,7},{10,4},{11,5},{12,2},{13,3},{14,0},{15,1},{0,30},{1,31... | collective-permute-start | bytes 98312 | tf_op jit(solution)/shard_map/ppermute | solution.py:436
  85.7 6.4 %collective-permute-start.35 = (bf16[16,16,128]{2,1,0:T(8,128)(2,1)S(1)}, bf16[16,16,128]{2,1,0:T(8,128)(2,1)S(1)}, u32[]{:S(2)}, u32[]{:S(2)}) collective-permute-start(bf16[16,16,128]{2,1,0:T(8,128)(2,1)S(1)} %get-tuple-element.67), channel_id=1, source_target_pairs={{8,0},{9,1},{10,2},{11,3},{12,4},{13,5},{14,6},{15,7},{0,8},{1,9},... | collective-permute-start | bytes 196616 | tf_op jit(solution)/shard_map/ppermute | solution.py:436
  88.9 5.2 %collective-permute-start.38 = (bf16[2,8,16,128]{3,2,1,0:T(8,128)(2,1)S(1)}, bf16[2,8,16,128]{3,2,1,0:T(8,128)(2,1)S(1)}, u32[]{:S(2)}, u32[]{:S(2)}) collective-permute-start(bf16[2,8,16,128]{3,2,1,0:T(8,128)(2,1)S(1)} %pad_maximum_fusion.13), channel_id=1, source_target_pairs={{8,2},{9,5},{10,0},{11,7},{12,6},{13,1},{14,4},{15,3},{0,10},{1,13... | collective-permute-start | bytes 196616 | tf_op jit(solution)/shard_map/ppermute | solution.py:436
  (16 other events, 22.8 us)

commit v19 on v18

--- a/solution.py
+++ b/solution.py
@@ -152,7 +152,7 @@
 
 
 def first_kernel(
-    width, layers_in, rhs_in, isc_in, fwd_in, bwd_in, picked_in, local, ahead, longer, place, front,
+    width, layers_in, rhs_in, isc_in, fwd_in, bwd_in, picked_in, local, ahead, longer, front,
     layers, rhs, isc, fwd, bwd, picked, counts, sems,
 ):
     pairs = (
@@ -202,15 +202,16 @@
     write_field(ahead.at[0:count], base_a + base_b)
     longer[0:ahead.shape[0], :] = ahead[...]
     longer[ahead.shape[0]:, :] = jnp.zeros((longer.shape[0] - ahead.shape[0], longer.shape[1]), F32)
-    for layer in range(2):
-        place[layer:layer + 1, :] = places(picked[layer:layer + 1, :], cells)
-
-
-def load_kernel(inverse, first, second, done, sem):
+
+
+def load_kernel(width, inverse, local, first, second, place, done, sem):
     load = pltpu.make_async_copy(inverse.at[0], first, sem.at[0])
     load.start()
     done[...] = jnp.zeros(done.shape, F32)
     second[:, 0:16, 0:LANES] = jnp.zeros((2, 16, LANES), BF16)
+    small = local.at[local.shape[0] - 8:]
+    for layer in range(2):
+        place[layer:layer + 1, :] = places(picks(small, PICK + layer, width), local.shape[1])
     load.wait()
 
 
@@ -490,14 +491,13 @@
     half_inverse = pltpu.VMEM(front_inverse.shape[1:], BF16)
     coefficients = (interior_scale, forward_coupling, backward_coupling)
     operands = [section_layers, rhs, *coefficients, picked]
-    local, ahead, longer, place, front, layers = call(
+    local, ahead, longer, front, layers = call(
         functools.partial(first_kernel, width),
         [in_hbm(a) for a in operands],
         [
             ((2 * rows + 8, cells), F32),
             ((rows + NEEDS, 2 * width), F32),
             ((2 * rows + NEEDS, 2 * width), F32),
-            ((2, cells), jnp.int32),
             front_shape,
             ((-(-sections // 8) * 8, LANES), jnp.int32),
         ],
@@ -512,10 +512,10 @@
         return pairs + [(j, i) for i, j in pairs] + [(i, i) for i in alone]
 
     near = [send(ahead, neighbours(0), 0, 0), None]
-    first_inverse, second_inverse, token = call(
-        load_kernel,
-        [inverse],
-        [half_inverse, half_inverse, ((8, LANES), F32)],
+    first_inverse, second_inverse, place, token = call(
+        functools.partial(load_kernel, width),
+        [inverse, local],
+        [half_inverse, half_inverse, ((2, cells), jnp.int32), ((8, LANES), F32)],
         [pltpu.SemaphoreType.DMA((1,))],
         "load_first",
         [0],

time: 102 us -> 101 us (level)
  no operation moved by 1% of the time
where the time goes in v19:
time: 101 us
  starting transfers between devices  47.2 us (47%)
  waiting for transfers between devices  34.8 us (34%)
  Pallas kernels  18.6 us (18%)
    ppermute x40, starting transfers between devices, send(): return lax.ppermute(block, ('sweep', 'plane'), route)  47.2 us
    ppermute x40, waiting for transfers between devices, send(): return lax.ppermute(block, ('sweep', 'plane'), route)  34.8 us
    pallas_call x11, Pallas kernels, call(): pl.pallas_call(kernel, in_specs=specs, out_specs=[whole(pltpu.SMEM if len...  18.6 us
  transfers between devices with their start and end apart: 40, of which 25 were waited for; matrix products, arithmetic and copies ran while one was open for 0% of the time, Pallas kernels for 3%

profile of v19, /device:TPU:0, one launch (start us, length us, event | category | flops | bytes accessed | tf_op | source)
XLA Modules:
  0.0 101.1 jit_solution(3167059699097042925)
XLA Ops:
  0.0 1.5 %first_fronts.1 = (f32[40,1024]{1,0:T(8,128)S(1)}, f32[24,1024]{1,0:T(8,128)S(1)}, f32[40,1024]{1,0:T(8,128)S(1)}, bf16[8,16,128]{2,1,0:T(8,128)(2,1)S(1)}, s32[8,128]{1,0:T(8,128)S(1)}) custom-call(s32[4]{0:T(128)} %layers_in.1, f32[2,16,1024]{2,1,0:T(8,128)} %bitcast.52, f32[2,1024]{1,0:T(2,128)} %isc_in.1, f32[2,1024]{1,0:T(2,128)} %fwd_in.1, ...), custom_call_target="tpu_custom_call" | custom-call | tf_op jit(solution)/shard_map/first_fronts/pallas_call | solution.py:385
  2.0 2.6 %collective-permute-start.3 = (f32[24,1024]{1,0:T(8,128)S(1)}, f32[24,1024]{1,0:T(8,128)S(1)}, u32[]{:S(2)}, u32[]{:S(2)}) collective-permute-start(f32[24,1024]{1,0:T(8,128)S(1)} %get-tuple-element.44), channel_id=1, source_target_pairs={{0,8},{1,9},{2,10},{3,11},{4,12},{5,13},{6,14},{7,15},{16,24},{17,... | collective-permute-start | bytes 294920 | tf_op jit(solution)/shard_map/ppermute | solution.py:437
  4.7 1.6 %collective-permute-start.2 = (bf16[2,8,16,128]{3,2,1,0:T(8,128)(2,1)S(1)}, bf16[2,8,16,128]{3,2,1,0:T(8,128)(2,1)S(1)}, u32[]{:S(2)}, u32[]{:S(2)}) collective-permute-start(bf16[2,8,16,128]{3,2,1,0:T(8,128)(2,1)S(1)} %pad_maximum_fusion.6), channel_id=1, source_target_pairs={{0,2},{1,5},{2,0},{3,7},{4,6},{5,1},{6,4},{7,3},{8,10},{9,13},{10,... | collective-permute-start | bytes 196616 | tf_op jit(solution)/shard_map/ppermute | solution.py:437
  6.2 1.5 %collective-permute-start = (bf16[8,16,128]{2,1,0:T(8,128)(2,1)S(1)}, bf16[8,16,128]{2,1,0:T(8,128)(2,1)S(1)}, u32[]{:S(2)}, u32[]{:S(2)}) collective-permute-start(bf16[8,16,128]{2,1,0:T(8,128)(2,1)S(1)} %get-tuple-element.43.refs_0_.rest_0_), channel_id=1, source_target_pairs={{0,6},{1,7},{2,4},{3,5},{4,2},{5,3},{6,0},{7,1},{8,14},{9,15},{10,... | collective-permute-start | bytes 98312 | tf_op jit(solution)/shard_map/ppermute | solution.py:437
  7.7 3.4 %load_first.1 = (bf16[2,512,4096]{2,1,0:T(8,128)(2,1)S(1)}, bf16[2,512,4096]{2,1,0:T(8,128)(2,1)S(1)}, s32[2,1024]{1,0:T(2,128)S(1)}, f32[8,128]{1,0:T(8,128)S(1)}) custom-call(bf16[2,2,512,4096]{3,2,1,0:T(8,128)(2,1)} %inverse.9, f32[40,1024]{1,0:T(8,128)S(1)} %get-tuple-element.39.local.packet), custom_call_target="tpu_custom_call" | custom-call | tf_op jit(solution)/shard_map/load_first/pallas_call | solution.py:385
  11.2 1.3 %collective-permute-done.4.rest_3_ = bf16[4,8,16,128]{3,2,1,0:T(8,128)(2,1)S(1)} collective-permute-done((bf16[4,8,16,128]{3,2,1,0:T(8,128)(2,1)S(1)}, bf16[4,8,16,128]{3,2,1,0:T(8,128)(2,1)S(1)}, u32[]{:S(2)}, u32[]{:S(2)}) %collective-permute-start.4) | collective-permute-done | bytes 131104 | tf_op jit(solution)/shard_map/ppermute | solution.py:437
  12.6 6.4 %forward_section_0.1 = (f32[2,16,1024]{2,1,0:T(8,128)S(1)}, bf16[8,16,128]{2,1,0:T(8,128)(2,1)S(1)}, bf16[16,16,128]{2,1,0:T(8,128)(2,1)S(1)}, bf16[2,512,4096]{2,1,0:T(8,128)(2,1)S(1)}) custom-call(s32[8,128]{1,0:T(8,128)S(1)} %get-tuple-element.38.layers, ...), custom_call_target="tpu_custom_call", output_to_operand_aliasing={{3}: (2, {})} | custom-call | tf_op jit(solution)/shard_map/forward_section_0/pallas_call | solution.py:385
  20.3 2.3 %collective-permute-start.8 = (bf16[2,8,16,128]{3,2,1,0:T(8,128)(2,1)S(1)}, bf16[2,8,16,128]{3,2,1,0:T(8,128)(2,1)S(1)}, u32[]{:S(2)}, u32[]{:S(2)}) collective-permute-start(bf16[2,8,16,128]{3,2,1,0:T(8,128)(2,1)S(1)} %pad_maximum_fusion.7), channel_id=1, source_target_pairs={{0,10},{1,13},{2,8},{3,15},{4,14},{5,9},{6,12},{7,11},{8,2},{9,5},... | collective-permute-start | bytes 196616 | tf_op jit(solution)/shard_map/ppermute | solution.py:437
  23.9 2.3 %collective-permute-done.6.rest_1_ = bf16[8,16,128]{2,1,0:T(8,128)(2,1)S(1)} collective-permute-done((bf16[8,16,128]{2,1,0:T(8,128)(2,1)S(1)}, bf16[8,16,128]{2,1,0:T(8,128)(2,1)S(1)}, u32[]{:S(2)}, u32[]{:S(2)}) %collective-permute-start.6) | collective-permute-done | bytes 32800 | tf_op jit(solution)/shard_map/ppermute | solution.py:437
  28.7 1.5 %collective-permute-start.12 = (bf16[8,16,128]{2,1,0:T(8,128)(2,1)S(1)}, bf16[8,16,128]{2,1,0:T(8,128)(2,1)S(1)}, u32[]{:S(2)}, u32[]{:S(2)}) collective-permute-start(bf16[8,16,128]{2,1,0:T(8,128)(2,1)S(1)} %get-tuple-element.52), channel_id=1, source_target_pairs={{8,22},{9,23},{10,20},{11,21},{12,18},{13,19},{14,16},{15,17},{16,... | collective-permute-start | bytes 98312 | tf_op jit(solution)/shard_map/ppermute | solution.py:437
  31.4 2.1 %collective-permute-done.12.rest_1_ = bf16[8,16,128]{2,1,0:T(8,128)(2,1)S(1)} collective-permute-done((bf16[8,16,128]{2,1,0:T(8,128)(2,1)S(1)}, bf16[8,16,128]{2,1,0:T(8,128)(2,1)S(1)}, u32[]{:S(2)}, u32[]{:S(2)}) %collective-permute-start.12) | collective-permute-done | bytes 32800 | tf_op jit(solution)/shard_map/ppermute | solution.py:437
  36.6 10.9 %collective-permute-start.17 = (bf16[8,16,128]{2,1,0:T(8,128)(2,1)S(1)}, bf16[8,16,128]{2,1,0:T(8,128)(2,1)S(1)}, u32[]{:S(2)}, u32[]{:S(2)}) collective-permute-start(bf16[8,16,128]{2,1,0:T(8,128)(2,1)S(1)} %get-tuple-element.55), channel_id=1, source_target_pairs={{16,30},{17,31},{18,28},{19,29},{20,26},{21,27},{22,24},{23,25},{2... | collective-permute-start | bytes 98312 | tf_op jit(solution)/shard_map/ppermute | solution.py:437
  49.1 2.8 %collective-permute-done.19.rest_2_ = bf16[2,8,16,128]{3,2,1,0:T(8,128)(2,1)S(1)} collective-permute-done((bf16[2,8,16,128]{3,2,1,0:T(8,128)(2,1)S(1)}, bf16[2,8,16,128]{3,2,1,0:T(8,128)(2,1)S(1)}, u32[]{:S(2)}, u32[]{:S(2)}) %collective-permute-start.19) | collective-permute-done | bytes 65568 | tf_op jit(solution)/shard_map/ppermute | solution.py:437
  53.9 1.6 %collective-permute-start.21 = (bf16[8,16,128]{2,1,0:T(8,128)(2,1)S(1)}, bf16[8,16,128]{2,1,0:T(8,128)(2,1)S(1)}, u32[]{:S(2)}, u32[]{:S(2)}) collective-permute-start(bf16[8,16,128]{2,1,0:T(8,128)(2,1)S(1)} %get-tuple-element.57.rest_0_), channel_id=1, source_target_pairs={{0,6},{1,7},{2,4},{3,5},{4,2},{5,3},{6,0},{7,1},{8,14},{9,15},{10,... | collective-permute-start | bytes 98312 | tf_op jit(solution)/shard_map/ppermute | solution.py:437
  56.6 2.2 %collective-permute-done.21.rest_1_ = bf16[8,16,128]{2,1,0:T(8,128)(2,1)S(1)} collective-permute-done((bf16[8,16,128]{2,1,0:T(8,128)(2,1)S(1)}, bf16[8,16,128]{2,1,0:T(8,128)(2,1)S(1)}, u32[]{:S(2)}, u32[]{:S(2)}) %collective-permute-start.21) | collective-permute-done | bytes 32800 | tf_op jit(solution)/shard_map/ppermute | solution.py:437
  61.2 1.4 %collective-permute-start.26 = (bf16[8,16,128]{2,1,0:T(8,128)(2,1)S(1)}, bf16[8,16,128]{2,1,0:T(8,128)(2,1)S(1)}, u32[]{:S(2)}, u32[]{:S(2)}) collective-permute-start(bf16[8,16,128]{2,1,0:T(8,128)(2,1)S(1)} %get-tuple-element.60), channel_id=1, source_target_pairs={{24,22},{25,23},{26,20},{27,21},{28,18},{29,19},{30,16},{31,17},{1... | collective-permute-start | bytes 98312 | tf_op jit(solution)/shard_map/ppermute | solution.py:437
  63.8 2.2 %collective-permute-done.26.rest_1_ = bf16[8,16,128]{2,1,0:T(8,128)(2,1)S(1)} collective-permute-done((bf16[8,16,128]{2,1,0:T(8,128)(2,1)S(1)}, bf16[8,16,128]{2,1,0:T(8,128)(2,1)S(1)}, u32[]{:S(2)}, u32[]{:S(2)}) %collective-permute-start.26) | collective-permute-done | bytes 32800 | tf_op jit(solution)/shard_map/ppermute | solution.py:437
  68.8 8.0 %collective-permute-start.31 = (bf16[8,16,128]{2,1,0:T(8,128)(2,1)S(1)}, bf16[8,16,128]{2,1,0:T(8,128)(2,1)S(1)}, u32[]{:S(2)}, u32[]{:S(2)}) collective-permute-start(bf16[8,16,128]{2,1,0:T(8,128)(2,1)S(1)} %get-tuple-element.64), channel_id=1, source_target_pairs={{16,14},{17,15},{18,12},{19,13},{20,10},{21,11},{22,8},{23,9},{8,6... | collective-permute-start | bytes 98312 | tf_op jit(solution)/shard_map/ppermute | solution.py:437
  78.5 2.8 %collective-permute-done.33.rest_2_ = bf16[2,8,16,128]{3,2,1,0:T(8,128)(2,1)S(1)} collective-permute-done((bf16[2,8,16,128]{3,2,1,0:T(8,128)(2,1)S(1)}, bf16[2,8,16,128]{3,2,1,0:T(8,128)(2,1)S(1)}, u32[]{:S(2)}, u32[]{:S(2)}) %collective-permute-start.33) | collective-permute-done | bytes 65568 | tf_op jit(solution)/shard_map/ppermute | solution.py:437
  83.4 5.4 %collective-permute-start.35 = (bf16[16,16,128]{2,1,0:T(8,128)(2,1)S(1)}, bf16[16,16,128]{2,1,0:T(8,128)(2,1)S(1)}, u32[]{:S(2)}, u32[]{:S(2)}) collective-permute-start(bf16[16,16,128]{2,1,0:T(8,128)(2,1)S(1)} %get-tuple-element.67), channel_id=1, source_target_pairs={{8,0},{9,1},{10,2},{11,3},{12,4},{13,5},{14,6},{15,7},{0,8},{1,9},... | collective-permute-start | bytes 196616 | tf_op jit(solution)/shard_map/ppermute | solution.py:437
  88.8 1.6 %collective-permute-start.38 = (bf16[2,8,16,128]{3,2,1,0:T(8,128)(2,1)S(1)}, bf16[2,8,16,128]{3,2,1,0:T(8,128)(2,1)S(1)}, u32[]{:S(2)}, u32[]{:S(2)}) collective-permute-start(bf16[2,8,16,128]{3,2,1,0:T(8,128)(2,1)S(1)} %pad_maximum_fusion.13), channel_id=1, source_target_pairs={{8,2},{9,5},{10,0},{11,7},{12,6},{13,1},{14,4},{15,3},{0,10},{1,13... | collective-permute-start | bytes 196616 | tf_op jit(solution)/shard_map/ppermute | solution.py:437
  90.4 1.6 %collective-permute-done.35.rest_0_.rest_5_ = bf16[16,16,128]{2,1,0:T(8,128)(2,1)S(1)} collective-permute-done((bf16[16,16,128]{2,1,0:T(8,128)(2,1)S(1)}, bf16[16,16,128]{2,1,0:T(8,128)(2,1)S(1)}, u32[]{:S(2)}, u32[]{:S(2)}) %collective-permute-start.35) | collective-permute-done | bytes 65568 | tf_op jit(solution)/shard_map/ppermute | solution.py:437
  92.1 1.9 %collective-permute-done.38.rest_2_ = bf16[2,8,16,128]{3,2,1,0:T(8,128)(2,1)S(1)} collective-permute-done((bf16[2,8,16,128]{3,2,1,0:T(8,128)(2,1)S(1)}, bf16[2,8,16,128]{3,2,1,0:T(8,128)(2,1)S(1)}, u32[]{:S(2)}, u32[]{:S(2)}) %collective-permute-start.38) | collective-permute-done | bytes 65568 | tf_op jit(solution)/shard_map/ppermute | solution.py:437
  95.4 5.6 %backward_section_0.1 = f32[2,16,1024]{2,1,0:T(8,128)} custom-call(s32[8,128]{1,0:T(8,128)S(1)} %get-tuple-element.38.layers, bf16[2,512,4096]{2,1,0:T(8,128)(2,1)S(1)} %get-tuple-element.40.first_inverse, bf16[2,512,4096]{2,1,0:T(8,128)(2,1)S(1)} %get-tuple-element.56.second_inverse, f32[40,1024]{1,0:T(8,128)S(1)} %get-tuple-element.39.local.packet, ...), custom_call_target="tpu_custom_call" | custom-call | tf_op jit(solution)/shard_map/backward_section_0/pallas_call | solution.py:385
  (90 shorter events, 26.1 us)
Async XLA Ops:
  1.5 3.2 %collective-permute-start.1 = (bf16[8,16,128]{2,1,0:T(8,128)(2,1)S(1)}, bf16[8,16,128]{2,1,0:T(8,128)(2,1)S(1)}, u32[]{:S(2)}, u32[]{:S(2)}) collective-permute-start(bf16[8,16,128]{2,1,0:T(8,128)(2,1)S(1)} %get-tuple-element.43.refs_0_.rest_0_), channel_id=1, source_target_pairs={{0,1},{1,0},{2,3},{3,2},{4,5},{5,4},{6,7},{7,6},{8,9},{9,8},{10,11... | collective-permute-start | bytes 98312 | tf_op jit(solution)/shard_map/ppermute | solution.py:437
  2.0 9.1 %collective-permute-start.3 = (f32[24,1024]{1,0:T(8,128)S(1)}, f32[24,1024]{1,0:T(8,128)S(1)}, u32[]{:S(2)}, u32[]{:S(2)}) collective-permute-start(f32[24,1024]{1,0:T(8,128)S(1)} %get-tuple-element.44), channel_id=1, source_target_pairs={{0,8},{1,9},{2,10},{3,11},{4,12},{5,13},{6,14},{7,15},{16,24},{17,... | collective-permute-start | bytes 294920 | tf_op jit(solution)/shard_map/ppermute | solution.py:437
  4.7 6.5 %collective-permute-start.2 = (bf16[2,8,16,128]{3,2,1,0:T(8,128)(2,1)S(1)}, bf16[2,8,16,128]{3,2,1,0:T(8,128)(2,1)S(1)}, u32[]{:S(2)}, u32[]{:S(2)}) collective-permute-start(bf16[2,8,16,128]{3,2,1,0:T(8,128)(2,1)S(1)} %pad_maximum_fusion.6), channel_id=1, source_target_pairs={{0,2},{1,5},{2,0},{3,7},{4,6},{5,1},{6,4},{7,3},{8,10},{9,13},{10,... | collective-permute-start | bytes 196616 | tf_op jit(solution)/shard_map/ppermute | solution.py:437
  6.2 4.9 %collective-permute-start = (bf16[8,16,128]{2,1,0:T(8,128)(2,1)S(1)}, bf16[8,16,128]{2,1,0:T(8,128)(2,1)S(1)}, u32[]{:S(2)}, u32[]{:S(2)}) collective-permute-start(bf16[8,16,128]{2,1,0:T(8,128)(2,1)S(1)} %get-tuple-element.43.refs_0_.rest_0_), channel_id=1, source_target_pairs={{0,6},{1,7},{2,4},{3,5},{4,2},{5,3},{6,0},{7,1},{8,14},{9,15},{10,... | collective-permute-start | bytes 98312 | tf_op jit(solution)/shard_map/ppermute | solution.py:437
  19.2 7.7 %collective-permute-start.10 = (f32[40,1024]{1,0:T(8,128)S(1)}, f32[40,1024]{1,0:T(8,128)S(1)}, u32[]{:S(2)}, u32[]{:S(2)}) collective-permute-start(f32[40,1024]{1,0:T(8,128)S(1)} %get-tuple-element.49), channel_id=1, source_target_pairs={{8,16},{9,17},{10,18},{11,19},{12,20},{13,21},{14,22},{15,23},{16,... | collective-permute-start | bytes 491528 | tf_op jit(solution)/shard_map/ppermute | solution.py:437
  19.6 6.6 %collective-permute-start.6 = (bf16[8,16,128]{2,1,0:T(8,128)(2,1)S(1)}, bf16[8,16,128]{2,1,0:T(8,128)(2,1)S(1)}, u32[]{:S(2)}, u32[]{:S(2)}) collective-permute-start(bf16[8,16,128]{2,1,0:T(8,128)(2,1)S(1)} %get-tuple-element.48), channel_id=1, source_target_pairs={{0,14},{1,15},{2,12},{3,13},{4,10},{5,11},{6,8},{7,9},{8,22},{9,23... | collective-permute-start | bytes 98312 | tf_op jit(solution)/shard_map/ppermute | solution.py:437
  19.6 4.3 %collective-permute-start.5 = (bf16[16,16,128]{2,1,0:T(8,128)(2,1)S(1)}, bf16[16,16,128]{2,1,0:T(8,128)(2,1)S(1)}, u32[]{:S(2)}, u32[]{:S(2)}) collective-permute-start(bf16[16,16,128]{2,1,0:T(8,128)(2,1)S(1)} %get-tuple-element.47), channel_id=1, source_target_pairs={{0,8},{1,9},{2,10},{3,11},{4,12},{5,13},{6,14},{7,15},{8,0},{9,1},... | collective-permute-start | bytes 196616 | tf_op jit(solution)/shard_map/ppermute | solution.py:437
  20.3 6.5 %collective-permute-start.8 = (bf16[2,8,16,128]{3,2,1,0:T(8,128)(2,1)S(1)}, bf16[2,8,16,128]{3,2,1,0:T(8,128)(2,1)S(1)}, u32[]{:S(2)}, u32[]{:S(2)}) collective-permute-start(bf16[2,8,16,128]{3,2,1,0:T(8,128)(2,1)S(1)} %pad_maximum_fusion.7), channel_id=1, source_target_pairs={{0,10},{1,13},{2,8},{3,15},{4,14},{5,9},{6,12},{7,11},{8,2},{9,5},... | collective-permute-start | bytes 196616 | tf_op jit(solution)/shard_map/ppermute | solution.py:437
  28.7 4.8 %collective-permute-start.12 = (bf16[8,16,128]{2,1,0:T(8,128)(2,1)S(1)}, bf16[8,16,128]{2,1,0:T(8,128)(2,1)S(1)}, u32[]{:S(2)}, u32[]{:S(2)}) collective-permute-start(bf16[8,16,128]{2,1,0:T(8,128)(2,1)S(1)} %get-tuple-element.52), channel_id=1, source_target_pairs={{8,22},{9,23},{10,20},{11,21},{12,18},{13,19},{14,16},{15,17},{16,... | collective-permute-start | bytes 98312 | tf_op jit(solution)/shard_map/ppermute | solution.py:437
  30.2 4.3 %collective-permute-start.14 = (bf16[2,8,16,128]{3,2,1,0:T(8,128)(2,1)S(1)}, bf16[2,8,16,128]{3,2,1,0:T(8,128)(2,1)S(1)}, u32[]{:S(2)}, u32[]{:S(2)}) collective-permute-start(bf16[2,8,16,128]{3,2,1,0:T(8,128)(2,1)S(1)} %pad_maximum_fusion.8), channel_id=1, source_target_pairs={{8,18},{9,21},{10,16},{11,23},{12,22},{13,17},{14,20},{15,19},{16,... | collective-permute-start | bytes 196616 | tf_op jit(solution)/shard_map/ppermute | solution.py:437
  36.4 11.2 %collective-permute-start.18 = (bf16[8,16,128]{2,1,0:T(8,128)(2,1)S(1)}, bf16[8,16,128]{2,1,0:T(8,128)(2,1)S(1)}, u32[]{:S(2)}, u32[]{:S(2)}) collective-permute-start(bf16[8,16,128]{2,1,0:T(8,128)(2,1)S(1)} %get-tuple-element.55), channel_id=1, source_target_pairs={{0,1},{1,0},{2,3},{3,2},{4,5},{5,4},{6,7},{7,6},{8,9},{9,8},{10,11... | collective-permute-start | bytes 98312 | tf_op jit(solution)/shard_map/ppermute | solution.py:437
  36.6 12.5 %collective-permute-start.17 = (bf16[8,16,128]{2,1,0:T(8,128)(2,1)S(1)}, bf16[8,16,128]{2,1,0:T(8,128)(2,1)S(1)}, u32[]{:S(2)}, u32[]{:S(2)}) collective-permute-start(bf16[8,16,128]{2,1,0:T(8,128)(2,1)S(1)} %get-tuple-element.55), channel_id=1, source_target_pairs={{16,30},{17,31},{18,28},{19,29},{20,26},{21,27},{22,24},{23,25},{2... | collective-permute-start | bytes 98312 | tf_op jit(solution)/shard_map/ppermute | solution.py:437
  47.6 4.3 %collective-permute-start.19 = (bf16[2,8,16,128]{3,2,1,0:T(8,128)(2,1)S(1)}, bf16[2,8,16,128]{3,2,1,0:T(8,128)(2,1)S(1)}, u32[]{:S(2)}, u32[]{:S(2)}) collective-permute-start(bf16[2,8,16,128]{3,2,1,0:T(8,128)(2,1)S(1)} %pad_maximum_fusion.9), channel_id=1, source_target_pairs={{16,26},{17,29},{18,24},{19,31},{20,30},{21,25},{22,28},{23,27},{2... | collective-permute-start | bytes 196616 | tf_op jit(solution)/shard_map/ppermute | solution.py:437
  53.9 4.9 %collective-permute-start.21 = (bf16[8,16,128]{2,1,0:T(8,128)(2,1)S(1)}, bf16[8,16,128]{2,1,0:T(8,128)(2,1)S(1)}, u32[]{:S(2)}, u32[]{:S(2)}) collective-permute-start(bf16[8,16,128]{2,1,0:T(8,128)(2,1)S(1)} %get-tuple-element.57.rest_0_), channel_id=1, source_target_pairs={{0,6},{1,7},{2,4},{3,5},{4,2},{5,3},{6,0},{7,1},{8,14},{9,15},{10,... | collective-permute-start | bytes 98312 | tf_op jit(solution)/shard_map/ppermute | solution.py:437
  55.4 4.0 %collective-permute-start.23 = (bf16[2,4,16,128]{3,2,1,0:T(8,128)(2,1)S(1)}, bf16[2,4,16,128]{3,2,1,0:T(8,128)(2,1)S(1)}, u32[]{:S(2)}, u32[]{:S(2)}) collective-permute-start(bf16[2,4,16,128]{3,2,1,0:T(8,128)(2,1)S(1)} %pad_maximum_fusion.14), channel_id=1, source_target_pairs={{0,2},{1,5},{2,0},{3,7},{4,6},{5,1},{6,4},{7,3},{8,10},{9,13},{10,... | collective-permute-start | bytes 98312 | tf_op jit(solution)/shard_map/ppermute | solution.py:437
  61.2 4.8 %collective-permute-start.26 = (bf16[8,16,128]{2,1,0:T(8,128)(2,1)S(1)}, bf16[8,16,128]{2,1,0:T(8,128)(2,1)S(1)}, u32[]{:S(2)}, u32[]{:S(2)}) collective-permute-start(bf16[8,16,128]{2,1,0:T(8,128)(2,1)S(1)} %get-tuple-element.60), channel_id=1, source_target_pairs={{24,22},{25,23},{26,20},{27,21},{28,18},{29,19},{30,16},{31,17},{1... | collective-permute-start | bytes 98312 | tf_op jit(solution)/shard_map/ppermute | solution.py:437
  62.6 4.3 %collective-permute-start.28 = (bf16[2,8,16,128]{3,2,1,0:T(8,128)(2,1)S(1)}, bf16[2,8,16,128]{3,2,1,0:T(8,128)(2,1)S(1)}, u32[]{:S(2)}, u32[]{:S(2)}) collective-permute-start(bf16[2,8,16,128]{3,2,1,0:T(8,128)(2,1)S(1)} %pad_maximum_fusion.11), channel_id=1, source_target_pairs={{24,18},{25,21},{26,16},{27,23},{28,22},{29,17},{30,20},{31,19},{1... | collective-permute-start | bytes 196616 | tf_op jit(solution)/shard_map/ppermute | solution.py:437
  68.6 8.3 %collective-permute-start.32 = (bf16[8,16,128]{2,1,0:T(8,128)(2,1)S(1)}, bf16[8,16,128]{2,1,0:T(8,128)(2,1)S(1)}, u32[]{:S(2)}, u32[]{:S(2)}) collective-permute-start(bf16[8,16,128]{2,1,0:T(8,128)(2,1)S(1)} %get-tuple-element.64), channel_id=1, source_target_pairs={{0,1},{1,0},{2,3},{3,2},{4,5},{5,4},{6,7},{7,6},{8,9},{9,8},{10,11... | collective-permute-start | bytes 98312 | tf_op jit(solution)/shard_map/ppermute | solution.py:437
  68.8 9.6 %collective-permute-start.31 = (bf16[8,16,128]{2,1,0:T(8,128)(2,1)S(1)}, bf16[8,16,128]{2,1,0:T(8,128)(2,1)S(1)}, u32[]{:S(2)}, u32[]{:S(2)}) collective-permute-start(bf16[8,16,128]{2,1,0:T(8,128)(2,1)S(1)} %get-tuple-element.64), channel_id=1, source_target_pairs={{16,14},{17,15},{18,12},{19,13},{20,10},{21,11},{22,8},{23,9},{8,6... | collective-permute-start | bytes 98312 | tf_op jit(solution)/shard_map/ppermute | solution.py:437
  77.0 4.3 %collective-permute-start.33 = (bf16[2,8,16,128]{3,2,1,0:T(8,128)(2,1)S(1)}, bf16[2,8,16,128]{3,2,1,0:T(8,128)(2,1)S(1)}, u32[]{:S(2)}, u32[]{:S(2)}) collective-permute-start(bf16[2,8,16,128]{3,2,1,0:T(8,128)(2,1)S(1)} %pad_maximum_fusion.12), channel_id=1, source_target_pairs={{16,10},{17,13},{18,8},{19,15},{20,14},{21,9},{22,12},{23,11},{8,1... | collective-permute-start | bytes 196616 | tf_op jit(solution)/shard_map/ppermute | solution.py:437
  83.2 5.6 %collective-permute-start.37 = (bf16[8,16,128]{2,1,0:T(8,128)(2,1)S(1)}, bf16[8,16,128]{2,1,0:T(8,128)(2,1)S(1)}, u32[]{:S(2)}, u32[]{:S(2)}) collective-permute-start(bf16[8,16,128]{2,1,0:T(8,128)(2,1)S(1)} %get-tuple-element.68), channel_id=1, source_target_pairs={{0,1},{1,0},{2,3},{3,2},{4,5},{5,4},{6,7},{7,6},{8,9},{9,8},{10,11... | collective-permute-start | bytes 98312 | tf_op jit(solution)/shard_map/ppermute | solution.py:437
  83.4 8.7 %collective-permute-start.36 = (bf16[8,16,128]{2,1,0:T(8,128)(2,1)S(1)}, bf16[8,16,128]{2,1,0:T(8,128)(2,1)S(1)}, u32[]{:S(2)}, u32[]{:S(2)}) collective-permute-start(bf16[8,16,128]{2,1,0:T(8,128)(2,1)S(1)} %get-tuple-element.68), channel_id=1, source_target_pairs={{8,6},{9,7},{10,4},{11,5},{12,2},{13,3},{14,0},{15,1},{0,30},{1,31... | collective-permute-start | bytes 98312 | tf_op jit(solution)/shard_map/ppermute | solution.py:437
  83.4 8.7 %collective-permute-start.35 = (bf16[16,16,128]{2,1,0:T(8,128)(2,1)S(1)}, bf16[16,16,128]{2,1,0:T(8,128)(2,1)S(1)}, u32[]{:S(2)}, u32[]{:S(2)}) collective-permute-start(bf16[16,16,128]{2,1,0:T(8,128)(2,1)S(1)} %get-tuple-element.67), channel_id=1, source_target_pairs={{8,0},{9,1},{10,2},{11,3},{12,4},{13,5},{14,6},{15,7},{0,8},{1,9},... | collective-permute-start | bytes 196616 | tf_op jit(solution)/shard_map/ppermute | solution.py:437
  88.8 5.2 %collective-permute-start.38 = (bf16[2,8,16,128]{3,2,1,0:T(8,128)(2,1)S(1)}, bf16[2,8,16,128]{3,2,1,0:T(8,128)(2,1)S(1)}, u32[]{:S(2)}, u32[]{:S(2)}) collective-permute-start(bf16[2,8,16,128]{3,2,1,0:T(8,128)(2,1)S(1)} %pad_maximum_fusion.13), channel_id=1, source_target_pairs={{8,2},{9,5},{10,0},{11,7},{12,6},{13,1},{14,4},{15,3},{0,10},{1,13... | collective-permute-start | bytes 196616 | tf_op jit(solution)/shard_map/ppermute | solution.py:437
  (16 other events, 22.8 us)

commit v20 on v19

--- a/solution.py
+++ b/solution.py
@@ -254,7 +254,9 @@
         pltpu.make_async_copy(inverse.at[1, part], second_inverse.at[part], sems.at[part])
         for part in range(2)
     ]
-    early = own >= 3
+    early = jnp.bool_(step >= 3)
+    if step in (1, 2):
+        early = two_layers(layers, step - 1)
 
     def when(condition, *actions):
         @pl.when(condition)
@@ -264,7 +266,10 @@
 
     starts, waits = [load.start for load in loads], [load.wait for load in loads]
     if step == 1:
-        when(early, *starts, *waits)
+        when(own >= 3, *starts, *waits)
+    if step < 2 and not final:
+        ahead = (own == step + 1) & two_layers(layers, step + 1)
+        when(ahead & both, *starts, *waits)
     when(mine & both & ~early, *starts)
 
     @pl.when(mine)

time: 101 us -> 102 us (level)
  starting transfers between devices: 47.2 us -> 54.3 us
  Pallas kernels: 18.6 us -> 13.1 us
  waiting for transfers between devices: 34.8 us -> 33.6 us
    ppermute x40, starting transfers between devices: 47.2 us -> 54.3 us  [send(): return lax.ppermute(block, ('sweep', 'plane'), route)]
    pallas_call x11, Pallas kernels: 18.6 us -> 13.1 us  [call(): pl.pallas_call(kernel, in_specs=specs, out_specs=[whole(pltpu.SMEM if len...]
    ppermute x40, waiting for transfers between devices: 34.8 us -> 33.6 us  [send(): return lax.ppermute(block, ('sweep', 'plane'), route)]
  transfers between devices with their start and end apart: 40 -> 40, of which waited for: 25 -> 24; matrix products, arithmetic and copies ran while one was open for 0% -> 0% of each run, Pallas kernels for 3% -> 3%
where the time goes in v20:
time: 102 us; the launch traced here: 101 us
  starting transfers between devices  54.3 us (53%)
  waiting for transfers between devices  33.6 us (33%)
  Pallas kernels  13.1 us (13%)
    ppermute x40, starting transfers between devices, send(): return lax.ppermute(block, ('sweep', 'plane'), route)  54.3 us
    ppermute x40, waiting for transfers between devices, send(): return lax.ppermute(block, ('sweep', 'plane'), route)  33.6 us
    pallas_call x11, Pallas kernels, call(): pl.pallas_call(kernel, in_specs=specs, out_specs=[whole(pltpu.SMEM if len...  13.1 us
  transfers between devices with their start and end apart: 40, of which 24 were waited for; matrix products, arithmetic and copies ran while one was open for 0% of the time, Pallas kernels for 3%

profile of v20, /device:TPU:0, one launch (start us, length us, event | category | flops | bytes accessed | tf_op | source)
XLA Modules:
  0.0 101.4 jit_solution(15972561663399234973)
XLA Ops:
  0.0 1.5 %first_fronts.1 = (f32[40,1024]{1,0:T(8,128)S(1)}, f32[24,1024]{1,0:T(8,128)S(1)}, f32[40,1024]{1,0:T(8,128)S(1)}, bf16[8,16,128]{2,1,0:T(8,128)(2,1)S(1)}, s32[8,128]{1,0:T(8,128)S(1)}) custom-call(s32[4]{0:T(128)} %layers_in.1, f32[2,16,1024]{2,1,0:T(8,128)} %bitcast.52, f32[2,1024]{1,0:T(2,128)} %isc_in.1, f32[2,1024]{1,0:T(2,128)} %fwd_in.1, ...), custom_call_target="tpu_custom_call" | custom-call | tf_op jit(solution)/shard_map/first_fronts/pallas_call | solution.py:390
  2.0 2.6 %collective-permute-start.3 = (f32[24,1024]{1,0:T(8,128)S(1)}, f32[24,1024]{1,0:T(8,128)S(1)}, u32[]{:S(2)}, u32[]{:S(2)}) collective-permute-start(f32[24,1024]{1,0:T(8,128)S(1)} %get-tuple-element.44), channel_id=1, source_target_pairs={{0,8},{1,9},{2,10},{3,11},{4,12},{5,13},{6,14},{7,15},{16,24},{17,... | collective-permute-start | bytes 294920 | tf_op jit(solution)/shard_map/ppermute | solution.py:442
  4.7 1.6 %collective-permute-start.2 = (bf16[2,8,16,128]{3,2,1,0:T(8,128)(2,1)S(1)}, bf16[2,8,16,128]{3,2,1,0:T(8,128)(2,1)S(1)}, u32[]{:S(2)}, u32[]{:S(2)}) collective-permute-start(bf16[2,8,16,128]{3,2,1,0:T(8,128)(2,1)S(1)} %pad_maximum_fusion.6), channel_id=1, source_target_pairs={{0,2},{1,5},{2,0},{3,7},{4,6},{5,1},{6,4},{7,3},{8,10},{9,13},{10,... | collective-permute-start | bytes 196616 | tf_op jit(solution)/shard_map/ppermute | solution.py:442
  6.2 1.5 %collective-permute-start = (bf16[8,16,128]{2,1,0:T(8,128)(2,1)S(1)}, bf16[8,16,128]{2,1,0:T(8,128)(2,1)S(1)}, u32[]{:S(2)}, u32[]{:S(2)}) collective-permute-start(bf16[8,16,128]{2,1,0:T(8,128)(2,1)S(1)} %get-tuple-element.43.refs_0_.rest_0_), channel_id=1, source_target_pairs={{0,6},{1,7},{2,4},{3,5},{4,2},{5,3},{6,0},{7,1},{8,14},{9,15},{10,... | collective-permute-start | bytes 98312 | tf_op jit(solution)/shard_map/ppermute | solution.py:442
  7.7 3.4 %load_first.1 = (bf16[2,512,4096]{2,1,0:T(8,128)(2,1)S(1)}, bf16[2,512,4096]{2,1,0:T(8,128)(2,1)S(1)}, s32[2,1024]{1,0:T(2,128)S(1)}, f32[8,128]{1,0:T(8,128)S(1)}) custom-call(bf16[2,2,512,4096]{3,2,1,0:T(8,128)(2,1)} %inverse.9, f32[40,1024]{1,0:T(8,128)S(1)} %get-tuple-element.39.local.packet), custom_call_target="tpu_custom_call" | custom-call | tf_op jit(solution)/shard_map/load_first/pallas_call | solution.py:390
  11.2 1.3 %collective-permute-done.4.rest_3_ = bf16[4,8,16,128]{3,2,1,0:T(8,128)(2,1)S(1)} collective-permute-done((bf16[4,8,16,128]{3,2,1,0:T(8,128)(2,1)S(1)}, bf16[4,8,16,128]{3,2,1,0:T(8,128)(2,1)S(1)}, u32[]{:S(2)}, u32[]{:S(2)}) %collective-permute-start.4) | collective-permute-done | bytes 131104 | tf_op jit(solution)/shard_map/ppermute | solution.py:442
  12.6 3.0 %forward_section_0.1 = (f32[2,16,1024]{2,1,0:T(8,128)S(1)}, bf16[8,16,128]{2,1,0:T(8,128)(2,1)S(1)}, bf16[16,16,128]{2,1,0:T(8,128)(2,1)S(1)}, bf16[2,512,4096]{2,1,0:T(8,128)(2,1)S(1)}) custom-call(s32[8,128]{1,0:T(8,128)S(1)} %get-tuple-element.38.layers, ...), custom_call_target="tpu_custom_call", output_to_operand_aliasing={{3}: (2, {})} | custom-call | tf_op jit(solution)/shard_map/forward_section_0/pallas_call | solution.py:390
  17.1 3.0 %collective-permute-start.8 = (bf16[2,8,16,128]{3,2,1,0:T(8,128)(2,1)S(1)}, bf16[2,8,16,128]{3,2,1,0:T(8,128)(2,1)S(1)}, u32[]{:S(2)}, u32[]{:S(2)}) collective-permute-start(bf16[2,8,16,128]{3,2,1,0:T(8,128)(2,1)S(1)} %pad_maximum_fusion.7), channel_id=1, source_target_pairs={{0,10},{1,13},{2,8},{3,15},{4,14},{5,9},{6,12},{7,11},{8,2},{9,5},... | collective-permute-start | bytes 196616 | tf_op jit(solution)/shard_map/ppermute | solution.py:442
  20.1 2.6 %collective-permute-done.5.rest_0_.rest_4_.rest_8_ = bf16[16,16,128]{2,1,0:T(8,128)(2,1)S(1)} collective-permute-done((bf16[16,16,128]{2,1,0:T(8,128)(2,1)S(1)}, bf16[16,16,128]{2,1,0:T(8,128)(2,1)S(1)}, u32[]{:S(2)}, u32[]{:S(2)}) %collective-permute-start.5) | collective-permute-done | bytes 65568 | tf_op jit(solution)/shard_map/ppermute | solution.py:442
  25.9 1.6 %collective-permute-start.12 = (bf16[8,16,128]{2,1,0:T(8,128)(2,1)S(1)}, bf16[8,16,128]{2,1,0:T(8,128)(2,1)S(1)}, u32[]{:S(2)}, u32[]{:S(2)}) collective-permute-start(bf16[8,16,128]{2,1,0:T(8,128)(2,1)S(1)} %get-tuple-element.52), channel_id=1, source_target_pairs={{8,22},{9,23},{10,20},{11,21},{12,18},{13,19},{14,16},{15,17},{16,... | collective-permute-start | bytes 98312 | tf_op jit(solution)/shard_map/ppermute | solution.py:442
  28.7 2.0 %collective-permute-done.12.rest_1_ = bf16[8,16,128]{2,1,0:T(8,128)(2,1)S(1)} collective-permute-done((bf16[8,16,128]{2,1,0:T(8,128)(2,1)S(1)}, bf16[8,16,128]{2,1,0:T(8,128)(2,1)S(1)}, u32[]{:S(2)}, u32[]{:S(2)}) %collective-permute-start.12) | collective-permute-done | bytes 32800 | tf_op jit(solution)/shard_map/ppermute | solution.py:442
  34.0 14.0 %collective-permute-start.17 = (bf16[8,16,128]{2,1,0:T(8,128)(2,1)S(1)}, bf16[8,16,128]{2,1,0:T(8,128)(2,1)S(1)}, u32[]{:S(2)}, u32[]{:S(2)}) collective-permute-start(bf16[8,16,128]{2,1,0:T(8,128)(2,1)S(1)} %get-tuple-element.55), channel_id=1, source_target_pairs={{16,30},{17,31},{18,28},{19,29},{20,26},{21,27},{22,24},{23,25},{2... | collective-permute-start | bytes 98312 | tf_op jit(solution)/shard_map/ppermute | solution.py:442
  49.5 2.8 %collective-permute-done.19.rest_2_ = bf16[2,8,16,128]{3,2,1,0:T(8,128)(2,1)S(1)} collective-permute-done((bf16[2,8,16,128]{3,2,1,0:T(8,128)(2,1)S(1)}, bf16[2,8,16,128]{3,2,1,0:T(8,128)(2,1)S(1)}, u32[]{:S(2)}, u32[]{:S(2)}) %collective-permute-start.19) | collective-permute-done | bytes 65568 | tf_op jit(solution)/shard_map/ppermute | solution.py:442
  54.2 1.4 %collective-permute-start.21 = (bf16[8,16,128]{2,1,0:T(8,128)(2,1)S(1)}, bf16[8,16,128]{2,1,0:T(8,128)(2,1)S(1)}, u32[]{:S(2)}, u32[]{:S(2)}) collective-permute-start(bf16[8,16,128]{2,1,0:T(8,128)(2,1)S(1)} %get-tuple-element.57.rest_0_), channel_id=1, source_target_pairs={{0,6},{1,7},{2,4},{3,5},{4,2},{5,3},{6,0},{7,1},{8,14},{9,15},{10,... | collective-permute-start | bytes 98312 | tf_op jit(solution)/shard_map/ppermute | solution.py:442
  56.8 2.3 %collective-permute-done.21.rest_1_ = bf16[8,16,128]{2,1,0:T(8,128)(2,1)S(1)} collective-permute-done((bf16[8,16,128]{2,1,0:T(8,128)(2,1)S(1)}, bf16[8,16,128]{2,1,0:T(8,128)(2,1)S(1)}, u32[]{:S(2)}, u32[]{:S(2)}) %collective-permute-start.21) | collective-permute-done | bytes 32800 | tf_op jit(solution)/shard_map/ppermute | solution.py:442
  61.4 1.5 %collective-permute-start.26 = (bf16[8,16,128]{2,1,0:T(8,128)(2,1)S(1)}, bf16[8,16,128]{2,1,0:T(8,128)(2,1)S(1)}, u32[]{:S(2)}, u32[]{:S(2)}) collective-permute-start(bf16[8,16,128]{2,1,0:T(8,128)(2,1)S(1)} %get-tuple-element.60), channel_id=1, source_target_pairs={{24,22},{25,23},{26,20},{27,21},{28,18},{29,19},{30,16},{31,17},{1... | collective-permute-start | bytes 98312 | tf_op jit(solution)/shard_map/ppermute | solution.py:442
  64.2 2.0 %collective-permute-done.26.rest_1_ = bf16[8,16,128]{2,1,0:T(8,128)(2,1)S(1)} collective-permute-done((bf16[8,16,128]{2,1,0:T(8,128)(2,1)S(1)}, bf16[8,16,128]{2,1,0:T(8,128)(2,1)S(1)}, u32[]{:S(2)}, u32[]{:S(2)}) %collective-permute-start.26) | collective-permute-done | bytes 32800 | tf_op jit(solution)/shard_map/ppermute | solution.py:442
  69.2 10.2 %collective-permute-start.31 = (bf16[8,16,128]{2,1,0:T(8,128)(2,1)S(1)}, bf16[8,16,128]{2,1,0:T(8,128)(2,1)S(1)}, u32[]{:S(2)}, u32[]{:S(2)}) collective-permute-start(bf16[8,16,128]{2,1,0:T(8,128)(2,1)S(1)} %get-tuple-element.64), channel_id=1, source_target_pairs={{16,14},{17,15},{18,12},{19,13},{20,10},{21,11},{22,8},{23,9},{8,6... | collective-permute-start | bytes 98312 | tf_op jit(solution)/shard_map/ppermute | solution.py:442
  81.0 2.8 %collective-permute-done.33.rest_2_ = bf16[2,8,16,128]{3,2,1,0:T(8,128)(2,1)S(1)} collective-permute-done((bf16[2,8,16,128]{3,2,1,0:T(8,128)(2,1)S(1)}, bf16[2,8,16,128]{3,2,1,0:T(8,128)(2,1)S(1)}, u32[]{:S(2)}, u32[]{:S(2)}) %collective-permute-start.33) | collective-permute-done | bytes 65568 | tf_op jit(solution)/shard_map/ppermute | solution.py:442
  85.9 5.5 %collective-permute-start.35 = (bf16[16,16,128]{2,1,0:T(8,128)(2,1)S(1)}, bf16[16,16,128]{2,1,0:T(8,128)(2,1)S(1)}, u32[]{:S(2)}, u32[]{:S(2)}) collective-permute-start(bf16[16,16,128]{2,1,0:T(8,128)(2,1)S(1)} %get-tuple-element.67), channel_id=1, source_target_pairs={{8,0},{9,1},{10,2},{11,3},{12,4},{13,5},{14,6},{15,7},{0,8},{1,9},... | collective-permute-start | bytes 196616 | tf_op jit(solution)/shard_map/ppermute | solution.py:442
  91.4 1.6 %collective-permute-start.38 = (bf16[2,8,16,128]{3,2,1,0:T(8,128)(2,1)S(1)}, bf16[2,8,16,128]{3,2,1,0:T(8,128)(2,1)S(1)}, u32[]{:S(2)}, u32[]{:S(2)}) collective-permute-start(bf16[2,8,16,128]{3,2,1,0:T(8,128)(2,1)S(1)} %pad_maximum_fusion.13), channel_id=1, source_target_pairs={{8,2},{9,5},{10,0},{11,7},{12,6},{13,1},{14,4},{15,3},{0,10},{1,13... | collective-permute-start | bytes 196616 | tf_op jit(solution)/shard_map/ppermute | solution.py:442
  93.1 1.7 %collective-permute-done.35.rest_0_.rest_5_ = bf16[16,16,128]{2,1,0:T(8,128)(2,1)S(1)} collective-permute-done((bf16[16,16,128]{2,1,0:T(8,128)(2,1)S(1)}, bf16[16,16,128]{2,1,0:T(8,128)(2,1)S(1)}, u32[]{:S(2)}, u32[]{:S(2)}) %collective-permute-start.35) | collective-permute-done | bytes 65568 | tf_op jit(solution)/shard_map/ppermute | solution.py:442
  94.8 1.9 %collective-permute-done.38.rest_2_ = bf16[2,8,16,128]{3,2,1,0:T(8,128)(2,1)S(1)} collective-permute-done((bf16[2,8,16,128]{3,2,1,0:T(8,128)(2,1)S(1)}, bf16[2,8,16,128]{3,2,1,0:T(8,128)(2,1)S(1)}, u32[]{:S(2)}, u32[]{:S(2)}) %collective-permute-start.38) | collective-permute-done | bytes 65568 | tf_op jit(solution)/shard_map/ppermute | solution.py:442
  98.1 3.3 %backward_section_0.1 = f32[2,16,1024]{2,1,0:T(8,128)} custom-call(s32[8,128]{1,0:T(8,128)S(1)} %get-tuple-element.38.layers, bf16[2,512,4096]{2,1,0:T(8,128)(2,1)S(1)} %get-tuple-element.40.first_inverse, bf16[2,512,4096]{2,1,0:T(8,128)(2,1)S(1)} %get-tuple-element.56.second_inverse, f32[40,1024]{1,0:T(8,128)S(1)} %get-tuple-element.39.local.packet, ...), custom_call_target="tpu_custom_call" | custom-call | tf_op jit(solution)/shard_map/backward_section_0/pallas_call | solution.py:390
  (90 shorter events, 26.1 us)
Async XLA Ops:
  1.5 3.2 %collective-permute-start.1 = (bf16[8,16,128]{2,1,0:T(8,128)(2,1)S(1)}, bf16[8,16,128]{2,1,0:T(8,128)(2,1)S(1)}, u32[]{:S(2)}, u32[]{:S(2)}) collective-permute-start(bf16[8,16,128]{2,1,0:T(8,128)(2,1)S(1)} %get-tuple-element.43.refs_0_.rest_0_), channel_id=1, source_target_pairs={{0,1},{1,0},{2,3},{3,2},{4,5},{5,4},{6,7},{7,6},{8,9},{9,8},{10,11... | collective-permute-start | bytes 98312 | tf_op jit(solution)/shard_map/ppermute | solution.py:442
  2.0 9.1 %collective-permute-start.3 = (f32[24,1024]{1,0:T(8,128)S(1)}, f32[24,1024]{1,0:T(8,128)S(1)}, u32[]{:S(2)}, u32[]{:S(2)}) collective-permute-start(f32[24,1024]{1,0:T(8,128)S(1)} %get-tuple-element.44), channel_id=1, source_target_pairs={{0,8},{1,9},{2,10},{3,11},{4,12},{5,13},{6,14},{7,15},{16,24},{17,... | collective-permute-start | bytes 294920 | tf_op jit(solution)/shard_map/ppermute | solution.py:442
  4.7 6.5 %collective-permute-start.2 = (bf16[2,8,16,128]{3,2,1,0:T(8,128)(2,1)S(1)}, bf16[2,8,16,128]{3,2,1,0:T(8,128)(2,1)S(1)}, u32[]{:S(2)}, u32[]{:S(2)}) collective-permute-start(bf16[2,8,16,128]{3,2,1,0:T(8,128)(2,1)S(1)} %pad_maximum_fusion.6), channel_id=1, source_target_pairs={{0,2},{1,5},{2,0},{3,7},{4,6},{5,1},{6,4},{7,3},{8,10},{9,13},{10,... | collective-permute-start | bytes 196616 | tf_op jit(solution)/shard_map/ppermute | solution.py:442
  6.2 4.9 %collective-permute-start = (bf16[8,16,128]{2,1,0:T(8,128)(2,1)S(1)}, bf16[8,16,128]{2,1,0:T(8,128)(2,1)S(1)}, u32[]{:S(2)}, u32[]{:S(2)}) collective-permute-start(bf16[8,16,128]{2,1,0:T(8,128)(2,1)S(1)} %get-tuple-element.43.refs_0_.rest_0_), channel_id=1, source_target_pairs={{0,6},{1,7},{2,4},{3,5},{4,2},{5,3},{6,0},{7,1},{8,14},{9,15},{10,... | collective-permute-start | bytes 98312 | tf_op jit(solution)/shard_map/ppermute | solution.py:442
  15.8 8.2 %collective-permute-start.10 = (f32[40,1024]{1,0:T(8,128)S(1)}, f32[40,1024]{1,0:T(8,128)S(1)}, u32[]{:S(2)}, u32[]{:S(2)}) collective-permute-start(f32[40,1024]{1,0:T(8,128)S(1)} %get-tuple-element.49), channel_id=1, source_target_pairs={{8,16},{9,17},{10,18},{11,19},{12,20},{13,21},{14,22},{15,23},{16,... | collective-permute-start | bytes 491528 | tf_op jit(solution)/shard_map/ppermute | solution.py:442
  16.1 6.6 %collective-permute-start.6 = (bf16[8,16,128]{2,1,0:T(8,128)(2,1)S(1)}, bf16[8,16,128]{2,1,0:T(8,128)(2,1)S(1)}, u32[]{:S(2)}, u32[]{:S(2)}) collective-permute-start(bf16[8,16,128]{2,1,0:T(8,128)(2,1)S(1)} %get-tuple-element.48), channel_id=1, source_target_pairs={{0,14},{1,15},{2,12},{3,13},{4,10},{5,11},{6,8},{7,9},{8,22},{9,23... | collective-permute-start | bytes 98312 | tf_op jit(solution)/shard_map/ppermute | solution.py:442
  17.1 5.5 %collective-permute-start.5 = (bf16[16,16,128]{2,1,0:T(8,128)(2,1)S(1)}, bf16[16,16,128]{2,1,0:T(8,128)(2,1)S(1)}, u32[]{:S(2)}, u32[]{:S(2)}) collective-permute-start(bf16[16,16,128]{2,1,0:T(8,128)(2,1)S(1)} %get-tuple-element.47), channel_id=1, source_target_pairs={{0,8},{1,9},{2,10},{3,11},{4,12},{5,13},{6,14},{7,15},{8,0},{9,1},... | collective-permute-start | bytes 196616 | tf_op jit(solution)/shard_map/ppermute | solution.py:442
  17.1 6.8 %collective-permute-start.8 = (bf16[2,8,16,128]{3,2,1,0:T(8,128)(2,1)S(1)}, bf16[2,8,16,128]{3,2,1,0:T(8,128)(2,1)S(1)}, u32[]{:S(2)}, u32[]{:S(2)}) collective-permute-start(bf16[2,8,16,128]{3,2,1,0:T(8,128)(2,1)S(1)} %pad_maximum_fusion.7), channel_id=1, source_target_pairs={{0,10},{1,13},{2,8},{3,15},{4,14},{5,9},{6,12},{7,11},{8,2},{9,5},... | collective-permute-start | bytes 196616 | tf_op jit(solution)/shard_map/ppermute | solution.py:442
  25.9 4.8 %collective-permute-start.12 = (bf16[8,16,128]{2,1,0:T(8,128)(2,1)S(1)}, bf16[8,16,128]{2,1,0:T(8,128)(2,1)S(1)}, u32[]{:S(2)}, u32[]{:S(2)}) collective-permute-start(bf16[8,16,128]{2,1,0:T(8,128)(2,1)S(1)} %get-tuple-element.52), channel_id=1, source_target_pairs={{8,22},{9,23},{10,20},{11,21},{12,18},{13,19},{14,16},{15,17},{16,... | collective-permute-start | bytes 98312 | tf_op jit(solution)/shard_map/ppermute | solution.py:442
  27.6 4.3 %collective-permute-start.14 = (bf16[2,8,16,128]{3,2,1,0:T(8,128)(2,1)S(1)}, bf16[2,8,16,128]{3,2,1,0:T(8,128)(2,1)S(1)}, u32[]{:S(2)}, u32[]{:S(2)}) collective-permute-start(bf16[2,8,16,128]{3,2,1,0:T(8,128)(2,1)S(1)} %pad_maximum_fusion.8), channel_id=1, source_target_pairs={{8,18},{9,21},{10,16},{11,23},{12,22},{13,17},{14,20},{15,19},{16,... | collective-permute-start | bytes 196616 | tf_op jit(solution)/shard_map/ppermute | solution.py:442
  33.7 14.3 %collective-permute-start.18 = (bf16[8,16,128]{2,1,0:T(8,128)(2,1)S(1)}, bf16[8,16,128]{2,1,0:T(8,128)(2,1)S(1)}, u32[]{:S(2)}, u32[]{:S(2)}) collective-permute-start(bf16[8,16,128]{2,1,0:T(8,128)(2,1)S(1)} %get-tuple-element.55), channel_id=1, source_target_pairs={{0,1},{1,0},{2,3},{3,2},{4,5},{5,4},{6,7},{7,6},{8,9},{9,8},{10,11... | collective-permute-start | bytes 98312 | tf_op jit(solution)/shard_map/ppermute | solution.py:442
  34.0 15.6 %collective-permute-start.17 = (bf16[8,16,128]{2,1,0:T(8,128)(2,1)S(1)}, bf16[8,16,128]{2,1,0:T(8,128)(2,1)S(1)}, u32[]{:S(2)}, u32[]{:S(2)}) collective-permute-start(bf16[8,16,128]{2,1,0:T(8,128)(2,1)S(1)} %get-tuple-element.55), channel_id=1, source_target_pairs={{16,30},{17,31},{18,28},{19,29},{20,26},{21,27},{22,24},{23,25},{2... | collective-permute-start | bytes 98312 | tf_op jit(solution)/shard_map/ppermute | solution.py:442
  48.0 4.3 %collective-permute-start.19 = (bf16[2,8,16,128]{3,2,1,0:T(8,128)(2,1)S(1)}, bf16[2,8,16,128]{3,2,1,0:T(8,128)(2,1)S(1)}, u32[]{:S(2)}, u32[]{:S(2)}) collective-permute-start(bf16[2,8,16,128]{3,2,1,0:T(8,128)(2,1)S(1)} %pad_maximum_fusion.9), channel_id=1, source_target_pairs={{16,26},{17,29},{18,24},{19,31},{20,30},{21,25},{22,28},{23,27},{2... | collective-permute-start | bytes 196616 | tf_op jit(solution)/shard_map/ppermute | solution.py:442
  54.2 4.9 %collective-permute-start.21 = (bf16[8,16,128]{2,1,0:T(8,128)(2,1)S(1)}, bf16[8,16,128]{2,1,0:T(8,128)(2,1)S(1)}, u32[]{:S(2)}, u32[]{:S(2)}) collective-permute-start(bf16[8,16,128]{2,1,0:T(8,128)(2,1)S(1)} %get-tuple-element.57.rest_0_), channel_id=1, source_target_pairs={{0,6},{1,7},{2,4},{3,5},{4,2},{5,3},{6,0},{7,1},{8,14},{9,15},{10,... | collective-permute-start | bytes 98312 | tf_op jit(solution)/shard_map/ppermute | solution.py:442
  55.7 4.0 %collective-permute-start.23 = (bf16[2,4,16,128]{3,2,1,0:T(8,128)(2,1)S(1)}, bf16[2,4,16,128]{3,2,1,0:T(8,128)(2,1)S(1)}, u32[]{:S(2)}, u32[]{:S(2)}) collective-permute-start(bf16[2,4,16,128]{3,2,1,0:T(8,128)(2,1)S(1)} %pad_maximum_fusion.14), channel_id=1, source_target_pairs={{0,2},{1,5},{2,0},{3,7},{4,6},{5,1},{6,4},{7,3},{8,10},{9,13},{10,... | collective-permute-start | bytes 98312 | tf_op jit(solution)/shard_map/ppermute | solution.py:442
  61.4 4.8 %collective-permute-start.26 = (bf16[8,16,128]{2,1,0:T(8,128)(2,1)S(1)}, bf16[8,16,128]{2,1,0:T(8,128)(2,1)S(1)}, u32[]{:S(2)}, u32[]{:S(2)}) collective-permute-start(bf16[8,16,128]{2,1,0:T(8,128)(2,1)S(1)} %get-tuple-element.60), channel_id=1, source_target_pairs={{24,22},{25,23},{26,20},{27,21},{28,18},{29,19},{30,16},{31,17},{1... | collective-permute-start | bytes 98312 | tf_op jit(solution)/shard_map/ppermute | solution.py:442
  63.0 4.3 %collective-permute-start.28 = (bf16[2,8,16,128]{3,2,1,0:T(8,128)(2,1)S(1)}, bf16[2,8,16,128]{3,2,1,0:T(8,128)(2,1)S(1)}, u32[]{:S(2)}, u32[]{:S(2)}) collective-permute-start(bf16[2,8,16,128]{3,2,1,0:T(8,128)(2,1)S(1)} %pad_maximum_fusion.11), channel_id=1, source_target_pairs={{24,18},{25,21},{26,16},{27,23},{28,22},{29,17},{30,20},{31,19},{1... | collective-permute-start | bytes 196616 | tf_op jit(solution)/shard_map/ppermute | solution.py:442
  69.0 10.4 %collective-permute-start.32 = (bf16[8,16,128]{2,1,0:T(8,128)(2,1)S(1)}, bf16[8,16,128]{2,1,0:T(8,128)(2,1)S(1)}, u32[]{:S(2)}, u32[]{:S(2)}) collective-permute-start(bf16[8,16,128]{2,1,0:T(8,128)(2,1)S(1)} %get-tuple-element.64), channel_id=1, source_target_pairs={{0,1},{1,0},{2,3},{3,2},{4,5},{5,4},{6,7},{7,6},{8,9},{9,8},{10,11... | collective-permute-start | bytes 98312 | tf_op jit(solution)/shard_map/ppermute | solution.py:442
  69.2 11.8 %collective-permute-start.31 = (bf16[8,16,128]{2,1,0:T(8,128)(2,1)S(1)}, bf16[8,16,128]{2,1,0:T(8,128)(2,1)S(1)}, u32[]{:S(2)}, u32[]{:S(2)}) collective-permute-start(bf16[8,16,128]{2,1,0:T(8,128)(2,1)S(1)} %get-tuple-element.64), channel_id=1, source_target_pairs={{16,14},{17,15},{18,12},{19,13},{20,10},{21,11},{22,8},{23,9},{8,6... | collective-permute-start | bytes 98312 | tf_op jit(solution)/shard_map/ppermute | solution.py:442
  79.5 4.3 %collective-permute-start.33 = (bf16[2,8,16,128]{3,2,1,0:T(8,128)(2,1)S(1)}, bf16[2,8,16,128]{3,2,1,0:T(8,128)(2,1)S(1)}, u32[]{:S(2)}, u32[]{:S(2)}) collective-permute-start(bf16[2,8,16,128]{3,2,1,0:T(8,128)(2,1)S(1)} %pad_maximum_fusion.12), channel_id=1, source_target_pairs={{16,10},{17,13},{18,8},{19,15},{20,14},{21,9},{22,12},{23,11},{8,1... | collective-permute-start | bytes 196616 | tf_op jit(solution)/shard_map/ppermute | solution.py:442
  85.7 5.8 %collective-permute-start.37 = (bf16[8,16,128]{2,1,0:T(8,128)(2,1)S(1)}, bf16[8,16,128]{2,1,0:T(8,128)(2,1)S(1)}, u32[]{:S(2)}, u32[]{:S(2)}) collective-permute-start(bf16[8,16,128]{2,1,0:T(8,128)(2,1)S(1)} %get-tuple-element.68), channel_id=1, source_target_pairs={{0,1},{1,0},{2,3},{3,2},{4,5},{5,4},{6,7},{7,6},{8,9},{9,8},{10,11... | collective-permute-start | bytes 98312 | tf_op jit(solution)/shard_map/ppermute | solution.py:442
  85.9 8.9 %collective-permute-start.36 = (bf16[8,16,128]{2,1,0:T(8,128)(2,1)S(1)}, bf16[8,16,128]{2,1,0:T(8,128)(2,1)S(1)}, u32[]{:S(2)}, u32[]{:S(2)}) collective-permute-start(bf16[8,16,128]{2,1,0:T(8,128)(2,1)S(1)} %get-tuple-element.68), channel_id=1, source_target_pairs={{8,6},{9,7},{10,4},{11,5},{12,2},{13,3},{14,0},{15,1},{0,30},{1,31... | collective-permute-start | bytes 98312 | tf_op jit(solution)/shard_map/ppermute | solution.py:442
  85.9 8.9 %collective-permute-start.35 = (bf16[16,16,128]{2,1,0:T(8,128)(2,1)S(1)}, bf16[16,16,128]{2,1,0:T(8,128)(2,1)S(1)}, u32[]{:S(2)}, u32[]{:S(2)}) collective-permute-start(bf16[16,16,128]{2,1,0:T(8,128)(2,1)S(1)} %get-tuple-element.67), channel_id=1, source_target_pairs={{8,0},{9,1},{10,2},{11,3},{12,4},{13,5},{14,6},{15,7},{0,8},{1,9},... | collective-permute-start | bytes 196616 | tf_op jit(solution)/shard_map/ppermute | solution.py:442
  91.4 5.2 %collective-permute-start.38 = (bf16[2,8,16,128]{3,2,1,0:T(8,128)(2,1)S(1)}, bf16[2,8,16,128]{3,2,1,0:T(8,128)(2,1)S(1)}, u32[]{:S(2)}, u32[]{:S(2)}) collective-permute-start(bf16[2,8,16,128]{3,2,1,0:T(8,128)(2,1)S(1)} %pad_maximum_fusion.13), channel_id=1, source_target_pairs={{8,2},{9,5},{10,0},{11,7},{12,6},{13,1},{14,4},{15,3},{0,10},{1,13... | collective-permute-start | bytes 196616 | tf_op jit(solution)/shard_map/ppermute | solution.py:442
  (16 other events, 23.1 us)
